TPU v7x, 32 devices: a whole 2x2x4 slice. The times are simulated.
32 devices in a mesh: copy: 2 (over x), ctx: 8 (over z, y), tp: 2 (over core).
Axes of the slice: x: 2, y: 2, z: 4, core: 2. Of those that a mesh axis runs over, the one named last changes fastest.
Arguments:
- clean_tokens: bfloat16 [2048, 4096], P('ctx', 'copy'), may hold values from -36 to 36
- norm_gain: bfloat16 [4096], replicated, may hold values from 0.5 to 1.5
- mask_embed: bfloat16 [4096], replicated, may hold values from -6 to 6
- time_shift: float32 [4096], replicated, may hold values from -0.5 to 0.5
- w_query: bfloat16 [4096, 2048], P(None, 'tp'), may hold values from -0.09375 to 0.09375
- w_key: bfloat16 [4096, 512], P(None, 'tp'), may hold values from -0.09375 to 0.09375
- w_value: bfloat16 [4096, 512], P(None, 'tp'), may hold values from -0.09375 to 0.09375
- w_out: bfloat16 [2048, 4096], P('tp'), may hold values from -0.125 to 0.125
- q_gain: float32 [128], replicated, may hold values from 2 to 3
- k_gain: float32 [128], replicated, may hold values from 0.5 to 1.5
- masked: int32 [2, 2048], P('copy', 'ctx'), may hold values 0 or 1
- block_live: int32 [2, 32], P('copy', 'ctx'), may hold values 0 or 1
- timesteps: int32 [2], P('copy'), may hold values from 1 to 1000
Outputs:
- clean_out: bfloat16 [2048, 4096], P('ctx', 'tp')
- noised_out: bfloat16 [2, 2048, 4096], P('copy', 'ctx', 'tp')
All inputs are finite; a program needn't handle non-finite values. No bound on the sum of `masked` or of `block_live` on one device may be relied on, other than what follows from the above.
Results may differ from a plain program's by a relative error of at most 0.012.
The roundings to bfloat16 on the way count: a program that leaves them out, or rounds other values in their place, can miss the bound.
Values may be sent and summed in bfloat16 or wider, within the bound.
No kernel may reach another device: no remote copies, remote signals or barrier semaphores. Data moves between devices by JAX's collectives and lax.ppermute only.
A program may use at most 320 MiB of HBM per device.

v0:
```python
import math

import jax
import jax.numpy as jnp
from jax import lax
from jax.sharding import PartitionSpec as P

HD = 128
BLK = 64
TSTEPS = 1000


EPS = 1e-06


def inverse_rms(values):
    return lax.rsqrt(jnp.mean(values * values, axis=-1, keepdims=True) + EPS)


def key_terms(state, queries, query_start, key_piece, value_piece, key_start):
    numerator, denominator = state
    streams_count, row_count, kv_local, group_size, head_dim = queries.shape
    piece_rows = key_piece.shape[0]
    key_heads = key_piece.reshape(piece_rows, kv_local, head_dim)
    value_heads = value_piece.reshape(piece_rows, kv_local, head_dim)

    def compute():
        scores = jnp.einsum(
            "srhgd,khd->srhgk", queries, key_heads, preferred_element_type=jnp.float32
        ) * (1.0 / math.sqrt(head_dim))
        query_blocks = (query_start + jnp.arange(row_count, dtype=jnp.int32)) // BLK
        key_blocks = jnp.arange(piece_rows, dtype=jnp.int32) // BLK
        offset = jnp.minimum(jnp.arange(streams_count, dtype=jnp.int32), 1)
        allowed = key_blocks[None, None, :] + offset[:, None, None] <= query_blocks[None, :, None]
        weights = jnp.where(allowed[:, :, None, None, :], jnp.exp(scores), 0.0)
        updated = jnp.einsum(
            "srhgk,khd->srhgd",
            weights.astype(jnp.bfloat16),
            value_heads,
            preferred_element_type=jnp.float32,
        )
        return (updated, jnp.sum(weights, axis=4))

    def unchanged():
        return (numerator, denominator)

    needed = key_start // BLK <= (query_start + row_count - 1) // BLK
    return lax.cond(needed, compute, unchanged)


def own_block(queries, key_heads, value_heads):
    copies, row_count, kv_local, group_size, head_dim = queries.shape
    count_blocks = row_count // BLK
    query_blocks = queries.reshape(copies, count_blocks, BLK, kv_local, group_size, head_dim)
    key_blocks = key_heads.reshape(copies, count_blocks, BLK, kv_local, head_dim)
    value_blocks = value_heads.reshape(copies, count_blocks, BLK, kv_local, head_dim)
    scores = jnp.einsum(
        "cbqhgd,cbkhd->cbqhgk", query_blocks, key_blocks, preferred_element_type=jnp.float32
    ) * (1.0 / math.sqrt(head_dim))
    weights = jnp.exp(scores)
    numerator = jnp.einsum(
        "cbqhgk,cbkhd->cbqhgd",
        weights.astype(jnp.bfloat16),
        value_blocks,
        preferred_element_type=jnp.float32,
    )
    denominator = jnp.sum(weights, axis=5)
    return (
        numerator.reshape(copies, row_count, kv_local, group_size, head_dim),
        denominator.reshape(copies, row_count, kv_local, group_size),
    )


def on_device(
    clean_tokens,
    norm_gain,
    mask_embed,
    time_shift,
    w_query,
    w_key,
    w_value,
    w_out,
    q_gain,
    k_gain,
    masked,
    block_live,
    timesteps,
):
    features = lax.all_gather(clean_tokens, "copy", axis=1, tiled=True)
    local_rows = features.shape[0]
    width = features.shape[1]
    copies = masked.shape[0]
    streams_count = 1 + copies
    kv_local = w_key.shape[1] // HD
    heads_local = w_query.shape[1] // HD
    group_size = heads_local // kv_local
    features_wide = features.astype(jnp.float32)
    gain_wide = norm_gain.astype(jnp.float32)
    normed_clean = (features_wide * inverse_rms(features_wide) * gain_wide).astype(jnp.bfloat16)
    noisy_tokens = jnp.where(
        masked[:, :, None] == 1, mask_embed[None, None, :], features[None, :, :]
    )
    noisy_wide = noisy_tokens.astype(jnp.float32)
    condition = (
        1.0 + timesteps.astype(jnp.float32)[:, None, None] / TSTEPS * time_shift[None, None, :]
    )
    normed_noisy = (noisy_wide * inverse_rms(noisy_wide) * gain_wide * condition).astype(
        jnp.bfloat16
    )
    all_rows = jnp.concatenate([normed_clean[None], normed_noisy], axis=0).reshape(-1, width)
    query_wide = jnp.dot(all_rows, w_query, preferred_element_type=jnp.float32).reshape(
        streams_count, local_rows, kv_local, group_size, HD
    )
    queries = (query_wide * inverse_rms(query_wide) * q_gain).astype(jnp.bfloat16)
    key_wide = jnp.dot(all_rows, w_key, preferred_element_type=jnp.float32).reshape(
        streams_count, local_rows, kv_local, HD
    )
    key_heads = (key_wide * inverse_rms(key_wide) * k_gain).astype(jnp.bfloat16)
    value_heads = (
        jnp.dot(all_rows, w_value, preferred_element_type=jnp.float32)
        .astype(jnp.bfloat16)
        .reshape(streams_count, local_rows, kv_local, HD)
    )
    clean_keys = key_heads[0].reshape(local_rows, kv_local * HD)
    clean_values = value_heads[0].reshape(local_rows, kv_local * HD)
    position = lax.axis_index("ctx")
    first_row = position * local_rows
    groups = ((queries, first_row, key_heads[1:], value_heads[1:]),)
    initial = tuple(
        (
            (jnp.zeros(member[0].shape, jnp.float32), jnp.zeros(member[0].shape[:-1], jnp.float32))
            for member in groups
        )
    )
    piece = (
        lax.all_gather(clean_keys, "ctx", axis=0, tiled=True),
        lax.all_gather(clean_values, "ctx", axis=0, tiled=True),
    )
    key_start = jnp.int32(0)
    totals = tuple(
        (
            key_terms(
                initial[number], groups[number][0], groups[number][1], piece[0], piece[1], key_start
            )
            for number in range(len(groups))
        )
    )
    number = 0
    numerator, denominator = totals[number]
    member = groups[number]
    self_numerator, own_den = own_block(member[0][1:], member[2], member[3])
    numerator = jnp.concatenate([numerator[:1], numerator[1:] + self_numerator], axis=0)
    denominator = jnp.concatenate([denominator[:1], denominator[1:] + own_den], axis=0)
    results = (numerator / denominator[..., None]).astype(jnp.bfloat16)
    head_rows = results.reshape(streams_count * local_rows, heads_local * HD)
    mixed = lax.psum_scatter(
        jnp.dot(head_rows, w_out, preferred_element_type=jnp.float32),
        "tp",
        scatter_dimension=1,
        tiled=True,
    )
    clean_out = mixed[:local_rows].astype(jnp.bfloat16)
    live_rows = jnp.repeat(block_live, BLK, axis=1).astype(jnp.float32)
    noised_out = (
        mixed[local_rows:].reshape(copies, local_rows, -1) * live_rows[:, :, None]
    ).astype(jnp.bfloat16)
    return (clean_out, noised_out)


def solution(mesh):
    in_specs = (
        P("ctx", "copy"),
        P(),
        P(),
        P(),
        P(None, "tp"),
        P(None, "tp"),
        P(None, "tp"),
        P("tp", None),
        P(),
        P(),
        P("copy", "ctx"),
        P("copy", "ctx"),
        P("copy"),
    )
    out_specs = (P("ctx", "tp"), P("copy", "ctx", "tp"))
    return jax.shard_map(
        on_device, mesh=mesh, in_specs=in_specs, out_specs=out_specs, check_vma=False
    )
```

profile of v0, /device:TPU:25, one launch (start us, length us, event | category | flops | bytes accessed | tf_op | source)
XLA Modules:
  0.0 213.6 jit_solution(5362972125185248230)
XLA Ops:
  9.3 4.1 %copy.93 = bf16[256,4096]{1,0:T(8,128)(2,1)} copy(bf16[256,4096]{0,1:T(8,128)(2,1)} %bitcast.75) | data formatting | bytes 4194304 | tf_op jit(solution)/shard_map/dot_general | solution.py:115
  13.5 30.2 %all-gather.4.cloned.1.call-done = bf16[256,4096]{1,0:T(8,128)(2,1)} async-done(((bf16[256,2048]{1,0:T(8,128)(2,1)}), bf16[256,4096]{1,0:T(8,128)(2,1)}) %all-gather.4.cloned.1.call-update) | async-done | bytes 2097168 | tf_op jit(solution)/shard_map/all_gather | solution.py:89
  43.7 3.4 %fusion.17 = (f32[256]{0:T(256)S(1)}, f32[256]{0:T(256)S(1)}) fusion(bf16[256,4096]{1,0:T(8,128)(2,1)} %all-gather.4.cloned.1.call-done, bf16[4096]{0:T(1024)(128)(2,1)S(1)} %copy-done.8, pred[256]{0:T(512)(128)(4,1)S(1)} %compare_reduce_fusion), kind=kLoop, calls=%fused_computation.30 | loop fusion | flops 7339520 | bytes 2107648 | tf_op jit(solution)/shard_map/reduce_sum | solution.py:17
  47.1 4.2 %fusion.29 = (bf16[1,256,4096]{2,1,0:T(8,128)(2,1)S(1)}, bf16[1,256,4096]{2,1,0:T(8,128)(2,1)S(1)}) fusion(bf16[256,4096]{1,0:T(8,128)(2,1)} %all-gather.4.cloned.1.call-done, f32[4096]{0:T(1024)S(1)} %convert_element_type.72, f32[256]{0:T(256)S(1)} %get-tuple-element.57, f32[4096]{0:T(1024)S(1)} %multiply_add_fusion, f32[256]{0:T(256)S(1)} %get-tuple-element.56, ...), kind=kLoop, calls=%fused_computation.43 | loop fusion | flops 10485760 | bytes 6334720 | tf_op jit(solution)/shard_map/broadcast_in_dim | solution.py:110
  51.4 1.3 multiply_reduce_fusion.1
  53.5 0.7 copy.66
  54.3 11.3 %copy.94 = bf16[1024,4096]{1,0:T(8,128)(2,1)} copy(bf16[1024,4096]{0,1:T(8,128)(2,1)} %bitcast.72) | data formatting | bytes 16777216 | tf_op jit(solution)/shard_map/dot_general | solution.py:111
  65.7 2.6 %pad_maximum_fusion = bf16[2,256,4096]{2,1,0:T(8,128)(2,1)S(1)} fusion(bf16[1,256,4096]{2,1,0:T(8,128)(2,1)} %copy-done.3, bf16[1,256,4096]{2,1,0:T(8,128)(2,1)} %copy-done.2), kind=kLoop, calls=%fused_computation.37 | loop fusion | flops 2097152 | bytes 8388608 | tf_op jit(solution)/shard_map/concatenate | solution.py:110
  68.3 1.3 convolution_convert_fusion
  70.4 8.2 %multiply_reduce_fusion = (f32[2,256,2,4]{1,3,2,0:T(4,128)S(1)}, f32[2,256,2,4,128]{4,1,3,2,0:T(8,128)S(1)}) fusion(bf16[2,4,128,4096,1]{3,2,1,0,4:T(8,128)(2,1)} %bitcast.73, bf16[1,256,4096]{2,1,0:T(8,128)(2,1)} %copy-done.3, bf16[1,256,4096]{2,1,0:T(8,128)(2,1)} %copy-done.2), kind=kOutput, calls=%fused_computation.50 | convolution fusion | flops 4304400384 | bytes 14696448 | tf_op jit(solution)/shard_map/dot_general | solution.py:111
  80.8 10.6 %all-gather.6.cloned.1.call-done = bf16[2048,256]{1,0:T(8,128)(2,1)} async-done(((bf16[256,256]{1,0:T(8,128)(2,1)}), bf16[2048,256]{1,0:T(8,128)(2,1)}) %all-gather.6.cloned.1.call-update) | async-done | bytes 1048592 | tf_op jit(solution)/shard_map/all_gather | solution.py:136
  91.4 41.6 %all-gather.8.cloned.1.call-done = bf16[2048,256]{1,0:T(8,128)(2,1)} async-done(((bf16[256,256]{1,0:T(8,128)(2,1)}), bf16[2048,256]{1,0:T(8,128)(2,1)}) %all-gather.8.cloned.1.call-update) | async-done | bytes 1048592 | tf_op jit(solution)/shard_map/all_gather | solution.py:137
  133.1 36.3 %conditional.1 = (f32[2,256,2,4,128]{4,1,3,0,2:T(8,128)S(1)}, f32[2,256,2,4]{1,3,0,2:T(4,128)S(1)}) conditional(s32[]{:T(128)} %convert_element_type.70, () %tuple.16, (s32[]{:T(128)}, bf16[2048,256]{1,0:T(8,128)(2,1)}, bf16[2,256,2,4,128]{4,1,3,2,0:T(8,128)(2,1)}, bf16[2048,256]{1,0:T(8,128)(2,1)}) %tuple.45), branch_computations={%region_4.5_spmd, %region_5.7_spmd} | conditional | flops 4346368000 | bytes 88148064 | solution.py:48
  133.1 0.9 broadcast_compare_fusion
  134.1 2.5 %reshape.217 = bf16[2048,2,128]{2,1,0:T(2,128)(2,1)} reshape(bf16[2048,256]{1,0:T(8,128)(2,1)} %get-tuple-element.11) | data formatting | bytes 2097152 | tf_op jit(solution)/shard_map/reshape | solution.py:24
  136.6 15.9 %fusion = (f32[2,256,2,4]{1,3,0,2:T(4,128)S(1)}, f32[2,2048,2,256,4]{3,1,4,2,0:T(8,128)}) fusion(pred[2,256,2048]{1,2,0:T(8,128)(4,1)S(1)} %broadcast_compare_fusion, bf16[2,256,2,4,128]{4,1,3,2,0:T(8,128)(2,1)} %get-tuple-element.34, bf16[2048,2,128,1,1]{2,1,0,4,3:T(2,128)(2,1)} %bitcast.77), kind=kOutput, calls=%fused_computation.1 | convolution fusion | flops 2172645376 | bytes 36716544 | tf_op jit(solution)/shard_map/cond/branch_1_fun/srhgd,khd->srhgk/dot_general | solution.py:28
  152.5 1.1 reshape.218
  153.6 15.6 %fusion.5 = f32[2,256,2,4,128]{4,1,3,0,2:T(8,128)S(1)} fusion(f32[2,2048,2,256,4]{3,1,4,2,0:T(8,128)} %get-tuple-element.39, pred[2,256,2048]{1,2,0:T(8,128)(4,1)} %copy-done.6, bf16[2048,2,128,1,1]{2,1,0,4,3:T(2,128)(2,1)} %bitcast.78), kind=kOutput, calls=%fused_computation.6 | convolution fusion | flops 2172649472 | bytes 37748736 | tf_op jit(solution)/shard_map/cond/branch_1_fun/srhgk,khd->srhgd/dot_general | solution.py:36
  170.4 0.8 copy.80
  171.2 0.8 convert_element_type.83
  171.9 10.0 %fusion.45 = f32[512,4096]{1,0:T(8,128)} fusion(bf16[512,1024]{1,0:T(8,128)(2,1)S(1)} %convert_element_type.83, bf16[1024,4096]{1,0:T(8,128)(2,1)} %param.22), kind=kOutput, calls=%fused_computation.80 | convolution fusion | flops 4294967296 | bytes 17825792 | tf_op jit(solution)/shard_map/dot_general | solution.py:157
  182.8 18.8 %reduce-scatter.2.cloned.1.call-done = f32[512,2048]{1,0:T(8,128)} async-done(((f32[512,4096]{1,0:T(8,128)}), f32[512,2048]{1,0:T(8,128)}) %reduce-scatter.2.cloned.1.call-update) | async-done | bytes 4194320 | tf_op jit(solution)/shard_map/reduce_scatter | solution.py:156
  201.6 2.7 %slice.66 = bf16[256,2048]{1,0:T(8,128)(2,1)} slice(f32[512,2048]{1,0:T(8,128)} %reduce-scatter.2.cloned.1.call-done), slice={[0:256], [0:2048]} | slice | bytes 2097152 | tf_op jit(solution)/shard_map/slice | solution.py:162
  204.3 2.7 %fusion.34 = bf16[1,256,2048]{2,1,0:T(8,128)(2,1)} fusion(f32[512,2048]{1,0:T(8,128)} %reduce-scatter.2.cloned.1.call-done, f32[256]{0:T(256)S(1)} %convert_element_type.86), kind=kLoop, calls=%fused_computation.57 | loop fusion | flops 1048576 | bytes 3146752 | tf_op jit(solution)/shard_map/convert_element_type | solution.py:166
  (65 shorter events, 7.1 us)
Async XLA Ops:
  7.2 61.2 %copy-start = (bf16[4096,256]{1,0:T(8,128)(2,1)S(1)}, bf16[4096,256]{1,0:T(8,128)(2,1)}, u32[]{:S(2)}) copy-start(bf16[4096,256]{1,0:T(8,128)(2,1)} %param.21) | copy-start | bytes 6291460
  7.2 6.3 %copy-start.12 = (s32[1,256]{1,0:T(1,128)S(1)}, s32[1,256]{1,0:T(1,128)}, u32[]{:S(2)}) copy-start(s32[1,256]{1,0:T(1,128)} %param.25) | copy-start | bytes 3076
  7.2 6.3 %copy-start.9 = (f32[4096]{0:T(1024)S(1)}, f32[4096]{0:T(1024)}, u32[]{:S(2)}) copy-start(f32[4096]{0:T(1024)} %param.18) | copy-start | bytes 49156
  7.2 36.5 %copy-start.8 = (bf16[4096]{0:T(1024)(128)(2,1)S(1)}, bf16[4096]{0:T(1024)(128)(2,1)}, u32[]{:S(2)}) copy-start(bf16[4096]{0:T(1024)(128)(2,1)} %param.17) | copy-start | bytes 24580
  7.2 36.5 %all-gather.4.cloned.1.call-start = ((), (), s32[]{:S(2)}) async-start(), calls=%async_computation.1 | async-start | bytes 3145728 | tf_op jit(solution)/shard_map/all_gather | solution.py:89
  7.9 83.5 %all-gather.6.cloned.1.call-start = ((), (), s32[]{:S(2)}) async-start(), calls=%async_computation.2 | async-start | bytes 1179648 | tf_op jit(solution)/shard_map/all_gather | solution.py:136
  43.7 7.6 %copy-start.5 = (bf16[256,4096]{1,0:T(8,128)(2,1)S(1)}, bf16[256,4096]{1,0:T(8,128)(2,1)}, u32[]{:S(2)}) copy-start(bf16[256,4096]{1,0:T(8,128)(2,1)} %copy.93) | copy-start | bytes 6291460
  51.3 1.4 copy-start.2
  51.3 2.0 copy-start.3
  51.3 2.0 copy-start.10
  54.2 78.8 %all-gather.8.cloned.1.call-start = ((), (), s32[]{:S(2)}) async-start(), calls=%async_computation.3 | async-start | bytes 1179648 | tf_op jit(solution)/shard_map/all_gather | solution.py:137
  70.3 131.3 %reduce-scatter.2.cloned.1.call-start = ((), (), s32[]{:S(2)}) async-start(), calls=%async_computation.4 | async-start | bytes 12582912 | tf_op jit(solution)/shard_map/reduce_scatter | solution.py:156
  70.4 8.3 %copy-start.11 = (f32[128]{0:T(128)S(1)}, f32[128]{0:T(128)}, u32[]{:S(2)}) copy-start(f32[128]{0:T(128)} %param.23) | copy-start | bytes 1540
  79.4 1.0 copy-start.4
  134.1 18.4 %copy-start.6 = (pred[2,256,2048]{1,2,0:T(8,128)(4,1)}, pred[2,256,2048]{1,2,0:T(8,128)(4,1)S(1)}, u32[]{:S(2)}) copy-start(pred[2,256,2048]{1,2,0:T(8,128)(4,1)S(1)} %broadcast_compare_fusion) | copy-start | bytes 3145732 | tf_op jit(solution)/shard_map/cond
  136.6 15.9 %copy-start.7 = (bf16[2048,256]{1,0:T(8,128)(2,1)S(1)}, bf16[2048,256]{1,0:T(8,128)(2,1)}, u32[]{:S(2)}) copy-start(bf16[2048,256]{1,0:T(8,128)(2,1)} %get-tuple-element.13) | copy-start | bytes 3145732 | tf_op jit(solution)/shard_map/cond
  182.0 0.7 copy-start.13
  182.6 24.4 %copy-start.1 = (bf16[4096,256]{1,0:T(8,128)(2,1)S(1)}, bf16[4096,256]{1,0:T(8,128)(2,1)}, u32[]{:S(2)}) copy-start(bf16[4096,256]{1,0:T(8,128)(2,1)} %param.21) | copy-start | bytes 6291460
Sparse Core Ops, SparseCore 0:
  9.6 34.0 all-gather.3
  54.4 36.9 all-gather.5
  94.1 38.8 all-gather.7
  182.1 19.4 reduce-scatter.1
where the time goes:
time: 215 us; the launch traced here: 214 us
  waiting for transfers between devices  102 us (47%)
  matrix products  53.3 us (25%)
  local copies, waits for them, and re-layouts  26.7 us (12%)
  other arithmetic  16.5 us (8%)
  between operations  14.7 us (7%)
    all_gather x1, waiting for transfers between devices, on_device(): lax.all_gather(clean_values, 'ctx', axis=0, tiled=True)  41.6 us
    all_gather x1, waiting for transfers between devices, on_device(): features = lax.all_gather(clean_tokens, 'copy', axis=1, tiled=True)  30.2 us
    reduce_scatter x1, waiting for transfers between devices, on_device(): lax.psum_scatter(jnp.dot(head_rows, w_out, preferred_element_type=jnp.flo...  18.8 us
    dot_general x1, matrix products, compute(): jnp.einsum('srhgd,khd->srhgk', queries, key_heads, preferred_element_type...  15.9 us
    dot_general x1, matrix products, compute(): jnp.einsum('srhgk,khd->srhgd', weights.astype(jnp.bfloat16), value_heads,...  15.6 us
    dot_general x1, local copies, waits for them, and re-layouts, on_device(): jnp.dot(all_rows, w_query, preferred_element_type=jnp.float32)  11.3 us
    all_gather x1, waiting for transfers between devices, on_device(): lax.all_gather(clean_keys, 'ctx', axis=0, tiled=True)  10.6 us
    dot_general x1, matrix products, on_device(): jnp.dot(head_rows, w_out, preferred_element_type=jnp.float32)  10 us
  transfers between devices with their start and end apart: 4, of which 4 were waited for; matrix products, arithmetic and copies ran while one was open for 15% of the time, Pallas kernels for 0%

commit v1 on v0

v1 whole, which is shorter than its diff:
```python
import functools
import math

import jax
import jax.numpy as jnp
from jax import lax
from jax.experimental import pallas as pl
from jax.experimental.pallas import tpu as pltpu
from jax.sharding import PartitionSpec as P

HD = 128
BLK = 64
TSTEPS = 1000
EPS = 1e-06
VMEM_LIMIT = 48 * 1024 * 1024
F32 = jnp.float32
BF16 = jnp.bfloat16
SCORE_SCALE = math.log2(math.e) / math.sqrt(HD)


def to_column(row, n):
    eye = lax.broadcasted_iota(jnp.int32, (n, n), 0) == lax.broadcasted_iota(jnp.int32, (n, n), 1)
    return jnp.sum(jnp.where(eye, jnp.broadcast_to(row, (n, n)), 0.0), axis=1, keepdims=True)


def row_scales(own_ref, other_ref, mask_ref, embed_ref, width):
    n = own_ref.shape[1]
    clean = lax.rsqrt(to_column(own_ref[...] + other_ref[...], n) * (1.0 / width) + EPS)
    embed = embed_ref[...].astype(F32)
    embed_scale = lax.rsqrt(jnp.sum(embed * embed, axis=1, keepdims=True) * (1.0 / width) + EPS)
    masked = to_column(mask_ref[...].astype(F32), n)
    return clean, embed_scale, masked


def normed_clean(x, clean_scale, gain):
    return (x * clean_scale * gain).astype(BF16)


def normed_noisy(x, clean_scale, embed_scale, masked, gain, embed, condition):
    is_masked = masked == 1.0
    noisy = jnp.where(is_masked, embed, x)
    scale = jnp.where(is_masked, embed_scale, clean_scale)
    return (noisy * scale * gain * condition).astype(BF16)


def dot(a, b):
    return jnp.dot(a, b, preferred_element_type=F32)


def head_norm(wide, gain):
    scale = lax.rsqrt(jnp.mean(wide * wide, axis=1, keepdims=True) + EPS)
    return (wide * scale * gain).astype(BF16)


def kv_out(ref, wide, gain):
    ref[:, :HD] = head_norm(wide[:, :HD], gain)
    ref[:, HD:] = wide[:, HD:].astype(BF16)


def first_half_kernel(
    info, x_ref, own_ref, other_ref, mask_ref, embed_all, gain_ref, embed_ref, shift_ref,
    wq_ref, wka_ref, wva_ref, wkb_ref, wvb_ref, q_ref, a_ref, b_ref, scales, *, width,
):
    step = pl.program_id(0)
    rows = x_ref.shape[0]

    @pl.when(step == 0)
    def _():
        clean, embed_scale, masked = row_scales(own_ref, other_ref, mask_ref, embed_all, width)
        scales[:, 0:1] = clean
        scales[:, 1:2] = jnp.broadcast_to(embed_scale, clean.shape)
        scales[:, 2:3] = masked

    x = x_ref[...].astype(F32)
    gain = gain_ref[...].astype(F32)
    condition = 1.0 + info[3].astype(F32) / TSTEPS * shift_ref[...]
    clean = normed_clean(x, scales[:, 0:1], gain)
    noisy = normed_noisy(
        x, scales[:, 0:1], scales[:, 1:2], scales[:, 2:3], gain, embed_ref[...].astype(F32), condition
    )
    both = jnp.concatenate([clean, noisy], axis=0)
    q = dot(both, wq_ref[...])
    a = dot(both, jnp.concatenate([wka_ref[...], wva_ref[...]], axis=1))
    b = dot(both, jnp.concatenate([wkb_ref[...], wvb_ref[...]], axis=1))

    @pl.when(step == 0)
    def _():
        q_ref[...] = q
        a_ref[...] = a
        b_ref[...] = b

    @pl.when(step > 0)
    def _():
        q_ref[...] += q
        a_ref[...] += a
        b_ref[...] += b


def other_rows(info, xs_ref, xt_ref):
    near, far = xs_ref[...].astype(F32), xt_ref[...].astype(F32)
    first = info[1] == 0
    return jnp.concatenate([jnp.where(first, near, far), jnp.where(first, far, near)], axis=0)


def clean_kv_kernel(
    info, xs_ref, xt_ref, own_ref, other_ref, mask_ref, embed_all, gain_ref,
    wka_ref, wva_ref, wkb_ref, wvb_ref, pa_ref, pb_ref, kgain_ref, a_ref, b_ref, scales, acc, *, width,
):
    step = pl.program_id(0)

    @pl.when(step == 0)
    def _():
        clean, _, _ = row_scales(own_ref, other_ref, mask_ref, embed_all, width)
        scales[...] = clean
        acc[:, : 2 * HD] = pa_ref[...]
        acc[:, 2 * HD :] = pb_ref[...]

    x = other_rows(info, xs_ref, xt_ref)
    clean = normed_clean(x, scales[...], gain_ref[...].astype(F32))
    weights = jnp.concatenate([wka_ref[...], wva_ref[...], wkb_ref[...], wvb_ref[...]], axis=1)
    acc[...] += dot(clean, weights)

    @pl.when(step == pl.num_programs(0) - 1)
    def _():
        kv_out(a_ref, acc[:, : 2 * HD], kgain_ref[...])
        kv_out(b_ref, acc[:, 2 * HD :], kgain_ref[...])


def second_half_kernel(
    info, xs_ref, xt_ref, own_ref, other_ref, mask_ref, embed_all, gain_ref, embed_ref, shift_ref,
    wq_ref, wka_ref, wva_ref, wkb_ref, wvb_ref, pq_ref, pa_ref, pb_ref, qgain_ref, kgain_ref,
    q_ref, a_ref, b_ref, scales, acc_q, acc_kv, *, width,
):
    step = pl.program_id(0)

    @pl.when(step == 0)
    def _():
        clean, embed_scale, masked = row_scales(own_ref, other_ref, mask_ref, embed_all, width)
        scales[:, 0:1] = clean
        scales[:, 1:2] = jnp.broadcast_to(embed_scale, clean.shape)
        scales[:, 2:3] = masked
        acc_q[...] = pq_ref[...]
        acc_kv[:, : 2 * HD] = pa_ref[...]
        acc_kv[:, 2 * HD :] = pb_ref[...]

    x = other_rows(info, xs_ref, xt_ref)
    gain = gain_ref[...].astype(F32)
    condition = 1.0 + info[3].astype(F32) / TSTEPS * shift_ref[...]
    clean = normed_clean(x, scales[:, 0:1], gain)
    noisy = normed_noisy(
        x, scales[:, 0:1], scales[:, 1:2], scales[:, 2:3], gain, embed_ref[...].astype(F32), condition
    )
    acc_q[...] += dot(jnp.concatenate([clean, noisy], axis=0), wq_ref[...])
    weights = jnp.concatenate([wka_ref[...], wva_ref[...], wkb_ref[...], wvb_ref[...]], axis=1)
    acc_kv[...] += dot(noisy, weights)

    @pl.when(step == pl.num_programs(0) - 1)
    def _():
        for head in range(q_ref.shape[1] // HD):
            cols = slice(head * HD, (head + 1) * HD)
            q_ref[:, cols] = head_norm(acc_q[:, cols], qgain_ref[...])
        kv_out(a_ref, acc_kv[:, : 2 * HD], kgain_ref[...])
        kv_out(b_ref, acc_kv[:, 2 * HD :], kgain_ref[...])


def terms(q, kv_ref, mask):
    scores = lax.dot_general(
        q, kv_ref[:, :HD], (((1,), (1,)), ((), ())), preferred_element_type=F32
    )
    e = jnp.exp2(scores * SCORE_SCALE)
    if mask is not None:
        e = jnp.where(mask, e, 0.0)
    den = e[:, :HD]
    for start in range(HD, e.shape[1], HD):
        den = den + e[:, start : start + HD]
    return dot(e.astype(BF16), kv_ref[:, HD:]), den


def attention_first_kernel(info, q_ref, kv_ref, self_ref, near_ref, num_ref, den_ref):
    rows = kv_ref.shape[0]
    row_block = lax.broadcasted_iota(jnp.int32, (rows, rows), 0) // BLK
    key_block = lax.broadcasted_iota(jnp.int32, (rows, rows), 1) // BLK
    q_clean, q_noisy = q_ref[:rows], q_ref[rows:]
    num, den = terms(q_clean, kv_ref, key_block <= row_block)
    num_ref[:rows], den_ref[:rows] = num, den
    num, den = terms(q_noisy, kv_ref, key_block < row_block)
    own_num, own_den = terms(q_noisy, self_ref, key_block == row_block)
    num_ref[rows:], den_ref[rows:] = num + own_num, den + own_den

    @pl.when(info[2] % 2 == 1)
    def _():
        for part in range(2):
            cut = slice(part * rows, (part + 1) * rows)
            num, den = terms(q_ref[cut], near_ref, None)
            num_ref[cut] += num
            den_ref[cut] += den


def attention_later_kernel(info, q_ref, *refs, offsets, last):
    kv_refs = refs[: len(offsets)]
    num_in, den_in = refs[len(offsets) : len(offsets) + 2]
    rest = refs[len(offsets) + 2 :]
    num_ref, den_ref = rest[-2:]
    rows = kv_refs[0].shape[0]
    num_ref[...] = num_in[...]
    den_ref[...] = den_in[...]
    for offset, kv_ref in zip(offsets, kv_refs):
        @pl.when(jnp.bitwise_xor(info[2], offset) < info[2])
        def _(kv_ref=kv_ref):
            for part in range(2):
                cut = slice(part * rows, (part + 1) * rows)
                num, den = terms(q_ref[cut], kv_ref, None)
                num_ref[cut] += num
                den_ref[cut] += den

    if last:
        total = jnp.sum(den_ref[...], axis=1, keepdims=True)
        rest[0][...] = (num_ref[...] / total).astype(BF16)


def out_kernel(info, live, ga, gb, ha, hb, wga, wgb, wha, whb, clean_ref, noisy_ref):
    mixed = dot(ga[...], wga[...]) + dot(gb[...], wgb[...]) + dot(ha[...], wha[...]) + dot(hb[...], whb[...])
    rows = clean_ref.shape[0]
    clean_ref[...] = mixed[:rows].astype(BF16)
    for block in range(rows // BLK):
        part = mixed[rows + block * BLK : rows + (block + 1) * BLK]
        noisy_ref[block * BLK : (block + 1) * BLK] = (part * live[block].astype(F32)).astype(BF16)


def call(kernel, grid, scalars, ins, outs, scratch, arrays, flops, num_bytes, exps=0, aliases=None):
    return pl.pallas_call(
        kernel,
        grid_spec=pltpu.PrefetchScalarGridSpec(
            num_scalar_prefetch=len(scalars),
            grid=(grid,),
            in_specs=ins,
            out_specs=[spec for spec, _ in outs],
            scratch_shapes=scratch,
        ),
        out_shape=[shape for _, shape in outs],
        compiler_params=pltpu.CompilerParams(vmem_limit_bytes=VMEM_LIMIT),
        cost_estimate=pl.CostEstimate(flops=flops, bytes_accessed=num_bytes, transcendentals=exps),
        input_output_aliases=aliases or {},
    )(*scalars, *arrays)


def on_device(
    mesh, clean_tokens, norm_gain, mask_embed, time_shift, w_query, w_key, w_value, w_out,
    q_gain, k_gain, masked, block_live, timesteps,
):
    rows, half = clean_tokens.shape
    width = norm_gain.shape[0]
    heads_width = w_query.shape[1]
    part = heads_width // 2
    group = part // HD
    ctx = mesh.shape["ctx"]
    c, p, t = lax.axis_index("copy"), lax.axis_index("ctx"), lax.axis_index("tp")
    info = jnp.stack([c, t, p, timesteps[0]]).astype(jnp.int32)
    pair = [(0, 1), (1, 0)]
    cross_x = lambda v: lax.ppermute(v, "copy", pair)
    cross_core = lambda v: lax.ppermute(v, "tp", pair)
    cross_ctx = lambda v, offset: lax.ppermute(v, "ctx", [(i, i ^ offset) for i in range(ctx)])

    cut = rows // 2
    near = cross_x(lax.dynamic_slice_in_dim(clean_tokens, t * cut, cut, 0))
    wide = clean_tokens.astype(F32)
    squares = jnp.sum(wide * wide, axis=1)
    other_squares = cross_x(squares)
    far = cross_core(near)
    out_cols = w_out.shape[1] // 2
    w_far = cross_core(lax.dynamic_slice_in_dim(w_out, (1 - t) * out_cols, out_cols, 1))

    gain2, embed2, shift2 = norm_gain[None], mask_embed[None], time_shift[None]
    squares2, other2 = squares[None], other_squares[None]
    qg, kg = q_gain[None], k_gain[None]
    depth = 512
    steps = half // depth
    full = lambda shape: pl.BlockSpec(shape, lambda k, s: (0,) * len(shape))

    def depth_specs(own):
        at = (lambda k, s: s[0] * steps + k) if own else (lambda k, s: (1 - s[0]) * steps + k)
        vec = pl.BlockSpec((1, depth), lambda k, s: (0, at(k, s)))
        wq = pl.BlockSpec((depth, heads_width), lambda k, s: (at(k, s), 0))
        wa = pl.BlockSpec((depth, HD), lambda k, s: (at(k, s), s[0]))
        wb = pl.BlockSpec((depth, HD), lambda k, s: (at(k, s), 1 - s[0]))
        return vec, wq, wa, wb

    stats = [full((1, rows)), full((1, rows)), full((1, rows)), full((1, width))]
    stat_arrays = [squares2, other2, masked, embed2]
    shape = jax.ShapeDtypeStruct
    kv_shape = shape((rows, 2 * HD), BF16)

    vec, wq, wa, wb = depth_specs(True)
    pq, pa, pb = call(
        functools.partial(first_half_kernel, width=width), steps, [info],
        [pl.BlockSpec((rows, depth), lambda k, s: (0, k))] + stats + [vec, vec, vec, wq, wa, wa, wb, wb],
        [
            (full((2 * rows, heads_width)), shape((2 * rows, heads_width), F32)),
            (full((2 * rows, 2 * HD)), shape((2 * rows, 2 * HD), F32)),
            (full((2 * rows, 2 * HD)), shape((2 * rows, 2 * HD), F32)),
        ],
        [pltpu.VMEM((rows, HD), F32)],
        [clean_tokens] + stat_arrays + [gain2, embed2, shift2, w_query, w_key, w_value, w_key, w_value],
        2 * 2 * rows * half * (heads_width + 4 * HD), half * (heads_width + 4 * HD) * 2,
    )

    vec, wq, wa, wb = depth_specs(False)
    strip = pl.BlockSpec((cut, depth), lambda k, s: (0, k))
    top = pl.BlockSpec((rows, 2 * HD), lambda k, s: (0, 0))
    bottom = pl.BlockSpec((rows, 2 * HD), lambda k, s: (1, 0))
    kva, kvb = call(
        functools.partial(clean_kv_kernel, width=width), steps, [info],
        [strip, strip] + stats + [vec, wa, wa, wb, wb, top, top, full((1, HD))],
        [(top, kv_shape), (top, kv_shape)],
        [pltpu.VMEM((rows, 1), F32), pltpu.VMEM((rows, 4 * HD), F32)],
        [near, far] + stat_arrays + [gain2, w_key, w_value, w_key, w_value, pa, pb, kg],
        2 * rows * half * 4 * HD, half * 4 * HD * 2,
    )

    a = {0: kva, 1: cross_ctx(kva, 1)}
    b = {0: kvb, 1: cross_ctx(kvb, 1)}
    for offset in range(2, ctx, 2):
        a[offset] = cross_ctx(kva, offset)
    for offset in range(2, ctx, 2):
        a[offset + 1] = cross_ctx(a[offset], 1)
        b[offset] = cross_x(a[offset])
        b[offset + 1] = cross_x(a[offset + 1])

    q, sa, sb = call(
        functools.partial(second_half_kernel, width=width), steps, [info],
        [strip, strip] + stats + [vec, vec, vec, wq, wa, wa, wb, wb]
        + [full((2 * rows, heads_width)), bottom, bottom, full((1, HD)), full((1, HD))],
        [(full((2 * rows, heads_width)), shape((2 * rows, heads_width), BF16)), (top, kv_shape), (top, kv_shape)],
        [pltpu.VMEM((rows, HD), F32), pltpu.VMEM((2 * rows, heads_width), F32), pltpu.VMEM((rows, 4 * HD), F32)],
        [near, far] + stat_arrays
        + [gain2, embed2, shift2, w_query, w_key, w_value, w_key, w_value, pq, pa, pb, qg, kg],
        2 * 2 * rows * half * heads_width + 2 * rows * half * 4 * HD, half * (heads_width + 4 * HD) * 2,
    )

    def attend(which, pieces, own):
        head = lambda h, s: (0, (s[0] if which == 0 else 1 - s[0]) * group + h)
        qspec = pl.BlockSpec((2 * rows, HD), head)
        acc = pl.BlockSpec((2 * rows, HD), lambda h, s: (0, h))
        acc_shape = shape((2 * rows, part), F32)
        kv_spec = full((rows, 2 * HD))
        unit = 2 * rows * rows * group
        num, den = call(
            attention_first_kernel, group, [info], [qspec] + [kv_spec] * 3,
            [(acc, acc_shape), (acc, acc_shape)], [], [q, pieces[0], own, pieces[1]],
            3 * unit * HD * 4, 3 * rows * HD * 4, 3 * unit,
        )
        offsets = list(range(2, ctx))
        middle, final = offsets[:-2], offsets[-2:]
        if middle:
            num, den = call(
                functools.partial(attention_later_kernel, offsets=middle, last=False), group, [info],
                [qspec] + [kv_spec] * len(middle) + [acc, acc],
                [(acc, acc_shape), (acc, acc_shape)], [], [q] + [pieces[o] for o in middle] + [num, den],
                len(middle) * unit * HD * 4, len(middle) * rows * HD * 4, len(middle) * unit,
            )
        return call(
            functools.partial(attention_later_kernel, offsets=final, last=True), group, [info],
            [qspec] + [kv_spec] * len(final) + [acc, acc],
            [(acc, shape((2 * rows, part), BF16))],
            [pltpu.VMEM((2 * rows, HD), F32), pltpu.VMEM((2 * rows, HD), F32)],
            [q] + [pieces[o] for o in final] + [num, den],
            len(final) * unit * HD * 4, len(final) * rows * HD * 4, len(final) * unit,
        )[0]

    ga = attend(0, a, sa)
    ha = cross_core(ga)
    gb = attend(1, b, sb)
    hb = cross_core(gb)

    tile = 512
    tiles = out_cols // tile
    att = pl.BlockSpec((2 * rows, part), lambda n, s, l: (0, 0))
    wide_tile = lambda which, base: pl.BlockSpec(
        (part, tile),
        lambda n, s, l: (s[0] if which == 0 else 1 - s[0], s[1] * base + n),
    )
    out = pl.BlockSpec((rows, tile), lambda n, s, l: (0, n))
    clean_out, noised_out = call(
        out_kernel, tiles, [info, block_live[0]],
        [att] * 4 + [wide_tile(0, tiles), wide_tile(1, tiles), wide_tile(0, 0), wide_tile(1, 0)],
        [(out, shape((rows, out_cols), BF16)), (out, shape((rows, out_cols), BF16))], [],
        [ga, gb, ha, hb, w_out, w_out, w_far, w_far],
        2 * 2 * rows * 2 * heads_width * out_cols, 2 * heads_width * out_cols * 2,
    )
    return (clean_out, noised_out[None])


def solution(mesh):
    in_specs = (
        P("ctx", "copy"),
        P(),
        P(),
        P(),
        P(None, "tp"),
        P(None, "tp"),
        P(None, "tp"),
        P("tp", None),
        P(),
        P(),
        P("copy", "ctx"),
        P("copy", "ctx"),
        P("copy"),
    )
    out_specs = (P("ctx", "tp"), P("copy", "ctx", "tp"))
    return jax.shard_map(
        functools.partial(on_device, mesh), mesh=mesh, in_specs=in_specs, out_specs=out_specs, check_vma=False
    )
```

time: 215 us -> 120 us (0.56)
  waiting for transfers between devices: 102 us -> 22.6 us
  Pallas kernels: 0 us -> 68.2 us
  matrix products: 53.3 us -> 0 us
  local copies, waits for them, and re-layouts: 26.7 us -> 6.28 us
  starting transfers between devices: 0.16 us -> 20 us
  other arithmetic: 16.5 us -> 0.36 us
  between operations: 14.7 us -> 1.54 us
    all_gather x3 -> x0, waiting for transfers between devices: 82.5 us -> none  [the longest x1 41.6 us: on_device(): lax.all_gather(clean_values, 'ctx', axis=0, tiled=True)]
    pallas_call x0 -> x10, Pallas kernels: none -> 68.2 us  [call(): pl.pallas_call(kernel, grid_spec=pltpu.PrefetchScalarGridSpec(num_scalar_...]
    dot_general x8 -> x0, matrix products: 53.3 us -> none  [the longest x1 15.9 us: compute(): jnp.einsum('srhgd,khd->srhgk', queries, key_heads, preferred_element_type...]
    ppermute x0 -> x20, waiting for transfers between devices: none -> 22.6 us  [the longest x8 12.8 us: on_device(): cross_x = lambda v: lax.ppermute(v, 'copy', pair)]
    ppermute x0 -> x20, starting transfers between devices: none -> 20 us  [the longest x8 7.14 us: on_device(): cross_x = lambda v: lax.ppermute(v, 'copy', pair)]
    reduce_scatter x1 -> x0, waiting for transfers between devices: 18.8 us -> none  [on_device(): lax.psum_scatter(jnp.dot(head_rows, w_out, preferred_element_type=jnp.flo...]
    dot_general x2 -> x0, local copies, waits for them, and re-layouts: 15.4 us -> none  [the longest x1 11.3 us: on_device(): jnp.dot(all_rows, w_query, preferred_element_type=jnp.float32)]
    convert_element_type x6 -> x0, other arithmetic: 4.99 us -> none  [the longest x1 2.74 us: on_device(): noised_out = (mixed[local_rows:].reshape(copies, local_rows, -1) * live_r...]
  transfers between devices with their start and end apart: 4 -> 20, of which waited for: 4 -> 5; matrix products, arithmetic and copies ran while one was open for 15% -> 0% of each run, Pallas kernels for 0% -> 50%
where the time goes in v1:
time: 120 us; the launch traced here: 119 us
  Pallas kernels  68.2 us (57%)
  waiting for transfers between devices  22.6 us (19%)
  starting transfers between devices  20 us (17%)
  local copies, waits for them, and re-layouts  6.28 us (5%)
  between operations  1.54 us (1%)
    pallas_call x10, Pallas kernels, call(): pl.pallas_call(kernel, grid_spec=pltpu.PrefetchScalarGridSpec(num_scalar_...  68.2 us
    ppermute x8, waiting for transfers between devices, on_device(): cross_x = lambda v: lax.ppermute(v, 'copy', pair)  12.8 us
    ppermute x8, waiting for transfers between devices, on_device(): lax.ppermute(v, 'ctx', [(i, i ^ offset) for i in range(ctx)])  7.96 us
    ppermute x8, starting transfers between devices, on_device(): cross_x = lambda v: lax.ppermute(v, 'copy', pair)  7.14 us
    ppermute x8, starting transfers between devices, on_device(): lax.ppermute(v, 'ctx', [(i, i ^ offset) for i in range(ctx)])  6.65 us
    ppermute x4, starting transfers between devices, on_device(): cross_core = lambda v: lax.ppermute(v, 'tp', pair)  6.25 us
    dynamic_slice x1, local copies, waits for them, and re-layouts, on_device(): lax.dynamic_slice_in_dim(w_out, (1 - t) * out_cols, out_cols, 1)  4.82 us
  transfers between devices with their start and end apart: 20, of which 5 were waited for; matrix products, arithmetic and copies ran while one was open for 0% of the time, Pallas kernels for 50%

profile of v1, /device:TPU:25, one launch (start us, length us, event | category | flops | bytes accessed | tf_op | source)
XLA Modules:
  0.0 119.0 jit_solution(5199090467610696599)
XLA Ops:
  0.7 4.8 %constant_dynamic-slice_fusion = bf16[1024,2048]{1,0:T(8,128)(2,1)} fusion(bf16[1024,4096]{1,0:T(8,128)(2,1)} %wgb.1, s32[]{:T(128)S(6)} %select_n.7), kind=kLoop, calls=%fused_computation.2 | loop fusion | bytes 8388612 | tf_op jit(solution)/shard_map/dynamic_slice | solution.py:271
  6.2 1.3 %collective-permute-start = (bf16[128,2048]{1,0:T(8,128)(2,1)S(1)}, bf16[128,2048]{1,0:T(8,128)(2,1)S(1)}, u32[]{:S(2)}, u32[]{:S(2)}) collective-permute-start(bf16[128,2048]{1,0:T(8,128)(2,1)S(1)} %constant_dynamic-slice_fusion.1), channel_id=1, source_target_pairs={{0,16},{16,0},{1,17},{17,1},{2,18},{18,2},{3,19},{19,3},{4,20},{20... | collective-permute-start | bytes 1572872 | tf_op jit(solution)/shard_map/ppermute | solution.py:260
  7.5 12.3 %collective-permute-done.xs_ref = bf16[128,2048]{1,0:T(8,128)(2,1)S(1)} collective-permute-done((bf16[128,2048]{1,0:T(8,128)(2,1)S(1)}, bf16[128,2048]{1,0:T(8,128)(2,1)S(1)}, u32[]{:S(2)}, u32[]{:S(2)}) %collective-permute-start) | collective-permute-done | bytes 524320 | tf_op jit(solution)/shard_map/ppermute | solution.py:260
  20.9 1.3 %collective-permute-start.2 = (f32[256]{0:T(256)S(1)}, f32[256]{0:T(256)S(1)}, u32[]{:S(2)}, u32[]{:S(2)}) collective-permute-start(f32[256]{0:T(256)S(1)} %multiply_reduce_fusion), channel_id=1, source_target_pairs={{0,16},{16,0},{1,17},{17,1},{2,18},{18,2},{3,19},{19,3},{4,20},{20... | collective-permute-start | bytes 3080 | tf_op jit(solution)/shard_map/ppermute | solution.py:260
  23.4 8.4 %shard_map.140 = (f32[512,1024]{1,0:T(8,128)S(1)}, f32[512,256]{1,0:T(8,128)S(1)}, f32[512,256]{1,0:T(8,128)S(1)}) custom-call(s32[4]{0:T(128)S(1)} %pad_add_fusion.info, bf16[256,2048]{1,0:T(8,128)(2,1)S(1)} %copy-done.1, f32[1,256]{1,0:T(1,128)S(1)} %bitcast.12, f32[1,256]{1,0:T(1,128)S(1)} %bitcast.15, s32[1,256]{1,0:T(1,128)S(1)} %copy-done.4, ...), custom_call_target="tpu_custom_call" | custom-call | flops 3221225472 | bytes 6291456 | tf_op jit(solution)/shard_map/pallas_call | solution.py:231
  31.9 1.4 %copy-done.2 = f32[512,1024]{1,0:T(8,128)} copy-done((f32[512,1024]{1,0:T(8,128)}, f32[512,1024]{1,0:T(8,128)S(1)}, u32[]{:S(2)}) %copy-start.2) | copy-done | bytes 2097176
  33.2 4.2 %shard_map.142 = (bf16[256,256]{1,0:T(8,128)(2,1)S(1)}, bf16[256,256]{1,0:T(8,128)(2,1)S(1)}) custom-call(s32[4]{0:T(128)S(1)} %pad_add_fusion.info, bf16[128,2048]{1,0:T(8,128)(2,1)S(1)} %collective-permute-done.xs_ref, bf16[128,2048]{1,0:T(8,128)(2,1)S(1)} %collective-permute-done.1.xt_ref, f32[1,256]{1,0:T(1,128)S(1)} %bitcast.13, f32[1,256]{1,0:T(1,128)S(1)} %bitcast.16, ...), custom_call_target="tpu_custom_call" | custom-call | flops 536870912 | bytes 2097152 | tf_op jit(solution)/shard_map/pallas_call | solution.py:231
  37.5 1.3 %collective-permute-start.16 = (bf16[256,256]{1,0:T(8,128)(2,1)S(1)}, bf16[256,256]{1,0:T(8,128)(2,1)S(1)}, u32[]{:S(2)}, u32[]{:S(2)}) collective-permute-start(bf16[256,256]{1,0:T(8,128)(2,1)S(1)} %get-tuple-element.30.kv_ref), channel_id=1, source_target_pairs={{0,2},{2,0},{4,6},{6,4},{8,10},{10,8},{12,14},{14,12},{1,3},{3,1},... | collective-permute-start | bytes 393224 | tf_op jit(solution)/shard_map/ppermute | solution.py:262
  39.2 2.2 %collective-permute-done.16.near_ref = bf16[256,256]{1,0:T(8,128)(2,1)S(1)} collective-permute-done((bf16[256,256]{1,0:T(8,128)(2,1)S(1)}, bf16[256,256]{1,0:T(8,128)(2,1)S(1)}, u32[]{:S(2)}, u32[]{:S(2)}) %collective-permute-start.16) | collective-permute-done | bytes 131104 | tf_op jit(solution)/shard_map/ppermute | solution.py:262
  41.3 1.2 %collective-permute-start.3 = (bf16[256,256]{1,0:T(8,128)(2,1)S(1)}, bf16[256,256]{1,0:T(8,128)(2,1)S(1)}, u32[]{:S(2)}, u32[]{:S(2)}) collective-permute-start(bf16[256,256]{1,0:T(8,128)(2,1)S(1)} %get-tuple-element.24.kv_ref), channel_id=1, source_target_pairs={{0,12},{2,14},{4,8},{6,10},{8,4},{10,6},{12,0},{14,2},{1,13},{3,15... | collective-permute-start | bytes 393224 | tf_op jit(solution)/shard_map/ppermute | solution.py:262
  42.5 5.8 %collective-permute-done.7.refs_2_ = bf16[256,256]{1,0:T(8,128)(2,1)S(1)} collective-permute-done((bf16[256,256]{1,0:T(8,128)(2,1)S(1)}, bf16[256,256]{1,0:T(8,128)(2,1)S(1)}, u32[]{:S(2)}, u32[]{:S(2)}) %collective-permute-start.7) | collective-permute-done | bytes 131104 | tf_op jit(solution)/shard_map/ppermute | solution.py:262
  49.4 8.1 %shard_map.141 = (bf16[512,1024]{1,0:T(8,128)(2,1)S(1)}, bf16[256,256]{1,0:T(8,128)(2,1)S(1)}, bf16[256,256]{1,0:T(8,128)(2,1)S(1)}) custom-call(s32[4]{0:T(128)S(1)} %pad_add_fusion.info, bf16[128,2048]{1,0:T(8,128)(2,1)S(1)} %collective-permute-done.xs_ref, bf16[128,2048]{1,0:T(8,128)(2,1)S(1)} %collective-permute-done.1.xt_ref, f32[1,256]{1,0:T(1,128)S(1)} %bitcast.14, ...), custom_call_target="tpu_custom_call" | custom-call | flops 2684354560 | bytes 6291456 | tf_op jit(solution)/shard_map/pallas_call | solution.py:231
  57.7 1.4 %collective-permute-start.6 = (bf16[256,256]{1,0:T(8,128)(2,1)S(1)}, bf16[256,256]{1,0:T(8,128)(2,1)S(1)}, u32[]{:S(2)}, u32[]{:S(2)}) collective-permute-start(bf16[256,256]{1,0:T(8,128)(2,1)S(1)} %collective-permute-done.5.refs_0_), channel_id=1, source_target_pairs={{0,2},{2,0},{4,6},{6,4},{8,10},{10,8},{12,14},{14,12},{1,3},{3,1},... | collective-permute-start | bytes 393224 | tf_op jit(solution)/shard_map/ppermute | solution.py:262
  59.1 3.3 %shard_map.146 = (f32[512,512]{1,0:T(8,128)S(1)}, f32[512,512]{1,0:T(8,128)S(1)}) custom-call(s32[4]{0:T(128)S(1)} %pad_add_fusion.info, bf16[512,1024]{1,0:T(8,128)(2,1)S(1)} %get-tuple-element.23.q_ref, bf16[256,256]{1,0:T(8,128)(2,1)S(1)} %get-tuple-element.30.kv_ref, bf16[256,256]{1,0:T(8,128)(2,1)S(1)} %get-tuple-element.31.self_ref, ...), custom_call_target="tpu_custom_call" | custom-call | flops 805306368 | bytes 393216 | tf_op jit(solution)/shard_map/pallas_call | solution.py:231
  62.8 2.2 %collective-permute-start.4 = (bf16[256,256]{1,0:T(8,128)(2,1)S(1)}, bf16[256,256]{1,0:T(8,128)(2,1)S(1)}, u32[]{:S(2)}, u32[]{:S(2)}) collective-permute-start(bf16[256,256]{1,0:T(8,128)(2,1)S(1)} %collective-permute-done.3.refs_0_), channel_id=1, source_target_pairs={{0,2},{2,0},{4,6},{6,4},{8,10},{10,8},{12,14},{14,12},{1,3},{3,1},... | collective-permute-start | bytes 393224 | tf_op jit(solution)/shard_map/ppermute | solution.py:262
  65.0 3.3 %shard_map.143 = (f32[512,512]{1,0:T(8,128)S(1)}, f32[512,512]{1,0:T(8,128)S(1)}) custom-call(s32[4]{0:T(128)S(1)} %pad_add_fusion.info, bf16[512,1024]{1,0:T(8,128)(2,1)S(1)} %get-tuple-element.23.q_ref, bf16[256,256]{1,0:T(8,128)(2,1)S(1)} %get-tuple-element.24.kv_ref, bf16[256,256]{1,0:T(8,128)(2,1)S(1)} %get-tuple-element.25.self_ref, ...), custom_call_target="tpu_custom_call" | custom-call | flops 805306368 | bytes 393216 | tf_op jit(solution)/shard_map/pallas_call | solution.py:231
  68.3 1.2 collective-permute-start.15
  69.8 10.1 %shard_map.144 = (f32[512,512]{1,0:T(8,128)S(1)}, f32[512,512]{1,0:T(8,128)S(1)}) custom-call(s32[4]{0:T(128)S(1)} %pad_add_fusion.info, bf16[512,1024]{1,0:T(8,128)(2,1)S(1)} %get-tuple-element.23.q_ref, bf16[256,256]{1,0:T(8,128)(2,1)S(1)} %collective-permute-done.5.refs_0_, bf16[256,256]{1,0:T(8,128)(2,1)S(1)} %collective-permute-done.6.refs_1_, ...), custom_call_target="tpu_custom_call" | custom-call | flops 1073741824 | bytes 524288 | tf_op jit(solution)/shard_map/pallas_call | solution.py:231
  81.5 6.2 %shard_map.145.ga = bf16[512,512]{1,0:T(8,128)(2,1)S(1)} custom-call(s32[4]{0:T(128)S(1)} %pad_add_fusion.info, bf16[512,1024]{1,0:T(8,128)(2,1)S(1)} %get-tuple-element.23.q_ref, bf16[256,256]{1,0:T(8,128)(2,1)S(1)} %collective-permute-done.3.refs_0_, bf16[256,256]{1,0:T(8,128)(2,1)S(1)} %collective-permute-done.4.refs_1_, ...), custom_call_target="tpu_custom_call" | custom-call | flops 536870912 | bytes 262144 | tf_op jit(solution)/shard_map/pallas_call | solution.py:231
  87.7 4.7 %collective-permute-start.17 = (bf16[512,512]{1,0:T(8,128)(2,1)S(1)}, bf16[512,512]{1,0:T(8,128)(2,1)S(1)}, u32[]{:S(2)}, u32[]{:S(2)}) collective-permute-start(bf16[512,512]{1,0:T(8,128)(2,1)S(1)} %shard_map.145.ga), channel_id=1, source_target_pairs={{0,1},{1,0},{2,3},{3,2},{4,5},{5,4},{6,7},{7,6},{8,9},{9,8},{10,11... | collective-permute-start | bytes 1572872 | tf_op jit(solution)/shard_map/ppermute | solution.py:261
  92.4 10.1 %shard_map.147 = (f32[512,512]{1,0:T(8,128)S(1)}, f32[512,512]{1,0:T(8,128)S(1)}) custom-call(s32[4]{0:T(128)S(1)} %pad_add_fusion.info, bf16[512,1024]{1,0:T(8,128)(2,1)S(1)} %get-tuple-element.23.q_ref, bf16[256,256]{1,0:T(8,128)(2,1)S(1)} %collective-permute-done.12.refs_0_, bf16[256,256]{1,0:T(8,128)(2,1)S(1)} %collective-permute-done.13.refs_1_, ...), custom_call_target="tpu_custom_call" | custom-call | flops 1073741824 | bytes 524288 | tf_op jit(solution)/shard_map/pallas_call | solution.py:231
  102.5 6.2 %shard_map.148.gb = bf16[512,512]{1,0:T(8,128)(2,1)S(1)} custom-call(s32[4]{0:T(128)S(1)} %pad_add_fusion.info, bf16[512,1024]{1,0:T(8,128)(2,1)S(1)} %get-tuple-element.23.q_ref, bf16[256,256]{1,0:T(8,128)(2,1)S(1)} %collective-permute-done.10.refs_0_, bf16[256,256]{1,0:T(8,128)(2,1)S(1)} %collective-permute-done.11.refs_1_, ...), custom_call_target="tpu_custom_call" | custom-call | flops 536870912 | bytes 262144 | tf_op jit(solution)/shard_map/pallas_call | solution.py:231
  108.8 1.9 %collective-permute-done.18.hb = bf16[512,512]{1,0:T(8,128)(2,1)S(1)} collective-permute-done((bf16[512,512]{1,0:T(8,128)(2,1)S(1)}, bf16[512,512]{1,0:T(8,128)(2,1)S(1)}, u32[]{:S(2)}, u32[]{:S(2)}) %collective-permute-start.18) | collective-permute-done | bytes 524320 | tf_op jit(solution)/shard_map/ppermute | solution.py:261
  110.7 8.4 %shard_map.149 = (bf16[256,2048]{1,0:T(8,128)(2,1)}, bf16[256,2048]{1,0:T(8,128)(2,1)}) custom-call(s32[4]{0:T(128)S(1)} %pad_add_fusion.info, s32[4]{0:T(128)S(1)} %bitcast.21, bf16[512,512]{1,0:T(8,128)(2,1)S(1)} %shard_map.145.ga, bf16[512,512]{1,0:T(8,128)(2,1)S(1)} %shard_map.148.gb, bf16[512,512]{1,0:T(8,128)(2,1)S(1)} %collective-permute-done.17.ha, ...), custom_call_target="tpu_custom_call" | custom-call | flops 4294967296 | bytes 8388608 | tf_op jit(solution)/shard_map/pallas_call | solution.py:231
  (52 shorter events, 6.4 us)
Async XLA Ops:
  0.7 22.3 %copy-start.9 = (bf16[4096]{0:T(1024)(128)(2,1)S(1)}, bf16[4096]{0:T(1024)(128)(2,1)}, u32[]{:S(2)}) copy-start(bf16[4096]{0:T(1024)(128)(2,1)} %param.15) | copy-start | bytes 24580
  0.7 22.7 %copy-start.3 = (f32[4096]{0:T(1024)S(1)}, f32[4096]{0:T(1024)}, u32[]{:S(2)}) copy-start(f32[4096]{0:T(1024)} %param.16) | copy-start | bytes 49156
  0.7 22.7 %copy-start.4 = (s32[1,256]{1,0:T(1,128)S(1)}, s32[1,256]{1,0:T(1,128)}, u32[]{:S(2)}) copy-start(s32[1,256]{1,0:T(1,128)} %mask_ref.5) | copy-start | bytes 3076
  5.5 105.2 %collective-permute-start.19 = (bf16[1024,2048]{1,0:T(8,128)(2,1)}, bf16[1024,2048]{1,0:T(8,128)(2,1)}, u32[]{:S(2)}, u32[]{:S(2)}) collective-permute-start(bf16[1024,2048]{1,0:T(8,128)(2,1)} %constant_dynamic-slice_fusion), channel_id=1, source_target_pairs={{0,1},{1,0},{2,3},{3,2},{4,5},{5,4},{6,7},{7,6},{8,9},{9,8},{10,11... | collective-permute-start | bytes 12582920 | tf_op jit(solution)/shard_map/ppermute | solution.py:261
  6.2 13.6 %collective-permute-start = (bf16[128,2048]{1,0:T(8,128)(2,1)S(1)}, bf16[128,2048]{1,0:T(8,128)(2,1)S(1)}, u32[]{:S(2)}, u32[]{:S(2)}) collective-permute-start(bf16[128,2048]{1,0:T(8,128)(2,1)S(1)} %constant_dynamic-slice_fusion.1), channel_id=1, source_target_pairs={{0,16},{16,0},{1,17},{17,1},{2,18},{18,2},{3,19},{19,3},{4,20},{20... | collective-permute-start | bytes 1572872 | tf_op jit(solution)/shard_map/ppermute | solution.py:260
  19.9 13.4 %collective-permute-start.1 = (bf16[128,2048]{1,0:T(8,128)(2,1)S(1)}, bf16[128,2048]{1,0:T(8,128)(2,1)S(1)}, u32[]{:S(2)}, u32[]{:S(2)}) collective-permute-start(bf16[128,2048]{1,0:T(8,128)(2,1)S(1)} %collective-permute-done.xs_ref), channel_id=1, source_target_pairs={{0,1},{1,0},{2,3},{3,2},{4,5},{5,4},{6,7},{7,6},{8,9},{9,8},{10,11... | collective-permute-start | bytes 1572872 | tf_op jit(solution)/shard_map/ppermute | solution.py:261
  20.9 2.5 %collective-permute-start.2 = (f32[256]{0:T(256)S(1)}, f32[256]{0:T(256)S(1)}, u32[]{:S(2)}, u32[]{:S(2)}) collective-permute-start(f32[256]{0:T(256)S(1)} %multiply_reduce_fusion), channel_id=1, source_target_pairs={{0,16},{16,0},{1,17},{17,1},{2,18},{18,2},{3,19},{19,3},{4,20},{20... | collective-permute-start | bytes 3080 | tf_op jit(solution)/shard_map/ppermute | solution.py:260
  37.5 3.9 %collective-permute-start.16 = (bf16[256,256]{1,0:T(8,128)(2,1)S(1)}, bf16[256,256]{1,0:T(8,128)(2,1)S(1)}, u32[]{:S(2)}, u32[]{:S(2)}) collective-permute-start(bf16[256,256]{1,0:T(8,128)(2,1)S(1)} %get-tuple-element.30.kv_ref), channel_id=1, source_target_pairs={{0,2},{2,0},{4,6},{6,4},{8,10},{10,8},{12,14},{14,12},{1,3},{3,1},... | collective-permute-start | bytes 393224 | tf_op jit(solution)/shard_map/ppermute | solution.py:262
  38.8 9.5 %collective-permute-start.7 = (bf16[256,256]{1,0:T(8,128)(2,1)S(1)}, bf16[256,256]{1,0:T(8,128)(2,1)S(1)}, u32[]{:S(2)}, u32[]{:S(2)}) collective-permute-start(bf16[256,256]{1,0:T(8,128)(2,1)S(1)} %get-tuple-element.24.kv_ref), channel_id=1, source_target_pairs={{0,8},{2,10},{4,12},{6,14},{8,0},{10,2},{12,4},{14,6},{1,9},{3,11}... | collective-permute-start | bytes 393224 | tf_op jit(solution)/shard_map/ppermute | solution.py:262
  38.8 18.7 %collective-permute-start.9 = (bf16[256,256]{1,0:T(8,128)(2,1)S(1)}, bf16[256,256]{1,0:T(8,128)(2,1)S(1)}, u32[]{:S(2)}, u32[]{:S(2)}) collective-permute-start(bf16[256,256]{1,0:T(8,128)(2,1)S(1)} %get-tuple-element.24.kv_ref), channel_id=1, source_target_pairs={{0,2},{2,0},{4,6},{6,4},{8,10},{10,8},{12,14},{14,12},{1,3},{3,1},... | collective-permute-start | bytes 393224 | tf_op jit(solution)/shard_map/ppermute | solution.py:262
  39.1 18.6 %collective-permute-start.5 = (bf16[256,256]{1,0:T(8,128)(2,1)S(1)}, bf16[256,256]{1,0:T(8,128)(2,1)S(1)}, u32[]{:S(2)}, u32[]{:S(2)}) collective-permute-start(bf16[256,256]{1,0:T(8,128)(2,1)S(1)} %get-tuple-element.24.kv_ref), channel_id=1, source_target_pairs={{0,4},{2,6},{4,0},{6,2},{8,12},{10,14},{12,8},{14,10},{1,5},{3,7},... | collective-permute-start | bytes 393224 | tf_op jit(solution)/shard_map/ppermute | solution.py:262
  41.3 21.0 %collective-permute-start.3 = (bf16[256,256]{1,0:T(8,128)(2,1)S(1)}, bf16[256,256]{1,0:T(8,128)(2,1)S(1)}, u32[]{:S(2)}, u32[]{:S(2)}) collective-permute-start(bf16[256,256]{1,0:T(8,128)(2,1)S(1)} %get-tuple-element.24.kv_ref), channel_id=1, source_target_pairs={{0,12},{2,14},{4,8},{6,10},{8,4},{10,6},{12,0},{14,2},{1,13},{3,15... | collective-permute-start | bytes 393224 | tf_op jit(solution)/shard_map/ppermute | solution.py:262
  48.3 14.5 %collective-permute-start.14 = (bf16[256,256]{1,0:T(8,128)(2,1)S(1)}, bf16[256,256]{1,0:T(8,128)(2,1)S(1)}, u32[]{:S(2)}, u32[]{:S(2)}) collective-permute-start(bf16[256,256]{1,0:T(8,128)(2,1)S(1)} %collective-permute-done.7.refs_2_), channel_id=1, source_target_pairs={{0,16},{16,0},{1,17},{17,1},{2,18},{18,2},{3,19},{19,3},{4,20},{20... | collective-permute-start | bytes 393224 | tf_op jit(solution)/shard_map/ppermute | solution.py:260
  57.6 10.7 %collective-permute-start.8 = (bf16[256,256]{1,0:T(8,128)(2,1)S(1)}, bf16[256,256]{1,0:T(8,128)(2,1)S(1)}, u32[]{:S(2)}, u32[]{:S(2)}) collective-permute-start(bf16[256,256]{1,0:T(8,128)(2,1)S(1)} %collective-permute-done.7.refs_2_), channel_id=1, source_target_pairs={{0,2},{2,0},{4,6},{6,4},{8,10},{10,8},{12,14},{14,12},{1,3},{3,1},... | collective-permute-start | bytes 393224 | tf_op jit(solution)/shard_map/ppermute | solution.py:262
  57.7 11.8 %collective-permute-start.6 = (bf16[256,256]{1,0:T(8,128)(2,1)S(1)}, bf16[256,256]{1,0:T(8,128)(2,1)S(1)}, u32[]{:S(2)}, u32[]{:S(2)}) collective-permute-start(bf16[256,256]{1,0:T(8,128)(2,1)S(1)} %collective-permute-done.5.refs_0_), channel_id=1, source_target_pairs={{0,2},{2,0},{4,6},{6,4},{8,10},{10,8},{12,14},{14,12},{1,3},{3,1},... | collective-permute-start | bytes 393224 | tf_op jit(solution)/shard_map/ppermute | solution.py:262
  62.4 17.6 %collective-permute-start.12 = (bf16[256,256]{1,0:T(8,128)(2,1)S(1)}, bf16[256,256]{1,0:T(8,128)(2,1)S(1)}, u32[]{:S(2)}, u32[]{:S(2)}) collective-permute-start(bf16[256,256]{1,0:T(8,128)(2,1)S(1)} %collective-permute-done.5.refs_0_), channel_id=1, source_target_pairs={{0,16},{16,0},{1,17},{17,1},{2,18},{18,2},{3,19},{19,3},{4,20},{20... | collective-permute-start | bytes 393224 | tf_op jit(solution)/shard_map/ppermute | solution.py:260
  62.8 18.3 %collective-permute-start.4 = (bf16[256,256]{1,0:T(8,128)(2,1)S(1)}, bf16[256,256]{1,0:T(8,128)(2,1)S(1)}, u32[]{:S(2)}, u32[]{:S(2)}) collective-permute-start(bf16[256,256]{1,0:T(8,128)(2,1)S(1)} %collective-permute-done.3.refs_0_), channel_id=1, source_target_pairs={{0,2},{2,0},{4,6},{6,4},{8,10},{10,8},{12,14},{14,12},{1,3},{3,1},... | collective-permute-start | bytes 393224 | tf_op jit(solution)/shard_map/ppermute | solution.py:262
  68.3 19.4 %collective-permute-start.15 = (bf16[256,256]{1,0:T(8,128)(2,1)S(1)}, bf16[256,256]{1,0:T(8,128)(2,1)S(1)}, u32[]{:S(2)}, u32[]{:S(2)}) collective-permute-start(bf16[256,256]{1,0:T(8,128)(2,1)S(1)} %collective-permute-done.8.refs_3_), channel_id=1, source_target_pairs={{0,16},{16,0},{1,17},{17,1},{2,18},{18,2},{3,19},{19,3},{4,20},{20... | collective-permute-start | bytes 393224 | tf_op jit(solution)/shard_map/ppermute | solution.py:260
  69.5 22.9 %collective-permute-start.13 = (bf16[256,256]{1,0:T(8,128)(2,1)S(1)}, bf16[256,256]{1,0:T(8,128)(2,1)S(1)}, u32[]{:S(2)}, u32[]{:S(2)}) collective-permute-start(bf16[256,256]{1,0:T(8,128)(2,1)S(1)} %collective-permute-done.6.refs_1_), channel_id=1, source_target_pairs={{0,16},{16,0},{1,17},{17,1},{2,18},{18,2},{3,19},{19,3},{4,20},{20... | collective-permute-start | bytes 393224 | tf_op jit(solution)/shard_map/ppermute | solution.py:260
  79.9 22.6 %collective-permute-start.10 = (bf16[256,256]{1,0:T(8,128)(2,1)S(1)}, bf16[256,256]{1,0:T(8,128)(2,1)S(1)}, u32[]{:S(2)}, u32[]{:S(2)}) collective-permute-start(bf16[256,256]{1,0:T(8,128)(2,1)S(1)} %collective-permute-done.3.refs_0_), channel_id=1, source_target_pairs={{0,16},{16,0},{1,17},{17,1},{2,18},{18,2},{3,19},{19,3},{4,20},{20... | collective-permute-start | bytes 393224 | tf_op jit(solution)/shard_map/ppermute | solution.py:260
  81.1 21.4 %collective-permute-start.11 = (bf16[256,256]{1,0:T(8,128)(2,1)S(1)}, bf16[256,256]{1,0:T(8,128)(2,1)S(1)}, u32[]{:S(2)}, u32[]{:S(2)}) collective-permute-start(bf16[256,256]{1,0:T(8,128)(2,1)S(1)} %collective-permute-done.4.refs_1_), channel_id=1, source_target_pairs={{0,16},{16,0},{1,17},{17,1},{2,18},{18,2},{3,19},{19,3},{4,20},{20... | collective-permute-start | bytes 393224 | tf_op jit(solution)/shard_map/ppermute | solution.py:260
  87.7 23.0 %copy-start.7 = (s32[1,4]{1,0:T(1,128)S(1)}, s32[1,4]{1,0:T(1,128)}, u32[]{:S(2)}) copy-start(s32[1,4]{1,0:T(1,128)} %param.24) | copy-start | bytes 52
  87.7 21.1 %collective-permute-start.17 = (bf16[512,512]{1,0:T(8,128)(2,1)S(1)}, bf16[512,512]{1,0:T(8,128)(2,1)S(1)}, u32[]{:S(2)}, u32[]{:S(2)}) collective-permute-start(bf16[512,512]{1,0:T(8,128)(2,1)S(1)} %shard_map.145.ga), channel_id=1, source_target_pairs={{0,1},{1,0},{2,3},{3,2},{4,5},{5,4},{6,7},{7,6},{8,9},{9,8},{10,11... | collective-permute-start | bytes 1572872 | tf_op jit(solution)/shard_map/ppermute | solution.py:261
  108.7 2.0 %collective-permute-start.18 = (bf16[512,512]{1,0:T(8,128)(2,1)S(1)}, bf16[512,512]{1,0:T(8,128)(2,1)S(1)}, u32[]{:S(2)}, u32[]{:S(2)}) collective-permute-start(bf16[512,512]{1,0:T(8,128)(2,1)S(1)} %shard_map.148.gb), channel_id=1, source_target_pairs={{0,1},{1,0},{2,3},{3,2},{4,5},{5,4},{6,7},{7,6},{8,9},{9,8},{10,11... | collective-permute-start | bytes 1572872 | tf_op jit(solution)/shard_map/ppermute | solution.py:261
  (6 other events, 65.0 us)

commit v2 on v1

v2 whole, which is shorter than its diff:
```python
import functools
import math

import jax
import jax.numpy as jnp
from jax import lax
from jax.experimental import pallas as pl
from jax.experimental.pallas import tpu as pltpu
from jax.sharding import PartitionSpec as P

HD = 128
BLK = 64
TSTEPS = 1000
EPS = 1e-06
VMEM_LIMIT = 32 * 1024 * 1024
F32 = jnp.float32
BF16 = jnp.bfloat16
SCORE_SCALE = math.log2(math.e) / math.sqrt(HD)


def to_column(row, n):
    eye = lax.broadcasted_iota(jnp.int32, (n, n), 0) == lax.broadcasted_iota(jnp.int32, (n, n), 1)
    return jnp.sum(jnp.where(eye, jnp.broadcast_to(row, (n, n)), 0.0), axis=1, keepdims=True)


def row_scales(own_ref, other_ref, mask_ref, embed_ref, width):
    n = own_ref.shape[1]
    clean = lax.rsqrt(to_column(own_ref[...] + other_ref[...], n) * (1.0 / width) + EPS)
    embed = embed_ref[...].astype(F32)
    embed_scale = lax.rsqrt(jnp.sum(embed * embed, axis=1, keepdims=True) * (1.0 / width) + EPS)
    masked = to_column(mask_ref[...].astype(F32), n)
    return clean, embed_scale, masked


def normed_clean(x, clean_scale, gain):
    return (x * clean_scale * gain).astype(BF16)


def normed_noisy(x, clean_scale, embed_scale, masked, gain, embed, condition):
    is_masked = masked == 1.0
    noisy = jnp.where(is_masked, embed, x)
    scale = jnp.where(is_masked, embed_scale, clean_scale)
    return (noisy * scale * gain * condition).astype(BF16)


def dot(a, b):
    return jnp.dot(a, b, preferred_element_type=F32)


def head_norm(wide, gain):
    scale = lax.rsqrt(jnp.mean(wide * wide, axis=1, keepdims=True) + EPS)
    return (wide * scale * gain).astype(BF16)


def both_streams(x, scales, gain, embed, condition):
    clean = normed_clean(x, scales[0], gain)
    noisy = normed_noisy(x, scales[0], scales[1], scales[2], gain, embed, condition)
    return clean, noisy


def half_vectors(at, info, gain_ref, embed_ref, shift_ref):
    gain = gain_ref[:, at].astype(F32)
    embed = embed_ref[:, at].astype(F32)
    condition = 1.0 + info[3].astype(F32) / TSTEPS * shift_ref[:, at]
    return gain, embed, condition


def first_half_kernel(
    info, x_ref, own_ref, other_ref, mask_ref, gain_ref, embed_ref, shift_ref,
    wq_ref, wk_ref, wv_ref, w_out, q_ref, k_ref, v_ref, w_send, w_mine, sems,
):
    half = x_ref.shape[1]
    cols = w_send.shape[1]
    moves = []
    for number, (target, side) in enumerate(((w_send, 1 - info[1]), (w_mine, info[1]))):
        start = pl.multiple_of(side * cols, 128)
        moves.append(pltpu.make_async_copy(w_out.at[:, pl.ds(start, cols)], target, sems.at[number]))
        moves[-1].start()
    scales = row_scales(own_ref, other_ref, mask_ref, embed_ref, embed_ref.shape[1])
    at = pl.ds(pl.multiple_of(info[0] * half, 128), half)
    gain, embed, condition = half_vectors(at, info, gain_ref, embed_ref, shift_ref)
    clean, noisy = both_streams(x_ref[...].astype(F32), scales, gain, embed, condition)
    both = jnp.concatenate([clean, noisy], axis=0)
    k_ref[...] = dot(both, wk_ref[at])
    v_ref[...] = dot(both, wv_ref[at])
    q_ref[...] = dot(both, wq_ref[at])
    for move in moves:
        move.wait()


def other_rows(info, near_ref, far_ref):
    near, far = near_ref[...].astype(F32), far_ref[...].astype(F32)
    first = info[1] == 0
    return jnp.concatenate([jnp.where(first, near, far), jnp.where(first, far, near)], axis=0)


def kv_out(ref, k, v, gain):
    for head in range(k.shape[1] // HD):
        cols = slice(head * HD, (head + 1) * HD)
        ref[:, 2 * head * HD : (2 * head + 1) * HD] = head_norm(k[:, cols], gain)
        ref[:, (2 * head + 1) * HD : 2 * (head + 1) * HD] = v[:, cols].astype(BF16)


def clean_kv_kernel(
    info, near_ref, far_ref, own_ref, other_ref, mask_ref, gain_ref, embed_ref,
    wk_ref, wv_ref, pk_ref, pv_ref, kgain_ref, all_ref, one_ref,
):
    half = near_ref.shape[1]
    rows = all_ref.shape[0]
    clean_scale = row_scales(own_ref, other_ref, mask_ref, embed_ref, embed_ref.shape[1])[0]
    at = pl.ds(pl.multiple_of((1 - info[0]) * half, 128), half)
    clean = normed_clean(other_rows(info, near_ref, far_ref), clean_scale, gain_ref[:, at].astype(F32))
    k = pk_ref[:rows] + dot(clean, wk_ref[at])
    v = pv_ref[:rows] + dot(clean, wv_ref[at])
    kv_out(all_ref, k, v, kgain_ref[...])
    width = one_ref.shape[1]
    one_ref[...] = all_ref[:, pl.ds(pl.multiple_of(info[0] * width, 128), width)]


def second_half_kernel(
    info, near_ref, far_ref, own_ref, other_ref, mask_ref, gain_ref, embed_ref, shift_ref,
    wq_ref, wk_ref, wv_ref, pq_ref, pk_ref, pv_ref, qgain_ref, kgain_ref, q_ref, self_ref,
):
    half = near_ref.shape[1]
    rows = self_ref.shape[0]
    scales = row_scales(own_ref, other_ref, mask_ref, embed_ref, embed_ref.shape[1])
    at = pl.ds(pl.multiple_of((1 - info[0]) * half, 128), half)
    gain, embed, condition = half_vectors(at, info, gain_ref, embed_ref, shift_ref)
    clean, noisy = both_streams(other_rows(info, near_ref, far_ref), scales, gain, embed, condition)
    k = pk_ref[rows:] + dot(noisy, wk_ref[at])
    v = pv_ref[rows:] + dot(noisy, wv_ref[at])
    kv_out(self_ref, k, v, kgain_ref[...])
    q = pq_ref[...] + dot(jnp.concatenate([clean, noisy], axis=0), wq_ref[at])
    for head in range(q_ref.shape[1] // HD):
        cols = slice(head * HD, (head + 1) * HD)
        q_ref[:, cols] = head_norm(q[:, cols], qgain_ref[...])


def terms(q, k, v, mask):
    scores = lax.dot_general(q, k, (((1,), (1,)), ((), ())), preferred_element_type=F32)
    e = jnp.exp2(scores * SCORE_SCALE)
    if mask is not None:
        e = jnp.where(mask, e, 0.0)
    den = e[:, :HD]
    for start in range(HD, e.shape[1], HD):
        den = den + e[:, start : start + HD]
    return dot(e.astype(BF16), v), den


def add_pieces(q_ref, num_ref, den_ref, first_head, heads, pieces, rows):
    k = jnp.concatenate([piece[:, :HD] for piece in pieces], axis=0)
    v = jnp.concatenate([piece[:, HD:] for piece in pieces], axis=0)
    for head in range(first_head, first_head + heads):
        cols = slice(head * HD, (head + 1) * HD)
        for part in range(2):
            cut = slice(part * rows, (part + 1) * rows)
            num, den = terms(q_ref[cut, cols], k, v, None)
            num_ref[cut, cols] += num
            den_ref[cut, cols] += den


def attention_first_kernel(info, q_ref, kv_ref, self_ref, near_ref, num_ref, den_ref):
    rows = kv_ref.shape[0]
    kv_heads = kv_ref.shape[1] // (2 * HD)
    group = q_ref.shape[1] // HD // kv_heads
    row_block = lax.broadcasted_iota(jnp.int32, (rows, rows), 0) // BLK
    key_block = lax.broadcasted_iota(jnp.int32, (rows, rows), 1) // BLK
    both = jnp.concatenate([key_block < row_block, key_block == row_block], axis=1)
    for kv_head in range(kv_heads):
        k_cols = slice(2 * kv_head * HD, (2 * kv_head + 1) * HD)
        v_cols = slice((2 * kv_head + 1) * HD, 2 * (kv_head + 1) * HD)
        k, v = kv_ref[:, k_cols], kv_ref[:, v_cols]
        k_both = jnp.concatenate([k, self_ref[:, k_cols]], axis=0)
        v_both = jnp.concatenate([v, self_ref[:, v_cols]], axis=0)
        for head in range(kv_head * group, (kv_head + 1) * group):
            cols = slice(head * HD, (head + 1) * HD)
            num_ref[:rows, cols], den_ref[:rows, cols] = terms(q_ref[:rows, cols], k, v, key_block <= row_block)
            num_ref[rows:, cols], den_ref[rows:, cols] = terms(q_ref[rows:, cols], k_both, v_both, both)

    @pl.when(info[2] % 2 == 1)
    def _():
        for kv_head in range(kv_heads):
            piece = near_ref[:, 2 * kv_head * HD : 2 * (kv_head + 1) * HD]
            add_pieces(q_ref, num_ref, den_ref, kv_head * group, group, [piece], rows)


def attention_near_kernel(info, q_ref, num_in, den_in, left_ref, right_ref, num_ref, den_ref):
    rows = left_ref.shape[0]
    kv_heads = left_ref.shape[1] // (2 * HD)
    group = q_ref.shape[1] // HD // kv_heads
    num_ref[...] = num_in[...]
    den_ref[...] = den_in[...]

    @pl.when(jnp.bitwise_xor(info[2], 2) < info[2])
    def _():
        for kv_head in range(kv_heads):
            cols = slice(2 * kv_head * HD, 2 * (kv_head + 1) * HD)
            add_pieces(
                q_ref, num_ref, den_ref, kv_head * group, group, [left_ref[:, cols], right_ref[:, cols]], rows
            )


def attention_far_kernel(info, q_all, num_in, den_in, *refs, offsets, which):
    kv_refs = refs[: 2 * len(offsets)]
    out_ref, q_ref, num_ref, den_ref = refs[2 * len(offsets) :]
    rows = kv_refs[0].shape[0] if kv_refs else out_ref.shape[0] // 2
    width = out_ref.shape[1]
    at = pl.ds(pl.multiple_of((info[0] if which == 0 else 1 - info[0]) * width, 128), width)
    q_ref[...] = q_all[:, at]
    num_ref[...] = num_in[:, at]
    den_ref[...] = den_in[:, at]
    for number, offset in enumerate(offsets):
        @pl.when(jnp.bitwise_xor(info[2], offset) < info[2])
        def _(number=number):
            pieces = [kv_refs[2 * number][...], kv_refs[2 * number + 1][...]]
            add_pieces(q_ref, num_ref, den_ref, 0, width // HD, pieces, rows)

    for head in range(width // HD):
        cols = slice(head * HD, (head + 1) * HD)
        total = jnp.sum(den_ref[:, cols], axis=1, keepdims=True)
        out_ref[:, cols] = (num_ref[:, cols] / total).astype(BF16)


def out_kernel(info, live, ga, gb, ha, hb, w_mine, w_far, clean_ref, noisy_ref):
    rows, tile = clean_ref.shape
    part = ga.shape[1]
    cols = pl.ds(pl.multiple_of(pl.program_id(0) * tile, 128), tile)
    first = pl.ds(pl.multiple_of(info[0] * part, 128), part)
    second = pl.ds(pl.multiple_of((1 - info[0]) * part, 128), part)
    mixed = dot(ga[...], w_mine[first, cols]) + dot(gb[...], w_mine[second, cols])
    mixed = mixed + dot(ha[...], w_far[first, cols]) + dot(hb[...], w_far[second, cols])
    clean_ref[...] = mixed[:rows].astype(BF16)
    for block in range(rows // BLK):
        part_rows = mixed[rows + block * BLK : rows + (block + 1) * BLK]
        noisy_ref[block * BLK : (block + 1) * BLK] = (part_rows * live[block].astype(F32)).astype(BF16)


WHOLE = pl.BlockSpec(memory_space=pltpu.VMEM)
HBM = pl.BlockSpec(memory_space=pl.ANY)


def call(kernel, scalars, ins, outs, arrays, flops, num_bytes, scratch=(), exps=0, grid=1):
    return pl.pallas_call(
        kernel,
        grid_spec=pltpu.PrefetchScalarGridSpec(
            num_scalar_prefetch=len(scalars),
            grid=(grid,),
            in_specs=ins,
            out_specs=[spec for spec, _ in outs],
            scratch_shapes=list(scratch),
        ),
        out_shape=[shape for _, shape in outs],
        compiler_params=pltpu.CompilerParams(vmem_limit_bytes=VMEM_LIMIT),
        cost_estimate=pl.CostEstimate(flops=flops, bytes_accessed=num_bytes, transcendentals=exps),
    )(*scalars, *arrays)


def on_device(
    mesh, clean_tokens, norm_gain, mask_embed, time_shift, w_query, w_key, w_value, w_out,
    q_gain, k_gain, masked, block_live, timesteps,
):
    rows, half = clean_tokens.shape
    heads_width = w_query.shape[1]
    kv_width = w_key.shape[1]
    part = heads_width // 2
    ctx = mesh.shape["ctx"]
    c, p, t = lax.axis_index("copy"), lax.axis_index("ctx"), lax.axis_index("tp")
    info = jnp.stack([c, t, p, timesteps[0]]).astype(jnp.int32)
    pair = [(0, 1), (1, 0)]
    cross_x = lambda v: lax.ppermute(v, "copy", pair)
    cross_core = lambda v: lax.ppermute(v, "tp", pair)
    cross_ctx = lambda v, offset: lax.ppermute(v, "ctx", [(i, i ^ offset) for i in range(ctx)])
    shape = jax.ShapeDtypeStruct

    cut = rows // 2
    near = cross_x(lax.dynamic_slice_in_dim(clean_tokens, t * cut, cut, 0))
    wide = clean_tokens.astype(F32)
    squares = jnp.sum(wide * wide, axis=1)
    other_squares = cross_x(squares)
    out_cols = w_out.shape[1] // 2
    stats = [squares[None], other_squares[None], masked]
    vectors = [norm_gain[None], mask_embed[None], time_shift[None]]
    qg, kg = q_gain[None], k_gain[None]

    w_half = shape((heads_width, out_cols), BF16)
    pq, pk, pv, w_send, w_mine = call(
        first_half_kernel, [info], [WHOLE] * 10 + [HBM],
        [
            (WHOLE, shape((2 * rows, heads_width), F32)),
            (WHOLE, shape((2 * rows, kv_width), F32)),
            (WHOLE, shape((2 * rows, kv_width), F32)),
            (HBM, w_half),
            (HBM, w_half),
        ],
        [clean_tokens] + stats + vectors + [w_query, w_key, w_value, w_out],
        2 * 2 * rows * half * (heads_width + 2 * kv_width), 4 * heads_width * out_cols * 2,
        [pltpu.SemaphoreType.DMA((2,))],
    )
    near, pk = lax.optimization_barrier((near, pk))
    far = cross_core(near)

    kv, kva = call(
        clean_kv_kernel, [info], [WHOLE] * 12,
        [(WHOLE, shape((rows, 2 * kv_width), BF16)), (WHOLE, shape((rows, kv_width), BF16))],
        [near, far] + stats + vectors[:2] + [w_key, w_value, pk, pv, kg],
        2 * rows * half * 2 * kv_width, half * 2 * kv_width * 2,
    )

    far_pieces = [{}, {}]
    beside = cross_ctx(kv, 1)
    left = cross_ctx(kv, 2) if ctx > 2 else None
    offsets = list(range(4, ctx, 2))
    for offset in offsets:
        far_pieces[0][offset] = cross_ctx(kva, offset)
    right = cross_ctx(left, 1) if ctx > 2 else None
    for offset in offsets:
        far_pieces[0][offset + 1] = cross_ctx(far_pieces[0][offset], 1)
        far_pieces[1][offset] = cross_x(far_pieces[0][offset])
        far_pieces[1][offset + 1] = cross_x(far_pieces[0][offset + 1])

    q, own = call(
        second_half_kernel, [info], [WHOLE] * 16,
        [(WHOLE, shape((2 * rows, heads_width), BF16)), (WHOLE, shape((rows, 2 * kv_width), BF16))],
        [near, far] + stats + vectors + [w_query, w_key, w_value, pq, pk, pv, qg, kg],
        2 * 2 * rows * half * heads_width + 2 * rows * half * 2 * kv_width, half * (heads_width + 2 * kv_width) * 2,
    )
    w_send, q = lax.optimization_barrier((w_send, q))
    w_far = cross_core(w_send)

    acc = (WHOLE, shape((2 * rows, heads_width), F32))
    unit = 2 * rows * rows * (heads_width // HD)
    num, den = call(
        attention_first_kernel, [info], [WHOLE] * 4, [acc, acc], [q, kv, own, beside],
        5 * unit * HD * 2, unit * 8, exps=2 * unit,
    )
    if ctx > 2:
        num, den = call(
            attention_near_kernel, [info], [WHOLE] * 5, [acc, acc], [q, num, den, left, right],
            2 * unit * HD * 4, unit * 8, exps=2 * unit,
        )

    def far_part(which):
        pieces = [far_pieces[which][o + side] for o in offsets for side in (0, 1)]
        return call(
            functools.partial(attention_far_kernel, offsets=offsets, which=which), [info],
            [WHOLE] * (3 + len(pieces)), [(WHOLE, shape((2 * rows, part), BF16))], [q, num, den] + pieces,
            len(pieces) * unit * HD * 2, unit * 8,
            [pltpu.VMEM((2 * rows, part), BF16)] + [pltpu.VMEM((2 * rows, part), F32)] * 2,
            exps=len(pieces) * unit // 2,
        )[0]

    ga = far_part(0)
    ha = cross_core(ga)
    gb = far_part(1)
    hb = cross_core(gb)

    tile = 512
    out = pl.BlockSpec((rows, tile), lambda n, s, l: (0, n))
    out_shape = shape((rows, out_cols), BF16)
    clean_out, noised_out = call(
        out_kernel, [info, block_live[0]], [WHOLE] * 6, [(out, out_shape), (out, out_shape)],
        [ga, gb, ha, hb, w_mine, w_far],
        2 * 2 * rows * 2 * heads_width * out_cols, 2 * heads_width * out_cols * 2, grid=out_cols // tile,
    )
    return (clean_out, noised_out[None])


def solution(mesh):
    in_specs = (
        P("ctx", "copy"),
        P(),
        P(),
        P(),
        P(None, "tp"),
        P(None, "tp"),
        P(None, "tp"),
        P("tp", None),
        P(),
        P(),
        P("copy", "ctx"),
        P("copy", "ctx"),
        P("copy"),
    )
    out_specs = (P("ctx", "tp"), P("copy", "ctx", "tp"))
    return jax.shard_map(
        functools.partial(on_device, mesh), mesh=mesh, in_specs=in_specs, out_specs=out_specs, check_vma=False
    )
```

time: 120 us -> 216 us (1.80)
  Pallas kernels: 68.2 us -> 162 us
    pallas_call x10 -> x8, Pallas kernels: 68.2 us -> 162 us  [call(): pl.pallas_call(kernel, grid_spec=pltpu.PrefetchScalarGridSpec(num_scalar_...]
    dynamic_slice x1 -> x0, local copies, waits for them, and re-layouts: 4.82 us -> none  [on_device(): lax.dynamic_slice_in_dim(w_out, (1 - t) * out_cols, out_cols, 1)]
    ppermute x8 -> x7, waiting for transfers between devices: 7.96 us -> 11.8 us  [on_device(): lax.ppermute(v, 'ctx', [(i, i ^ offset) for i in range(ctx)])]
    ppermute x8 -> x6, waiting for transfers between devices: 12.8 us -> 9.01 us  [on_device(): cross_x = lambda v: lax.ppermute(v, 'copy', pair)]
    ppermute x8 -> x6, starting transfers between devices: 7.14 us -> 5.44 us  [on_device(): cross_x = lambda v: lax.ppermute(v, 'copy', pair)]
    ppermute x8 -> x7, starting transfers between devices: 6.65 us -> 7.57 us  [on_device(): lax.ppermute(v, 'ctx', [(i, i ^ offset) for i in range(ctx)])]
  transfers between devices with their start and end apart: 20 -> 17, of which waited for: 5 -> 7; matrix products, arithmetic and copies ran while one was open for 0% -> 1% of each run, Pallas kernels for 50% -> 71%
where the time goes in v2:
time: 216 us; the launch traced here: 215 us
  Pallas kernels  162 us (75%)
  waiting for transfers between devices  24.2 us (11%)
  starting transfers between devices  20.7 us (10%)
  local copies, waits for them, and re-layouts  4.4 us (2%)
    pallas_call x8, Pallas kernels, call(): pl.pallas_call(kernel, grid_spec=pltpu.PrefetchScalarGridSpec(num_scalar_...  162 us
    ppermute x7, waiting for transfers between devices, on_device(): lax.ppermute(v, 'ctx', [(i, i ^ offset) for i in range(ctx)])  11.8 us
    ppermute x6, waiting for transfers between devices, on_device(): cross_x = lambda v: lax.ppermute(v, 'copy', pair)  9.01 us
    ppermute x4, starting transfers between devices, on_device(): cross_core = lambda v: lax.ppermute(v, 'tp', pair)  7.67 us
    ppermute x7, starting transfers between devices, on_device(): lax.ppermute(v, 'ctx', [(i, i ^ offset) for i in range(ctx)])  7.57 us
    ppermute x6, starting transfers between devices, on_device(): cross_x = lambda v: lax.ppermute(v, 'copy', pair)  5.44 us
  transfers between devices with their start and end apart: 17, of which 7 were waited for; matrix products, arithmetic and copies ran while one was open for 1% of the time, Pallas kernels for 71%

profile of v2, /device:TPU:25, one launch (start us, length us, event | category | flops | bytes accessed | tf_op | source)
XLA Modules:
  0.0 214.6 jit_solution(15646577109767370270)
XLA Ops:
  0.7 1.2 constant_dynamic-slice_fusion
  1.9 1.3 collective-permute-start.1
  3.2 1.5 multiply_reduce_fusion
  5.8 9.0 %collective-permute-done = f32[256]{0:T(256)S(1)} collective-permute-done((f32[256]{0:T(256)S(1)}, f32[256]{0:T(256)S(1)}, u32[]{:S(2)}, u32[]{:S(2)}) %collective-permute-start) | collective-permute-done | bytes 1056 | tf_op jit(solution)/shard_map/ppermute | solution.py:270
  14.8 1.7 copy-done.1
  16.6 1.4 copy-done.2
  17.9 132.4 %shard_map.140 = (f32[512,1024]{1,0:T(8,128)S(1)}, f32[512,256]{1,0:T(8,128)S(1)}, f32[512,256]{1,0:T(8,128)S(1)}, bf16[1024,2048]{1,0:T(8,128)(2,1)}, bf16[1024,2048]{1,0:T(8,128)(2,1)S(1)}) custom-call(s32[4]{0:T(128)S(1)} %pad_add_fusion.info, bf16[256,2048]{1,0:T(8,128)(2,1)S(1)} %copy-done.2, f32[1,256]{1,0:T(1,128)S(1)} %bitcast.14, ...), custom_call_target="tpu_custom_call" | custom-call | flops 3221225472 | bytes 16777216 | tf_op jit(solution)/shard_map/pallas_call | solution.py:243
  150.3 1.7 collective-permute-start.2
  152.0 1.5 collective-permute-done.2.far_ref
  153.5 4.0 %shard_map.141 = (bf16[512,1024]{1,0:T(8,128)(2,1)S(1)}, bf16[256,512]{1,0:T(8,128)(2,1)S(1)}) custom-call(s32[4]{0:T(128)S(1)} %pad_add_fusion.info, bf16[128,2048]{1,0:T(8,128)(2,1)S(1)} %collective-permute-done.1.near_ref, bf16[128,2048]{1,0:T(8,128)(2,1)S(1)} %collective-permute-done.2.far_ref, f32[1,256]{1,0:T(1,128)S(1)} %bitcast.15, ...), custom_call_target="tpu_custom_call" | custom-call | flops 2684354560 | bytes 6291456 | tf_op jit(solution)/shard_map/pallas_call | solution.py:243
  158.0 1.5 shard_map.142
  159.8 3.4 %collective-permute-start.8 = (bf16[256,256]{1,0:T(8,128)(2,1)S(1)}, bf16[256,256]{1,0:T(8,128)(2,1)S(1)}, u32[]{:S(2)}, u32[]{:S(2)}) collective-permute-start(bf16[256,256]{1,0:T(8,128)(2,1)S(1)} %get-tuple-element.35), channel_id=1, source_target_pairs={{0,12},{2,14},{4,8},{6,10},{8,4},{10,6},{12,0},{14,2},{1,13},{3,15... | collective-permute-start | bytes 393224 | tf_op jit(solution)/shard_map/ppermute | solution.py:272
  163.2 1.2 collective-permute-start.3
  164.4 5.9 %collective-permute-done.4.left_ref = bf16[256,512]{1,0:T(8,128)(2,1)S(1)} collective-permute-done((bf16[256,512]{1,0:T(8,128)(2,1)S(1)}, bf16[256,512]{1,0:T(8,128)(2,1)S(1)}, u32[]{:S(2)}, u32[]{:S(2)}) %collective-permute-start.4) | collective-permute-done | bytes 262176 | tf_op jit(solution)/shard_map/ppermute | solution.py:272
  172.8 1.2 collective-permute-start.9
  174.1 3.2 %collective-permute-done.7.refs_1_ = bf16[256,256]{1,0:T(8,128)(2,1)S(1)} collective-permute-done((bf16[256,256]{1,0:T(8,128)(2,1)S(1)}, bf16[256,256]{1,0:T(8,128)(2,1)S(1)}, u32[]{:S(2)}, u32[]{:S(2)}) %collective-permute-start.7) | collective-permute-done | bytes 131104 | tf_op jit(solution)/shard_map/ppermute | solution.py:272
  178.5 1.6 collective-permute-done.9.refs_3_
  182.7 3.1 %shard_map.143 = (f32[512,1024]{1,0:T(8,128)S(1)}, f32[512,1024]{1,0:T(8,128)S(1)}) custom-call(s32[4]{0:T(128)S(1)} %pad_add_fusion.info, bf16[512,1024]{1,0:T(8,128)(2,1)S(1)} %get-tuple-element.28.q_ref.q_all, bf16[256,512]{1,0:T(8,128)(2,1)S(1)} %get-tuple-element.29.kv_ref, bf16[256,512]{1,0:T(8,128)(2,1)S(1)} %get-tuple-element.30.self_ref, ...), custom_call_target="tpu_custom_call" | custom-call | flops 1342177280 | bytes 8388608 | tf_op jit(solution)/shard_map/pallas_call | solution.py:243
  185.8 4.8 %shard_map.144 = (f32[512,1024]{1,0:T(8,128)S(1)}, f32[512,1024]{1,0:T(8,128)S(1)}) custom-call(s32[4]{0:T(128)S(1)} %pad_add_fusion.info, bf16[512,1024]{1,0:T(8,128)(2,1)S(1)} %get-tuple-element.28.q_ref.q_all, f32[512,1024]{1,0:T(8,128)S(1)} %get-tuple-element.31.num_in, f32[512,1024]{1,0:T(8,128)S(1)} %get-tuple-element.32.den_in, ...), custom_call_target="tpu_custom_call" | custom-call | flops 1073741824 | bytes 8388608 | tf_op jit(solution)/shard_map/pallas_call | solution.py:243
  190.7 5.0 %shard_map.146.gb = bf16[512,512]{1,0:T(8,128)(2,1)S(1)} custom-call(s32[4]{0:T(128)S(1)} %pad_add_fusion.info, bf16[512,1024]{1,0:T(8,128)(2,1)S(1)} %get-tuple-element.28.q_ref.q_all, f32[512,1024]{1,0:T(8,128)S(1)} %get-tuple-element.33.num_in, f32[512,1024]{1,0:T(8,128)S(1)} %get-tuple-element.34.den_in, ...), custom_call_target="tpu_custom_call" | custom-call | flops 1073741824 | bytes 8388608 | tf_op jit(solution)/shard_map/pallas_call | solution.py:243
  195.7 5.5 %collective-permute-start.15 = (bf16[512,512]{1,0:T(8,128)(2,1)S(1)}, bf16[512,512]{1,0:T(8,128)(2,1)S(1)}, u32[]{:S(2)}, u32[]{:S(2)}) collective-permute-start(bf16[512,512]{1,0:T(8,128)(2,1)S(1)} %shard_map.146.gb), channel_id=1, source_target_pairs={{0,1},{1,0},{2,3},{3,2},{4,5},{5,4},{6,7},{7,6},{8,9},{9,8},{10,11... | collective-permute-start | bytes 1572872 | tf_op jit(solution)/shard_map/ppermute | solution.py:271
  201.2 5.0 %shard_map.145.ga = bf16[512,512]{1,0:T(8,128)(2,1)S(1)} custom-call(s32[4]{0:T(128)S(1)} %pad_add_fusion.info, bf16[512,1024]{1,0:T(8,128)(2,1)S(1)} %get-tuple-element.28.q_ref.q_all, f32[512,1024]{1,0:T(8,128)S(1)} %get-tuple-element.33.num_in, f32[512,1024]{1,0:T(8,128)S(1)} %get-tuple-element.34.den_in, ...), custom_call_target="tpu_custom_call" | custom-call | flops 1073741824 | bytes 8388608 | tf_op jit(solution)/shard_map/pallas_call | solution.py:243
  206.3 1.9 collective-permute-done.14.ha
  208.2 6.4 %shard_map.147 = (bf16[256,2048]{1,0:T(8,128)(2,1)}, bf16[256,2048]{1,0:T(8,128)(2,1)}) custom-call(s32[4]{0:T(128)S(1)} %pad_add_fusion.info, s32[4]{0:T(128)S(1)} %bitcast.23, bf16[512,512]{1,0:T(8,128)(2,1)S(1)} %shard_map.145.ga, bf16[512,512]{1,0:T(8,128)(2,1)S(1)} %shard_map.146.gb, bf16[512,512]{1,0:T(8,128)(2,1)S(1)} %collective-permute-done.14.ha, ...), custom_call_target="tpu_custom_call" | custom-call | flops 4294967296 | bytes 8388608 | tf_op jit(solution)/shard_map/pallas_call | solution.py:243
  (52 shorter events, 7.6 us)
Async XLA Ops:
  0.7 14.1 %copy-start.3 = (f32[4096]{0:T(1024)S(1)}, f32[4096]{0:T(1024)}, u32[]{:S(2)}) copy-start(f32[4096]{0:T(1024)} %param.16) | copy-start | bytes 49156
  0.7 14.1 %copy-start = (bf16[4096,256]{1,0:T(8,128)(2,1)S(1)}, bf16[4096,256]{1,0:T(8,128)(2,1)}, u32[]{:S(2)}) copy-start(bf16[4096,256]{1,0:T(8,128)(2,1)} %wk_ref.5) | copy-start | bytes 6291460
  0.7 14.1 %copy-start.4 = (s32[1,256]{1,0:T(1,128)S(1)}, s32[1,256]{1,0:T(1,128)}, u32[]{:S(2)}) copy-start(s32[1,256]{1,0:T(1,128)} %mask_ref.5) | copy-start | bytes 3076
  1.9 148.4 %collective-permute-start.1 = (bf16[128,2048]{1,0:T(8,128)(2,1)S(1)}, bf16[128,2048]{1,0:T(8,128)(2,1)S(1)}, u32[]{:S(2)}, u32[]{:S(2)}) collective-permute-start(bf16[128,2048]{1,0:T(8,128)(2,1)S(1)} %constant_dynamic-slice_fusion), channel_id=1, source_target_pairs={{0,16},{16,0},{1,17},{17,1},{2,18},{18,2},{3,19},{19,3},{4,20},{20... | collective-permute-start | bytes 1572872 | tf_op jit(solution)/shard_map/ppermute | solution.py:270
  4.7 10.1 %collective-permute-start = (f32[256]{0:T(256)S(1)}, f32[256]{0:T(256)S(1)}, u32[]{:S(2)}, u32[]{:S(2)}) collective-permute-start(f32[256]{0:T(256)S(1)} %multiply_reduce_fusion), channel_id=1, source_target_pairs={{0,16},{16,0},{1,17},{17,1},{2,18},{18,2},{3,19},{19,3},{4,20},{20... | collective-permute-start | bytes 3080 | tf_op jit(solution)/shard_map/ppermute | solution.py:270
  14.8 138.7 %slice-start = ((s8[8388608]{0:T(1024)(128)(4,1)}), s8[4194304]{0:T(1024)(128)(4,1)S(1)}, s32[]{:S(2)}) async-start(s8[8388608]{0:T(1024)(128)(4,1)} %bitcast.10), calls=%async_computation | async-start | bytes 8388608
  17.9 135.6 %slice-start.1 = ((s8[8388608]{0:T(1024)(128)(4,1)}), s8[4194304]{0:T(1024)(128)(4,1)S(1)}, s32[]{:S(2)}) async-start(s8[8388608]{0:T(1024)(128)(4,1)} %bitcast.10), calls=%async_computation.1 | async-start | bytes 8388608
  17.9 135.6 %copy-start.5 = (f32[128]{0:T(128)S(1)}, f32[128]{0:T(128)}, u32[]{:S(2)}) copy-start(f32[128]{0:T(128)} %param.22) | copy-start | bytes 1540
  17.9 135.6 %copy-start.6 = (f32[128]{0:T(128)S(1)}, f32[128]{0:T(128)}, u32[]{:S(2)}) copy-start(f32[128]{0:T(128)} %param.21) | copy-start | bytes 1540
  150.3 3.2 %collective-permute-start.2 = (bf16[128,2048]{1,0:T(8,128)(2,1)S(1)}, bf16[128,2048]{1,0:T(8,128)(2,1)S(1)}, u32[]{:S(2)}, u32[]{:S(2)}) collective-permute-start(bf16[128,2048]{1,0:T(8,128)(2,1)S(1)} %collective-permute-done.1.near_ref), channel_id=1, source_target_pairs={{0,1},{1,0},{2,3},{3,2},{4,5},{5,4},{6,7},{7,6},{8,9},{9,8},{10,11... | collective-permute-start | bytes 1572872 | tf_op jit(solution)/shard_map/ppermute | solution.py:271
  157.5 50.6 %collective-permute-start.16 = (bf16[1024,2048]{1,0:T(8,128)(2,1)}, bf16[1024,2048]{1,0:T(8,128)(2,1)S(1)}, u32[]{:S(2)}, u32[]{:S(2)}) collective-permute-start(bf16[1024,2048]{1,0:T(8,128)(2,1)} %get-tuple-element.37), channel_id=1, source_target_pairs={{0,1},{1,0},{2,3},{3,2},{4,5},{5,4},{6,7},{7,6},{8,9},{9,8},{10,11... | collective-permute-start | bytes 12582920 | tf_op jit(solution)/shard_map/ppermute | solution.py:271
  159.5 10.8 %collective-permute-start.4 = (bf16[256,512]{1,0:T(8,128)(2,1)S(1)}, bf16[256,512]{1,0:T(8,128)(2,1)S(1)}, u32[]{:S(2)}, u32[]{:S(2)}) collective-permute-start(bf16[256,512]{1,0:T(8,128)(2,1)S(1)} %get-tuple-element.29.kv_ref), channel_id=1, source_target_pairs={{0,4},{2,6},{4,0},{6,2},{8,12},{10,14},{12,8},{14,10},{1,5},{3,7},... | collective-permute-start | bytes 786440 | tf_op jit(solution)/shard_map/ppermute | solution.py:272
  159.8 11.8 %collective-permute-start.6 = (bf16[256,256]{1,0:T(8,128)(2,1)S(1)}, bf16[256,256]{1,0:T(8,128)(2,1)S(1)}, u32[]{:S(2)}, u32[]{:S(2)}) collective-permute-start(bf16[256,256]{1,0:T(8,128)(2,1)S(1)} %get-tuple-element.35), channel_id=1, source_target_pairs={{0,8},{2,10},{4,12},{6,14},{8,0},{10,2},{12,4},{14,6},{1,9},{3,11}... | collective-permute-start | bytes 393224 | tf_op jit(solution)/shard_map/ppermute | solution.py:272
  159.8 13.0 %collective-permute-start.8 = (bf16[256,256]{1,0:T(8,128)(2,1)S(1)}, bf16[256,256]{1,0:T(8,128)(2,1)S(1)}, u32[]{:S(2)}, u32[]{:S(2)}) collective-permute-start(bf16[256,256]{1,0:T(8,128)(2,1)S(1)} %get-tuple-element.35), channel_id=1, source_target_pairs={{0,12},{2,14},{4,8},{6,10},{8,4},{10,6},{12,0},{14,2},{1,13},{3,15... | collective-permute-start | bytes 393224 | tf_op jit(solution)/shard_map/ppermute | solution.py:272
  163.2 18.1 %collective-permute-start.3 = (bf16[256,512]{1,0:T(8,128)(2,1)S(1)}, bf16[256,512]{1,0:T(8,128)(2,1)S(1)}, u32[]{:S(2)}, u32[]{:S(2)}) collective-permute-start(bf16[256,512]{1,0:T(8,128)(2,1)S(1)} %get-tuple-element.29.kv_ref), channel_id=1, source_target_pairs={{0,2},{2,0},{4,6},{6,4},{8,10},{10,8},{12,14},{14,12},{1,3},{3,1},... | collective-permute-start | bytes 786440 | tf_op jit(solution)/shard_map/ppermute | solution.py:272
  170.3 11.2 %collective-permute-start.5 = (bf16[256,512]{1,0:T(8,128)(2,1)S(1)}, bf16[256,512]{1,0:T(8,128)(2,1)S(1)}, u32[]{:S(2)}, u32[]{:S(2)}) collective-permute-start(bf16[256,512]{1,0:T(8,128)(2,1)S(1)} %collective-permute-done.4.left_ref), channel_id=1, source_target_pairs={{0,2},{2,0},{4,6},{6,4},{8,10},{10,8},{12,14},{14,12},{1,3},{3,1},... | collective-permute-start | bytes 786440 | tf_op jit(solution)/shard_map/ppermute | solution.py:272
  171.5 5.7 %collective-permute-start.7 = (bf16[256,256]{1,0:T(8,128)(2,1)S(1)}, bf16[256,256]{1,0:T(8,128)(2,1)S(1)}, u32[]{:S(2)}, u32[]{:S(2)}) collective-permute-start(bf16[256,256]{1,0:T(8,128)(2,1)S(1)} %collective-permute-done.6.refs_0_), channel_id=1, source_target_pairs={{0,2},{2,0},{4,6},{6,4},{8,10},{10,8},{12,14},{14,12},{1,3},{3,1},... | collective-permute-start | bytes 393224 | tf_op jit(solution)/shard_map/ppermute | solution.py:272
  172.8 7.3 %collective-permute-start.9 = (bf16[256,256]{1,0:T(8,128)(2,1)S(1)}, bf16[256,256]{1,0:T(8,128)(2,1)S(1)}, u32[]{:S(2)}, u32[]{:S(2)}) collective-permute-start(bf16[256,256]{1,0:T(8,128)(2,1)S(1)} %collective-permute-done.8.refs_2_), channel_id=1, source_target_pairs={{0,2},{2,0},{4,6},{6,4},{8,10},{10,8},{12,14},{14,12},{1,3},{3,1},... | collective-permute-start | bytes 393224 | tf_op jit(solution)/shard_map/ppermute | solution.py:272
  177.3 13.4 %collective-permute-start.10 = (bf16[256,256]{1,0:T(8,128)(2,1)S(1)}, bf16[256,256]{1,0:T(8,128)(2,1)S(1)}, u32[]{:S(2)}, u32[]{:S(2)}) collective-permute-start(bf16[256,256]{1,0:T(8,128)(2,1)S(1)} %collective-permute-done.6.refs_0_), channel_id=1, source_target_pairs={{0,16},{16,0},{1,17},{17,1},{2,18},{18,2},{3,19},{19,3},{4,20},{20... | collective-permute-start | bytes 393224 | tf_op jit(solution)/shard_map/ppermute | solution.py:270
  180.1 10.6 %collective-permute-start.12 = (bf16[256,256]{1,0:T(8,128)(2,1)S(1)}, bf16[256,256]{1,0:T(8,128)(2,1)S(1)}, u32[]{:S(2)}, u32[]{:S(2)}) collective-permute-start(bf16[256,256]{1,0:T(8,128)(2,1)S(1)} %collective-permute-done.8.refs_2_), channel_id=1, source_target_pairs={{0,16},{16,0},{1,17},{17,1},{2,18},{18,2},{3,19},{19,3},{4,20},{20... | collective-permute-start | bytes 393224 | tf_op jit(solution)/shard_map/ppermute | solution.py:270
  181.3 9.4 %collective-permute-start.11 = (bf16[256,256]{1,0:T(8,128)(2,1)S(1)}, bf16[256,256]{1,0:T(8,128)(2,1)S(1)}, u32[]{:S(2)}, u32[]{:S(2)}) collective-permute-start(bf16[256,256]{1,0:T(8,128)(2,1)S(1)} %collective-permute-done.7.refs_1_), channel_id=1, source_target_pairs={{0,16},{16,0},{1,17},{17,1},{2,18},{18,2},{3,19},{19,3},{4,20},{20... | collective-permute-start | bytes 393224 | tf_op jit(solution)/shard_map/ppermute | solution.py:270
  181.5 9.1 %collective-permute-start.13 = (bf16[256,256]{1,0:T(8,128)(2,1)S(1)}, bf16[256,256]{1,0:T(8,128)(2,1)S(1)}, u32[]{:S(2)}, u32[]{:S(2)}) collective-permute-start(bf16[256,256]{1,0:T(8,128)(2,1)S(1)} %collective-permute-done.9.refs_3_), channel_id=1, source_target_pairs={{0,16},{16,0},{1,17},{17,1},{2,18},{18,2},{3,19},{19,3},{4,20},{20... | collective-permute-start | bytes 393224 | tf_op jit(solution)/shard_map/ppermute | solution.py:270
  195.7 10.6 %collective-permute-start.15 = (bf16[512,512]{1,0:T(8,128)(2,1)S(1)}, bf16[512,512]{1,0:T(8,128)(2,1)S(1)}, u32[]{:S(2)}, u32[]{:S(2)}) collective-permute-start(bf16[512,512]{1,0:T(8,128)(2,1)S(1)} %shard_map.146.gb), channel_id=1, source_target_pairs={{0,1},{1,0},{2,3},{3,2},{4,5},{5,4},{6,7},{7,6},{8,9},{9,8},{10,11... | collective-permute-start | bytes 1572872 | tf_op jit(solution)/shard_map/ppermute | solution.py:271
  206.2 2.0 collective-permute-start.14
  (7 other events, 45.6 us)

commit v3 on v2

v3 whole, which is shorter than its diff:
```python
import functools
import math

import jax
import jax.numpy as jnp
from jax import lax
from jax.experimental import pallas as pl
from jax.experimental.pallas import tpu as pltpu
from jax.sharding import PartitionSpec as P

HD = 128
BLK = 64
TSTEPS = 1000
EPS = 1e-06
F32 = jnp.float32
BF16 = jnp.bfloat16
SCORE_SCALE = math.log2(math.e) / math.sqrt(HD)


def to_column(row, n):
    eye = lax.broadcasted_iota(jnp.int32, (n, n), 0) == lax.broadcasted_iota(jnp.int32, (n, n), 1)
    return jnp.sum(jnp.where(eye, jnp.broadcast_to(row, (n, n)), 0.0), axis=1, keepdims=True)


def row_scales(own_ref, other_ref, mask_ref, embed_ref, width):
    n = own_ref.shape[1]
    clean = lax.rsqrt(to_column(own_ref[...] + other_ref[...], n) * (1.0 / width) + EPS)
    embed = embed_ref[...].astype(F32)
    embed_scale = lax.rsqrt(jnp.sum(embed * embed, axis=1, keepdims=True) * (1.0 / width) + EPS)
    masked = to_column(mask_ref[...].astype(F32), n)
    return clean, embed_scale, masked


def normed_clean(x, clean_scale, gain):
    return (x * clean_scale * gain).astype(BF16)


def normed_noisy(x, clean_scale, embed_scale, masked, gain, embed, condition):
    is_masked = masked == 1.0
    noisy = jnp.where(is_masked, embed, x)
    scale = jnp.where(is_masked, embed_scale, clean_scale)
    return (noisy * scale * gain * condition).astype(BF16)


def dot(a, b):
    return jnp.dot(a, b, preferred_element_type=F32)


def head_norm(wide, gain):
    scale = lax.rsqrt(jnp.mean(wide * wide, axis=1, keepdims=True) + EPS)
    return (wide * scale * gain).astype(BF16)


def both_streams(x, scales, gain, embed, condition):
    clean = normed_clean(x, scales[0], gain)
    noisy = normed_noisy(x, scales[0], scales[1], scales[2], gain, embed, condition)
    return clean, noisy


def half_vectors(at, info, gain_ref, embed_ref, shift_ref):
    gain = gain_ref[:, at].astype(F32)
    embed = embed_ref[:, at].astype(F32)
    condition = 1.0 + info[3].astype(F32) / TSTEPS * shift_ref[:, at]
    return gain, embed, condition


def both_streams(x, scales, gain, embed, condition):
    clean = normed_clean(x, scales[0], gain)
    noisy = normed_noisy(x, scales[0], scales[1], scales[2], gain, embed, condition)
    return clean, noisy


def vectors_at(at, info, gain_ref, embed_ref, shift_ref):
    gain = gain_ref[:, at].astype(F32)
    embed = embed_ref[:, at].astype(F32)
    condition = 1.0 + info[3].astype(F32) / TSTEPS * shift_ref[:, at]
    return gain, embed, condition


def own_half_kernel(
    info, x_ref, own_ref, other_ref, mask_ref, gain_ref, embed_ref, shift_ref, wq, wk, wv, w_out,
    q_ref, k_ref, v_ref, rest_q, rest_k, rest_v, w_send, own_q, own_k, own_v, sems,
):
    half = x_ref.shape[1]
    depth = half // 2
    cols = w_send.shape[1]
    first = info[0] * half
    moves = []

    def move(source, target):
        moves.append(pltpu.make_async_copy(source, target, sems.at[len(moves)]))
        moves[-1].start()

    for chunk in range(2):
        there = pl.ds(pl.multiple_of(first + chunk * depth, 128), depth)
        here = pl.ds(chunk * depth, depth)
        for source, target in ((wk, own_k), (wv, own_v), (wq, own_q)):
            move(source.at[there], target.at[here])
    rest = pl.ds(pl.multiple_of(half - first, 128), half)
    for source, target in ((wk, rest_k), (wv, rest_v), (wq, rest_q)):
        move(source.at[rest], target)
    side = pl.ds(pl.multiple_of((1 - info[1]) * cols, 128), cols)
    move(w_out.at[:, side], w_send)

    scales = row_scales(own_ref, other_ref, mask_ref, embed_ref, embed_ref.shape[1])
    at = pl.ds(pl.multiple_of(first, 128), half)
    gain, embed, condition = vectors_at(at, info, gain_ref, embed_ref, shift_ref)
    clean, noisy = both_streams(x_ref[...].astype(F32), scales, gain, embed, condition)
    both = jnp.concatenate([clean, noisy], axis=0)
    for chunk in range(2):
        here = slice(chunk * depth, (chunk + 1) * depth)
        for number, (target, weight) in enumerate(((k_ref, own_k), (v_ref, own_v), (q_ref, own_q))):
            moves[3 * chunk + number].wait()
            product = dot(both[:, here], weight[here])
            target[...] = product if chunk == 0 else target[...] + product
    for copy in moves[6:]:
        copy.wait()


def other_rows(info, near_ref, far_ref):
    near, far = near_ref[...].astype(F32), far_ref[...].astype(F32)
    first = info[1] == 0
    return jnp.concatenate([jnp.where(first, near, far), jnp.where(first, far, near)], axis=0)


def chunk_at(info, chunk, depth, width):
    return pl.ds(pl.multiple_of((1 - info[0]) * (width // 2) + chunk * depth, 128), depth)


def chunk_kernel(
    info, near_ref, far_ref, own_ref, other_ref, mask_ref, gain_ref, embed_ref, shift_ref,
    wq_ref, wk_ref, wv_ref, pq_ref, pk_ref, pv_ref, q_ref, k_ref, v_ref,
):
    width = embed_ref.shape[1]
    scales = row_scales(own_ref, other_ref, mask_ref, embed_ref, width)
    at = chunk_at(info, 0, near_ref.shape[1], width)
    gain, embed, condition = vectors_at(at, info, gain_ref, embed_ref, shift_ref)
    clean, noisy = both_streams(other_rows(info, near_ref, far_ref), scales, gain, embed, condition)
    both = jnp.concatenate([clean, noisy], axis=0)
    here = slice(0, near_ref.shape[1])
    k_ref[...] = pk_ref[...] + dot(both, wk_ref[here])
    v_ref[...] = pv_ref[...] + dot(both, wv_ref[here])
    q_ref[...] = pq_ref[...] + dot(both, wq_ref[here])


def kv_out(ref, k, v, gain):
    for head in range(k.shape[1] // HD):
        cols = slice(head * HD, (head + 1) * HD)
        ref[:, 2 * head * HD : (2 * head + 1) * HD] = head_norm(k[:, cols], gain)
        ref[:, (2 * head + 1) * HD : 2 * (head + 1) * HD] = v[:, cols].astype(BF16)


def clean_kv_kernel(
    info, near_ref, far_ref, own_ref, other_ref, mask_ref, gain_ref, embed_ref,
    wk_ref, wv_ref, pk_ref, pv_ref, kgain_ref, all_ref, one_ref,
):
    rows = all_ref.shape[0]
    width = embed_ref.shape[1]
    clean_scale = row_scales(own_ref, other_ref, mask_ref, embed_ref, width)[0]
    at = chunk_at(info, 1, near_ref.shape[1], width)
    clean = normed_clean(other_rows(info, near_ref, far_ref), clean_scale, gain_ref[:, at].astype(F32))
    here = slice(near_ref.shape[1], 2 * near_ref.shape[1])
    k = pk_ref[:rows] + dot(clean, wk_ref[here])
    v = pv_ref[:rows] + dot(clean, wv_ref[here])
    kv_out(all_ref, k, v, kgain_ref[...])
    cols = one_ref.shape[1]
    one_ref[...] = all_ref[:, pl.ds(pl.multiple_of(info[0] * cols, 128), cols)]


def last_chunk_kernel(
    info, near_ref, far_ref, own_ref, other_ref, mask_ref, gain_ref, embed_ref, shift_ref,
    wq_ref, wk_ref, wv_ref, pq_ref, pk_ref, pv_ref, qgain_ref, kgain_ref, q_ref, self_ref,
):
    rows = self_ref.shape[0]
    width = embed_ref.shape[1]
    scales = row_scales(own_ref, other_ref, mask_ref, embed_ref, width)
    at = chunk_at(info, 1, near_ref.shape[1], width)
    gain, embed, condition = vectors_at(at, info, gain_ref, embed_ref, shift_ref)
    clean, noisy = both_streams(other_rows(info, near_ref, far_ref), scales, gain, embed, condition)
    here = slice(near_ref.shape[1], 2 * near_ref.shape[1])
    k = pk_ref[rows:] + dot(noisy, wk_ref[here])
    v = pv_ref[rows:] + dot(noisy, wv_ref[here])
    kv_out(self_ref, k, v, kgain_ref[...])
    q = pq_ref[...] + dot(jnp.concatenate([clean, noisy], axis=0), wq_ref[here])
    for head in range(q_ref.shape[1] // HD):
        cols = slice(head * HD, (head + 1) * HD)
        q_ref[:, cols] = head_norm(q[:, cols], qgain_ref[...])


def terms(q, k, v, mask):
    scores = lax.dot_general(q, k, (((1,), (1,)), ((), ())), preferred_element_type=F32)
    e = jnp.exp2(scores * SCORE_SCALE)
    if mask is not None:
        e = jnp.where(mask, e, 0.0)
    den = e[:, :HD]
    for start in range(HD, e.shape[1], HD):
        den = den + e[:, start : start + HD]
    return dot(e.astype(BF16), v), den


def add_pieces(q_ref, num_ref, den_ref, base, heads, pieces, rows):
    k = jnp.concatenate([piece[:, :HD] for piece in pieces], axis=0)
    v = jnp.concatenate([piece[:, HD:] for piece in pieces], axis=0)
    for head in range(heads):
        cols = pl.ds(base + head * HD, HD)
        for part in range(2):
            cut = slice(part * rows, (part + 1) * rows)
            num, den = terms(q_ref[cut, cols], k, v, None)
            num_ref[cut, cols] += num
            den_ref[cut, cols] += den


def add_all_heads(q_ref, num_ref, den_ref, piece_refs, rows):
    kv_heads = piece_refs[0].shape[1] // (2 * HD)
    group_cols = q_ref.shape[1] // kv_heads
    for kv_head in range(kv_heads):
        cols = slice(2 * kv_head * HD, 2 * (kv_head + 1) * HD)
        pieces = [ref[:, cols] for ref in piece_refs]
        add_pieces(q_ref, num_ref, den_ref, kv_head * group_cols, group_cols // HD, pieces, rows)


def add_far(info, q_ref, num_ref, den_ref, which, offsets, refs, rows):
    cols = q_ref.shape[1] // 2
    base = pl.multiple_of((info[0] if which == 0 else 1 - info[0]) * cols, 128)
    for bit in sorted({offset.bit_length() for offset in offsets}):
        group = [ref for offset, ref in zip(offsets, refs) if offset.bit_length() == bit]

        @pl.when(jnp.bitwise_and(info[2], 1 << (bit - 1)) != 0)
        def _(group=group):
            add_pieces(q_ref, num_ref, den_ref, base, cols // HD, [ref[...] for ref in group], rows)


def finish(info, num_ref, den_ref, which, out_ref):
    width = out_ref.shape[1]
    base = pl.multiple_of((info[0] if which == 0 else 1 - info[0]) * width, 128)
    for head in range(width // HD):
        cols = pl.ds(base + head * HD, HD)
        total = jnp.sum(den_ref[:, cols], axis=1, keepdims=True)
        out_ref[:, head * HD : (head + 1) * HD] = (num_ref[:, cols] / total).astype(BF16)


def attention_own_kernel(info, q_ref, kv_ref, self_ref, near_ref, num_ref, den_ref):
    rows = kv_ref.shape[0]
    kv_heads = kv_ref.shape[1] // (2 * HD)
    group = q_ref.shape[1] // HD // kv_heads
    row_block = lax.broadcasted_iota(jnp.int32, (rows, rows), 0) // BLK
    key_block = lax.broadcasted_iota(jnp.int32, (rows, rows), 1) // BLK
    both = jnp.concatenate([key_block < row_block, key_block == row_block], axis=1)
    for kv_head in range(kv_heads):
        k_cols = slice(2 * kv_head * HD, (2 * kv_head + 1) * HD)
        v_cols = slice((2 * kv_head + 1) * HD, 2 * (kv_head + 1) * HD)
        k, v = kv_ref[:, k_cols], kv_ref[:, v_cols]
        k_both = jnp.concatenate([k, self_ref[:, k_cols]], axis=0)
        v_both = jnp.concatenate([v, self_ref[:, v_cols]], axis=0)
        for head in range(kv_head * group, (kv_head + 1) * group):
            cols = slice(head * HD, (head + 1) * HD)
            num_ref[:rows, cols], den_ref[:rows, cols] = terms(q_ref[:rows, cols], k, v, key_block <= row_block)
            num_ref[rows:, cols], den_ref[rows:, cols] = terms(q_ref[rows:, cols], k_both, v_both, both)

    @pl.when(jnp.bitwise_and(info[2], 1) != 0)
    def _():
        add_all_heads(q_ref, num_ref, den_ref, [near_ref], rows)


def attention_column_kernel(info, q_ref, num_in, den_in, left_ref, *refs, offsets):
    num_ref, den_ref = refs[-2:]
    rows = left_ref.shape[0]

    @pl.when(jnp.bitwise_and(info[2], 2) != 0)
    def _():
        add_all_heads(q_ref, num_ref, den_ref, [left_ref], rows)

    add_far(info, q_ref, num_ref, den_ref, 0, offsets, refs[: len(offsets)], rows)


def attention_first_head_kernel(info, q_ref, num_in, den_in, right_ref, *refs, offsets):
    num_ref, den_ref, out_ref = refs[-3:]
    rows = right_ref.shape[0]
    count = len(offsets)

    @pl.when(jnp.bitwise_and(info[2], 2) != 0)
    def _():
        add_all_heads(q_ref, num_ref, den_ref, [right_ref], rows)

    add_far(info, q_ref, num_ref, den_ref, 0, offsets, refs[:count], rows)
    finish(info, num_ref, den_ref, 0, out_ref)
    add_far(info, q_ref, num_ref, den_ref, 1, offsets, refs[count : 2 * count], rows)


def attention_second_head_kernel(info, q_ref, num_in, den_in, *refs, offsets):
    num_ref, den_ref, out_ref = refs[-3:]
    rows = out_ref.shape[0] // 2
    add_far(info, q_ref, num_ref, den_ref, 1, offsets, refs[: len(offsets)], rows)
    finish(info, num_ref, den_ref, 1, out_ref)


def out_kernel(info, live, ga, gb, ha, hb, w_mine, w_far, clean_ref, noisy_ref):
    rows, tile = clean_ref.shape
    part = ga.shape[1]
    cols = pl.ds(pl.multiple_of(pl.program_id(0) * tile, 128), tile)
    first = pl.ds(pl.multiple_of(info[0] * part, 128), part)
    second = pl.ds(pl.multiple_of((1 - info[0]) * part, 128), part)
    mixed = dot(ga[...], w_mine[first]) + dot(gb[...], w_mine[second])
    mixed = mixed + dot(ha[...], w_far[first, cols]) + dot(hb[...], w_far[second, cols])
    clean_ref[...] = mixed[:rows].astype(BF16)
    for block in range(rows // BLK):
        part_rows = mixed[rows + block * BLK : rows + (block + 1) * BLK]
        noisy_ref[block * BLK : (block + 1) * BLK] = (part_rows * live[block].astype(F32)).astype(BF16)


WHOLE = pl.BlockSpec(memory_space=pltpu.VMEM)
HBM = pl.BlockSpec(memory_space=pltpu.HBM)
HINT = 1


def call(kernel, scalars, ins, outs, arrays, flops, num_bytes, scratch=(), exps=0, grid=1, aliases=None, limit=20):
    return pl.pallas_call(
        kernel,
        grid_spec=pltpu.PrefetchScalarGridSpec(
            num_scalar_prefetch=len(scalars),
            grid=(grid,),
            in_specs=ins,
            out_specs=[spec for spec, _ in outs],
            scratch_shapes=list(scratch),
        ),
        out_shape=[shape for _, shape in outs],
        compiler_params=pltpu.CompilerParams(vmem_limit_bytes=limit << 20),
        cost_estimate=pl.CostEstimate(
            flops=flops // HINT, bytes_accessed=num_bytes // HINT, transcendentals=exps // HINT
        ),
        input_output_aliases=aliases or {},
    )(*scalars, *arrays)


def after(value, *others):
    return lax.optimization_barrier((value, *others))[0]


def on_device(
    mesh, clean_tokens, norm_gain, mask_embed, time_shift, w_query, w_key, w_value, w_out,
    q_gain, k_gain, masked, block_live, timesteps,
):
    rows, half = clean_tokens.shape
    heads_width = w_query.shape[1]
    kv_width = w_key.shape[1]
    part = heads_width // 2
    ctx = mesh.shape["ctx"]
    c, p, t = lax.axis_index("copy"), lax.axis_index("ctx"), lax.axis_index("tp")
    info = jnp.stack([c, t, p, timesteps[0]]).astype(jnp.int32)
    pair = [(0, 1), (1, 0)]
    cross_x = lambda v: lax.ppermute(v, "copy", pair)
    cross_core = lambda v: lax.ppermute(v, "tp", pair)
    cross_ctx = lambda v, offset: lax.ppermute(v, "ctx", [(i, i ^ offset) for i in range(ctx)])
    shape = jax.ShapeDtypeStruct

    cut, depth = rows // 2, half // 2
    strip = lambda v, chunk: lax.dynamic_slice(v, (t * cut, chunk * depth), (cut, depth))
    near_first = cross_x(strip(clean_tokens, 0))
    wide = clean_tokens.astype(F32)
    squares = jnp.sum(wide * wide, axis=1)
    other_squares = cross_x(squares)
    near_last = cross_x(strip(after(clean_tokens, squares), 1))
    out_cols = w_out.shape[1] // 2
    stats = [squares[None], other_squares[None], masked]
    vectors = [norm_gain[None], mask_embed[None], time_shift[None]]
    qg, kg = q_gain[None], k_gain[None]
    partial = [
        (WHOLE, shape((2 * rows, heads_width), F32)),
        (WHOLE, shape((2 * rows, kv_width), F32)),
        (WHOLE, shape((2 * rows, kv_width), F32)),
    ]
    per_row = heads_width + 2 * kv_width

    bf = lambda *dims: (WHOLE, shape(dims, BF16))
    buffers = [(half, heads_width), (half, kv_width), (half, kv_width)]
    pq, pk, pv, *weights, w_send = call(
        own_half_kernel, [info], [WHOLE] * 7 + [HBM] * 4,
        partial + [bf(*dims) for dims in buffers] + [bf(heads_width, out_cols)],
        [clean_tokens] + stats + vectors + [w_query, w_key, w_value, w_out],
        4 * rows * half * per_row, heads_width * out_cols * 2,
        [pltpu.VMEM(dims, BF16) for dims in buffers] + [pltpu.SemaphoreType.DMA((10,))],
        limit=40,
    )
    far_first = cross_core(near_first)
    pq, pk, pv = call(
        chunk_kernel, [info], [WHOLE] * 14, partial,
        [near_first, far_first] + stats + vectors + weights + [pq, pk, pv],
        4 * rows * depth * per_row, depth * per_row * 2, aliases={12: 0, 13: 1, 14: 2},
    )
    near_last = after(near_last, pk)
    far_last = cross_core(near_last)

    kv, kva = call(
        clean_kv_kernel, [info], [WHOLE] * 12,
        [(WHOLE, shape((rows, 2 * kv_width), BF16)), (WHOLE, shape((rows, kv_width), BF16))],
        [near_last, far_last] + stats + vectors[:2] + weights[1:] + [pk, pv, kg],
        4 * rows * depth * kv_width, depth * 2 * kv_width * 2,
    )

    offsets = list(range(4, ctx, 2))
    beside = cross_ctx(kv, 1)
    left = cross_ctx(kv, 2)
    column = [cross_ctx(kva, offset) for offset in offsets]

    near_last = after(near_last, kv)
    q, own = call(
        last_chunk_kernel, [info], [WHOLE] * 16,
        [(WHOLE, shape((2 * rows, heads_width), BF16)), (WHOLE, shape((rows, 2 * kv_width), BF16))],
        [near_last, far_last] + stats + vectors + weights + [pq, pk, pv, qg, kg],
        4 * rows * depth * per_row, depth * per_row * 2,
    )
    w_far = cross_core(after(w_send, kv))

    acc_shape = shape((2 * rows, heads_width), F32)
    acc = [(WHOLE, acc_shape), (WHOLE, acc_shape)]
    attended = (WHOLE, shape((2 * rows, part), BF16))
    unit = rows * rows * heads_width // HD
    cost = lambda units: (4 * HD * unit * units, 8 * unit, (), unit * units)
    in_place = {2: 0, 3: 1}
    num, den = call(attention_own_kernel, [info], [WHOLE] * 4, acc, [q, kv, own, beside], *cost(5))
    column = [after(piece, num) for piece in column]
    left = after(left, num)
    column_right = [cross_ctx(piece, 1) for piece in column]
    other = [cross_x(piece) for piece in column]
    right = cross_ctx(left, 1)
    num, den = call(
        functools.partial(attention_column_kernel, offsets=offsets), [info], [WHOLE] * (4 + len(column)), acc,
        [q, num, den, left] + column, *cost(4), aliases=in_place,
    )
    column_right = [after(piece, num) for piece in column_right]
    other_right = [cross_x(piece) for piece in column_right]
    num, den, ga = call(
        functools.partial(attention_first_head_kernel, offsets=offsets), [info],
        [WHOLE] * (4 + 2 * len(column)), acc + [attended],
        [q, num, den, right] + column_right + other, *cost(6), aliases=in_place,
    )
    ha = cross_core(ga)
    num, den, gb = call(
        functools.partial(attention_second_head_kernel, offsets=offsets), [info],
        [WHOLE] * (3 + len(column)), acc + [attended], [q, num, den] + other_right, *cost(2), aliases=in_place,
    )
    hb = cross_core(gb)

    tile = 512
    tiles = out_cols // tile
    mine = pl.BlockSpec((heads_width, tile), lambda n, s, l: (0, s[1] * tiles + n))
    out = pl.BlockSpec((rows, tile), lambda n, s, l: (0, n))
    out_shape = shape((rows, out_cols), BF16)
    clean_out, noised_out = call(
        out_kernel, [info, block_live[0]], [WHOLE] * 4 + [mine, WHOLE], [(out, out_shape), (out, out_shape)],
        [ga, gb, ha, hb, w_out, w_far],
        8 * rows * heads_width * out_cols, 2 * heads_width * out_cols * 2, grid=tiles,
    )
    return (clean_out, noised_out[None])


def solution(mesh):
    in_specs = (
        P("ctx", "copy"),
        P(),
        P(),
        P(),
        P(None, "tp"),
        P(None, "tp"),
        P(None, "tp"),
        P("tp", None),
        P(),
        P(),
        P("copy", "ctx"),
        P("copy", "ctx"),
        P("copy"),
    )
    out_specs = (P("ctx", "tp"), P("copy", "ctx", "tp"))
    return jax.shard_map(
        functools.partial(on_device, mesh), mesh=mesh, in_specs=in_specs, out_specs=out_specs, check_vma=False
    )
```

time: 216 us -> 84.7 us (0.39)
  Pallas kernels: 162 us -> 39.6 us
  waiting for transfers between devices: 24.2 us -> 15.8 us
  local copies, waits for them, and re-layouts: 4.4 us -> 7.45 us
  starting transfers between devices: 20.7 us -> 18.3 us
    pallas_call x8 -> x9, Pallas kernels: 162 us -> 39.6 us  [call(): pl.pallas_call(kernel, grid_spec=pltpu.PrefetchScalarGridSpec(num_scalar_...]
    ppermute x6 -> x7, waiting for transfers between devices: 9.01 us -> 1.13 us  [on_device(): cross_x = lambda v: lax.ppermute(v, 'copy', pair)]
    ppermute x4 -> x5, starting transfers between devices: 7.67 us -> 5.06 us  [on_device(): cross_core = lambda v: lax.ppermute(v, 'tp', pair)]
    unnamed x28 -> x30, local copies, waits for them, and re-layouts: 3.15 us -> 5.41 us
    ppermute x6 -> x7, starting transfers between devices: 5.44 us -> 6.78 us  [on_device(): cross_x = lambda v: lax.ppermute(v, 'copy', pair)]
  transfers between devices with their start and end apart: 17 -> 19, of which waited for: 7 -> 8; matrix products, arithmetic and copies ran while one was open for 1% -> 3% of each run, Pallas kernels for 71% -> 38%
where the time goes in v3:
time: 84.7 us; the launch traced here: 84.3 us
  Pallas kernels  39.6 us (47%)
  starting transfers between devices  18.3 us (22%)
  waiting for transfers between devices  15.8 us (19%)
  local copies, waits for them, and re-layouts  7.45 us (9%)
  other arithmetic  1.59 us (2%)
  between operations  1.54 us (2%)
    pallas_call x9, Pallas kernels, call(): pl.pallas_call(kernel, grid_spec=pltpu.PrefetchScalarGridSpec(num_scalar_...  39.6 us
    ppermute x7, waiting for transfers between devices, on_device(): lax.ppermute(v, 'ctx', [(i, i ^ offset) for i in range(ctx)])  11 us
    ppermute x7, starting transfers between devices, on_device(): cross_x = lambda v: lax.ppermute(v, 'copy', pair)  6.78 us
    ppermute x7, starting transfers between devices, on_device(): lax.ppermute(v, 'ctx', [(i, i ^ offset) for i in range(ctx)])  6.47 us
    unnamed x30, local copies, waits for them, and re-layouts  5.41 us
    ppermute x5, starting transfers between devices, on_device(): cross_core = lambda v: lax.ppermute(v, 'tp', pair)  5.06 us
    ppermute x5, waiting for transfers between devices, on_device(): cross_core = lambda v: lax.ppermute(v, 'tp', pair)  3.7 us
    dynamic_slice x2, local copies, waits for them, and re-layouts, on_device(): lax.dynamic_slice(v, (t * cut, chunk * depth), (cut, depth))  2.02 us
  transfers between devices with their start and end apart: 19, of which 8 were waited for; matrix products, arithmetic and copies ran while one was open for 3% of the time, Pallas kernels for 38%

profile of v3, /device:TPU:25, one launch (start us, length us, event | category | flops | bytes accessed | tf_op | source)
XLA Modules:
  0.0 84.3 jit_solution(10912359567488643745)
XLA Ops:
  1.7 1.3 %collective-permute-start.1 = (bf16[128,1024]{1,0:T(8,128)(2,1)S(1)}, bf16[128,1024]{1,0:T(8,128)(2,1)S(1)}, u32[]{:S(2)}, u32[]{:S(2)}) collective-permute-start(bf16[128,1024]{1,0:T(8,128)(2,1)S(1)} %constant_dynamic-slice_fusion.1), channel_id=1, source_target_pairs={{0,16},{16,0},{1,17},{17,1},{2,18},{18,2},{3,19},{19,3},{4,20},{20... | collective-permute-start | bytes 786440 | tf_op jit(solution)/shard_map/ppermute | solution.py:351
  3.0 1.5 %multiply_reduce_fusion = f32[256]{0:T(256)S(1)} fusion(bf16[256,2048]{1,0:T(8,128)(2,1)} %x_ref.1), kind=kLoop, calls=%fused_computation | loop fusion | flops 1572608 | bytes 1049600 | tf_op jit(solution)/shard_map/reduce_sum | solution.py:360
  5.8 1.3 %collective-permute-start = (bf16[128,1024]{1,0:T(8,128)(2,1)S(1)}, bf16[128,1024]{1,0:T(8,128)(2,1)S(1)}, u32[]{:S(2)}, u32[]{:S(2)}) collective-permute-start(bf16[128,1024]{1,0:T(8,128)(2,1)S(1)} %constant_dynamic-slice_fusion), channel_id=1, source_target_pairs={{0,16},{16,0},{1,17},{17,1},{2,18},{18,2},{3,19},{19,3},{4,20},{20... | collective-permute-start | bytes 786440 | tf_op jit(solution)/shard_map/ppermute | solution.py:351
  9.0 2.7 %collective-permute-start.2 = (bf16[128,1024]{1,0:T(8,128)(2,1)S(1)}, bf16[128,1024]{1,0:T(8,128)(2,1)S(1)}, u32[]{:S(2)}, u32[]{:S(2)}) collective-permute-start(bf16[128,1024]{1,0:T(8,128)(2,1)S(1)} %collective-permute-done.1.near_ref), channel_id=1, source_target_pairs={{0,1},{1,0},{2,3},{3,2},{4,5},{5,4},{6,7},{7,6},{8,9},{9,8},{10,11... | collective-permute-start | bytes 786440 | tf_op jit(solution)/shard_map/ppermute | solution.py:352
  11.7 1.6 %copy-done.3 = bf16[4096,256]{1,0:T(8,128)(2,1)S(1)} copy-done((bf16[4096,256]{1,0:T(8,128)(2,1)S(1)}, bf16[4096,256]{1,0:T(8,128)(2,1)}, u32[]{:S(2)}) %copy-start.3) | copy-done | bytes 2097176
  13.3 1.6 %copy-done.4 = bf16[4096,256]{1,0:T(8,128)(2,1)S(1)} copy-done((bf16[4096,256]{1,0:T(8,128)(2,1)S(1)}, bf16[4096,256]{1,0:T(8,128)(2,1)}, u32[]{:S(2)}) %copy-start.4) | copy-done | bytes 2097176
  14.9 9.9 %shard_map.140 = (f32[512,1024]{1,0:T(8,128)S(1)}, f32[512,256]{1,0:T(8,128)S(1)}, f32[512,256]{1,0:T(8,128)S(1)}, bf16[2048,1024]{1,0:T(8,128)(2,1)}, bf16[2048...) custom-call(s32[4]{0:T(128)S(1)} %pad_add_fusion.info, ...), custom_call_target="tpu_custom_call" | custom-call | flops 3221225472 | bytes 4194304 | tf_op jit(solution)/shard_map/pallas_call | solution.py:317
  24.8 2.2 %copy-done = bf16[2048,1024]{1,0:T(8,128)(2,1)S(1)} copy-done((bf16[2048,1024]{1,0:T(8,128)(2,1)S(1)}, bf16[2048,1024]{1,0:T(8,128)(2,1)}, u32[]{:S(2)}) %copy-start) | copy-done | bytes 4194328
  27.0 2.6 %shard_map.141 = (f32[512,1024]{1,0:T(8,128)S(1)}, f32[512,256]{1,0:T(8,128)S(1)}, f32[512,256]{1,0:T(8,128)S(1)}) custom-call(s32[4]{0:T(128)S(1)} %pad_add_fusion.info, bf16[128,1024]{1,0:T(8,128)(2,1)S(1)} %collective-permute-done.1.near_ref, ...), custom_call_target="tpu_custom_call", output_to_operand_aliasing={{0}: (12, {}), {1}: (13, {}), {2}: (14, {})} | custom-call | flops 1610612736 | bytes 3145728 | tf_op jit(solution)/shard_map/pallas_call | solution.py:317
  29.7 1.5 %collective-permute-done.4.far_ref = bf16[128,1024]{1,0:T(8,128)(2,1)S(1)} collective-permute-done((bf16[128,1024]{1,0:T(8,128)(2,1)S(1)}, bf16[128,1024]{1,0:T(8,128)(2,1)S(1)}, u32[]{:S(2)}, u32[]{:S(2)}) %collective-permute-start.4) | collective-permute-done | bytes 262176 | tf_op jit(solution)/shard_map/ppermute | solution.py:352
  33.9 1.4 %collective-permute-start.7 = (bf16[256,256]{1,0:T(8,128)(2,1)S(1)}, bf16[256,256]{1,0:T(8,128)(2,1)S(1)}, u32[]{:S(2)}, u32[]{:S(2)}) collective-permute-start(bf16[256,256]{1,0:T(8,128)(2,1)S(1)} %get-tuple-element.53), channel_id=1, source_target_pairs={{0,8},{2,10},{4,12},{6,14},{8,0},{10,2},{12,4},{14,6},{1,9},{3,11}... | collective-permute-start | bytes 393224 | tf_op jit(solution)/shard_map/ppermute | solution.py:353
  35.3 2.2 %collective-permute-start.6 = (bf16[256,512]{1,0:T(8,128)(2,1)S(1)}, bf16[256,512]{1,0:T(8,128)(2,1)S(1)}, u32[]{:S(2)}, u32[]{:S(2)}) collective-permute-start(bf16[256,512]{1,0:T(8,128)(2,1)S(1)} %get-tuple-element.45.kv_ref), channel_id=1, source_target_pairs={{0,4},{2,6},{4,0},{6,2},{8,12},{10,14},{12,8},{14,10},{1,5},{3,7},... | collective-permute-start | bytes 786440 | tf_op jit(solution)/shard_map/ppermute | solution.py:353
  37.5 2.6 %shard_map.143 = (bf16[512,1024]{1,0:T(8,128)(2,1)S(1)}, bf16[256,512]{1,0:T(8,128)(2,1)S(1)}) custom-call(s32[4]{0:T(128)S(1)} %pad_add_fusion.info, bf16[128,1024]{1,0:T(8,128)(2,1)S(1)} %collective-permute-done.near_ref, bf16[128,1024]{1,0:T(8,128)(2,1)S(1)} %collective-permute-done.4.far_ref, f32[1,256]{1,0:T(1,128)S(1)} %bitcast.18, ...), custom_call_target="tpu_custom_call" | custom-call | flops 1610612736 | bytes 3145728 | tf_op jit(solution)/shard_map/pallas_call | solution.py:317
  40.2 3.3 %shard_map.144 = (f32[512,1024]{1,0:T(8,128)S(1)}, f32[512,1024]{1,0:T(8,128)S(1)}) custom-call(s32[4]{0:T(128)S(1)} %pad_add_fusion.info, bf16[512,1024]{1,0:T(8,128)(2,1)S(1)} %get-tuple-element.48.q_ref, bf16[256,512]{1,0:T(8,128)(2,1)S(1)} %get-tuple-element.45.kv_ref, bf16[256,512]{1,0:T(8,128)(2,1)S(1)} %get-tuple-element.49.self_ref, ...), custom_call_target="tpu_custom_call" | custom-call | flops 1342177280 | bytes 4194304 | tf_op jit(solution)/shard_map/pallas_call | solution.py:317
  43.4 6.1 %collective-permute-done.6.left_ref = bf16[256,512]{1,0:T(8,128)(2,1)S(1)} collective-permute-done((bf16[256,512]{1,0:T(8,128)(2,1)S(1)}, bf16[256,512]{1,0:T(8,128)(2,1)S(1)}, u32[]{:S(2)}, u32[]{:S(2)}) %collective-permute-start.6) | collective-permute-done | bytes 262176 | tf_op jit(solution)/shard_map/ppermute | solution.py:353
  49.7 1.3 %collective-permute-start.9 = (bf16[256,512]{1,0:T(8,128)(2,1)S(1)}, bf16[256,512]{1,0:T(8,128)(2,1)S(1)}, u32[]{:S(2)}, u32[]{:S(2)}) collective-permute-start(bf16[256,512]{1,0:T(8,128)(2,1)S(1)} %collective-permute-done.6.left_ref), channel_id=1, source_target_pairs={{0,2},{2,0},{4,6},{6,4},{8,10},{10,8},{12,14},{14,12},{1,3},{3,1},... | collective-permute-start | bytes 786440 | tf_op jit(solution)/shard_map/ppermute | solution.py:353
  52.4 1.7 %collective-permute-done.11.refs_1_ = bf16[256,256]{1,0:T(8,128)(2,1)S(1)} collective-permute-done((bf16[256,256]{1,0:T(8,128)(2,1)S(1)}, bf16[256,256]{1,0:T(8,128)(2,1)S(1)}, u32[]{:S(2)}, u32[]{:S(2)}) %collective-permute-start.11) | collective-permute-done | bytes 131104 | tf_op jit(solution)/shard_map/ppermute | solution.py:353
  55.3 4.0 %shard_map.145 = (f32[512,1024]{1,0:T(8,128)S(1)}, f32[512,1024]{1,0:T(8,128)S(1)}) custom-call(s32[4]{0:T(128)S(1)} %pad_add_fusion.info, bf16[512,1024]{1,0:T(8,128)(2,1)S(1)} %get-tuple-element.48.q_ref, f32[512,1024]{1,0:T(8,128)S(1)} %get-tuple-element.50.num_in, ...), custom_call_target="tpu_custom_call", output_to_operand_aliasing={{0}: (2, {}), {1}: (3, {})} | custom-call | flops 1073741824 | bytes 4194304 | tf_op jit(solution)/shard_map/pallas_call | solution.py:317
  59.3 3.2 %collective-permute-done.10.refs_0_ = bf16[256,256]{1,0:T(8,128)(2,1)S(1)} collective-permute-done((bf16[256,256]{1,0:T(8,128)(2,1)S(1)}, bf16[256,256]{1,0:T(8,128)(2,1)S(1)}, u32[]{:S(2)}, u32[]{:S(2)}) %collective-permute-start.10) | collective-permute-done | bytes 131104 | tf_op jit(solution)/shard_map/ppermute | solution.py:353
  64.0 6.4 %shard_map.146 = (f32[512,1024]{1,0:T(8,128)S(1)}, f32[512,1024]{1,0:T(8,128)S(1)}, bf16[512,512]{1,0:T(8,128)(2,1)S(1)}) custom-call(s32[4]{0:T(128)S(1)} %pad_add_fusion.info, bf16[512,1024]{1,0:T(8,128)(2,1)S(1)} %get-tuple-element.48.q_ref, f32[512,1024]{1,0:T(8,128)S(1)} %get-tuple-element.56.num_in, ...), custom_call_target="tpu_custom_call", output_to_operand_aliasing={{0}: (2, {}), {1}: (3, {})} | custom-call | flops 1610612736 | bytes 4194304 | tf_op jit(solution)/shard_map/pallas_call | solution.py:317
  70.4 2.9 %shard_map.147 = (f32[512,1024]{1,0:T(8,128)S(1)}, f32[512,1024]{1,0:T(8,128)S(1)}, bf16[512,512]{1,0:T(8,128)(2,1)S(1)}) custom-call(s32[4]{0:T(128)S(1)} %pad_add_fusion.info, bf16[512,1024]{1,0:T(8,128)(2,1)S(1)} %get-tuple-element.48.q_ref, f32[512,1024]{1,0:T(8,128)S(1)} %get-tuple-element.61.num_in, ...), custom_call_target="tpu_custom_call", output_to_operand_aliasing={{0}: (2, {}), {1}: (3, {})} | custom-call | flops 536870912 | bytes 4194304 | tf_op jit(solution)/shard_map/pallas_call | solution.py:317
  73.3 2.0 %collective-permute-start.17 = (bf16[512,512]{1,0:T(8,128)(2,1)S(1)}, bf16[512,512]{1,0:T(8,128)(2,1)S(1)}, u32[]{:S(2)}, u32[]{:S(2)}) collective-permute-start(bf16[512,512]{1,0:T(8,128)(2,1)S(1)} %get-tuple-element.63.gb), channel_id=1, source_target_pairs={{0,1},{1,0},{2,3},{3,2},{4,5},{5,4},{6,7},{7,6},{8,9},{9,8},{10,11... | collective-permute-start | bytes 1572872 | tf_op jit(solution)/shard_map/ppermute | solution.py:352
  75.4 1.5 %collective-permute-done.17.hb = bf16[512,512]{1,0:T(8,128)(2,1)S(1)} collective-permute-done((bf16[512,512]{1,0:T(8,128)(2,1)S(1)}, bf16[512,512]{1,0:T(8,128)(2,1)S(1)}, u32[]{:S(2)}, u32[]{:S(2)}) %collective-permute-start.17) | collective-permute-done | bytes 524320 | tf_op jit(solution)/shard_map/ppermute | solution.py:352
  77.6 6.7 %shard_map.148 = (bf16[256,2048]{1,0:T(8,128)(2,1)}, bf16[256,2048]{1,0:T(8,128)(2,1)}) custom-call(s32[4]{0:T(128)S(1)} %pad_add_fusion.info, s32[4]{0:T(128)S(1)} %bitcast.26, bf16[512,512]{1,0:T(8,128)(2,1)S(1)} %get-tuple-element.60.ga, bf16[512,512]{1,0:T(8,128)(2,1)S(1)} %get-tuple-element.63.gb, bf16[512,512]{1,0:T(8,128)(2,1)S(1)} %collective-permute-done.16.ha, ...), custom_call_target="tpu_custom_call" | custom-call | flops 4294967296 | bytes 8388608 | tf_op jit(solution)/shard_map/pallas_call | solution.py:317
  (60 shorter events, 11.7 us)
Async XLA Ops:
  0.6 11.1 %copy-start.2 = (bf16[256,2048]{1,0:T(8,128)(2,1)S(1)}, bf16[256,2048]{1,0:T(8,128)(2,1)}, u32[]{:S(2)}) copy-start(bf16[256,2048]{1,0:T(8,128)(2,1)} %x_ref.1) | copy-start | bytes 3145732
  0.7 11.0 %copy-start.5 = (f32[4096]{0:T(1024)S(1)}, f32[4096]{0:T(1024)}, u32[]{:S(2)}) copy-start(f32[4096]{0:T(1024)} %param.16) | copy-start | bytes 49156
  0.7 11.0 %copy-start.6 = (s32[1,256]{1,0:T(1,128)S(1)}, s32[1,256]{1,0:T(1,128)}, u32[]{:S(2)}) copy-start(s32[1,256]{1,0:T(1,128)} %mask_ref.7) | copy-start | bytes 3076
  1.7 7.2 %collective-permute-start.1 = (bf16[128,1024]{1,0:T(8,128)(2,1)S(1)}, bf16[128,1024]{1,0:T(8,128)(2,1)S(1)}, u32[]{:S(2)}, u32[]{:S(2)}) collective-permute-start(bf16[128,1024]{1,0:T(8,128)(2,1)S(1)} %constant_dynamic-slice_fusion.1), channel_id=1, source_target_pairs={{0,16},{16,0},{1,17},{17,1},{2,18},{18,2},{3,19},{19,3},{4,20},{20... | collective-permute-start | bytes 786440 | tf_op jit(solution)/shard_map/ppermute | solution.py:351
  4.5 7.2 %collective-permute-start.3 = (f32[256]{0:T(256)S(1)}, f32[256]{0:T(256)S(1)}, u32[]{:S(2)}, u32[]{:S(2)}) collective-permute-start(f32[256]{0:T(256)S(1)} %multiply_reduce_fusion), channel_id=1, source_target_pairs={{0,16},{16,0},{1,17},{17,1},{2,18},{18,2},{3,19},{19,3},{4,20},{20... | collective-permute-start | bytes 3080 | tf_op jit(solution)/shard_map/ppermute | solution.py:351
  5.8 23.8 %collective-permute-start = (bf16[128,1024]{1,0:T(8,128)(2,1)S(1)}, bf16[128,1024]{1,0:T(8,128)(2,1)S(1)}, u32[]{:S(2)}, u32[]{:S(2)}) collective-permute-start(bf16[128,1024]{1,0:T(8,128)(2,1)S(1)} %constant_dynamic-slice_fusion), channel_id=1, source_target_pairs={{0,16},{16,0},{1,17},{17,1},{2,18},{18,2},{3,19},{19,3},{4,20},{20... | collective-permute-start | bytes 786440 | tf_op jit(solution)/shard_map/ppermute | solution.py:351
  9.0 15.8 %collective-permute-start.2 = (bf16[128,1024]{1,0:T(8,128)(2,1)S(1)}, bf16[128,1024]{1,0:T(8,128)(2,1)S(1)}, u32[]{:S(2)}, u32[]{:S(2)}) collective-permute-start(bf16[128,1024]{1,0:T(8,128)(2,1)S(1)} %collective-permute-done.1.near_ref), channel_id=1, source_target_pairs={{0,1},{1,0},{2,3},{3,2},{4,5},{5,4},{6,7},{7,6},{8,9},{9,8},{10,11... | collective-permute-start | bytes 786440 | tf_op jit(solution)/shard_map/ppermute | solution.py:352
  29.6 1.6 %collective-permute-start.4 = (bf16[128,1024]{1,0:T(8,128)(2,1)S(1)}, bf16[128,1024]{1,0:T(8,128)(2,1)S(1)}, u32[]{:S(2)}, u32[]{:S(2)}) collective-permute-start(bf16[128,1024]{1,0:T(8,128)(2,1)S(1)} %collective-permute-done.near_ref), channel_id=1, source_target_pairs={{0,1},{1,0},{2,3},{3,2},{4,5},{5,4},{6,7},{7,6},{8,9},{9,8},{10,11... | collective-permute-start | bytes 786440 | tf_op jit(solution)/shard_map/ppermute | solution.py:352
  32.5 45.2 %collective-permute-start.18 = (bf16[1024,2048]{1,0:T(8,128)(2,1)S(1)}, bf16[1024,2048]{1,0:T(8,128)(2,1)S(1)}, u32[]{:S(2)}, u32[]{:S(2)}) collective-permute-start(bf16[1024,2048]{1,0:T(8,128)(2,1)S(1)} %copy-done.12), channel_id=1, source_target_pairs={{0,1},{1,0},{2,3},{3,2},{4,5},{5,4},{6,7},{7,6},{8,9},{9,8},{10,11... | collective-permute-start | bytes 12582920 | tf_op jit(solution)/shard_map/ppermute | solution.py:352
  32.7 7.5 %collective-permute-start.5 = (bf16[256,512]{1,0:T(8,128)(2,1)S(1)}, bf16[256,512]{1,0:T(8,128)(2,1)S(1)}, u32[]{:S(2)}, u32[]{:S(2)}) collective-permute-start(bf16[256,512]{1,0:T(8,128)(2,1)S(1)} %get-tuple-element.45.kv_ref), channel_id=1, source_target_pairs={{0,2},{2,0},{4,6},{6,4},{8,10},{10,8},{12,14},{14,12},{1,3},{3,1},... | collective-permute-start | bytes 786440 | tf_op jit(solution)/shard_map/ppermute | solution.py:353
  33.9 9.5 %collective-permute-start.8 = (bf16[256,256]{1,0:T(8,128)(2,1)S(1)}, bf16[256,256]{1,0:T(8,128)(2,1)S(1)}, u32[]{:S(2)}, u32[]{:S(2)}) collective-permute-start(bf16[256,256]{1,0:T(8,128)(2,1)S(1)} %get-tuple-element.53), channel_id=1, source_target_pairs={{0,12},{2,14},{4,8},{6,10},{8,4},{10,6},{12,0},{14,2},{1,13},{3,15... | collective-permute-start | bytes 393224 | tf_op jit(solution)/shard_map/ppermute | solution.py:353
  33.9 17.1 %collective-permute-start.7 = (bf16[256,256]{1,0:T(8,128)(2,1)S(1)}, bf16[256,256]{1,0:T(8,128)(2,1)S(1)}, u32[]{:S(2)}, u32[]{:S(2)}) collective-permute-start(bf16[256,256]{1,0:T(8,128)(2,1)S(1)} %get-tuple-element.53), channel_id=1, source_target_pairs={{0,8},{2,10},{4,12},{6,14},{8,0},{10,2},{12,4},{14,6},{1,9},{3,11}... | collective-permute-start | bytes 393224 | tf_op jit(solution)/shard_map/ppermute | solution.py:353
  35.3 14.2 %collective-permute-start.6 = (bf16[256,512]{1,0:T(8,128)(2,1)S(1)}, bf16[256,512]{1,0:T(8,128)(2,1)S(1)}, u32[]{:S(2)}, u32[]{:S(2)}) collective-permute-start(bf16[256,512]{1,0:T(8,128)(2,1)S(1)} %get-tuple-element.45.kv_ref), channel_id=1, source_target_pairs={{0,4},{2,6},{4,0},{6,2},{8,12},{10,14},{12,8},{14,10},{1,5},{3,7},... | collective-permute-start | bytes 786440 | tf_op jit(solution)/shard_map/ppermute | solution.py:353
  49.5 4.6 %collective-permute-start.11 = (bf16[256,256]{1,0:T(8,128)(2,1)S(1)}, bf16[256,256]{1,0:T(8,128)(2,1)S(1)}, u32[]{:S(2)}, u32[]{:S(2)}) collective-permute-start(bf16[256,256]{1,0:T(8,128)(2,1)S(1)} %collective-permute-done.8.refs_1_), channel_id=1, source_target_pairs={{0,2},{2,0},{4,6},{6,4},{8,10},{10,8},{12,14},{14,12},{1,3},{3,1},... | collective-permute-start | bytes 393224 | tf_op jit(solution)/shard_map/ppermute | solution.py:353
  49.7 14.3 %collective-permute-start.9 = (bf16[256,512]{1,0:T(8,128)(2,1)S(1)}, bf16[256,512]{1,0:T(8,128)(2,1)S(1)}, u32[]{:S(2)}, u32[]{:S(2)}) collective-permute-start(bf16[256,512]{1,0:T(8,128)(2,1)S(1)} %collective-permute-done.6.left_ref), channel_id=1, source_target_pairs={{0,2},{2,0},{4,6},{6,4},{8,10},{10,8},{12,14},{14,12},{1,3},{3,1},... | collective-permute-start | bytes 786440 | tf_op jit(solution)/shard_map/ppermute | solution.py:353
  51.0 11.5 %collective-permute-start.10 = (bf16[256,256]{1,0:T(8,128)(2,1)S(1)}, bf16[256,256]{1,0:T(8,128)(2,1)S(1)}, u32[]{:S(2)}, u32[]{:S(2)}) collective-permute-start(bf16[256,256]{1,0:T(8,128)(2,1)S(1)} %collective-permute-done.7.refs_0_), channel_id=1, source_target_pairs={{0,2},{2,0},{4,6},{6,4},{8,10},{10,8},{12,14},{14,12},{1,3},{3,1},... | collective-permute-start | bytes 393224 | tf_op jit(solution)/shard_map/ppermute | solution.py:353
  51.2 12.5 %collective-permute-start.13 = (bf16[256,256]{1,0:T(8,128)(2,1)S(1)}, bf16[256,256]{1,0:T(8,128)(2,1)S(1)}, u32[]{:S(2)}, u32[]{:S(2)}) collective-permute-start(bf16[256,256]{1,0:T(8,128)(2,1)S(1)} %collective-permute-done.8.refs_1_), channel_id=1, source_target_pairs={{0,16},{16,0},{1,17},{17,1},{2,18},{18,2},{3,19},{19,3},{4,20},{20... | collective-permute-start | bytes 393224 | tf_op jit(solution)/shard_map/ppermute | solution.py:351
  54.1 9.9 %collective-permute-start.12 = (bf16[256,256]{1,0:T(8,128)(2,1)S(1)}, bf16[256,256]{1,0:T(8,128)(2,1)S(1)}, u32[]{:S(2)}, u32[]{:S(2)}) collective-permute-start(bf16[256,256]{1,0:T(8,128)(2,1)S(1)} %collective-permute-done.7.refs_0_), channel_id=1, source_target_pairs={{0,16},{16,0},{1,17},{17,1},{2,18},{18,2},{3,19},{19,3},{4,20},{20... | collective-permute-start | bytes 393224 | tf_op jit(solution)/shard_map/ppermute | solution.py:351
  55.3 22.3 %slice-start = ((s8[8388608]{0:T(1024)(128)(4,1)}), s8[4194304]{0:T(1024)(128)(4,1)S(1)}, s32[]{:S(2)}) async-start(s8[8388608]{0:T(1024)(128)(4,1)} %bitcast.10), calls=%async_computation | async-start | bytes 8388608
  62.5 7.9 %collective-permute-start.15 = (bf16[256,256]{1,0:T(8,128)(2,1)S(1)}, bf16[256,256]{1,0:T(8,128)(2,1)S(1)}, u32[]{:S(2)}, u32[]{:S(2)}) collective-permute-start(bf16[256,256]{1,0:T(8,128)(2,1)S(1)} %collective-permute-done.11.refs_1_), channel_id=1, source_target_pairs={{0,16},{16,0},{1,17},{17,1},{2,18},{18,2},{3,19},{19,3},{4,20},{20... | collective-permute-start | bytes 393224 | tf_op jit(solution)/shard_map/ppermute | solution.py:351
  63.7 6.7 %collective-permute-start.14 = (bf16[256,256]{1,0:T(8,128)(2,1)S(1)}, bf16[256,256]{1,0:T(8,128)(2,1)S(1)}, u32[]{:S(2)}, u32[]{:S(2)}) collective-permute-start(bf16[256,256]{1,0:T(8,128)(2,1)S(1)} %collective-permute-done.10.refs_0_), channel_id=1, source_target_pairs={{0,16},{16,0},{1,17},{17,1},{2,18},{18,2},{3,19},{19,3},{4,20},{20... | collective-permute-start | bytes 393224 | tf_op jit(solution)/shard_map/ppermute | solution.py:351
  64.0 13.7 %slice-start.1 = ((s8[8388608]{0:T(1024)(128)(4,1)}), s8[4194304]{0:T(1024)(128)(4,1)S(1)}, s32[]{:S(2)}) async-start(s8[8388608]{0:T(1024)(128)(4,1)} %bitcast.10), calls=%async_computation.1 | async-start | bytes 8388608
  73.3 3.5 %collective-permute-start.17 = (bf16[512,512]{1,0:T(8,128)(2,1)S(1)}, bf16[512,512]{1,0:T(8,128)(2,1)S(1)}, u32[]{:S(2)}, u32[]{:S(2)}) collective-permute-start(bf16[512,512]{1,0:T(8,128)(2,1)S(1)} %get-tuple-element.63.gb), channel_id=1, source_target_pairs={{0,1},{1,0},{2,3},{3,2},{4,5},{5,4},{6,7},{7,6},{8,9},{9,8},{10,11... | collective-permute-start | bytes 1572872 | tf_op jit(solution)/shard_map/ppermute | solution.py:352
  75.3 2.3 %collective-permute-start.16 = (bf16[512,512]{1,0:T(8,128)(2,1)S(1)}, bf16[512,512]{1,0:T(8,128)(2,1)S(1)}, u32[]{:S(2)}, u32[]{:S(2)}) collective-permute-start(bf16[512,512]{1,0:T(8,128)(2,1)S(1)} %get-tuple-element.60.ga), channel_id=1, source_target_pairs={{0,1},{1,0},{2,3},{3,2},{4,5},{5,4},{6,7},{7,6},{8,9},{9,8},{10,11... | collective-permute-start | bytes 1572872 | tf_op jit(solution)/shard_map/ppermute | solution.py:352
  (10 other events, 55.0 us)

commit v4 on v3

--- a/solution.py
+++ b/solution.py
@@ -77,13 +77,24 @@
     return gain, embed, condition
 
 
+def squares_kernel(info, x_ref, squares_ref, first_ref, last_ref):
+    rows = x_ref.shape[0]
+    cut, depth = first_ref.shape
+    x = x_ref[...].astype(F32)
+    sums = jnp.sum(x * x, axis=1, keepdims=True)
+    eye = lax.broadcasted_iota(jnp.int32, (rows, rows), 0) == lax.broadcasted_iota(jnp.int32, (rows, rows), 1)
+    squares_ref[...] = jnp.sum(jnp.where(eye, jnp.broadcast_to(sums, (rows, rows)), 0.0), axis=0, keepdims=True)
+    strip = pl.ds(pl.multiple_of(info[1] * cut, 128), cut)
+    first_ref[...] = x_ref[strip, :depth]
+    last_ref[...] = x_ref[strip, depth:]
+
+
 def own_half_kernel(
-    info, x_ref, own_ref, other_ref, mask_ref, gain_ref, embed_ref, shift_ref, wq, wk, wv, w_out,
-    q_ref, k_ref, v_ref, rest_q, rest_k, rest_v, w_send, own_q, own_k, own_v, sems,
+    info, x_ref, own_ref, other_ref, mask_ref, gain_ref, embed_ref, shift_ref, wq, wk, wv,
+    q_ref, k_ref, v_ref, rest_q, rest_k, rest_v, own_q, own_k, own_v, sems,
 ):
     half = x_ref.shape[1]
     depth = half // 2
-    cols = w_send.shape[1]
     first = info[0] * half
     moves = []
 
@@ -99,8 +110,6 @@
     rest = pl.ds(pl.multiple_of(half - first, 128), half)
     for source, target in ((wk, rest_k), (wv, rest_v), (wq, rest_q)):
         move(source.at[rest], target)
-    side = pl.ds(pl.multiple_of((1 - info[1]) * cols, 128), cols)
-    move(w_out.at[:, side], w_send)
 
     scales = row_scales(own_ref, other_ref, mask_ref, embed_ref, embed_ref.shape[1])
     at = pl.ds(pl.multiple_of(first, 128), half)
@@ -129,9 +138,13 @@
 
 def chunk_kernel(
     info, near_ref, far_ref, own_ref, other_ref, mask_ref, gain_ref, embed_ref, shift_ref,
-    wq_ref, wk_ref, wv_ref, pq_ref, pk_ref, pv_ref, q_ref, k_ref, v_ref,
+    wq_ref, wk_ref, wv_ref, pq_ref, pk_ref, pv_ref, w_out, q_ref, k_ref, v_ref, w_send, sem,
 ):
     width = embed_ref.shape[1]
+    cols = w_send.shape[1]
+    side = pl.ds(pl.multiple_of((1 - info[1]) * cols, 128), cols)
+    move = pltpu.make_async_copy(w_out.at[:, side], w_send, sem)
+    move.start()
     scales = row_scales(own_ref, other_ref, mask_ref, embed_ref, width)
     at = chunk_at(info, 0, near_ref.shape[1], width)
     gain, embed, condition = vectors_at(at, info, gain_ref, embed_ref, shift_ref)
@@ -141,6 +154,7 @@
     k_ref[...] = pk_ref[...] + dot(both, wk_ref[here])
     v_ref[...] = pv_ref[...] + dot(both, wv_ref[here])
     q_ref[...] = pq_ref[...] + dot(both, wq_ref[here])
+    move.wait()
 
 
 def kv_out(ref, k, v, gain):
@@ -152,7 +166,7 @@
 
 def clean_kv_kernel(
     info, near_ref, far_ref, own_ref, other_ref, mask_ref, gain_ref, embed_ref,
-    wk_ref, wv_ref, pk_ref, pv_ref, kgain_ref, all_ref, one_ref,
+    wk_ref, wv_ref, pk_ref, pv_ref, kgain_ref, all_ref,
 ):
     rows = all_ref.shape[0]
     width = embed_ref.shape[1]
@@ -163,8 +177,6 @@
     k = pk_ref[:rows] + dot(clean, wk_ref[here])
     v = pv_ref[:rows] + dot(clean, wv_ref[here])
     kv_out(all_ref, k, v, kgain_ref[...])
-    cols = one_ref.shape[1]
-    one_ref[...] = all_ref[:, pl.ds(pl.multiple_of(info[0] * cols, 128), cols)]
 
 
 def last_chunk_kernel(
@@ -198,11 +210,14 @@
     return dot(e.astype(BF16), v), den
 
 
-def add_pieces(q_ref, num_ref, den_ref, base, heads, pieces, rows):
-    k = jnp.concatenate([piece[:, :HD] for piece in pieces], axis=0)
-    v = jnp.concatenate([piece[:, HD:] for piece in pieces], axis=0)
-    for head in range(heads):
-        cols = pl.ds(base + head * HD, HD)
+def add_pieces(q_ref, num_ref, den_ref, kv_head, piece_refs):
+    rows, width = piece_refs[0].shape
+    group = q_ref.shape[1] // HD // (width // (2 * HD))
+    base = 2 * kv_head * HD
+    k = jnp.concatenate([ref[:, base : base + HD] for ref in piece_refs], axis=0)
+    v = jnp.concatenate([ref[:, base + HD : base + 2 * HD] for ref in piece_refs], axis=0)
+    for head in range(kv_head * group, (kv_head + 1) * group):
+        cols = slice(head * HD, (head + 1) * HD)
         for part in range(2):
             cut = slice(part * rows, (part + 1) * rows)
             num, den = terms(q_ref[cut, cols], k, v, None)
@@ -210,36 +225,7 @@
             den_ref[cut, cols] += den
 
 
-def add_all_heads(q_ref, num_ref, den_ref, piece_refs, rows):
-    kv_heads = piece_refs[0].shape[1] // (2 * HD)
-    group_cols = q_ref.shape[1] // kv_heads
-    for kv_head in range(kv_heads):
-        cols = slice(2 * kv_head * HD, 2 * (kv_head + 1) * HD)
-        pieces = [ref[:, cols] for ref in piece_refs]
-        add_pieces(q_ref, num_ref, den_ref, kv_head * group_cols, group_cols // HD, pieces, rows)
-
-
-def add_far(info, q_ref, num_ref, den_ref, which, offsets, refs, rows):
-    cols = q_ref.shape[1] // 2
-    base = pl.multiple_of((info[0] if which == 0 else 1 - info[0]) * cols, 128)
-    for bit in sorted({offset.bit_length() for offset in offsets}):
-        group = [ref for offset, ref in zip(offsets, refs) if offset.bit_length() == bit]
-
-        @pl.when(jnp.bitwise_and(info[2], 1 << (bit - 1)) != 0)
-        def _(group=group):
-            add_pieces(q_ref, num_ref, den_ref, base, cols // HD, [ref[...] for ref in group], rows)
-
-
-def finish(info, num_ref, den_ref, which, out_ref):
-    width = out_ref.shape[1]
-    base = pl.multiple_of((info[0] if which == 0 else 1 - info[0]) * width, 128)
-    for head in range(width // HD):
-        cols = pl.ds(base + head * HD, HD)
-        total = jnp.sum(den_ref[:, cols], axis=1, keepdims=True)
-        out_ref[:, head * HD : (head + 1) * HD] = (num_ref[:, cols] / total).astype(BF16)
-
-
-def attention_own_kernel(info, q_ref, kv_ref, self_ref, near_ref, num_ref, den_ref):
+def attention_own_kernel(info, q_ref, kv_ref, self_ref, num_ref, den_ref):
     rows = kv_ref.shape[0]
     kv_heads = kv_ref.shape[1] // (2 * HD)
     group = q_ref.shape[1] // HD // kv_heads
@@ -257,51 +243,51 @@
             num_ref[:rows, cols], den_ref[:rows, cols] = terms(q_ref[:rows, cols], k, v, key_block <= row_block)
             num_ref[rows:, cols], den_ref[rows:, cols] = terms(q_ref[rows:, cols], k_both, v_both, both)
 
-    @pl.when(jnp.bitwise_and(info[2], 1) != 0)
+
+def attention_pair_kernel(info, q_ref, num_in, den_in, first_ref, second_ref, num_ref, den_ref, *, step):
+    first_valid = jnp.bitwise_and(info[2], 1) == 1 if step == 1 else info[2] >= 2 * (step - 1)
+    second_valid = info[2] >= 2 * step
+    cases = (
+        (jnp.logical_and(first_valid, second_valid), [first_ref, second_ref]),
+        (jnp.logical_and(first_valid, jnp.logical_not(second_valid)), [first_ref]),
+        (jnp.logical_and(jnp.logical_not(first_valid), second_valid), [second_ref]),
+    )
+    for valid, refs in cases:
+        @pl.when(valid)
+        def _(refs=refs):
+            for kv_head in range(refs[0].shape[1] // (2 * HD)):
+                add_pieces(q_ref, num_ref, den_ref, kv_head, refs)
+
+
+def attention_last_kernel(info, q_ref, num_in, den_in, piece_ref, num_ref, den_ref, out_ref, *, step, kv_head):
+    valid = jnp.bitwise_and(info[2], 1) == 1 if step == 0 else info[2] >= 2 * step
+
+    @pl.when(valid)
     def _():
-        add_all_heads(q_ref, num_ref, den_ref, [near_ref], rows)
-
-
-def attention_column_kernel(info, q_ref, num_in, den_in, left_ref, *refs, offsets):
-    num_ref, den_ref = refs[-2:]
-    rows = left_ref.shape[0]
-
-    @pl.when(jnp.bitwise_and(info[2], 2) != 0)
-    def _():
-        add_all_heads(q_ref, num_ref, den_ref, [left_ref], rows)
-
-    add_far(info, q_ref, num_ref, den_ref, 0, offsets, refs[: len(offsets)], rows)
-
-
-def attention_first_head_kernel(info, q_ref, num_in, den_in, right_ref, *refs, offsets):
-    num_ref, den_ref, out_ref = refs[-3:]
-    rows = right_ref.shape[0]
-    count = len(offsets)
-
-    @pl.when(jnp.bitwise_and(info[2], 2) != 0)
-    def _():
-        add_all_heads(q_ref, num_ref, den_ref, [right_ref], rows)
-
-    add_far(info, q_ref, num_ref, den_ref, 0, offsets, refs[:count], rows)
-    finish(info, num_ref, den_ref, 0, out_ref)
-    add_far(info, q_ref, num_ref, den_ref, 1, offsets, refs[count : 2 * count], rows)
-
-
-def attention_second_head_kernel(info, q_ref, num_in, den_in, *refs, offsets):
-    num_ref, den_ref, out_ref = refs[-3:]
-    rows = out_ref.shape[0] // 2
-    add_far(info, q_ref, num_ref, den_ref, 1, offsets, refs[: len(offsets)], rows)
-    finish(info, num_ref, den_ref, 1, out_ref)
-
-
-def out_kernel(info, live, ga, gb, ha, hb, w_mine, w_far, clean_ref, noisy_ref):
+        add_pieces(q_ref, num_ref, den_ref, kv_head, [piece_ref])
+
+    width = out_ref.shape[1]
+    for head in range(width // HD):
+        cols = slice(kv_head * width + head * HD, kv_head * width + (head + 1) * HD)
+        total = jnp.sum(den_ref[:, cols], axis=1, keepdims=True)
+        out_ref[:, head * HD : (head + 1) * HD] = (num_ref[:, cols] / total).astype(BF16)
+
+
+def out_first_kernel(info, ga, gb, ha, w_out, w_far, mixed_ref, *, tile):
+    part = ga.shape[1]
+    total = mixed_ref.shape[1]
+    for start in range(0, total, tile):
+        mine = pl.ds(pl.multiple_of(info[1] * total + start, 128), tile)
+        cols = slice(start, start + tile)
+        mixed = dot(ga[...], w_out[:part, mine]) + dot(gb[...], w_out[part:, mine])
+        mixed_ref[:, cols] = mixed + dot(ha[...], w_far[:part, cols])
+
+
+def out_last_kernel(info, live, hb, mixed_ref, w_far, clean_ref, noisy_ref):
     rows, tile = clean_ref.shape
-    part = ga.shape[1]
+    part = hb.shape[1]
     cols = pl.ds(pl.multiple_of(pl.program_id(0) * tile, 128), tile)
-    first = pl.ds(pl.multiple_of(info[0] * part, 128), part)
-    second = pl.ds(pl.multiple_of((1 - info[0]) * part, 128), part)
-    mixed = dot(ga[...], w_mine[first]) + dot(gb[...], w_mine[second])
-    mixed = mixed + dot(ha[...], w_far[first, cols]) + dot(hb[...], w_far[second, cols])
+    mixed = mixed_ref[:, cols] + dot(hb[...], w_far[part:, cols])
     clean_ref[...] = mixed[:rows].astype(BF16)
     for block in range(rows // BLK):
         part_rows = mixed[rows + block * BLK : rows + (block + 1) * BLK]
@@ -350,106 +336,96 @@
     pair = [(0, 1), (1, 0)]
     cross_x = lambda v: lax.ppermute(v, "copy", pair)
     cross_core = lambda v: lax.ppermute(v, "tp", pair)
-    cross_ctx = lambda v, offset: lax.ppermute(v, "ctx", [(i, i ^ offset) for i in range(ctx)])
     shape = jax.ShapeDtypeStruct
 
     cut, depth = rows // 2, half // 2
-    strip = lambda v, chunk: lax.dynamic_slice(v, (t * cut, chunk * depth), (cut, depth))
-    near_first = cross_x(strip(clean_tokens, 0))
-    wide = clean_tokens.astype(F32)
-    squares = jnp.sum(wide * wide, axis=1)
+    out_cols = w_out.shape[1] // 2
+    qg, kg = q_gain[None], k_gain[None]
+    vmem = lambda dims, kind: (WHOLE, pltpu.VMEM(dims, kind))
+    in_hbm = lambda v: pltpu.with_memory_space_constraint(v, pltpu.HBM)
+
+    squares, strip_first, strip_last = call(
+        squares_kernel, [info], [WHOLE], [vmem((1, rows), F32)] + [vmem((cut, depth), BF16)] * 2, [clean_tokens],
+        2 * rows * half, rows * half * 2,
+    )
     other_squares = cross_x(squares)
-    near_last = cross_x(strip(after(clean_tokens, squares), 1))
-    out_cols = w_out.shape[1] // 2
-    stats = [squares[None], other_squares[None], masked]
+    near_first = cross_x(strip_first)
+    near_last = cross_x(strip_last)
+    stats = [squares, other_squares, masked]
     vectors = [norm_gain[None], mask_embed[None], time_shift[None]]
-    qg, kg = q_gain[None], k_gain[None]
-    partial = [
-        (WHOLE, shape((2 * rows, heads_width), F32)),
-        (WHOLE, shape((2 * rows, kv_width), F32)),
-        (WHOLE, shape((2 * rows, kv_width), F32)),
-    ]
+    partial = [vmem((2 * rows, width), F32) for width in (heads_width, kv_width, kv_width)]
+    buffers = [(half, heads_width), (half, kv_width), (half, kv_width)]
     per_row = heads_width + 2 * kv_width
 
-    bf = lambda *dims: (WHOLE, shape(dims, BF16))
-    buffers = [(half, heads_width), (half, kv_width), (half, kv_width)]
-    pq, pk, pv, *weights, w_send = call(
-        own_half_kernel, [info], [WHOLE] * 7 + [HBM] * 4,
-        partial + [bf(*dims) for dims in buffers] + [bf(heads_width, out_cols)],
-        [clean_tokens] + stats + vectors + [w_query, w_key, w_value, w_out],
-        4 * rows * half * per_row, heads_width * out_cols * 2,
-        [pltpu.VMEM(dims, BF16) for dims in buffers] + [pltpu.SemaphoreType.DMA((10,))],
-        limit=40,
+    pq, pk, pv, *weights = call(
+        own_half_kernel, [info], [WHOLE] * 7 + [HBM] * 3, partial + [vmem(dims, BF16) for dims in buffers],
+        [clean_tokens] + stats + vectors + [in_hbm(w_query), in_hbm(w_key), in_hbm(w_value)],
+        4 * rows * half * per_row, 2 * half * per_row * 2,
+        [pltpu.VMEM(dims, BF16) for dims in buffers] + [pltpu.SemaphoreType.DMA((9,))], limit=32,
     )
     far_first = cross_core(near_first)
-    pq, pk, pv = call(
-        chunk_kernel, [info], [WHOLE] * 14, partial,
-        [near_first, far_first] + stats + vectors + weights + [pq, pk, pv],
-        4 * rows * depth * per_row, depth * per_row * 2, aliases={12: 0, 13: 1, 14: 2},
+    pq, pk, pv, w_send = call(
+        chunk_kernel, [info], [WHOLE] * 14 + [HBM], partial + [vmem((heads_width, out_cols), BF16)],
+        [near_first, far_first] + stats + vectors + weights + [pq, pk, pv, in_hbm(w_out)],
+        4 * rows * depth * per_row, depth * per_row * 2, [pltpu.SemaphoreType.DMA(())],
+        aliases={12: 0, 13: 1, 14: 2},
     )
     near_last = after(near_last, pk)
     far_last = cross_core(near_last)
 
-    kv, kva = call(
-        clean_kv_kernel, [info], [WHOLE] * 12,
-        [(WHOLE, shape((rows, 2 * kv_width), BF16)), (WHOLE, shape((rows, kv_width), BF16))],
+    kv, = call(
+        clean_kv_kernel, [info], [WHOLE] * 12, [vmem((rows, 2 * kv_width), BF16)],
         [near_last, far_last] + stats + vectors[:2] + weights[1:] + [pk, pv, kg],
         4 * rows * depth * kv_width, depth * 2 * kv_width * 2,
     )
 
-    offsets = list(range(4, ctx, 2))
-    beside = cross_ctx(kv, 1)
-    left = cross_ctx(kv, 2)
-    column = [cross_ctx(kva, offset) for offset in offsets]
-
+    steps = ctx // 2
+    along = lambda v: lax.ppermute(v, "ctx", [(i, (i + 2) % ctx) for i in range(ctx)])
+    across = lambda v: lax.ppermute(v, "ctx", [(i, i ^ 1) for i in range(ctx)])
+    crossed = across(kv)
+    column = along(kv)
+    w_far = cross_core(after(w_send, kv))
     near_last = after(near_last, kv)
     q, own = call(
         last_chunk_kernel, [info], [WHOLE] * 16,
-        [(WHOLE, shape((2 * rows, heads_width), BF16)), (WHOLE, shape((rows, 2 * kv_width), BF16))],
+        [vmem((2 * rows, heads_width), BF16), vmem((rows, 2 * kv_width), BF16)],
         [near_last, far_last] + stats + vectors + weights + [pq, pk, pv, qg, kg],
         4 * rows * depth * per_row, depth * per_row * 2,
     )
-    w_far = cross_core(after(w_send, kv))
-
-    acc_shape = shape((2 * rows, heads_width), F32)
-    acc = [(WHOLE, acc_shape), (WHOLE, acc_shape)]
-    attended = (WHOLE, shape((2 * rows, part), BF16))
+
+    acc = [vmem((2 * rows, heads_width), F32)] * 2
     unit = rows * rows * heads_width // HD
     cost = lambda units: (4 * HD * unit * units, 8 * unit, (), unit * units)
     in_place = {2: 0, 3: 1}
-    num, den = call(attention_own_kernel, [info], [WHOLE] * 4, acc, [q, kv, own, beside], *cost(5))
-    column = [after(piece, num) for piece in column]
-    left = after(left, num)
-    column_right = [cross_ctx(piece, 1) for piece in column]
-    other = [cross_x(piece) for piece in column]
-    right = cross_ctx(left, 1)
-    num, den = call(
-        functools.partial(attention_column_kernel, offsets=offsets), [info], [WHOLE] * (4 + len(column)), acc,
-        [q, num, den, left] + column, *cost(4), aliases=in_place,
-    )
-    column_right = [after(piece, num) for piece in column_right]
-    other_right = [cross_x(piece) for piece in column_right]
-    num, den, ga = call(
-        functools.partial(attention_first_head_kernel, offsets=offsets), [info],
-        [WHOLE] * (4 + 2 * len(column)), acc + [attended],
-        [q, num, den, right] + column_right + other, *cost(6), aliases=in_place,
-    )
-    ha = cross_core(ga)
-    num, den, gb = call(
-        functools.partial(attention_second_head_kernel, offsets=offsets), [info],
-        [WHOLE] * (3 + len(column)), acc + [attended], [q, num, den] + other_right, *cost(2), aliases=in_place,
-    )
-    hb = cross_core(gb)
-
+    num, den = call(attention_own_kernel, [info], [WHOLE] * 3, acc, [q, kv, own], *cost(3))
+    w_far = after(w_far, num)
+    for step in range(1, steps):
+        column = after(column, num)
+        before, crossed = crossed, across(column)
+        here, column = column, along(column) if step < steps - 1 else None
+        num, den = call(
+            functools.partial(attention_pair_kernel, step=step), [info], [WHOLE] * 5, acc,
+            [q, num, den, before, here], *cost(4), aliases=in_place,
+        )
+    attended = []
+    for kv_head in range(2):
+        num, den, result = call(
+            functools.partial(attention_last_kernel, step=steps - 1, kv_head=kv_head), [info], [WHOLE] * 4,
+            acc + [vmem((2 * rows, part), BF16)], [q, num, den, crossed], *cost(1), aliases=in_place,
+        )
+        attended.append((result, cross_core(result)))
+
+    (ga, ha), (gb, hb) = attended
     tile = 512
-    tiles = out_cols // tile
-    mine = pl.BlockSpec((heads_width, tile), lambda n, s, l: (0, s[1] * tiles + n))
+    mixed, = call(
+        functools.partial(out_first_kernel, tile=tile), [info], [WHOLE] * 5, [vmem((2 * rows, out_cols), F32)],
+        [ga, gb, ha, w_out, w_far], 6 * rows * heads_width * out_cols, 2 * heads_width * out_cols * 2,
+    )
     out = pl.BlockSpec((rows, tile), lambda n, s, l: (0, n))
     out_shape = shape((rows, out_cols), BF16)
     clean_out, noised_out = call(
-        out_kernel, [info, block_live[0]], [WHOLE] * 4 + [mine, WHOLE], [(out, out_shape), (out, out_shape)],
-        [ga, gb, ha, hb, w_out, w_far],
-        8 * rows * heads_width * out_cols, 2 * heads_width * out_cols * 2, grid=tiles,
+        out_last_kernel, [info, block_live[0]], [WHOLE] * 3, [(out, out_shape), (out, out_shape)],
+        [hb, mixed, w_far], 2 * rows * heads_width * out_cols, heads_width * out_cols * 2, grid=out_cols // tile,
     )
     return (clean_out, noised_out[None])
 

time: 84.7 us -> 76.4 us (0.902)
  the two profiles are of different devices: /device:TPU:25 before, /device:TPU:0 now
where the time goes in v4:
time: 76.4 us; the launch traced here: 76 us
  Pallas kernels  29.4 us (38%)
  waiting for transfers between devices  25.7 us (34%)
  starting transfers between devices  14.1 us (18%)
  local copies, waits for them, and re-layouts  5.3 us (7%)
  between operations  1.47 us (2%)
    pallas_call x13, Pallas kernels, call(): pl.pallas_call(kernel, grid_spec=pltpu.PrefetchScalarGridSpec(num_scalar_...  29.4 us
    ppermute x3, waiting for transfers between devices, on_device(): lax.ppermute(v, 'ctx', [(i, (i + 2) % ctx) for i in range(ctx)])  15.8 us
    ppermute x4, starting transfers between devices, on_device(): across = lambda v: lax.ppermute(v, 'ctx', [(i, i ^ 1) for i in range(ctx)])  5.16 us
    ppermute x3, starting transfers between devices, on_device(): cross_x = lambda v: lax.ppermute(v, 'copy', pair)  5.02 us
    ppermute x4, waiting for transfers between devices, on_device(): across = lambda v: lax.ppermute(v, 'ctx', [(i, i ^ 1) for i in range(ctx)])  4.59 us
    unnamed x22, local copies, waits for them, and re-layouts  3.88 us
    ppermute x3, waiting for transfers between devices, on_device(): cross_x = lambda v: lax.ppermute(v, 'copy', pair)  3.74 us
    ppermute x3, starting transfers between devices, on_device(): lax.ppermute(v, 'ctx', [(i, (i + 2) % ctx) for i in range(ctx)])  2.31 us
  transfers between devices with their start and end apart: 15, of which 8 were waited for; matrix products, arithmetic and copies ran while one was open for 2% of the time, Pallas kernels for 30%

profile of v4, /device:TPU:0, one launch (start us, length us, event | category | flops | bytes accessed | tf_op | source)
XLA Modules:
  0.0 76.0 jit_solution(6518664289167703439)
XLA Ops:
  1.4 1.2 %copy-done = bf16[256,2048]{1,0:T(8,128)(2,1)S(1)} copy-done((bf16[256,2048]{1,0:T(8,128)(2,1)S(1)}, bf16[256,2048]{1,0:T(8,128)(2,1)}, u32[]{:S(2)}) %copy-start) | copy-done | bytes 1048600
  3.4 3.0 %collective-permute-start.1 = (bf16[128,1024]{1,0:T(8,128)(2,1)S(1)}, bf16[128,1024]{1,0:T(8,128)(2,1)S(1)}, u32[]{:S(2)}, u32[]{:S(2)}) collective-permute-start(bf16[128,1024]{1,0:T(8,128)(2,1)S(1)} %get-tuple-element.39), channel_id=1, source_target_pairs={{0,16},{16,0},{1,17},{17,1},{2,18},{18,2},{3,19},{19,3},{4,20},{20... | collective-permute-start | bytes 786440 | tf_op jit(solution)/shard_map/ppermute | solution.py:337
  6.5 1.9 %collective-permute-start = (bf16[128,1024]{1,0:T(8,128)(2,1)S(1)}, bf16[128,1024]{1,0:T(8,128)(2,1)S(1)}, u32[]{:S(2)}, u32[]{:S(2)}) collective-permute-start(bf16[128,1024]{1,0:T(8,128)(2,1)S(1)} %get-tuple-element.38), channel_id=1, source_target_pairs={{0,16},{16,0},{1,17},{17,1},{2,18},{18,2},{3,19},{19,3},{4,20},{20... | collective-permute-start | bytes 786440 | tf_op jit(solution)/shard_map/ppermute | solution.py:337
  9.9 3.7 %collective-permute-done.1.near_ref = bf16[128,1024]{1,0:T(8,128)(2,1)S(1)} collective-permute-done((bf16[128,1024]{1,0:T(8,128)(2,1)S(1)}, bf16[128,1024]{1,0:T(8,128)(2,1)S(1)}, u32[]{:S(2)}, u32[]{:S(2)}) %collective-permute-start.1) | collective-permute-done | bytes 262176 | tf_op jit(solution)/shard_map/ppermute | solution.py:337
  13.6 1.2 %copy-done.1 = bf16[256,2048]{1,0:T(8,128)(2,1)S(1)} copy-done((bf16[256,2048]{1,0:T(8,128)(2,1)S(1)}, bf16[256,2048]{1,0:T(8,128)(2,1)}, u32[]{:S(2)}) %copy-start.1) | copy-done | bytes 1048600
  16.2 6.8 %shard_map.141 = (f32[512,1024]{1,0:T(8,128)S(1)}, f32[512,256]{1,0:T(8,128)S(1)}, f32[512,256]{1,0:T(8,128)S(1)}, bf16[2048,1024]{1,0:T(8,128)(2,1)S(1)}, bf16[...) custom-call(s32[4]{0:T(128)S(1)} %pad_add_fusion.info, bf16[256,2048]{1,0:T(8,128)(2,1)S(1)} %copy-done.1, ...), custom_call_target="tpu_custom_call" | custom-call | flops 3221225472 | bytes 12582912 | tf_op jit(solution)/shard_map/pallas_call | solution.py:303
  23.1 3.7 %shard_map.142 = (f32[512,1024]{1,0:T(8,128)S(1)}, f32[512,256]{1,0:T(8,128)S(1)}, f32[512,256]{1,0:T(8,128)S(1)}, bf16[1024,2048]{1,0:T(8,128)(2,1)S(1)}) custom-call(s32[4]{0:T(128)S(1)} %pad_add_fusion.info, bf16[128,1024]{1,0:T(8,128)(2,1)S(1)} %collective-permute-done.1.near_ref, ...), custom_call_target="tpu_custom_call", output_to_operand_aliasing={{0}: (12, {}), {1}: (13, {}), {2}: (14, {})} | custom-call | flops 1610612736 | bytes 3145728 | tf_op jit(solution)/shard_map/pallas_call | solution.py:303
  27.4 1.2 %collective-permute-done.4.far_ref = bf16[128,1024]{1,0:T(8,128)(2,1)S(1)} collective-permute-done((bf16[128,1024]{1,0:T(8,128)(2,1)S(1)}, bf16[128,1024]{1,0:T(8,128)(2,1)S(1)}, u32[]{:S(2)}, u32[]{:S(2)}) %collective-permute-start.4) | collective-permute-done | bytes 262176 | tf_op jit(solution)/shard_map/ppermute | solution.py:338
  28.5 1.2 %shard_map.143.kv_ref = bf16[256,512]{1,0:T(8,128)(2,1)S(1)} custom-call(s32[4]{0:T(128)S(1)} %pad_add_fusion.info, bf16[128,1024]{1,0:T(8,128)(2,1)S(1)} %collective-permute-done.near_ref, bf16[128,1024]{1,0:T(8,128)(2,1)S(1)} %collective-permute-done.4.far_ref, f32[1,256]{1,0:T(1,128)S(1)} %get-tuple-element.40.own_ref, ...), custom_call_target="tpu_custom_call" | custom-call | flops 268435456 | bytes 1048576 | tf_op jit(solution)/shard_map/pallas_call | solution.py:303
  30.2 2.2 %collective-permute-start.6 = (bf16[256,512]{1,0:T(8,128)(2,1)S(1)}, bf16[256,512]{1,0:T(8,128)(2,1)S(1)}, u32[]{:S(2)}, u32[]{:S(2)}) collective-permute-start(bf16[256,512]{1,0:T(8,128)(2,1)S(1)} %shard_map.143.kv_ref), channel_id=1, source_target_pairs={{0,4},{2,6},{4,8},{6,10},{8,12},{10,14},{12,0},{14,2},{1,5},{3,7},... | collective-permute-start | bytes 786440 | tf_op jit(solution)/shard_map/ppermute | solution.py:383
  32.3 1.5 %collective-permute-start.5 = (bf16[256,512]{1,0:T(8,128)(2,1)S(1)}, bf16[256,512]{1,0:T(8,128)(2,1)S(1)}, u32[]{:S(2)}, u32[]{:S(2)}) collective-permute-start(bf16[256,512]{1,0:T(8,128)(2,1)S(1)} %shard_map.143.kv_ref), channel_id=1, source_target_pairs={{0,2},{2,0},{4,6},{6,4},{8,10},{10,8},{12,14},{14,12},{1,3},{3,1},... | collective-permute-start | bytes 786440 | tf_op jit(solution)/shard_map/ppermute | solution.py:384
  33.9 2.5 %shard_map.144 = (bf16[512,1024]{1,0:T(8,128)(2,1)S(1)}, bf16[256,512]{1,0:T(8,128)(2,1)S(1)}) custom-call(s32[4]{0:T(128)S(1)} %pad_add_fusion.info, bf16[128,1024]{1,0:T(8,128)(2,1)S(1)} %collective-permute-done.near_ref, bf16[128,1024]{1,0:T(8,128)(2,1)S(1)} %collective-permute-done.4.far_ref, f32[1,256]{1,0:T(1,128)S(1)} %get-tuple-element.40.own_ref, ...), custom_call_target="tpu_custom_call" | custom-call | flops 1610612736 | bytes 3145728 | tf_op jit(solution)/shard_map/pallas_call | solution.py:303
  36.4 3.1 %shard_map.145 = (f32[512,1024]{1,0:T(8,128)S(1)}, f32[512,1024]{1,0:T(8,128)S(1)}) custom-call(s32[4]{0:T(128)S(1)} %pad_add_fusion.info, bf16[512,1024]{1,0:T(8,128)(2,1)S(1)} %get-tuple-element.52.q_ref, bf16[256,512]{1,0:T(8,128)(2,1)S(1)} %shard_map.143.kv_ref, bf16[256,512]{1,0:T(8,128)(2,1)S(1)} %get-tuple-element.53.self_ref), custom_call_target="tpu_custom_call" | custom-call | flops 805306368 | bytes 4194304 | tf_op jit(solution)/shard_map/pallas_call | solution.py:303
  39.5 1.5 %collective-permute-done.6.second_ref = bf16[256,512]{1,0:T(8,128)(2,1)S(1)} collective-permute-done((bf16[256,512]{1,0:T(8,128)(2,1)S(1)}, bf16[256,512]{1,0:T(8,128)(2,1)S(1)}, u32[]{:S(2)}, u32[]{:S(2)}) %collective-permute-start.6) | collective-permute-done | bytes 262176 | tf_op jit(solution)/shard_map/ppermute | solution.py:383
  41.1 1.4 %collective-permute-start.7 = (bf16[256,512]{1,0:T(8,128)(2,1)S(1)}, bf16[256,512]{1,0:T(8,128)(2,1)S(1)}, u32[]{:S(2)}, u32[]{:S(2)}) collective-permute-start(bf16[256,512]{1,0:T(8,128)(2,1)S(1)} %collective-permute-done.6.second_ref), channel_id=1, source_target_pairs={{0,2},{2,0},{4,6},{6,4},{8,10},{10,8},{12,14},{14,12},{1,3},{3,1},... | collective-permute-start | bytes 786440 | tf_op jit(solution)/shard_map/ppermute | solution.py:384
  43.3 7.4 %collective-permute-done.8.second_ref = bf16[256,512]{1,0:T(8,128)(2,1)S(1)} collective-permute-done((bf16[256,512]{1,0:T(8,128)(2,1)S(1)}, bf16[256,512]{1,0:T(8,128)(2,1)S(1)}, u32[]{:S(2)}, u32[]{:S(2)}) %collective-permute-start.8) | collective-permute-done | bytes 262176 | tf_op jit(solution)/shard_map/ppermute | solution.py:383
  50.6 1.3 %collective-permute-start.9 = (bf16[256,512]{1,0:T(8,128)(2,1)S(1)}, bf16[256,512]{1,0:T(8,128)(2,1)S(1)}, u32[]{:S(2)}, u32[]{:S(2)}) collective-permute-start(bf16[256,512]{1,0:T(8,128)(2,1)S(1)} %collective-permute-done.8.second_ref), channel_id=1, source_target_pairs={{0,2},{2,0},{4,6},{6,4},{8,10},{10,8},{12,14},{14,12},{1,3},{3,1},... | collective-permute-start | bytes 786440 | tf_op jit(solution)/shard_map/ppermute | solution.py:384
  52.5 6.9 %collective-permute-done.10.second_ref = bf16[256,512]{1,0:T(8,128)(2,1)S(1)} collective-permute-done((bf16[256,512]{1,0:T(8,128)(2,1)S(1)}, bf16[256,512]{1,0:T(8,128)(2,1)S(1)}, u32[]{:S(2)}, u32[]{:S(2)}) %collective-permute-start.10) | collective-permute-done | bytes 262176 | tf_op jit(solution)/shard_map/ppermute | solution.py:383
  59.4 1.0 %collective-permute-start.11 = (bf16[256,512]{1,0:T(8,128)(2,1)S(1)}, bf16[256,512]{1,0:T(8,128)(2,1)S(1)}, u32[]{:S(2)}, u32[]{:S(2)}) collective-permute-start(bf16[256,512]{1,0:T(8,128)(2,1)S(1)} %collective-permute-done.10.second_ref), channel_id=1, source_target_pairs={{0,2},{2,0},{4,6},{6,4},{8,10},{10,8},{12,14},{14,12},{1,3},{3,1},... | collective-permute-start | bytes 786440 | tf_op jit(solution)/shard_map/ppermute | solution.py:384
  61.2 4.6 %collective-permute-done.11.piece_ref = bf16[256,512]{1,0:T(8,128)(2,1)S(1)} collective-permute-done((bf16[256,512]{1,0:T(8,128)(2,1)S(1)}, bf16[256,512]{1,0:T(8,128)(2,1)S(1)}, u32[]{:S(2)}, u32[]{:S(2)}) %collective-permute-start.11) | collective-permute-done | bytes 262176 | tf_op jit(solution)/shard_map/ppermute | solution.py:384
  65.8 0.9 %shard_map.149 = (f32[512,1024]{1,0:T(8,128)S(1)}, f32[512,1024]{1,0:T(8,128)S(1)}, bf16[512,512]{1,0:T(8,128)(2,1)S(1)}) custom-call(s32[4]{0:T(128)S(1)} %pad_add_fusion.info, bf16[512,1024]{1,0:T(8,128)(2,1)S(1)} %get-tuple-element.52.q_ref, f32[512,1024]{1,0:T(8,128)S(1)} %get-tuple-element.63.num_in, ...), custom_call_target="tpu_custom_call", output_to_operand_aliasing={{0}: (2, {}), {1}: (3, {})} | custom-call | flops 268435456 | bytes 4194304 | tf_op jit(solution)/shard_map/pallas_call | solution.py:303
  66.7 0.9 %shard_map.150 = (f32[512,1024]{1,0:T(8,128)S(1)}, f32[512,1024]{1,0:T(8,128)S(1)}, bf16[512,512]{1,0:T(8,128)(2,1)S(1)}) custom-call(s32[4]{0:T(128)S(1)} %pad_add_fusion.info, bf16[512,1024]{1,0:T(8,128)(2,1)S(1)} %get-tuple-element.52.q_ref, f32[512,1024]{1,0:T(8,128)S(1)} %get-tuple-element.65.num_in, ...), custom_call_target="tpu_custom_call", output_to_operand_aliasing={{0}: (2, {}), {1}: (3, {})} | custom-call | flops 268435456 | bytes 4194304 | tf_op jit(solution)/shard_map/pallas_call | solution.py:303
  68.6 4.0 %shard_map.151.mixed_ref = f32[512,2048]{1,0:T(8,128)S(1)} custom-call(s32[4]{0:T(128)S(1)} %pad_add_fusion.info, bf16[512,512]{1,0:T(8,128)(2,1)S(1)} %get-tuple-element.68.ga, bf16[512,512]{1,0:T(8,128)(2,1)S(1)} %get-tuple-element.67.gb, bf16[512,512]{1,0:T(8,128)(2,1)S(1)} %collective-permute-done.13.ha, bf16[1024,4096]{1,0:T(8,128)(2,1)S(1)} %bitcast.9, ...), custom_call_target="tpu_custom_call" | custom-call | flops 3221225472 | bytes 8388608 | tf_op jit(solution)/shard_map/pallas_call | solution.py:303
  72.6 3.3 %shard_map.152 = (bf16[256,2048]{1,0:T(8,128)(2,1)}, bf16[256,2048]{1,0:T(8,128)(2,1)}) custom-call(s32[4]{0:T(128)S(1)} %pad_add_fusion.info, s32[4]{0:T(128)S(1)} %bitcast.16, bf16[512,512]{1,0:T(8,128)(2,1)S(1)} %collective-permute-done.12.hb, f32[512,2048]{1,0:T(8,128)S(1)} %shard_map.151.mixed_ref, bf16[1024,2048]{1,0:T(8,128)(2,1)S(1)} %collective-permute-done.14.w_far), custom_call_target="tpu_custom_call" | custom-call | flops 1073741824 | bytes 4194304 | tf_op jit(solution)/shard_map/pallas_call | solution.py:303
  (45 shorter events, 8.1 us)
Async XLA Ops:
  1.4 1.2 %copy-start = (bf16[256,2048]{1,0:T(8,128)(2,1)S(1)}, bf16[256,2048]{1,0:T(8,128)(2,1)}, u32[]{:S(2)}) copy-start(bf16[256,2048]{1,0:T(8,128)(2,1)} %x_ref.3) | copy-start | bytes 3145732
  3.4 10.1 %collective-permute-start.1 = (bf16[128,1024]{1,0:T(8,128)(2,1)S(1)}, bf16[128,1024]{1,0:T(8,128)(2,1)S(1)}, u32[]{:S(2)}, u32[]{:S(2)}) collective-permute-start(bf16[128,1024]{1,0:T(8,128)(2,1)S(1)} %get-tuple-element.39), channel_id=1, source_target_pairs={{0,16},{16,0},{1,17},{17,1},{2,18},{18,2},{3,19},{19,3},{4,20},{20... | collective-permute-start | bytes 786440 | tf_op jit(solution)/shard_map/ppermute | solution.py:337
  6.4 7.2 %collective-permute-start.3 = (f32[1,256]{1,0:T(1,128)S(1)}, f32[1,256]{1,0:T(1,128)S(1)}, u32[]{:S(2)}, u32[]{:S(2)}) collective-permute-start(f32[1,256]{1,0:T(1,128)S(1)} %get-tuple-element.40.own_ref), channel_id=1, source_target_pairs={{0,16},{16,0},{1,17},{17,1},{2,18},{18,2},{3,19},{19,3},{4,20},{20... | collective-permute-start | bytes 3080 | tf_op jit(solution)/shard_map/ppermute | solution.py:337
  6.5 20.4 %collective-permute-start = (bf16[128,1024]{1,0:T(8,128)(2,1)S(1)}, bf16[128,1024]{1,0:T(8,128)(2,1)S(1)}, u32[]{:S(2)}, u32[]{:S(2)}) collective-permute-start(bf16[128,1024]{1,0:T(8,128)(2,1)S(1)} %get-tuple-element.38), channel_id=1, source_target_pairs={{0,16},{16,0},{1,17},{17,1},{2,18},{18,2},{3,19},{19,3},{4,20},{20... | collective-permute-start | bytes 786440 | tf_op jit(solution)/shard_map/ppermute | solution.py:337
  13.6 9.5 %collective-permute-start.2 = (bf16[128,1024]{1,0:T(8,128)(2,1)S(1)}, bf16[128,1024]{1,0:T(8,128)(2,1)S(1)}, u32[]{:S(2)}, u32[]{:S(2)}) collective-permute-start(bf16[128,1024]{1,0:T(8,128)(2,1)S(1)} %collective-permute-done.1.near_ref), channel_id=1, source_target_pairs={{0,1},{1,0},{2,3},{3,2},{4,5},{5,4},{6,7},{7,6},{8,9},{9,8},{10,11... | collective-permute-start | bytes 786440 | tf_op jit(solution)/shard_map/ppermute | solution.py:338
  13.6 1.2 %copy-start.1 = (bf16[256,2048]{1,0:T(8,128)(2,1)S(1)}, bf16[256,2048]{1,0:T(8,128)(2,1)}, u32[]{:S(2)}) copy-start(bf16[256,2048]{1,0:T(8,128)(2,1)} %x_ref.3) | copy-start | bytes 3145732
  16.2 6.9 %copy-start.3 = (f32[4096]{0:T(1024)S(1)}, f32[4096]{0:T(1024)}, u32[]{:S(2)}) copy-start(f32[4096]{0:T(1024)} %param.16) | copy-start | bytes 49156
  16.2 6.9 %copy-start.5 = (s32[1,256]{1,0:T(1,128)S(1)}, s32[1,256]{1,0:T(1,128)}, u32[]{:S(2)}) copy-start(s32[1,256]{1,0:T(1,128)} %mask_ref.7) | copy-start | bytes 3076
  23.1 5.4 %copy-start.6 = (f32[128]{0:T(128)S(1)}, f32[128]{0:T(128)}, u32[]{:S(2)}) copy-start(f32[128]{0:T(128)} %param.22) | copy-start | bytes 1540
  26.8 7.0 %copy-start.7 = (f32[128]{0:T(128)S(1)}, f32[128]{0:T(128)}, u32[]{:S(2)}) copy-start(f32[128]{0:T(128)} %param.21) | copy-start | bytes 1540
  26.9 1.7 %collective-permute-start.4 = (bf16[128,1024]{1,0:T(8,128)(2,1)S(1)}, bf16[128,1024]{1,0:T(8,128)(2,1)S(1)}, u32[]{:S(2)}, u32[]{:S(2)}) collective-permute-start(bf16[128,1024]{1,0:T(8,128)(2,1)S(1)} %collective-permute-done.near_ref), channel_id=1, source_target_pairs={{0,1},{1,0},{2,3},{3,2},{4,5},{5,4},{6,7},{7,6},{8,9},{9,8},{10,11... | collective-permute-start | bytes 786440 | tf_op jit(solution)/shard_map/ppermute | solution.py:338
  29.8 12.7 %collective-permute-start.14 = (bf16[1024,2048]{1,0:T(8,128)(2,1)S(1)}, bf16[1024,2048]{1,0:T(8,128)(2,1)S(1)}, u32[]{:S(2)}, u32[]{:S(2)}) collective-permute-start(bf16[1024,2048]{1,0:T(8,128)(2,1)S(1)} %get-tuple-element.70), channel_id=1, source_target_pairs={{0,1},{1,0},{2,3},{3,2},{4,5},{5,4},{6,7},{7,6},{8,9},{9,8},{10,11... | collective-permute-start | bytes 12582920 | tf_op jit(solution)/shard_map/ppermute | solution.py:338
  30.2 10.8 %collective-permute-start.6 = (bf16[256,512]{1,0:T(8,128)(2,1)S(1)}, bf16[256,512]{1,0:T(8,128)(2,1)S(1)}, u32[]{:S(2)}, u32[]{:S(2)}) collective-permute-start(bf16[256,512]{1,0:T(8,128)(2,1)S(1)} %shard_map.143.kv_ref), channel_id=1, source_target_pairs={{0,4},{2,6},{4,8},{6,10},{8,12},{10,14},{12,0},{14,2},{1,5},{3,7},... | collective-permute-start | bytes 786440 | tf_op jit(solution)/shard_map/ppermute | solution.py:383
  32.3 10.2 %collective-permute-start.5 = (bf16[256,512]{1,0:T(8,128)(2,1)S(1)}, bf16[256,512]{1,0:T(8,128)(2,1)S(1)}, u32[]{:S(2)}, u32[]{:S(2)}) collective-permute-start(bf16[256,512]{1,0:T(8,128)(2,1)S(1)} %shard_map.143.kv_ref), channel_id=1, source_target_pairs={{0,2},{2,0},{4,6},{6,4},{8,10},{10,8},{12,14},{14,12},{1,3},{3,1},... | collective-permute-start | bytes 786440 | tf_op jit(solution)/shard_map/ppermute | solution.py:384
  41.0 9.7 %collective-permute-start.8 = (bf16[256,512]{1,0:T(8,128)(2,1)S(1)}, bf16[256,512]{1,0:T(8,128)(2,1)S(1)}, u32[]{:S(2)}, u32[]{:S(2)}) collective-permute-start(bf16[256,512]{1,0:T(8,128)(2,1)S(1)} %collective-permute-done.6.second_ref), channel_id=1, source_target_pairs={{0,4},{2,6},{4,8},{6,10},{8,12},{10,14},{12,0},{14,2},{1,5},{3,7},... | collective-permute-start | bytes 786440 | tf_op jit(solution)/shard_map/ppermute | solution.py:383
  41.1 10.8 %collective-permute-start.7 = (bf16[256,512]{1,0:T(8,128)(2,1)S(1)}, bf16[256,512]{1,0:T(8,128)(2,1)S(1)}, u32[]{:S(2)}, u32[]{:S(2)}) collective-permute-start(bf16[256,512]{1,0:T(8,128)(2,1)S(1)} %collective-permute-done.6.second_ref), channel_id=1, source_target_pairs={{0,2},{2,0},{4,6},{6,4},{8,10},{10,8},{12,14},{14,12},{1,3},{3,1},... | collective-permute-start | bytes 786440 | tf_op jit(solution)/shard_map/ppermute | solution.py:384
  50.6 8.8 %collective-permute-start.10 = (bf16[256,512]{1,0:T(8,128)(2,1)S(1)}, bf16[256,512]{1,0:T(8,128)(2,1)S(1)}, u32[]{:S(2)}, u32[]{:S(2)}) collective-permute-start(bf16[256,512]{1,0:T(8,128)(2,1)S(1)} %collective-permute-done.8.second_ref), channel_id=1, source_target_pairs={{0,4},{2,6},{4,8},{6,10},{8,12},{10,14},{12,0},{14,2},{1,5},{3,7},... | collective-permute-start | bytes 786440 | tf_op jit(solution)/shard_map/ppermute | solution.py:383
  50.6 9.8 %collective-permute-start.9 = (bf16[256,512]{1,0:T(8,128)(2,1)S(1)}, bf16[256,512]{1,0:T(8,128)(2,1)S(1)}, u32[]{:S(2)}, u32[]{:S(2)}) collective-permute-start(bf16[256,512]{1,0:T(8,128)(2,1)S(1)} %collective-permute-done.8.second_ref), channel_id=1, source_target_pairs={{0,2},{2,0},{4,6},{6,4},{8,10},{10,8},{12,14},{14,12},{1,3},{3,1},... | collective-permute-start | bytes 786440 | tf_op jit(solution)/shard_map/ppermute | solution.py:384
  59.4 6.4 %collective-permute-start.11 = (bf16[256,512]{1,0:T(8,128)(2,1)S(1)}, bf16[256,512]{1,0:T(8,128)(2,1)S(1)}, u32[]{:S(2)}, u32[]{:S(2)}) collective-permute-start(bf16[256,512]{1,0:T(8,128)(2,1)S(1)} %collective-permute-done.10.second_ref), channel_id=1, source_target_pairs={{0,2},{2,0},{4,6},{6,4},{8,10},{10,8},{12,14},{14,12},{1,3},{3,1},... | collective-permute-start | bytes 786440 | tf_op jit(solution)/shard_map/ppermute | solution.py:384
  60.4 8.3 %slice-start = ((s8[8388608]{0:T(1024)(128)(4,1)}), s8[4194304]{0:T(1024)(128)(4,1)S(1)}, s32[]{:S(2)}) async-start(s8[8388608]{0:T(1024)(128)(4,1)} %bitcast.8), calls=%async_computation | async-start | bytes 8388608
  65.8 2.9 %slice-start.1 = ((s8[8388608]{0:T(1024)(128)(4,1)}), s8[4194304]{0:T(1024)(128)(4,1)S(1)}, s32[]{:S(2)}) async-start(s8[8388608]{0:T(1024)(128)(4,1)} %bitcast.8), calls=%async_computation.1 | async-start | bytes 8388608
  66.7 2.0 %collective-permute-start.13 = (bf16[512,512]{1,0:T(8,128)(2,1)S(1)}, bf16[512,512]{1,0:T(8,128)(2,1)S(1)}, u32[]{:S(2)}, u32[]{:S(2)}) collective-permute-start(bf16[512,512]{1,0:T(8,128)(2,1)S(1)} %get-tuple-element.68.ga), channel_id=1, source_target_pairs={{0,1},{1,0},{2,3},{3,2},{4,5},{5,4},{6,7},{7,6},{8,9},{9,8},{10,11... | collective-permute-start | bytes 1572872 | tf_op jit(solution)/shard_map/ppermute | solution.py:338
  67.6 5.0 %copy-start.8 = (s32[1,4]{1,0:T(1,128)S(1)}, s32[1,4]{1,0:T(1,128)}, u32[]{:S(2)}) copy-start(s32[1,4]{1,0:T(1,128)} %param.24) | copy-start | bytes 52
  67.7 4.9 %collective-permute-start.12 = (bf16[512,512]{1,0:T(8,128)(2,1)S(1)}, bf16[512,512]{1,0:T(8,128)(2,1)S(1)}, u32[]{:S(2)}, u32[]{:S(2)}) collective-permute-start(bf16[512,512]{1,0:T(8,128)(2,1)S(1)} %get-tuple-element.67.gb), channel_id=1, source_target_pairs={{0,1},{1,0},{2,3},{3,2},{4,5},{5,4},{6,7},{7,6},{8,9},{9,8},{10,11... | collective-permute-start | bytes 1572872 | tf_op jit(solution)/shard_map/ppermute | solution.py:338
  (2 other events, 1.4 us)

commit v5 on v4

--- a/solution.py
+++ b/solution.py
@@ -77,21 +77,30 @@
     return gain, embed, condition
 
 
-def squares_kernel(info, x_ref, squares_ref, first_ref, last_ref):
+def squares_kernel(x_hbm, mask_hbm, shift_hbm, x_ref, mask_ref, shift_ref, squares_ref, sems):
+    moves = [
+        pltpu.make_async_copy(source, target, sems.at[number])
+        for number, (source, target) in enumerate(((x_hbm, x_ref), (mask_hbm, mask_ref), (shift_hbm, shift_ref)))
+    ]
+    for move in moves:
+        move.start()
+    for move in moves:
+        move.wait()
     rows = x_ref.shape[0]
-    cut, depth = first_ref.shape
     x = x_ref[...].astype(F32)
     sums = jnp.sum(x * x, axis=1, keepdims=True)
     eye = lax.broadcasted_iota(jnp.int32, (rows, rows), 0) == lax.broadcasted_iota(jnp.int32, (rows, rows), 1)
     squares_ref[...] = jnp.sum(jnp.where(eye, jnp.broadcast_to(sums, (rows, rows)), 0.0), axis=0, keepdims=True)
-    strip = pl.ds(pl.multiple_of(info[1] * cut, 128), cut)
-    first_ref[...] = x_ref[strip, :depth]
-    last_ref[...] = x_ref[strip, depth:]
+
+
+def strip_kernel(info, x_ref, strip_ref):
+    rows = strip_ref.shape[0]
+    strip_ref[...] = x_ref[pl.ds(pl.multiple_of(info[1] * rows, 128), rows)]
 
 
 def own_half_kernel(
-    info, x_ref, own_ref, other_ref, mask_ref, gain_ref, embed_ref, shift_ref, wq, wk, wv,
-    q_ref, k_ref, v_ref, rest_q, rest_k, rest_v, own_q, own_k, own_v, sems,
+    info, x_ref, own_ref, other_ref, mask_ref, gain_ref, embed_ref, shift_ref, wq, wk, wv, w_out,
+    q_ref, k_ref, v_ref, rest_q, rest_k, rest_v, w_send, own_q, own_k, own_v, sems,
 ):
     half = x_ref.shape[1]
     depth = half // 2
@@ -110,6 +119,8 @@
     rest = pl.ds(pl.multiple_of(half - first, 128), half)
     for source, target in ((wk, rest_k), (wv, rest_v), (wq, rest_q)):
         move(source.at[rest], target)
+    cols = w_send.shape[1]
+    move(w_out.at[:, pl.ds(pl.multiple_of((1 - info[1]) * cols, 128), cols)], w_send)
 
     scales = row_scales(own_ref, other_ref, mask_ref, embed_ref, embed_ref.shape[1])
     at = pl.ds(pl.multiple_of(first, 128), half)
@@ -132,29 +143,8 @@
     return jnp.concatenate([jnp.where(first, near, far), jnp.where(first, far, near)], axis=0)
 
 
-def chunk_at(info, chunk, depth, width):
-    return pl.ds(pl.multiple_of((1 - info[0]) * (width // 2) + chunk * depth, 128), depth)
-
-
-def chunk_kernel(
-    info, near_ref, far_ref, own_ref, other_ref, mask_ref, gain_ref, embed_ref, shift_ref,
-    wq_ref, wk_ref, wv_ref, pq_ref, pk_ref, pv_ref, w_out, q_ref, k_ref, v_ref, w_send, sem,
-):
-    width = embed_ref.shape[1]
-    cols = w_send.shape[1]
-    side = pl.ds(pl.multiple_of((1 - info[1]) * cols, 128), cols)
-    move = pltpu.make_async_copy(w_out.at[:, side], w_send, sem)
-    move.start()
-    scales = row_scales(own_ref, other_ref, mask_ref, embed_ref, width)
-    at = chunk_at(info, 0, near_ref.shape[1], width)
-    gain, embed, condition = vectors_at(at, info, gain_ref, embed_ref, shift_ref)
-    clean, noisy = both_streams(other_rows(info, near_ref, far_ref), scales, gain, embed, condition)
-    both = jnp.concatenate([clean, noisy], axis=0)
-    here = slice(0, near_ref.shape[1])
-    k_ref[...] = pk_ref[...] + dot(both, wk_ref[here])
-    v_ref[...] = pv_ref[...] + dot(both, wv_ref[here])
-    q_ref[...] = pq_ref[...] + dot(both, wq_ref[here])
-    move.wait()
+def other_half(info, half):
+    return pl.ds(pl.multiple_of((1 - info[0]) * half, 128), half)
 
 
 def kv_out(ref, k, v, gain):
@@ -171,29 +161,27 @@
     rows = all_ref.shape[0]
     width = embed_ref.shape[1]
     clean_scale = row_scales(own_ref, other_ref, mask_ref, embed_ref, width)[0]
-    at = chunk_at(info, 1, near_ref.shape[1], width)
+    at = other_half(info, near_ref.shape[1])
     clean = normed_clean(other_rows(info, near_ref, far_ref), clean_scale, gain_ref[:, at].astype(F32))
-    here = slice(near_ref.shape[1], 2 * near_ref.shape[1])
-    k = pk_ref[:rows] + dot(clean, wk_ref[here])
-    v = pv_ref[:rows] + dot(clean, wv_ref[here])
+    k = pk_ref[:rows] + dot(clean, wk_ref[...])
+    v = pv_ref[:rows] + dot(clean, wv_ref[...])
     kv_out(all_ref, k, v, kgain_ref[...])
 
 
-def last_chunk_kernel(
+def other_half_kernel(
     info, near_ref, far_ref, own_ref, other_ref, mask_ref, gain_ref, embed_ref, shift_ref,
     wq_ref, wk_ref, wv_ref, pq_ref, pk_ref, pv_ref, qgain_ref, kgain_ref, q_ref, self_ref,
 ):
     rows = self_ref.shape[0]
     width = embed_ref.shape[1]
     scales = row_scales(own_ref, other_ref, mask_ref, embed_ref, width)
-    at = chunk_at(info, 1, near_ref.shape[1], width)
+    at = other_half(info, near_ref.shape[1])
     gain, embed, condition = vectors_at(at, info, gain_ref, embed_ref, shift_ref)
     clean, noisy = both_streams(other_rows(info, near_ref, far_ref), scales, gain, embed, condition)
-    here = slice(near_ref.shape[1], 2 * near_ref.shape[1])
-    k = pk_ref[rows:] + dot(noisy, wk_ref[here])
-    v = pv_ref[rows:] + dot(noisy, wv_ref[here])
+    k = pk_ref[rows:] + dot(noisy, wk_ref[...])
+    v = pv_ref[rows:] + dot(noisy, wv_ref[...])
     kv_out(self_ref, k, v, kgain_ref[...])
-    q = pq_ref[...] + dot(jnp.concatenate([clean, noisy], axis=0), wq_ref[here])
+    q = pq_ref[...] + dot(jnp.concatenate([clean, noisy], axis=0), wq_ref[...])
     for head in range(q_ref.shape[1] // HD):
         cols = slice(head * HD, (head + 1) * HD)
         q_ref[:, cols] = head_norm(q[:, cols], qgain_ref[...])
@@ -283,15 +271,22 @@
         mixed_ref[:, cols] = mixed + dot(ha[...], w_far[:part, cols])
 
 
-def out_last_kernel(info, live, hb, mixed_ref, w_far, clean_ref, noisy_ref):
-    rows, tile = clean_ref.shape
+def out_last_kernel(info, live, hb, mixed_ref, w_far, clean_out, noisy_out, clean_ref, noisy_ref, sems, *, tile):
+    rows, total = clean_ref.shape
     part = hb.shape[1]
-    cols = pl.ds(pl.multiple_of(pl.program_id(0) * tile, 128), tile)
-    mixed = mixed_ref[:, cols] + dot(hb[...], w_far[part:, cols])
-    clean_ref[...] = mixed[:rows].astype(BF16)
-    for block in range(rows // BLK):
-        part_rows = mixed[rows + block * BLK : rows + (block + 1) * BLK]
-        noisy_ref[block * BLK : (block + 1) * BLK] = (part_rows * live[block].astype(F32)).astype(BF16)
+    moves = []
+    for start in range(0, total, tile):
+        cols = slice(start, start + tile)
+        mixed = mixed_ref[:, cols] + dot(hb[...], w_far[part:, cols])
+        clean_ref[:, cols] = mixed[:rows].astype(BF16)
+        for block in range(rows // BLK):
+            part_rows = mixed[rows + block * BLK : rows + (block + 1) * BLK]
+            noisy_ref[block * BLK : (block + 1) * BLK, cols] = (part_rows * live[block].astype(F32)).astype(BF16)
+        for source, target in ((clean_ref, clean_out), (noisy_ref, noisy_out)):
+            moves.append(pltpu.make_async_copy(source.at[:, cols], target.at[:, cols], sems.at[len(moves)]))
+            moves[-1].start()
+    for move in moves:
+        move.wait()
 
 
 WHOLE = pl.BlockSpec(memory_space=pltpu.VMEM)
@@ -338,59 +333,55 @@
     cross_core = lambda v: lax.ppermute(v, "tp", pair)
     shape = jax.ShapeDtypeStruct
 
-    cut, depth = rows // 2, half // 2
+    cut = rows // 2
     out_cols = w_out.shape[1] // 2
     qg, kg = q_gain[None], k_gain[None]
     vmem = lambda dims, kind: (WHOLE, pltpu.VMEM(dims, kind))
     in_hbm = lambda v: pltpu.with_memory_space_constraint(v, pltpu.HBM)
 
-    squares, strip_first, strip_last = call(
-        squares_kernel, [info], [WHOLE], [vmem((1, rows), F32)] + [vmem((cut, depth), BF16)] * 2, [clean_tokens],
-        2 * rows * half, rows * half * 2,
+    x, mask, shift, squares = call(
+        squares_kernel, [], [HBM] * 3,
+        [vmem((rows, half), BF16), vmem((1, rows), jnp.int32), vmem((1, 2 * half), F32), vmem((1, rows), F32)],
+        [in_hbm(clean_tokens), in_hbm(masked), in_hbm(time_shift[None])], 2 * rows * half, rows * half * 2,
+        [pltpu.SemaphoreType.DMA((3,))],
     )
     other_squares = cross_x(squares)
-    near_first = cross_x(strip_first)
-    near_last = cross_x(strip_last)
-    stats = [squares, other_squares, masked]
-    vectors = [norm_gain[None], mask_embed[None], time_shift[None]]
-    partial = [vmem((2 * rows, width), F32) for width in (heads_width, kv_width, kv_width)]
+    strip, = call(strip_kernel, [info], [WHOLE], [vmem((cut, half), BF16)], [x], 0, rows * half)
+    near = cross_x(strip)
+    stats = [squares, other_squares, mask]
+    vectors = [norm_gain[None], mask_embed[None], shift]
     buffers = [(half, heads_width), (half, kv_width), (half, kv_width)]
     per_row = heads_width + 2 * kv_width
 
-    pq, pk, pv, *weights = call(
-        own_half_kernel, [info], [WHOLE] * 7 + [HBM] * 3, partial + [vmem(dims, BF16) for dims in buffers],
-        [clean_tokens] + stats + vectors + [in_hbm(w_query), in_hbm(w_key), in_hbm(w_value)],
-        4 * rows * half * per_row, 2 * half * per_row * 2,
-        [pltpu.VMEM(dims, BF16) for dims in buffers] + [pltpu.SemaphoreType.DMA((9,))], limit=32,
-    )
-    far_first = cross_core(near_first)
-    pq, pk, pv, w_send = call(
-        chunk_kernel, [info], [WHOLE] * 14 + [HBM], partial + [vmem((heads_width, out_cols), BF16)],
-        [near_first, far_first] + stats + vectors + weights + [pq, pk, pv, in_hbm(w_out)],
-        4 * rows * depth * per_row, depth * per_row * 2, [pltpu.SemaphoreType.DMA(())],
-        aliases={12: 0, 13: 1, 14: 2},
-    )
-    near_last = after(near_last, pk)
-    far_last = cross_core(near_last)
+    pq, pk, pv, *weights, w_send = call(
+        own_half_kernel, [info], [WHOLE] * 7 + [HBM] * 4,
+        [vmem((2 * rows, width), F32) for width in (heads_width, kv_width, kv_width)]
+        + [vmem(dims, BF16) for dims in buffers] + [vmem((heads_width, out_cols), BF16)],
+        [x] + stats + vectors + [in_hbm(w) for w in (w_query, w_key, w_value, w_out)],
+        32 * rows * half * per_row, 2 * half * per_row * 2,
+        [pltpu.VMEM(dims, BF16) for dims in buffers] + [pltpu.SemaphoreType.DMA((10,))], limit=32,
+    )
+    near = after(near, pk)
+    far = cross_core(near)
 
     kv, = call(
         clean_kv_kernel, [info], [WHOLE] * 12, [vmem((rows, 2 * kv_width), BF16)],
-        [near_last, far_last] + stats + vectors[:2] + weights[1:] + [pk, pv, kg],
-        4 * rows * depth * kv_width, depth * 2 * kv_width * 2,
+        [near, far] + stats + vectors[:2] + weights[1:] + [pk, pv, kg],
+        4 * rows * half * kv_width, half * 2 * kv_width * 2,
     )
 
     steps = ctx // 2
-    along = lambda v: lax.ppermute(v, "ctx", [(i, (i + 2) % ctx) for i in range(ctx)])
+    along = lambda v: lax.ppermute(v, "ctx", [(i, i + 2) for i in range(ctx - 2)])
     across = lambda v: lax.ppermute(v, "ctx", [(i, i ^ 1) for i in range(ctx)])
     crossed = across(kv)
     column = along(kv)
     w_far = cross_core(after(w_send, kv))
-    near_last = after(near_last, kv)
+    near = after(near, kv)
     q, own = call(
-        last_chunk_kernel, [info], [WHOLE] * 16,
+        other_half_kernel, [info], [WHOLE] * 16,
         [vmem((2 * rows, heads_width), BF16), vmem((rows, 2 * kv_width), BF16)],
-        [near_last, far_last] + stats + vectors + weights + [pq, pk, pv, qg, kg],
-        4 * rows * depth * per_row, depth * per_row * 2,
+        [near, far] + stats + vectors + weights + [pq, pk, pv, qg, kg],
+        4 * rows * half * per_row, half * per_row * 2,
     )
 
     acc = [vmem((2 * rows, heads_width), F32)] * 2
@@ -421,11 +412,11 @@
         functools.partial(out_first_kernel, tile=tile), [info], [WHOLE] * 5, [vmem((2 * rows, out_cols), F32)],
         [ga, gb, ha, w_out, w_far], 6 * rows * heads_width * out_cols, 2 * heads_width * out_cols * 2,
     )
-    out = pl.BlockSpec((rows, tile), lambda n, s, l: (0, n))
-    out_shape = shape((rows, out_cols), BF16)
+    out = shape((rows, out_cols), BF16)
     clean_out, noised_out = call(
-        out_last_kernel, [info, block_live[0]], [WHOLE] * 3, [(out, out_shape), (out, out_shape)],
-        [hb, mixed, w_far], 2 * rows * heads_width * out_cols, heads_width * out_cols * 2, grid=out_cols // tile,
+        functools.partial(out_last_kernel, tile=tile), [info, block_live[0]], [WHOLE] * 3, [(HBM, out), (HBM, out)],
+        [hb, mixed, w_far], 2 * rows * heads_width * out_cols, heads_width * out_cols * 2,
+        [pltpu.VMEM((rows, out_cols), BF16)] * 2 + [pltpu.SemaphoreType.DMA((2 * (out_cols // tile),))],
     )
     return (clean_out, noised_out[None])
 

time: 76.4 us -> 71.5 us (0.936)
  the two profiles are of different devices: /device:TPU:0 before, /device:TPU:25 now
where the time goes in v5:
time: 71.5 us; the launch traced here: 70.1 us
  Pallas kernels  39 us (55%)
  waiting for transfers between devices  15.7 us (22%)
  starting transfers between devices  13.7 us (19%)
  between operations  1.7 us (2%)
    pallas_call x13, Pallas kernels, call(): pl.pallas_call(kernel, grid_spec=pltpu.PrefetchScalarGridSpec(num_scalar_...  39 us
    ppermute x3, waiting for transfers between devices, on_device(): lax.ppermute(v, 'ctx', [(i, i + 2) for i in range(ctx - 2)])  7.81 us
    ppermute x4, starting transfers between devices, on_device(): cross_core = lambda v: lax.ppermute(v, 'tp', pair)  5.57 us
    ppermute x2, waiting for transfers between devices, on_device(): cross_x = lambda v: lax.ppermute(v, 'copy', pair)  5.28 us
    ppermute x3, starting transfers between devices, on_device(): lax.ppermute(v, 'ctx', [(i, i + 2) for i in range(ctx - 2)])  3.84 us
    ppermute x4, starting transfers between devices, on_device(): across = lambda v: lax.ppermute(v, 'ctx', [(i, i ^ 1) for i in range(ctx)])  2.68 us
    ppermute x2, starting transfers between devices, on_device(): cross_x = lambda v: lax.ppermute(v, 'copy', pair)  1.6 us
    ppermute x4, waiting for transfers between devices, on_device(): cross_core = lambda v: lax.ppermute(v, 'tp', pair)  1.54 us
  transfers between devices with their start and end apart: 13, of which 5 were waited for; matrix products, arithmetic and copies ran while one was open for 0% of the time, Pallas kernels for 45%

profile of v5, /device:TPU:25, one launch (start us, length us, event | category | flops | bytes accessed | tf_op | source)
XLA Modules:
  0.0 70.1 jit_solution(1953464082462760642)
XLA Ops:
  0.7 1.6 %shard_map.140 = (bf16[256,2048]{1,0:T(8,128)(2,1)S(1)}, s32[1,256]{1,0:T(1,128)S(1)}, f32[1,4096]{1,0:T(1,128)S(1)}, f32[1,256]{1,0:T(1,128)S(1)}) custom-call(bf16[256,2048]{1,0:T(8,128)(2,1)} %x_hbm.1, s32[1,256]{1,0:T(1,128)} %mask_hbm.1, f32[1,4096]{1,0:T(1,128)} %bitcast.14), custom_call_target="tpu_custom_call" | custom-call | flops 1048576 | bytes 1048576 | tf_op jit(solution)/shard_map/pallas_call | solution.py:298
  2.2 1.3 %collective-permute-start.1 = (f32[1,256]{1,0:T(1,128)S(1)}, f32[1,256]{1,0:T(1,128)S(1)}, u32[]{:S(2)}, u32[]{:S(2)}) collective-permute-start(f32[1,256]{1,0:T(1,128)S(1)} %get-tuple-element.37.own_ref), channel_id=1, source_target_pairs={{0,16},{16,0},{1,17},{17,1},{2,18},{18,2},{3,19},{19,3},{4,20},{20... | collective-permute-start | bytes 3080 | tf_op jit(solution)/shard_map/ppermute | solution.py:332
  5.2 6.9 %shard_map.142 = (f32[512,1024]{1,0:T(8,128)S(1)}, f32[512,256]{1,0:T(8,128)S(1)}, f32[512,256]{1,0:T(8,128)S(1)}, bf16[2048,1024]{1,0:T(8,128)(2,1)S(1)}, bf16[...) custom-call(s32[4]{0:T(128)S(1)} %pad_add_fusion.info, ...), custom_call_target="tpu_custom_call" | custom-call | flops 25769803776 | bytes 12582912 | tf_op jit(solution)/shard_map/pallas_call | solution.py:298
  12.1 5.3 %collective-permute-done.near_ref = bf16[128,2048]{1,0:T(8,128)(2,1)S(1)} collective-permute-done((bf16[128,2048]{1,0:T(8,128)(2,1)S(1)}, bf16[128,2048]{1,0:T(8,128)(2,1)S(1)}, u32[]{:S(2)}, u32[]{:S(2)}) %collective-permute-start) | collective-permute-done | bytes 524320 | tf_op jit(solution)/shard_map/ppermute | solution.py:332
  17.4 1.9 %collective-permute-start.2 = (bf16[128,2048]{1,0:T(8,128)(2,1)S(1)}, bf16[128,2048]{1,0:T(8,128)(2,1)S(1)}, u32[]{:S(2)}, u32[]{:S(2)}) collective-permute-start(bf16[128,2048]{1,0:T(8,128)(2,1)S(1)} %collective-permute-done.near_ref), channel_id=1, source_target_pairs={{0,1},{1,0},{2,3},{3,2},{4,5},{5,4},{6,7},{7,6},{8,9},{9,8},{10,11... | collective-permute-start | bytes 1572872 | tf_op jit(solution)/shard_map/ppermute | solution.py:333
  19.2 1.5 %collective-permute-done.2.far_ref = bf16[128,2048]{1,0:T(8,128)(2,1)S(1)} collective-permute-done((bf16[128,2048]{1,0:T(8,128)(2,1)S(1)}, bf16[128,2048]{1,0:T(8,128)(2,1)S(1)}, u32[]{:S(2)}, u32[]{:S(2)}) %collective-permute-start.2) | collective-permute-done | bytes 524320 | tf_op jit(solution)/shard_map/ppermute | solution.py:333
  20.8 1.5 %shard_map.143.kv_ref = bf16[256,512]{1,0:T(8,128)(2,1)S(1)} custom-call(s32[4]{0:T(128)S(1)} %pad_add_fusion.info, bf16[128,2048]{1,0:T(8,128)(2,1)S(1)} %collective-permute-done.near_ref, bf16[128,2048]{1,0:T(8,128)(2,1)S(1)} %collective-permute-done.2.far_ref, f32[1,256]{1,0:T(1,128)S(1)} %get-tuple-element.37.own_ref, ...), custom_call_target="tpu_custom_call" | custom-call | flops 536870912 | bytes 2097152 | tf_op jit(solution)/shard_map/pallas_call | solution.py:298
  22.7 1.3 %collective-permute-start.4 = (bf16[256,512]{1,0:T(8,128)(2,1)S(1)}, bf16[256,512]{1,0:T(8,128)(2,1)S(1)}, u32[]{:S(2)}, u32[]{:S(2)}) collective-permute-start(bf16[256,512]{1,0:T(8,128)(2,1)S(1)} %shard_map.143.kv_ref), channel_id=1, source_target_pairs={{0,4},{2,6},{4,8},{6,10},{8,12},{10,14},{1,5},{3,7},{5,9},{7,11},{... | collective-permute-start | bytes 786440 | tf_op jit(solution)/shard_map/ppermute | solution.py:374
  24.0 1.3 %collective-permute-start.3 = (bf16[256,512]{1,0:T(8,128)(2,1)S(1)}, bf16[256,512]{1,0:T(8,128)(2,1)S(1)}, u32[]{:S(2)}, u32[]{:S(2)}) collective-permute-start(bf16[256,512]{1,0:T(8,128)(2,1)S(1)} %shard_map.143.kv_ref), channel_id=1, source_target_pairs={{0,2},{2,0},{4,6},{6,4},{8,10},{10,8},{12,14},{14,12},{1,3},{3,1},... | collective-permute-start | bytes 786440 | tf_op jit(solution)/shard_map/ppermute | solution.py:375
  25.3 3.9 %shard_map.144 = (bf16[512,1024]{1,0:T(8,128)(2,1)S(1)}, bf16[256,512]{1,0:T(8,128)(2,1)S(1)}) custom-call(s32[4]{0:T(128)S(1)} %pad_add_fusion.info, bf16[128,2048]{1,0:T(8,128)(2,1)S(1)} %collective-permute-done.near_ref, bf16[128,2048]{1,0:T(8,128)(2,1)S(1)} %collective-permute-done.2.far_ref, f32[1,256]{1,0:T(1,128)S(1)} %get-tuple-element.37.own_ref, ...), custom_call_target="tpu_custom_call" | custom-call | flops 3221225472 | bytes 6291456 | tf_op jit(solution)/shard_map/pallas_call | solution.py:298
  29.2 3.1 %shard_map.145 = (f32[512,1024]{1,0:T(8,128)S(1)}, f32[512,1024]{1,0:T(8,128)S(1)}) custom-call(s32[4]{0:T(128)S(1)} %pad_add_fusion.info, bf16[512,1024]{1,0:T(8,128)(2,1)S(1)} %get-tuple-element.48.q_ref, bf16[256,512]{1,0:T(8,128)(2,1)S(1)} %shard_map.143.kv_ref, bf16[256,512]{1,0:T(8,128)(2,1)S(1)} %get-tuple-element.49.self_ref), custom_call_target="tpu_custom_call" | custom-call | flops 805306368 | bytes 4194304 | tf_op jit(solution)/shard_map/pallas_call | solution.py:298
  32.4 1.3 %collective-permute-start.6 = (bf16[256,512]{1,0:T(8,128)(2,1)S(1)}, bf16[256,512]{1,0:T(8,128)(2,1)S(1)}, u32[]{:S(2)}, u32[]{:S(2)}) collective-permute-start(bf16[256,512]{1,0:T(8,128)(2,1)S(1)} %collective-permute-done.4.second_ref), channel_id=1, source_target_pairs={{0,4},{2,6},{4,8},{6,10},{8,12},{10,14},{1,5},{3,7},{5,9},{7,11},{... | collective-permute-start | bytes 786440 | tf_op jit(solution)/shard_map/ppermute | solution.py:374
  33.7 1.3 %collective-permute-start.5 = (bf16[256,512]{1,0:T(8,128)(2,1)S(1)}, bf16[256,512]{1,0:T(8,128)(2,1)S(1)}, u32[]{:S(2)}, u32[]{:S(2)}) collective-permute-start(bf16[256,512]{1,0:T(8,128)(2,1)S(1)} %collective-permute-done.4.second_ref), channel_id=1, source_target_pairs={{0,2},{2,0},{4,6},{6,4},{8,10},{10,8},{12,14},{14,12},{1,3},{3,1},... | collective-permute-start | bytes 786440 | tf_op jit(solution)/shard_map/ppermute | solution.py:375
  35.0 2.3 %shard_map.146 = (f32[512,1024]{1,0:T(8,128)S(1)}, f32[512,1024]{1,0:T(8,128)S(1)}) custom-call(s32[4]{0:T(128)S(1)} %pad_add_fusion.info, bf16[512,1024]{1,0:T(8,128)(2,1)S(1)} %get-tuple-element.48.q_ref, f32[512,1024]{1,0:T(8,128)S(1)} %get-tuple-element.50.num_in, ...), custom_call_target="tpu_custom_call", output_to_operand_aliasing={{0}: (2, {}), {1}: (3, {})} | custom-call | flops 1073741824 | bytes 4194304 | tf_op jit(solution)/shard_map/pallas_call | solution.py:298
  37.2 5.1 %collective-permute-done.6.second_ref = bf16[256,512]{1,0:T(8,128)(2,1)S(1)} collective-permute-done((bf16[256,512]{1,0:T(8,128)(2,1)S(1)}, bf16[256,512]{1,0:T(8,128)(2,1)S(1)}, u32[]{:S(2)}, u32[]{:S(2)}) %collective-permute-start.6) | collective-permute-done | bytes 262176 | tf_op jit(solution)/shard_map/ppermute | solution.py:374
  42.3 1.3 %collective-permute-start.8 = (bf16[256,512]{1,0:T(8,128)(2,1)S(1)}, bf16[256,512]{1,0:T(8,128)(2,1)S(1)}, u32[]{:S(2)}, u32[]{:S(2)}) collective-permute-start(bf16[256,512]{1,0:T(8,128)(2,1)S(1)} %collective-permute-done.6.second_ref), channel_id=1, source_target_pairs={{0,4},{2,6},{4,8},{6,10},{8,12},{10,14},{1,5},{3,7},{5,9},{7,11},{... | collective-permute-start | bytes 786440 | tf_op jit(solution)/shard_map/ppermute | solution.py:374
  43.7 4.3 %shard_map.147 = (f32[512,1024]{1,0:T(8,128)S(1)}, f32[512,1024]{1,0:T(8,128)S(1)}) custom-call(s32[4]{0:T(128)S(1)} %pad_add_fusion.info, bf16[512,1024]{1,0:T(8,128)(2,1)S(1)} %get-tuple-element.48.q_ref, f32[512,1024]{1,0:T(8,128)S(1)} %get-tuple-element.53.num_in, ...), custom_call_target="tpu_custom_call", output_to_operand_aliasing={{0}: (2, {}), {1}: (3, {})} | custom-call | flops 1073741824 | bytes 4194304 | tf_op jit(solution)/shard_map/pallas_call | solution.py:298
  48.1 2.7 %collective-permute-done.8.second_ref = bf16[256,512]{1,0:T(8,128)(2,1)S(1)} collective-permute-done((bf16[256,512]{1,0:T(8,128)(2,1)S(1)}, bf16[256,512]{1,0:T(8,128)(2,1)S(1)}, u32[]{:S(2)}, u32[]{:S(2)}) %collective-permute-start.8) | collective-permute-done | bytes 262176 | tf_op jit(solution)/shard_map/ppermute | solution.py:374
  50.7 4.6 %shard_map.148 = (f32[512,1024]{1,0:T(8,128)S(1)}, f32[512,1024]{1,0:T(8,128)S(1)}) custom-call(s32[4]{0:T(128)S(1)} %pad_add_fusion.info, bf16[512,1024]{1,0:T(8,128)(2,1)S(1)} %get-tuple-element.48.q_ref, f32[512,1024]{1,0:T(8,128)S(1)} %get-tuple-element.56.num_in, ...), custom_call_target="tpu_custom_call", output_to_operand_aliasing={{0}: (2, {}), {1}: (3, {})} | custom-call | flops 1073741824 | bytes 4194304 | tf_op jit(solution)/shard_map/pallas_call | solution.py:298
  56.3 1.9 %shard_map.149 = (f32[512,1024]{1,0:T(8,128)S(1)}, f32[512,1024]{1,0:T(8,128)S(1)}, bf16[512,512]{1,0:T(8,128)(2,1)S(1)}) custom-call(s32[4]{0:T(128)S(1)} %pad_add_fusion.info, bf16[512,1024]{1,0:T(8,128)(2,1)S(1)} %get-tuple-element.48.q_ref, f32[512,1024]{1,0:T(8,128)S(1)} %get-tuple-element.59.num_in, ...), custom_call_target="tpu_custom_call", output_to_operand_aliasing={{0}: (2, {}), {1}: (3, {})} | custom-call | flops 268435456 | bytes 4194304 | tf_op jit(solution)/shard_map/pallas_call | solution.py:298
  58.2 3.2 %collective-permute-start.11 = (bf16[512,512]{1,0:T(8,128)(2,1)S(1)}, bf16[512,512]{1,0:T(8,128)(2,1)S(1)}, u32[]{:S(2)}, u32[]{:S(2)}) collective-permute-start(bf16[512,512]{1,0:T(8,128)(2,1)S(1)} %get-tuple-element.64.ga), channel_id=1, source_target_pairs={{0,1},{1,0},{2,3},{3,2},{4,5},{5,4},{6,7},{7,6},{8,9},{9,8},{10,11... | collective-permute-start | bytes 1572872 | tf_op jit(solution)/shard_map/ppermute | solution.py:333
  61.4 1.9 %shard_map.150 = (f32[512,1024]{1,0:T(8,128)S(1)}, f32[512,1024]{1,0:T(8,128)S(1)}, bf16[512,512]{1,0:T(8,128)(2,1)S(1)}) custom-call(s32[4]{0:T(128)S(1)} %pad_add_fusion.info, bf16[512,1024]{1,0:T(8,128)(2,1)S(1)} %get-tuple-element.48.q_ref, f32[512,1024]{1,0:T(8,128)S(1)} %get-tuple-element.61.num_in, ...), custom_call_target="tpu_custom_call", output_to_operand_aliasing={{0}: (2, {}), {1}: (3, {})} | custom-call | flops 268435456 | bytes 4194304 | tf_op jit(solution)/shard_map/pallas_call | solution.py:298
  63.4 4.0 %shard_map.151.mixed_ref = f32[512,2048]{1,0:T(8,128)S(1)} custom-call(s32[4]{0:T(128)S(1)} %pad_add_fusion.info, bf16[512,512]{1,0:T(8,128)(2,1)S(1)} %get-tuple-element.64.ga, bf16[512,512]{1,0:T(8,128)(2,1)S(1)} %get-tuple-element.63.gb, bf16[512,512]{1,0:T(8,128)(2,1)S(1)} %collective-permute-done.11.ha, bf16[1024,4096]{1,0:T(8,128)(2,1)S(1)} %bitcast.9, ...), custom_call_target="tpu_custom_call" | custom-call | flops 3221225472 | bytes 8388608 | tf_op jit(solution)/shard_map/pallas_call | solution.py:298
  67.4 2.6 %shard_map.152 = (bf16[256,2048]{1,0:T(8,128)(2,1)}, bf16[256,2048]{1,0:T(8,128)(2,1)}) custom-call(s32[4]{0:T(128)S(1)} %pad_add_fusion.info, s32[4]{0:T(128)S(1)} %bitcast.12, bf16[512,512]{1,0:T(8,128)(2,1)S(1)} %collective-permute-done.10.hb, f32[512,2048]{1,0:T(8,128)S(1)} %shard_map.151.mixed_ref, bf16[1024,2048]{1,0:T(8,128)(2,1)S(1)} %collective-permute-done.12.w_far), custom_call_target="tpu_custom_call" | custom-call | flops 1073741824 | bytes 4194304 | tf_op jit(solution)/shard_map/pallas_call | solution.py:298
  (33 shorter events, 2.7 us)
Async XLA Ops:
  0.6 4.5 %copy-start.3 = (bf16[4096]{0:T(1024)(128)(2,1)S(1)}, bf16[4096]{0:T(1024)(128)(2,1)}, u32[]{:S(2)}) copy-start(bf16[4096]{0:T(1024)(128)(2,1)} %param.14) | copy-start | bytes 24580
  0.6 4.5 %copy-start.4 = (bf16[4096]{0:T(1024)(128)(2,1)S(1)}, bf16[4096]{0:T(1024)(128)(2,1)}, u32[]{:S(2)}) copy-start(bf16[4096]{0:T(1024)(128)(2,1)} %param.15) | copy-start | bytes 24580
  2.2 3.0 %collective-permute-start.1 = (f32[1,256]{1,0:T(1,128)S(1)}, f32[1,256]{1,0:T(1,128)S(1)}, u32[]{:S(2)}, u32[]{:S(2)}) collective-permute-start(f32[1,256]{1,0:T(1,128)S(1)} %get-tuple-element.37.own_ref), channel_id=1, source_target_pairs={{0,16},{16,0},{1,17},{17,1},{2,18},{18,2},{3,19},{19,3},{4,20},{20... | collective-permute-start | bytes 3080 | tf_op jit(solution)/shard_map/ppermute | solution.py:332
  4.8 12.5 %collective-permute-start = (bf16[128,2048]{1,0:T(8,128)(2,1)S(1)}, bf16[128,2048]{1,0:T(8,128)(2,1)S(1)}, u32[]{:S(2)}, u32[]{:S(2)}) collective-permute-start(bf16[128,2048]{1,0:T(8,128)(2,1)S(1)} %shard_map.141), channel_id=1, source_target_pairs={{0,16},{16,0},{1,17},{17,1},{2,18},{18,2},{3,19},{19,3},{4,20},{20... | collective-permute-start | bytes 1572872 | tf_op jit(solution)/shard_map/ppermute | solution.py:332
  5.2 15.6 %copy-start = (f32[128]{0:T(128)S(1)}, f32[128]{0:T(128)}, u32[]{:S(2)}) copy-start(f32[128]{0:T(128)} %param.22) | copy-start | bytes 1540
  17.4 3.4 %collective-permute-start.2 = (bf16[128,2048]{1,0:T(8,128)(2,1)S(1)}, bf16[128,2048]{1,0:T(8,128)(2,1)S(1)}, u32[]{:S(2)}, u32[]{:S(2)}) collective-permute-start(bf16[128,2048]{1,0:T(8,128)(2,1)S(1)} %collective-permute-done.near_ref), channel_id=1, source_target_pairs={{0,1},{1,0},{2,3},{3,2},{4,5},{5,4},{6,7},{7,6},{8,9},{9,8},{10,11... | collective-permute-start | bytes 1572872 | tf_op jit(solution)/shard_map/ppermute | solution.py:333
  20.8 4.6 %copy-start.2 = (f32[128]{0:T(128)S(1)}, f32[128]{0:T(128)}, u32[]{:S(2)}) copy-start(f32[128]{0:T(128)} %param.21) | copy-start | bytes 1540
  22.3 12.7 %collective-permute-start.12 = (bf16[1024,2048]{1,0:T(8,128)(2,1)S(1)}, bf16[1024,2048]{1,0:T(8,128)(2,1)S(1)}, u32[]{:S(2)}, u32[]{:S(2)}) collective-permute-start(bf16[1024,2048]{1,0:T(8,128)(2,1)S(1)} %get-tuple-element.66), channel_id=1, source_target_pairs={{0,1},{1,0},{2,3},{3,2},{4,5},{5,4},{6,7},{7,6},{8,9},{9,8},{10,11... | collective-permute-start | bytes 12582920 | tf_op jit(solution)/shard_map/ppermute | solution.py:333
  22.7 9.7 %collective-permute-start.4 = (bf16[256,512]{1,0:T(8,128)(2,1)S(1)}, bf16[256,512]{1,0:T(8,128)(2,1)S(1)}, u32[]{:S(2)}, u32[]{:S(2)}) collective-permute-start(bf16[256,512]{1,0:T(8,128)(2,1)S(1)} %shard_map.143.kv_ref), channel_id=1, source_target_pairs={{0,4},{2,6},{4,8},{6,10},{8,12},{10,14},{1,5},{3,7},{5,9},{7,11},{... | collective-permute-start | bytes 786440 | tf_op jit(solution)/shard_map/ppermute | solution.py:374
  24.0 11.0 %collective-permute-start.3 = (bf16[256,512]{1,0:T(8,128)(2,1)S(1)}, bf16[256,512]{1,0:T(8,128)(2,1)S(1)}, u32[]{:S(2)}, u32[]{:S(2)}) collective-permute-start(bf16[256,512]{1,0:T(8,128)(2,1)S(1)} %shard_map.143.kv_ref), channel_id=1, source_target_pairs={{0,2},{2,0},{4,6},{6,4},{8,10},{10,8},{12,14},{14,12},{1,3},{3,1},... | collective-permute-start | bytes 786440 | tf_op jit(solution)/shard_map/ppermute | solution.py:375
  32.4 10.0 %collective-permute-start.6 = (bf16[256,512]{1,0:T(8,128)(2,1)S(1)}, bf16[256,512]{1,0:T(8,128)(2,1)S(1)}, u32[]{:S(2)}, u32[]{:S(2)}) collective-permute-start(bf16[256,512]{1,0:T(8,128)(2,1)S(1)} %collective-permute-done.4.second_ref), channel_id=1, source_target_pairs={{0,4},{2,6},{4,8},{6,10},{8,12},{10,14},{1,5},{3,7},{5,9},{7,11},{... | collective-permute-start | bytes 786440 | tf_op jit(solution)/shard_map/ppermute | solution.py:374
  33.7 10.0 %collective-permute-start.5 = (bf16[256,512]{1,0:T(8,128)(2,1)S(1)}, bf16[256,512]{1,0:T(8,128)(2,1)S(1)}, u32[]{:S(2)}, u32[]{:S(2)}) collective-permute-start(bf16[256,512]{1,0:T(8,128)(2,1)S(1)} %collective-permute-done.4.second_ref), channel_id=1, source_target_pairs={{0,2},{2,0},{4,6},{6,4},{8,10},{10,8},{12,14},{14,12},{1,3},{3,1},... | collective-permute-start | bytes 786440 | tf_op jit(solution)/shard_map/ppermute | solution.py:375
  42.3 8.4 %collective-permute-start.8 = (bf16[256,512]{1,0:T(8,128)(2,1)S(1)}, bf16[256,512]{1,0:T(8,128)(2,1)S(1)}, u32[]{:S(2)}, u32[]{:S(2)}) collective-permute-start(bf16[256,512]{1,0:T(8,128)(2,1)S(1)} %collective-permute-done.6.second_ref), channel_id=1, source_target_pairs={{0,4},{2,6},{4,8},{6,10},{8,12},{10,14},{1,5},{3,7},{5,9},{7,11},{... | collective-permute-start | bytes 786440 | tf_op jit(solution)/shard_map/ppermute | solution.py:374
  43.6 7.1 %collective-permute-start.7 = (bf16[256,512]{1,0:T(8,128)(2,1)S(1)}, bf16[256,512]{1,0:T(8,128)(2,1)S(1)}, u32[]{:S(2)}, u32[]{:S(2)}) collective-permute-start(bf16[256,512]{1,0:T(8,128)(2,1)S(1)} %collective-permute-done.6.second_ref), channel_id=1, source_target_pairs={{0,2},{2,0},{4,6},{6,4},{8,10},{10,8},{12,14},{14,12},{1,3},{3,1},... | collective-permute-start | bytes 786440 | tf_op jit(solution)/shard_map/ppermute | solution.py:375
  50.7 5.6 %collective-permute-start.9 = (bf16[256,512]{1,0:T(8,128)(2,1)S(1)}, bf16[256,512]{1,0:T(8,128)(2,1)S(1)}, u32[]{:S(2)}, u32[]{:S(2)}) collective-permute-start(bf16[256,512]{1,0:T(8,128)(2,1)S(1)} %collective-permute-done.8.second_ref), channel_id=1, source_target_pairs={{0,2},{2,0},{4,6},{6,4},{8,10},{10,8},{12,14},{14,12},{1,3},{3,1},... | collective-permute-start | bytes 786440 | tf_op jit(solution)/shard_map/ppermute | solution.py:375
  50.7 12.6 %slice-start = ((s8[8388608]{0:T(1024)(128)(4,1)}), s8[4194304]{0:T(1024)(128)(4,1)S(1)}, s32[]{:S(2)}) async-start(s8[8388608]{0:T(1024)(128)(4,1)} %bitcast.8), calls=%async_computation | async-start | bytes 8388608
  56.3 7.0 %slice-start.1 = ((s8[8388608]{0:T(1024)(128)(4,1)}), s8[4194304]{0:T(1024)(128)(4,1)S(1)}, s32[]{:S(2)}) async-start(s8[8388608]{0:T(1024)(128)(4,1)} %bitcast.8), calls=%async_computation.1 | async-start | bytes 8388608
  58.2 5.1 %collective-permute-start.11 = (bf16[512,512]{1,0:T(8,128)(2,1)S(1)}, bf16[512,512]{1,0:T(8,128)(2,1)S(1)}, u32[]{:S(2)}, u32[]{:S(2)}) collective-permute-start(bf16[512,512]{1,0:T(8,128)(2,1)S(1)} %get-tuple-element.64.ga), channel_id=1, source_target_pairs={{0,1},{1,0},{2,3},{3,2},{4,5},{5,4},{6,7},{7,6},{8,9},{9,8},{10,11... | collective-permute-start | bytes 1572872 | tf_op jit(solution)/shard_map/ppermute | solution.py:333
  63.2 4.1 %copy-start.1 = (s32[1,4]{1,0:T(1,128)S(1)}, s32[1,4]{1,0:T(1,128)}, u32[]{:S(2)}) copy-start(s32[1,4]{1,0:T(1,128)} %param.24) | copy-start | bytes 52
  63.3 4.1 %collective-permute-start.10 = (bf16[512,512]{1,0:T(8,128)(2,1)S(1)}, bf16[512,512]{1,0:T(8,128)(2,1)S(1)}, u32[]{:S(2)}, u32[]{:S(2)}) collective-permute-start(bf16[512,512]{1,0:T(8,128)(2,1)S(1)} %get-tuple-element.63.gb), channel_id=1, source_target_pairs={{0,1},{1,0},{2,3},{3,2},{4,5},{5,4},{6,7},{7,6},{8,9},{9,8},{10,11... | collective-permute-start | bytes 1572872 | tf_op jit(solution)/shard_map/ppermute | solution.py:333

commit v6 on v5

--- a/solution.py
+++ b/solution.py
@@ -77,7 +77,7 @@
     return gain, embed, condition
 
 
-def squares_kernel(x_hbm, mask_hbm, shift_hbm, x_ref, mask_ref, shift_ref, squares_ref, sems):
+def squares_kernel(x_hbm, mask_hbm, shift_hbm, x_ref, mask_ref, shift_ref, squares_ref, strip_ref, sems):
     moves = [
         pltpu.make_async_copy(source, target, sems.at[number])
         for number, (source, target) in enumerate(((x_hbm, x_ref), (mask_hbm, mask_ref), (shift_hbm, shift_ref)))
@@ -91,11 +91,9 @@
     sums = jnp.sum(x * x, axis=1, keepdims=True)
     eye = lax.broadcasted_iota(jnp.int32, (rows, rows), 0) == lax.broadcasted_iota(jnp.int32, (rows, rows), 1)
     squares_ref[...] = jnp.sum(jnp.where(eye, jnp.broadcast_to(sums, (rows, rows)), 0.0), axis=0, keepdims=True)
-
-
-def strip_kernel(info, x_ref, strip_ref):
-    rows = strip_ref.shape[0]
-    strip_ref[...] = x_ref[pl.ds(pl.multiple_of(info[1] * rows, 128), rows)]
+    cut = strip_ref.shape[0]
+    strip = pl.ds(pl.multiple_of(lax.axis_index("tp") * cut, 128), cut)
+    strip_ref[...] = x_ref[strip]
 
 
 def own_half_kernel(
@@ -206,30 +204,33 @@
     v = jnp.concatenate([ref[:, base + HD : base + 2 * HD] for ref in piece_refs], axis=0)
     for head in range(kv_head * group, (kv_head + 1) * group):
         cols = slice(head * HD, (head + 1) * HD)
-        for part in range(2):
-            cut = slice(part * rows, (part + 1) * rows)
-            num, den = terms(q_ref[cut, cols], k, v, None)
-            num_ref[cut, cols] += num
-            den_ref[cut, cols] += den
+        num, den = terms(q_ref[:, cols], k, v, None)
+        num_ref[:, cols] += num
+        den_ref[:, cols] += den
 
 
 def attention_own_kernel(info, q_ref, kv_ref, self_ref, num_ref, den_ref):
     rows = kv_ref.shape[0]
     kv_heads = kv_ref.shape[1] // (2 * HD)
     group = q_ref.shape[1] // HD // kv_heads
-    row_block = lax.broadcasted_iota(jnp.int32, (rows, rows), 0) // BLK
-    key_block = lax.broadcasted_iota(jnp.int32, (rows, rows), 1) // BLK
-    both = jnp.concatenate([key_block < row_block, key_block == row_block], axis=1)
+    row = lax.broadcasted_iota(jnp.int32, (2 * rows, rows), 0)
+    key_block = lax.broadcasted_iota(jnp.int32, (2 * rows, rows), 1) // BLK
+    noisy = row >= rows
+    row_block = jnp.where(noisy, row - rows, row) // BLK
+    same = key_block == row_block
+    allowed = jnp.logical_or(key_block < row_block, jnp.logical_and(same, jnp.logical_not(noisy)))
     for kv_head in range(kv_heads):
         k_cols = slice(2 * kv_head * HD, (2 * kv_head + 1) * HD)
         v_cols = slice((2 * kv_head + 1) * HD, 2 * (kv_head + 1) * HD)
-        k, v = kv_ref[:, k_cols], kv_ref[:, v_cols]
-        k_both = jnp.concatenate([k, self_ref[:, k_cols]], axis=0)
-        v_both = jnp.concatenate([v, self_ref[:, v_cols]], axis=0)
-        for head in range(kv_head * group, (kv_head + 1) * group):
-            cols = slice(head * HD, (head + 1) * HD)
-            num_ref[:rows, cols], den_ref[:rows, cols] = terms(q_ref[:rows, cols], k, v, key_block <= row_block)
-            num_ref[rows:, cols], den_ref[rows:, cols] = terms(q_ref[rows:, cols], k_both, v_both, both)
+        for head in range(kv_head * group, (kv_head + 1) * group, 2):
+            pair = [slice(one * HD, (one + 1) * HD) for one in (head, head + 1)]
+            for cols in pair:
+                num_ref[:, cols], den_ref[:, cols] = terms(q_ref[:, cols], kv_ref[:, k_cols], kv_ref[:, v_cols], allowed)
+            q_noisy = jnp.concatenate([q_ref[rows:, cols] for cols in pair], axis=0)
+            num, den = terms(q_noisy, self_ref[:, k_cols], self_ref[:, v_cols], same)
+            for number, cols in enumerate(pair):
+                num_ref[rows:, cols] += num[number * rows : (number + 1) * rows]
+                den_ref[rows:, cols] += den[number * rows : (number + 1) * rows]
 
 
 def attention_pair_kernel(info, q_ref, num_in, den_in, first_ref, second_ref, num_ref, den_ref, *, step):
@@ -339,14 +340,14 @@
     vmem = lambda dims, kind: (WHOLE, pltpu.VMEM(dims, kind))
     in_hbm = lambda v: pltpu.with_memory_space_constraint(v, pltpu.HBM)
 
-    x, mask, shift, squares = call(
+    x, mask, shift, squares, strip = call(
         squares_kernel, [], [HBM] * 3,
-        [vmem((rows, half), BF16), vmem((1, rows), jnp.int32), vmem((1, 2 * half), F32), vmem((1, rows), F32)],
+        [vmem((rows, half), BF16), vmem((1, rows), jnp.int32), vmem((1, 2 * half), F32), vmem((1, rows), F32),
+         vmem((cut, half), BF16)],
         [in_hbm(clean_tokens), in_hbm(masked), in_hbm(time_shift[None])], 2 * rows * half, rows * half * 2,
         [pltpu.SemaphoreType.DMA((3,))],
     )
     other_squares = cross_x(squares)
-    strip, = call(strip_kernel, [info], [WHOLE], [vmem((cut, half), BF16)], [x], 0, rows * half)
     near = cross_x(strip)
     stats = [squares, other_squares, mask]
     vectors = [norm_gain[None], mask_embed[None], shift]

time: 71.5 us -> 69.6 us (0.973)
  the two profiles are of different devices: /device:TPU:25 before, /device:TPU:0 now
where the time goes in v6:
time: 69.6 us; the launch traced here: 69.3 us
  Pallas kernels  26.8 us (39%)
  waiting for transfers between devices  20.9 us (30%)
  starting transfers between devices  18.5 us (27%)
  between operations  1.64 us (2%)
  local copies, waits for them, and re-layouts  1.44 us (2%)
    pallas_call x12, Pallas kernels, call(): pl.pallas_call(kernel, grid_spec=pltpu.PrefetchScalarGridSpec(num_scalar_...  26.8 us
    ppermute x3, starting transfers between devices, on_device(): lax.ppermute(v, 'ctx', [(i, i + 2) for i in range(ctx - 2)])  11.4 us
    ppermute x3, waiting for transfers between devices, on_device(): lax.ppermute(v, 'ctx', [(i, i + 2) for i in range(ctx - 2)])  7.63 us
    ppermute x4, waiting for transfers between devices, on_device(): across = lambda v: lax.ppermute(v, 'ctx', [(i, i ^ 1) for i in range(ctx)])  6.64 us
    ppermute x2, waiting for transfers between devices, on_device(): cross_x = lambda v: lax.ppermute(v, 'copy', pair)  4.26 us
    ppermute x4, starting transfers between devices, on_device(): across = lambda v: lax.ppermute(v, 'ctx', [(i, i ^ 1) for i in range(ctx)])  3.21 us
    ppermute x2, starting transfers between devices, on_device(): cross_x = lambda v: lax.ppermute(v, 'copy', pair)  3.08 us
    ppermute x4, waiting for transfers between devices, on_device(): cross_core = lambda v: lax.ppermute(v, 'tp', pair)  2.33 us
  transfers between devices with their start and end apart: 13, of which 7 were waited for; matrix products, arithmetic and copies ran while one was open for 2% of the time, Pallas kernels for 29%

profile of v6, /device:TPU:0, one launch (start us, length us, event | category | flops | bytes accessed | tf_op | source)
XLA Modules:
  0.0 69.3 jit_solution(8067748165347531416)
XLA Ops:
  0.6 1.6 %shard_map.140 = (bf16[256,2048]{1,0:T(8,128)(2,1)S(1)}, s32[1,256]{1,0:T(1,128)S(1)}, f32[1,4096]{1,0:T(1,128)S(1)}, f32[1,256]{1,0:T(1,128)S(1)}, bf16[128,2048]{1,0:T(8,128)(2,1)S(1)}) custom-call(bf16[256,2048]{1,0:T(8,128)(2,1)} %x_hbm.1, s32[1,256]{1,0:T(1,128)} %mask_hbm.1, f32[1,4096]{1,0:T(1,128)} %bitcast.14), custom_call_target="tpu_custom_call" | custom-call | flops 1048576 | bytes 1048576 | tf_op jit(solution)/shard_map/pallas_call | solution.py:299
  2.2 3.0 %collective-permute-start.1 = (f32[1,256]{1,0:T(1,128)S(1)}, f32[1,256]{1,0:T(1,128)S(1)}, u32[]{:S(2)}, u32[]{:S(2)}) collective-permute-start(f32[1,256]{1,0:T(1,128)S(1)} %get-tuple-element.39.own_ref), channel_id=1, source_target_pairs={{0,16},{16,0},{1,17},{17,1},{2,18},{18,2},{3,19},{19,3},{4,20},{20... | collective-permute-start | bytes 3080 | tf_op jit(solution)/shard_map/ppermute | solution.py:333
  6.0 0.7 %broadcast_in_dim.19.gain_ref = bf16[1,4096]{1,0:T(2,128)(2,1)S(1)} reshape(bf16[4096]{0:T(1024)(128)(2,1)} %param.14) | data formatting | bytes 16384 | tf_op jit(solution)/shard_map/broadcast_in_dim | solution.py:353
  6.7 0.7 %broadcast_in_dim.20.embed_ref = bf16[1,4096]{1,0:T(2,128)(2,1)S(1)} reshape(bf16[4096]{0:T(1024)(128)(2,1)} %param.15) | data formatting | bytes 16384 | tf_op jit(solution)/shard_map/broadcast_in_dim | solution.py:353
  7.5 6.9 %shard_map.141 = (f32[512,1024]{1,0:T(8,128)S(1)}, f32[512,256]{1,0:T(8,128)S(1)}, f32[512,256]{1,0:T(8,128)S(1)}, bf16[2048,1024]{1,0:T(8,128)(2,1)S(1)}, bf16[...) custom-call(s32[4]{0:T(128)S(1)} %pad_add_fusion.info, ...), custom_call_target="tpu_custom_call" | custom-call | flops 25769803776 | bytes 12582912 | tf_op jit(solution)/shard_map/pallas_call | solution.py:299
  14.3 4.3 %collective-permute-done.near_ref = bf16[128,2048]{1,0:T(8,128)(2,1)S(1)} collective-permute-done((bf16[128,2048]{1,0:T(8,128)(2,1)S(1)}, bf16[128,2048]{1,0:T(8,128)(2,1)S(1)}, u32[]{:S(2)}, u32[]{:S(2)}) %collective-permute-start) | collective-permute-done | bytes 524320 | tf_op jit(solution)/shard_map/ppermute | solution.py:333
  18.6 1.9 %collective-permute-done.2.far_ref = bf16[128,2048]{1,0:T(8,128)(2,1)S(1)} collective-permute-done((bf16[128,2048]{1,0:T(8,128)(2,1)S(1)}, bf16[128,2048]{1,0:T(8,128)(2,1)S(1)}, u32[]{:S(2)}, u32[]{:S(2)}) %collective-permute-start.2) | collective-permute-done | bytes 524320 | tf_op jit(solution)/shard_map/ppermute | solution.py:334
  20.5 1.5 %shard_map.142.kv_ref = bf16[256,512]{1,0:T(8,128)(2,1)S(1)} custom-call(s32[4]{0:T(128)S(1)} %pad_add_fusion.info, bf16[128,2048]{1,0:T(8,128)(2,1)S(1)} %collective-permute-done.near_ref, bf16[128,2048]{1,0:T(8,128)(2,1)S(1)} %collective-permute-done.2.far_ref, f32[1,256]{1,0:T(1,128)S(1)} %get-tuple-element.39.own_ref, ...), custom_call_target="tpu_custom_call" | custom-call | flops 536870912 | bytes 2097152 | tf_op jit(solution)/shard_map/pallas_call | solution.py:299
  22.2 3.5 %collective-permute-start.4 = (bf16[256,512]{1,0:T(8,128)(2,1)S(1)}, bf16[256,512]{1,0:T(8,128)(2,1)S(1)}, u32[]{:S(2)}, u32[]{:S(2)}) collective-permute-start(bf16[256,512]{1,0:T(8,128)(2,1)S(1)} %shard_map.142.kv_ref), channel_id=1, source_target_pairs={{0,4},{2,6},{4,8},{6,10},{8,12},{10,14},{1,5},{3,7},{5,9},{7,11},{... | collective-permute-start | bytes 786440 | tf_op jit(solution)/shard_map/ppermute | solution.py:375
  25.7 1.6 %collective-permute-start.3 = (bf16[256,512]{1,0:T(8,128)(2,1)S(1)}, bf16[256,512]{1,0:T(8,128)(2,1)S(1)}, u32[]{:S(2)}, u32[]{:S(2)}) collective-permute-start(bf16[256,512]{1,0:T(8,128)(2,1)S(1)} %shard_map.142.kv_ref), channel_id=1, source_target_pairs={{0,2},{2,0},{4,6},{6,4},{8,10},{10,8},{12,14},{14,12},{1,3},{3,1},... | collective-permute-start | bytes 786440 | tf_op jit(solution)/shard_map/ppermute | solution.py:376
  27.3 3.9 %shard_map.143 = (bf16[512,1024]{1,0:T(8,128)(2,1)S(1)}, bf16[256,512]{1,0:T(8,128)(2,1)S(1)}) custom-call(s32[4]{0:T(128)S(1)} %pad_add_fusion.info, bf16[128,2048]{1,0:T(8,128)(2,1)S(1)} %collective-permute-done.near_ref, bf16[128,2048]{1,0:T(8,128)(2,1)S(1)} %collective-permute-done.2.far_ref, f32[1,256]{1,0:T(1,128)S(1)} %get-tuple-element.39.own_ref, ...), custom_call_target="tpu_custom_call" | custom-call | flops 3221225472 | bytes 6291456 | tf_op jit(solution)/shard_map/pallas_call | solution.py:299
  31.2 2.5 %shard_map.144 = (f32[512,1024]{1,0:T(8,128)S(1)}, f32[512,1024]{1,0:T(8,128)S(1)}) custom-call(s32[4]{0:T(128)S(1)} %pad_add_fusion.info, bf16[512,1024]{1,0:T(8,128)(2,1)S(1)} %get-tuple-element.50.q_ref, bf16[256,512]{1,0:T(8,128)(2,1)S(1)} %shard_map.142.kv_ref, bf16[256,512]{1,0:T(8,128)(2,1)S(1)} %get-tuple-element.51.self_ref), custom_call_target="tpu_custom_call" | custom-call | flops 805306368 | bytes 4194304 | tf_op jit(solution)/shard_map/pallas_call | solution.py:299
  33.7 3.5 %collective-permute-start.6 = (bf16[256,512]{1,0:T(8,128)(2,1)S(1)}, bf16[256,512]{1,0:T(8,128)(2,1)S(1)}, u32[]{:S(2)}, u32[]{:S(2)}) collective-permute-start(bf16[256,512]{1,0:T(8,128)(2,1)S(1)} %collective-permute-done.4.second_ref), channel_id=1, source_target_pairs={{0,4},{2,6},{4,8},{6,10},{8,12},{10,14},{1,5},{3,7},{5,9},{7,11},{... | collective-permute-start | bytes 786440 | tf_op jit(solution)/shard_map/ppermute | solution.py:375
  37.8 0.7 %shard_map.145 = (f32[512,1024]{1,0:T(8,128)S(1)}, f32[512,1024]{1,0:T(8,128)S(1)}) custom-call(s32[4]{0:T(128)S(1)} %pad_add_fusion.info, bf16[512,1024]{1,0:T(8,128)(2,1)S(1)} %get-tuple-element.50.q_ref, f32[512,1024]{1,0:T(8,128)S(1)} %get-tuple-element.52.num_in, ...), custom_call_target="tpu_custom_call", output_to_operand_aliasing={{0}: (2, {}), {1}: (3, {})} | custom-call | flops 1073741824 | bytes 4194304 | tf_op jit(solution)/shard_map/pallas_call | solution.py:299
  38.6 4.2 %collective-permute-done.6.second_ref = bf16[256,512]{1,0:T(8,128)(2,1)S(1)} collective-permute-done((bf16[256,512]{1,0:T(8,128)(2,1)S(1)}, bf16[256,512]{1,0:T(8,128)(2,1)S(1)}, u32[]{:S(2)}, u32[]{:S(2)}) %collective-permute-start.6) | collective-permute-done | bytes 262176 | tf_op jit(solution)/shard_map/ppermute | solution.py:375
  42.7 4.4 %collective-permute-start.8 = (bf16[256,512]{1,0:T(8,128)(2,1)S(1)}, bf16[256,512]{1,0:T(8,128)(2,1)S(1)}, u32[]{:S(2)}, u32[]{:S(2)}) collective-permute-start(bf16[256,512]{1,0:T(8,128)(2,1)S(1)} %collective-permute-done.6.second_ref), channel_id=1, source_target_pairs={{0,4},{2,6},{4,8},{6,10},{8,12},{10,14},{1,5},{3,7},{5,9},{7,11},{... | collective-permute-start | bytes 786440 | tf_op jit(solution)/shard_map/ppermute | solution.py:375
  48.3 3.5 %collective-permute-done.8.second_ref = bf16[256,512]{1,0:T(8,128)(2,1)S(1)} collective-permute-done((bf16[256,512]{1,0:T(8,128)(2,1)S(1)}, bf16[256,512]{1,0:T(8,128)(2,1)S(1)}, u32[]{:S(2)}, u32[]{:S(2)}) %collective-permute-start.8) | collective-permute-done | bytes 262176 | tf_op jit(solution)/shard_map/ppermute | solution.py:375
  52.2 3.4 %collective-permute-done.7.first_ref = bf16[256,512]{1,0:T(8,128)(2,1)S(1)} collective-permute-done((bf16[256,512]{1,0:T(8,128)(2,1)S(1)}, bf16[256,512]{1,0:T(8,128)(2,1)S(1)}, u32[]{:S(2)}, u32[]{:S(2)}) %collective-permute-start.7) | collective-permute-done | bytes 262176 | tf_op jit(solution)/shard_map/ppermute | solution.py:376
  55.7 0.8 %shard_map.147 = (f32[512,1024]{1,0:T(8,128)S(1)}, f32[512,1024]{1,0:T(8,128)S(1)}) custom-call(s32[4]{0:T(128)S(1)} %pad_add_fusion.info, bf16[512,1024]{1,0:T(8,128)(2,1)S(1)} %get-tuple-element.50.q_ref, f32[512,1024]{1,0:T(8,128)S(1)} %get-tuple-element.58.num_in, ...), custom_call_target="tpu_custom_call", output_to_operand_aliasing={{0}: (2, {}), {1}: (3, {})} | custom-call | flops 1073741824 | bytes 4194304 | tf_op jit(solution)/shard_map/pallas_call | solution.py:299
  56.5 3.2 %collective-permute-done.9.piece_ref = bf16[256,512]{1,0:T(8,128)(2,1)S(1)} collective-permute-done((bf16[256,512]{1,0:T(8,128)(2,1)S(1)}, bf16[256,512]{1,0:T(8,128)(2,1)S(1)}, u32[]{:S(2)}, u32[]{:S(2)}) %collective-permute-start.9) | collective-permute-done | bytes 262176 | tf_op jit(solution)/shard_map/ppermute | solution.py:376
  59.6 0.9 %shard_map.148 = (f32[512,1024]{1,0:T(8,128)S(1)}, f32[512,1024]{1,0:T(8,128)S(1)}, bf16[512,512]{1,0:T(8,128)(2,1)S(1)}) custom-call(s32[4]{0:T(128)S(1)} %pad_add_fusion.info, bf16[512,1024]{1,0:T(8,128)(2,1)S(1)} %get-tuple-element.50.q_ref, f32[512,1024]{1,0:T(8,128)S(1)} %get-tuple-element.61.num_in, ...), custom_call_target="tpu_custom_call", output_to_operand_aliasing={{0}: (2, {}), {1}: (3, {})} | custom-call | flops 268435456 | bytes 4194304 | tf_op jit(solution)/shard_map/pallas_call | solution.py:299
  60.6 0.9 %shard_map.149 = (f32[512,1024]{1,0:T(8,128)S(1)}, f32[512,1024]{1,0:T(8,128)S(1)}, bf16[512,512]{1,0:T(8,128)(2,1)S(1)}) custom-call(s32[4]{0:T(128)S(1)} %pad_add_fusion.info, bf16[512,1024]{1,0:T(8,128)(2,1)S(1)} %get-tuple-element.50.q_ref, f32[512,1024]{1,0:T(8,128)S(1)} %get-tuple-element.63.num_in, ...), custom_call_target="tpu_custom_call", output_to_operand_aliasing={{0}: (2, {}), {1}: (3, {})} | custom-call | flops 268435456 | bytes 4194304 | tf_op jit(solution)/shard_map/pallas_call | solution.py:299
  62.5 4.0 %shard_map.150.mixed_ref = f32[512,2048]{1,0:T(8,128)S(1)} custom-call(s32[4]{0:T(128)S(1)} %pad_add_fusion.info, bf16[512,512]{1,0:T(8,128)(2,1)S(1)} %get-tuple-element.66.ga, bf16[512,512]{1,0:T(8,128)(2,1)S(1)} %get-tuple-element.65.gb, bf16[512,512]{1,0:T(8,128)(2,1)S(1)} %collective-permute-done.11.ha, bf16[1024,4096]{1,0:T(8,128)(2,1)S(1)} %bitcast.9, ...), custom_call_target="tpu_custom_call" | custom-call | flops 3221225472 | bytes 8388608 | tf_op jit(solution)/shard_map/pallas_call | solution.py:299
  66.5 2.6 %shard_map.151 = (bf16[256,2048]{1,0:T(8,128)(2,1)}, bf16[256,2048]{1,0:T(8,128)(2,1)}) custom-call(s32[4]{0:T(128)S(1)} %pad_add_fusion.info, s32[4]{0:T(128)S(1)} %bitcast.12, bf16[512,512]{1,0:T(8,128)(2,1)S(1)} %collective-permute-done.10.hb, f32[512,2048]{1,0:T(8,128)S(1)} %shard_map.150.mixed_ref, bf16[1024,2048]{1,0:T(8,128)(2,1)S(1)} %collective-permute-done.12.w_far), custom_call_target="tpu_custom_call" | custom-call | flops 1073741824 | bytes 4194304 | tf_op jit(solution)/shard_map/pallas_call | solution.py:299
  (28 shorter events, 3.6 us)
Async XLA Ops:
  2.2 5.2 %collective-permute-start.1 = (f32[1,256]{1,0:T(1,128)S(1)}, f32[1,256]{1,0:T(1,128)S(1)}, u32[]{:S(2)}, u32[]{:S(2)}) collective-permute-start(f32[1,256]{1,0:T(1,128)S(1)} %get-tuple-element.39.own_ref), channel_id=1, source_target_pairs={{0,16},{16,0},{1,17},{17,1},{2,18},{18,2},{3,19},{19,3},{4,20},{20... | collective-permute-start | bytes 3080 | tf_op jit(solution)/shard_map/ppermute | solution.py:333
  5.2 13.4 %collective-permute-start = (bf16[128,2048]{1,0:T(8,128)(2,1)S(1)}, bf16[128,2048]{1,0:T(8,128)(2,1)S(1)}, u32[]{:S(2)}, u32[]{:S(2)}) collective-permute-start(bf16[128,2048]{1,0:T(8,128)(2,1)S(1)} %get-tuple-element.37), channel_id=1, source_target_pairs={{0,16},{16,0},{1,17},{17,1},{2,18},{18,2},{3,19},{19,3},{4,20},{20... | collective-permute-start | bytes 1572872 | tf_op jit(solution)/shard_map/ppermute | solution.py:333
  7.5 13.1 %copy-start = (f32[128]{0:T(128)S(1)}, f32[128]{0:T(128)}, u32[]{:S(2)}) copy-start(f32[128]{0:T(128)} %param.22) | copy-start | bytes 1540
  18.6 1.9 %collective-permute-start.2 = (bf16[128,2048]{1,0:T(8,128)(2,1)S(1)}, bf16[128,2048]{1,0:T(8,128)(2,1)S(1)}, u32[]{:S(2)}, u32[]{:S(2)}) collective-permute-start(bf16[128,2048]{1,0:T(8,128)(2,1)S(1)} %collective-permute-done.near_ref), channel_id=1, source_target_pairs={{0,1},{1,0},{2,3},{3,2},{4,5},{5,4},{6,7},{7,6},{8,9},{9,8},{10,11... | collective-permute-start | bytes 1572872 | tf_op jit(solution)/shard_map/ppermute | solution.py:334
  20.5 6.8 %copy-start.2 = (f32[128]{0:T(128)S(1)}, f32[128]{0:T(128)}, u32[]{:S(2)}) copy-start(f32[128]{0:T(128)} %param.21) | copy-start | bytes 1540
  22.0 15.8 %collective-permute-start.12 = (bf16[1024,2048]{1,0:T(8,128)(2,1)S(1)}, bf16[1024,2048]{1,0:T(8,128)(2,1)S(1)}, u32[]{:S(2)}, u32[]{:S(2)}) collective-permute-start(bf16[1024,2048]{1,0:T(8,128)(2,1)S(1)} %get-tuple-element.68), channel_id=1, source_target_pairs={{0,1},{1,0},{2,3},{3,2},{4,5},{5,4},{6,7},{7,6},{8,9},{9,8},{10,11... | collective-permute-start | bytes 12582920 | tf_op jit(solution)/shard_map/ppermute | solution.py:334
  22.2 11.5 %collective-permute-start.4 = (bf16[256,512]{1,0:T(8,128)(2,1)S(1)}, bf16[256,512]{1,0:T(8,128)(2,1)S(1)}, u32[]{:S(2)}, u32[]{:S(2)}) collective-permute-start(bf16[256,512]{1,0:T(8,128)(2,1)S(1)} %shard_map.142.kv_ref), channel_id=1, source_target_pairs={{0,4},{2,6},{4,8},{6,10},{8,12},{10,14},{1,5},{3,7},{5,9},{7,11},{... | collective-permute-start | bytes 786440 | tf_op jit(solution)/shard_map/ppermute | solution.py:375
  25.7 12.1 %collective-permute-start.3 = (bf16[256,512]{1,0:T(8,128)(2,1)S(1)}, bf16[256,512]{1,0:T(8,128)(2,1)S(1)}, u32[]{:S(2)}, u32[]{:S(2)}) collective-permute-start(bf16[256,512]{1,0:T(8,128)(2,1)S(1)} %shard_map.142.kv_ref), channel_id=1, source_target_pairs={{0,2},{2,0},{4,6},{6,4},{8,10},{10,8},{12,14},{14,12},{1,3},{3,1},... | collective-permute-start | bytes 786440 | tf_op jit(solution)/shard_map/ppermute | solution.py:376
  33.7 9.0 %collective-permute-start.6 = (bf16[256,512]{1,0:T(8,128)(2,1)S(1)}, bf16[256,512]{1,0:T(8,128)(2,1)S(1)}, u32[]{:S(2)}, u32[]{:S(2)}) collective-permute-start(bf16[256,512]{1,0:T(8,128)(2,1)S(1)} %collective-permute-done.4.second_ref), channel_id=1, source_target_pairs={{0,4},{2,6},{4,8},{6,10},{8,12},{10,14},{1,5},{3,7},{5,9},{7,11},{... | collective-permute-start | bytes 786440 | tf_op jit(solution)/shard_map/ppermute | solution.py:375
  37.2 10.5 %collective-permute-start.5 = (bf16[256,512]{1,0:T(8,128)(2,1)S(1)}, bf16[256,512]{1,0:T(8,128)(2,1)S(1)}, u32[]{:S(2)}, u32[]{:S(2)}) collective-permute-start(bf16[256,512]{1,0:T(8,128)(2,1)S(1)} %collective-permute-done.4.second_ref), channel_id=1, source_target_pairs={{0,2},{2,0},{4,6},{6,4},{8,10},{10,8},{12,14},{14,12},{1,3},{3,1},... | collective-permute-start | bytes 786440 | tf_op jit(solution)/shard_map/ppermute | solution.py:376
  42.7 9.0 %collective-permute-start.8 = (bf16[256,512]{1,0:T(8,128)(2,1)S(1)}, bf16[256,512]{1,0:T(8,128)(2,1)S(1)}, u32[]{:S(2)}, u32[]{:S(2)}) collective-permute-start(bf16[256,512]{1,0:T(8,128)(2,1)S(1)} %collective-permute-done.6.second_ref), channel_id=1, source_target_pairs={{0,4},{2,6},{4,8},{6,10},{8,12},{10,14},{1,5},{3,7},{5,9},{7,11},{... | collective-permute-start | bytes 786440 | tf_op jit(solution)/shard_map/ppermute | solution.py:375
  47.1 8.6 %collective-permute-start.7 = (bf16[256,512]{1,0:T(8,128)(2,1)S(1)}, bf16[256,512]{1,0:T(8,128)(2,1)S(1)}, u32[]{:S(2)}, u32[]{:S(2)}) collective-permute-start(bf16[256,512]{1,0:T(8,128)(2,1)S(1)} %collective-permute-done.6.second_ref), channel_id=1, source_target_pairs={{0,2},{2,0},{4,6},{6,4},{8,10},{10,8},{12,14},{14,12},{1,3},{3,1},... | collective-permute-start | bytes 786440 | tf_op jit(solution)/shard_map/ppermute | solution.py:376
  51.7 7.9 %collective-permute-start.9 = (bf16[256,512]{1,0:T(8,128)(2,1)S(1)}, bf16[256,512]{1,0:T(8,128)(2,1)S(1)}, u32[]{:S(2)}, u32[]{:S(2)}) collective-permute-start(bf16[256,512]{1,0:T(8,128)(2,1)S(1)} %collective-permute-done.8.second_ref), channel_id=1, source_target_pairs={{0,2},{2,0},{4,6},{6,4},{8,10},{10,8},{12,14},{14,12},{1,3},{3,1},... | collective-permute-start | bytes 786440 | tf_op jit(solution)/shard_map/ppermute | solution.py:376
  55.7 6.9 %slice-start = ((s8[8388608]{0:T(1024)(128)(4,1)}), s8[4194304]{0:T(1024)(128)(4,1)S(1)}, s32[]{:S(2)}) async-start(s8[8388608]{0:T(1024)(128)(4,1)} %bitcast.8), calls=%async_computation | async-start | bytes 8388608
  59.6 2.9 %slice-start.1 = ((s8[8388608]{0:T(1024)(128)(4,1)}), s8[4194304]{0:T(1024)(128)(4,1)S(1)}, s32[]{:S(2)}) async-start(s8[8388608]{0:T(1024)(128)(4,1)} %bitcast.8), calls=%async_computation.1 | async-start | bytes 8388608
  60.5 2.0 %collective-permute-start.11 = (bf16[512,512]{1,0:T(8,128)(2,1)S(1)}, bf16[512,512]{1,0:T(8,128)(2,1)S(1)}, u32[]{:S(2)}, u32[]{:S(2)}) collective-permute-start(bf16[512,512]{1,0:T(8,128)(2,1)S(1)} %get-tuple-element.66.ga), channel_id=1, source_target_pairs={{0,1},{1,0},{2,3},{3,2},{4,5},{5,4},{6,7},{7,6},{8,9},{9,8},{10,11... | collective-permute-start | bytes 1572872 | tf_op jit(solution)/shard_map/ppermute | solution.py:334
  61.5 5.0 %copy-start.1 = (s32[1,4]{1,0:T(1,128)S(1)}, s32[1,4]{1,0:T(1,128)}, u32[]{:S(2)}) copy-start(s32[1,4]{1,0:T(1,128)} %param.24) | copy-start | bytes 52
  61.5 4.9 %collective-permute-start.10 = (bf16[512,512]{1,0:T(8,128)(2,1)S(1)}, bf16[512,512]{1,0:T(8,128)(2,1)S(1)}, u32[]{:S(2)}, u32[]{:S(2)}) collective-permute-start(bf16[512,512]{1,0:T(8,128)(2,1)S(1)} %get-tuple-element.65.gb), channel_id=1, source_target_pairs={{0,1},{1,0},{2,3},{3,2},{4,5},{5,4},{6,7},{7,6},{8,9},{9,8},{10,11... | collective-permute-start | bytes 1572872 | tf_op jit(solution)/shard_map/ppermute | solution.py:334

commit v7 on v6

--- a/solution.py
+++ b/solution.py
@@ -154,7 +154,7 @@
 
 def clean_kv_kernel(
     info, near_ref, far_ref, own_ref, other_ref, mask_ref, gain_ref, embed_ref,
-    wk_ref, wv_ref, pk_ref, pv_ref, kgain_ref, all_ref,
+    wk_ref, wv_ref, pk_ref, pv_ref, kgain_ref, all_ref, one_ref,
 ):
     rows = all_ref.shape[0]
     width = embed_ref.shape[1]
@@ -164,6 +164,8 @@
     k = pk_ref[:rows] + dot(clean, wk_ref[...])
     v = pv_ref[:rows] + dot(clean, wv_ref[...])
     kv_out(all_ref, k, v, kgain_ref[...])
+    cols = one_ref.shape[1]
+    one_ref[...] = all_ref[:, pl.ds(pl.multiple_of(info[0] * cols, 128), cols)]
 
 
 def other_half_kernel(
@@ -196,17 +198,18 @@
     return dot(e.astype(BF16), v), den
 
 
-def add_pieces(q_ref, num_ref, den_ref, kv_head, piece_refs):
-    rows, width = piece_refs[0].shape
-    group = q_ref.shape[1] // HD // (width // (2 * HD))
-    base = 2 * kv_head * HD
-    k = jnp.concatenate([ref[:, base : base + HD] for ref in piece_refs], axis=0)
-    v = jnp.concatenate([ref[:, base + HD : base + 2 * HD] for ref in piece_refs], axis=0)
-    for head in range(kv_head * group, (kv_head + 1) * group):
-        cols = slice(head * HD, (head + 1) * HD)
+def add_pieces(q_ref, num_ref, den_ref, base, heads, pieces):
+    k = jnp.concatenate([piece[:, :HD] for piece in pieces], axis=0)
+    v = jnp.concatenate([piece[:, HD:] for piece in pieces], axis=0)
+    for head in range(heads):
+        cols = pl.ds(base + head * HD, HD)
         num, den = terms(q_ref[:, cols], k, v, None)
         num_ref[:, cols] += num
         den_ref[:, cols] += den
+
+
+def head_base(info, which, width):
+    return pl.multiple_of((info[0] if which == 0 else 1 - info[0]) * width, 128)
 
 
 def attention_own_kernel(info, q_ref, kv_ref, self_ref, num_ref, den_ref):
@@ -233,52 +236,53 @@
                 den_ref[rows:, cols] += den[number * rows : (number + 1) * rows]
 
 
-def attention_pair_kernel(info, q_ref, num_in, den_in, first_ref, second_ref, num_ref, den_ref, *, step):
-    first_valid = jnp.bitwise_and(info[2], 1) == 1 if step == 1 else info[2] >= 2 * (step - 1)
-    second_valid = info[2] >= 2 * step
-    cases = (
-        (jnp.logical_and(first_valid, second_valid), [first_ref, second_ref]),
-        (jnp.logical_and(first_valid, jnp.logical_not(second_valid)), [first_ref]),
-        (jnp.logical_and(jnp.logical_not(first_valid), second_valid), [second_ref]),
-    )
-    for valid, refs in cases:
-        @pl.when(valid)
-        def _(refs=refs):
-            for kv_head in range(refs[0].shape[1] // (2 * HD)):
-                add_pieces(q_ref, num_ref, den_ref, kv_head, refs)
-
-
-def attention_last_kernel(info, q_ref, num_in, den_in, piece_ref, num_ref, den_ref, out_ref, *, step, kv_head):
-    valid = jnp.bitwise_and(info[2], 1) == 1 if step == 0 else info[2] >= 2 * step
-
-    @pl.when(valid)
-    def _():
-        add_pieces(q_ref, num_ref, den_ref, kv_head, [piece_ref])
-
-    width = out_ref.shape[1]
-    for head in range(width // HD):
-        cols = slice(kv_head * width + head * HD, kv_head * width + (head + 1) * HD)
-        total = jnp.sum(den_ref[:, cols], axis=1, keepdims=True)
-        out_ref[:, head * HD : (head + 1) * HD] = (num_ref[:, cols] / total).astype(BF16)
+def attention_kernel(info, q_ref, num_in, den_in, *refs, pieces, ends):
+    count = len(pieces)
+    num_ref, den_ref = refs[count : count + 2]
+    width = q_ref.shape[1] // 2
+    heads = width // HD
+    for bit in sorted({offset.bit_length() for offset, _ in pieces}):
+        group = [(which, ref) for (offset, which), ref in zip(pieces, refs) if offset.bit_length() == bit]
+
+        @pl.when(jnp.bitwise_and(info[2], 1 << (bit - 1)) != 0)
+        def _(group=group):
+            for which in range(2):
+                found = [ref[...] for one, ref in group if one == which]
+                if found:
+                    add_pieces(q_ref, num_ref, den_ref, head_base(info, which, width), heads, found)
+            found = [ref for one, ref in group if one == 2]
+            for kv_head in range(2 if found else 0):
+                cols = slice(2 * kv_head * HD, 2 * (kv_head + 1) * HD)
+                add_pieces(q_ref, num_ref, den_ref, kv_head * width, heads, [ref[:, cols] for ref in found])
+
+    for which, out_ref in zip(ends, refs[count + 2 :]):
+        base = head_base(info, which, width)
+        for head in range(heads):
+            cols = pl.ds(base + head * HD, HD)
+            total = jnp.sum(den_ref[:, cols], axis=1, keepdims=True)
+            out_ref[:, head * HD : (head + 1) * HD] = (num_ref[:, cols] / total).astype(BF16)
 
 
 def out_first_kernel(info, ga, gb, ha, w_out, w_far, mixed_ref, *, tile):
     part = ga.shape[1]
     total = mixed_ref.shape[1]
+    first = pl.ds(pl.multiple_of(info[0] * part, 128), part)
+    second = pl.ds(pl.multiple_of((1 - info[0]) * part, 128), part)
     for start in range(0, total, tile):
         mine = pl.ds(pl.multiple_of(info[1] * total + start, 128), tile)
         cols = slice(start, start + tile)
-        mixed = dot(ga[...], w_out[:part, mine]) + dot(gb[...], w_out[part:, mine])
-        mixed_ref[:, cols] = mixed + dot(ha[...], w_far[:part, cols])
+        mixed = dot(ga[...], w_out[first, mine]) + dot(gb[...], w_out[second, mine])
+        mixed_ref[:, cols] = mixed + dot(ha[...], w_far[first, cols])
 
 
 def out_last_kernel(info, live, hb, mixed_ref, w_far, clean_out, noisy_out, clean_ref, noisy_ref, sems, *, tile):
     rows, total = clean_ref.shape
     part = hb.shape[1]
+    second = pl.ds(pl.multiple_of((1 - info[0]) * part, 128), part)
     moves = []
     for start in range(0, total, tile):
         cols = slice(start, start + tile)
-        mixed = mixed_ref[:, cols] + dot(hb[...], w_far[part:, cols])
+        mixed = mixed_ref[:, cols] + dot(hb[...], w_far[second, cols])
         clean_ref[:, cols] = mixed[:rows].astype(BF16)
         for block in range(rows // BLK):
             part_rows = mixed[rows + block * BLK : rows + (block + 1) * BLK]
@@ -365,17 +369,17 @@
     near = after(near, pk)
     far = cross_core(near)
 
-    kv, = call(
-        clean_kv_kernel, [info], [WHOLE] * 12, [vmem((rows, 2 * kv_width), BF16)],
+    kv, kva = call(
+        clean_kv_kernel, [info], [WHOLE] * 12,
+        [vmem((rows, 2 * kv_width), BF16), vmem((rows, kv_width), BF16)],
         [near, far] + stats + vectors[:2] + weights[1:] + [pk, pv, kg],
         4 * rows * half * kv_width, half * 2 * kv_width * 2,
     )
 
-    steps = ctx // 2
-    along = lambda v: lax.ppermute(v, "ctx", [(i, i + 2) for i in range(ctx - 2)])
-    across = lambda v: lax.ppermute(v, "ctx", [(i, i ^ 1) for i in range(ctx)])
-    crossed = across(kv)
-    column = along(kv)
+    trade = lambda v, offset: lax.ppermute(v, "ctx", [(i, i ^ offset) for i in range(ctx)])
+    offsets = list(range(2, ctx, 2))
+    beside = trade(kv, 1)
+    column = {offset: trade(kva, offset) for offset in offsets}
     w_far = cross_core(after(w_send, kv))
     near = after(near, kv)
     q, own = call(
@@ -387,27 +391,41 @@
 
     acc = [vmem((2 * rows, heads_width), F32)] * 2
     unit = rows * rows * heads_width // HD
-    cost = lambda units: (4 * HD * unit * units, 8 * unit, (), unit * units)
+    cost = lambda units: (16 * HD * unit * units, 8 * unit, (), unit * units)
     in_place = {2: 0, 3: 1}
     num, den = call(attention_own_kernel, [info], [WHOLE] * 3, acc, [q, kv, own], *cost(3))
-    w_far = after(w_far, num)
-    for step in range(1, steps):
-        column = after(column, num)
-        before, crossed = crossed, across(column)
-        here, column = column, along(column) if step < steps - 1 else None
-        num, den = call(
-            functools.partial(attention_pair_kernel, step=step), [info], [WHOLE] * 5, acc,
-            [q, num, den, before, here], *cost(4), aliases=in_place,
+    first, later = offsets[0], offsets[1:]
+
+    def attend(num, den, pieces, ends=()):
+        return call(
+            functools.partial(attention_kernel, pieces=tuple(key for key, _ in pieces), ends=ends), [info],
+            [WHOLE] * (3 + len(pieces)), acc + [vmem((2 * rows, part), BF16)] * len(ends),
+            [q, num, den] + [piece for _, piece in pieces], *cost(len(pieces)), aliases=in_place,
         )
-    attended = []
-    for kv_head in range(2):
-        num, den, result = call(
-            functools.partial(attention_last_kernel, step=steps - 1, kv_head=kv_head), [info], [WHOLE] * 4,
-            acc + [vmem((2 * rows, part), BF16)], [q, num, den, crossed], *cost(1), aliases=in_place,
-        )
-        attended.append((result, cross_core(result)))
-
-    (ga, ha), (gb, hb) = attended
+
+    column[first] = after(column[first], num, w_far)
+    over_x, over_y, corner = {}, {}, {}
+    over_x[first], over_y[first] = cross_x(column[first]), trade(column[first], 1)
+    num, den = attend(num, den, [((1, 2), beside), ((first, 0), column[first])])
+    corner[first] = cross_x(over_y[first])
+    for offset in later:
+        column[offset] = after(column[offset], num)
+        over_x[offset], over_y[offset] = cross_x(column[offset]), trade(column[offset], 1)
+    num, den = attend(
+        num, den,
+        [((first, 1), over_x[first]), ((first, 0), over_y[first])] + [((o, 0), column[o]) for o in later],
+    )
+    for number, offset in enumerate(later):
+        corner[offset] = trade(over_x[offset], 1) if number % 2 else cross_x(over_y[offset])
+    num, den, ga = attend(
+        num, den,
+        [((first, 1), corner[first])]
+        + [((o, 0), over_y[o]) for o in later] + [((o, 1), over_x[o]) for o in later], (0,),
+    )
+    ha = cross_core(ga)
+    num, den, gb = attend(num, den, [((o, 1), corner[o]) for o in later], (1,))
+    hb = cross_core(gb)
+
     tile = 512
     mixed, = call(
         functools.partial(out_first_kernel, tile=tile), [info], [WHOLE] * 5, [vmem((2 * rows, out_cols), F32)],

time: 69.6 us -> 66.5 us (0.955)
  the two profiles are of different devices: /device:TPU:0 before, /device:TPU:25 now
where the time goes in v7:
time: 66.5 us; the launch traced here: 66.3 us
  Pallas kernels  33.9 us (51%)
  starting transfers between devices  17.6 us (26%)
  waiting for transfers between devices  11.6 us (17%)
  between operations  1.64 us (2%)
  local copies, waits for them, and re-layouts  1.44 us (2%)
    pallas_call x11, Pallas kernels, call(): pl.pallas_call(kernel, grid_spec=pltpu.PrefetchScalarGridSpec(num_scalar_...  33.9 us
    ppermute x8, starting transfers between devices, on_device(): lax.ppermute(v, 'ctx', [(i, i ^ offset) for i in range(ctx)])  7.96 us
    ppermute x7, waiting for transfers between devices, on_device(): cross_x = lambda v: lax.ppermute(v, 'copy', pair)  7.84 us
    ppermute x4, starting transfers between devices, on_device(): cross_core = lambda v: lax.ppermute(v, 'tp', pair)  5.56 us
    ppermute x7, starting transfers between devices, on_device(): cross_x = lambda v: lax.ppermute(v, 'copy', pair)  4.11 us
    ppermute x8, waiting for transfers between devices, on_device(): lax.ppermute(v, 'ctx', [(i, i ^ offset) for i in range(ctx)])  2.18 us
    ppermute x4, waiting for transfers between devices, on_device(): cross_core = lambda v: lax.ppermute(v, 'tp', pair)  1.54 us
    broadcast_in_dim x2, local copies, waits for them, and re-layouts, on_device(): vectors = [norm_gain[None], mask_embed[None], shift]  1.42 us
  transfers between devices with their start and end apart: 19, of which 7 were waited for; matrix products, arithmetic and copies ran while one was open for 2% of the time, Pallas kernels for 43%

profile of v7, /device:TPU:25, one launch (start us, length us, event | category | flops | bytes accessed | tf_op | source)
XLA Modules:
  0.0 66.3 jit_solution(14339692469464227098)
XLA Ops:
  0.6 1.6 %shard_map.140 = (bf16[256,2048]{1,0:T(8,128)(2,1)S(1)}, s32[1,256]{1,0:T(1,128)S(1)}, f32[1,4096]{1,0:T(1,128)S(1)}, f32[1,256]{1,0:T(1,128)S(1)}, bf16[128,2048]{1,0:T(8,128)(2,1)S(1)}) custom-call(bf16[256,2048]{1,0:T(8,128)(2,1)} %x_hbm.1, s32[1,256]{1,0:T(1,128)} %mask_hbm.1, f32[1,4096]{1,0:T(1,128)} %bitcast.14), custom_call_target="tpu_custom_call" | custom-call | flops 1048576 | bytes 1048576 | tf_op jit(solution)/shard_map/pallas_call | solution.py:303
  2.2 1.3 %collective-permute-start.1 = (f32[1,256]{1,0:T(1,128)S(1)}, f32[1,256]{1,0:T(1,128)S(1)}, u32[]{:S(2)}, u32[]{:S(2)}) collective-permute-start(f32[1,256]{1,0:T(1,128)S(1)} %get-tuple-element.38.own_ref), channel_id=1, source_target_pairs={{0,16},{16,0},{1,17},{17,1},{2,18},{18,2},{3,19},{19,3},{4,20},{20... | collective-permute-start | bytes 3080 | tf_op jit(solution)/shard_map/ppermute | solution.py:337
  5.9 6.9 %shard_map.141 = (f32[512,1024]{1,0:T(8,128)S(1)}, f32[512,256]{1,0:T(8,128)S(1)}, f32[512,256]{1,0:T(8,128)S(1)}, bf16[2048,1024]{1,0:T(8,128)(2,1)S(1)}, bf16[...) custom-call(s32[4]{0:T(128)S(1)} %pad_add_fusion.info, ...), custom_call_target="tpu_custom_call" | custom-call | flops 25769803776 | bytes 12582912 | tf_op jit(solution)/shard_map/pallas_call | solution.py:303
  12.8 3.2 %collective-permute-done.near_ref = bf16[128,2048]{1,0:T(8,128)(2,1)S(1)} collective-permute-done((bf16[128,2048]{1,0:T(8,128)(2,1)S(1)}, bf16[128,2048]{1,0:T(8,128)(2,1)S(1)}, u32[]{:S(2)}, u32[]{:S(2)}) %collective-permute-start) | collective-permute-done | bytes 524320 | tf_op jit(solution)/shard_map/ppermute | solution.py:337
  16.0 1.9 %collective-permute-start.2 = (bf16[128,2048]{1,0:T(8,128)(2,1)S(1)}, bf16[128,2048]{1,0:T(8,128)(2,1)S(1)}, u32[]{:S(2)}, u32[]{:S(2)}) collective-permute-start(bf16[128,2048]{1,0:T(8,128)(2,1)S(1)} %collective-permute-done.near_ref), channel_id=1, source_target_pairs={{0,1},{1,0},{2,3},{3,2},{4,5},{5,4},{6,7},{7,6},{8,9},{9,8},{10,11... | collective-permute-start | bytes 1572872 | tf_op jit(solution)/shard_map/ppermute | solution.py:338
  17.8 1.5 %collective-permute-done.2.far_ref = bf16[128,2048]{1,0:T(8,128)(2,1)S(1)} collective-permute-done((bf16[128,2048]{1,0:T(8,128)(2,1)S(1)}, bf16[128,2048]{1,0:T(8,128)(2,1)S(1)}, u32[]{:S(2)}, u32[]{:S(2)}) %collective-permute-start.2) | collective-permute-done | bytes 524320 | tf_op jit(solution)/shard_map/ppermute | solution.py:338
  19.4 1.5 %shard_map.142 = (bf16[256,512]{1,0:T(8,128)(2,1)S(1)}, bf16[256,256]{1,0:T(8,128)(2,1)S(1)}) custom-call(s32[4]{0:T(128)S(1)} %pad_add_fusion.info, bf16[128,2048]{1,0:T(8,128)(2,1)S(1)} %collective-permute-done.near_ref, bf16[128,2048]{1,0:T(8,128)(2,1)S(1)} %collective-permute-done.2.far_ref, f32[1,256]{1,0:T(1,128)S(1)} %get-tuple-element.38.own_ref, ...), custom_call_target="tpu_custom_call" | custom-call | flops 536870912 | bytes 2097152 | tf_op jit(solution)/shard_map/pallas_call | solution.py:303
  21.3 1.3 %collective-permute-start.8 = (bf16[256,256]{1,0:T(8,128)(2,1)S(1)}, bf16[256,256]{1,0:T(8,128)(2,1)S(1)}, u32[]{:S(2)}, u32[]{:S(2)}) collective-permute-start(bf16[256,256]{1,0:T(8,128)(2,1)S(1)} %get-tuple-element.54), channel_id=1, source_target_pairs={{0,8},{2,10},{4,12},{6,14},{8,0},{10,2},{12,4},{14,6},{1,9},{3,11}... | collective-permute-start | bytes 393224 | tf_op jit(solution)/shard_map/ppermute | solution.py:379
  22.6 2.2 %collective-permute-start.4 = (bf16[256,256]{1,0:T(8,128)(2,1)S(1)}, bf16[256,256]{1,0:T(8,128)(2,1)S(1)}, u32[]{:S(2)}, u32[]{:S(2)}) collective-permute-start(bf16[256,256]{1,0:T(8,128)(2,1)S(1)} %get-tuple-element.54), channel_id=1, source_target_pairs={{0,4},{2,6},{4,0},{6,2},{8,12},{10,14},{12,8},{14,10},{1,5},{3,7},... | collective-permute-start | bytes 393224 | tf_op jit(solution)/shard_map/ppermute | solution.py:379
  24.8 1.2 %collective-permute-start.3 = (bf16[256,512]{1,0:T(8,128)(2,1)S(1)}, bf16[256,512]{1,0:T(8,128)(2,1)S(1)}, u32[]{:S(2)}, u32[]{:S(2)}) collective-permute-start(bf16[256,512]{1,0:T(8,128)(2,1)S(1)} %get-tuple-element.46.kv_ref), channel_id=1, source_target_pairs={{0,2},{2,0},{4,6},{6,4},{8,10},{10,8},{12,14},{14,12},{1,3},{3,1},... | collective-permute-start | bytes 786440 | tf_op jit(solution)/shard_map/ppermute | solution.py:379
  26.1 3.9 %shard_map.143 = (bf16[512,1024]{1,0:T(8,128)(2,1)S(1)}, bf16[256,512]{1,0:T(8,128)(2,1)S(1)}) custom-call(s32[4]{0:T(128)S(1)} %pad_add_fusion.info, bf16[128,2048]{1,0:T(8,128)(2,1)S(1)} %collective-permute-done.near_ref, bf16[128,2048]{1,0:T(8,128)(2,1)S(1)} %collective-permute-done.2.far_ref, f32[1,256]{1,0:T(1,128)S(1)} %get-tuple-element.38.own_ref, ...), custom_call_target="tpu_custom_call" | custom-call | flops 3221225472 | bytes 6291456 | tf_op jit(solution)/shard_map/pallas_call | solution.py:303
  30.0 2.5 %shard_map.144 = (f32[512,1024]{1,0:T(8,128)S(1)}, f32[512,1024]{1,0:T(8,128)S(1)}) custom-call(s32[4]{0:T(128)S(1)} %pad_add_fusion.info, bf16[512,1024]{1,0:T(8,128)(2,1)S(1)} %get-tuple-element.50.q_ref, bf16[256,512]{1,0:T(8,128)(2,1)S(1)} %get-tuple-element.46.kv_ref, bf16[256,512]{1,0:T(8,128)(2,1)S(1)} %get-tuple-element.51.self_ref), custom_call_target="tpu_custom_call" | custom-call | flops 3221225472 | bytes 4194304 | tf_op jit(solution)/shard_map/pallas_call | solution.py:303
  32.5 1.6 %shard_map.145 = (f32[512,1024]{1,0:T(8,128)S(1)}, f32[512,1024]{1,0:T(8,128)S(1)}) custom-call(s32[4]{0:T(128)S(1)} %pad_add_fusion.info, bf16[512,1024]{1,0:T(8,128)(2,1)S(1)} %get-tuple-element.50.q_ref, f32[512,1024]{1,0:T(8,128)S(1)} %get-tuple-element.52.num_in, ...), custom_call_target="tpu_custom_call", output_to_operand_aliasing={{0}: (2, {}), {1}: (3, {})} | custom-call | flops 2147483648 | bytes 4194304 | tf_op jit(solution)/shard_map/pallas_call | solution.py:303
  34.6 1.3 %collective-permute-start.11 = (bf16[256,256]{1,0:T(8,128)(2,1)S(1)}, bf16[256,256]{1,0:T(8,128)(2,1)S(1)}, u32[]{:S(2)}, u32[]{:S(2)}) collective-permute-start(bf16[256,256]{1,0:T(8,128)(2,1)S(1)} %collective-permute-done.8.refs_2_), channel_id=1, source_target_pairs={{0,2},{2,0},{4,6},{6,4},{8,10},{10,8},{12,14},{14,12},{1,3},{3,1},... | collective-permute-start | bytes 393224 | tf_op jit(solution)/shard_map/ppermute | solution.py:379
  36.3 1.2 %collective-permute-start.6 = (bf16[256,256]{1,0:T(8,128)(2,1)S(1)}, bf16[256,256]{1,0:T(8,128)(2,1)S(1)}, u32[]{:S(2)}, u32[]{:S(2)}) collective-permute-start(bf16[256,256]{1,0:T(8,128)(2,1)S(1)} %collective-permute-done.4.refs_1_), channel_id=1, source_target_pairs={{0,16},{16,0},{1,17},{17,1},{2,18},{18,2},{3,19},{19,3},{4,20},{20... | collective-permute-start | bytes 393224 | tf_op jit(solution)/shard_map/ppermute | solution.py:337
  38.4 1.3 %collective-permute-start.12 = (bf16[256,256]{1,0:T(8,128)(2,1)S(1)}, bf16[256,256]{1,0:T(8,128)(2,1)S(1)}, u32[]{:S(2)}, u32[]{:S(2)}) collective-permute-start(bf16[256,256]{1,0:T(8,128)(2,1)S(1)} %collective-permute-done.9.refs_3_), channel_id=1, source_target_pairs={{0,2},{2,0},{4,6},{6,4},{8,10},{10,8},{12,14},{14,12},{1,3},{3,1},... | collective-permute-start | bytes 393224 | tf_op jit(solution)/shard_map/ppermute | solution.py:379
  40.3 1.1 %collective-permute-done.7.refs_1_ = bf16[256,256]{1,0:T(8,128)(2,1)S(1)} collective-permute-done((bf16[256,256]{1,0:T(8,128)(2,1)S(1)}, bf16[256,256]{1,0:T(8,128)(2,1)S(1)}, u32[]{:S(2)}, u32[]{:S(2)}) %collective-permute-start.7) | collective-permute-done | bytes 131104 | tf_op jit(solution)/shard_map/ppermute | solution.py:379
  42.3 3.2 %shard_map.146 = (f32[512,1024]{1,0:T(8,128)S(1)}, f32[512,1024]{1,0:T(8,128)S(1)}) custom-call(s32[4]{0:T(128)S(1)} %pad_add_fusion.info, bf16[512,1024]{1,0:T(8,128)(2,1)S(1)} %get-tuple-element.50.q_ref, f32[512,1024]{1,0:T(8,128)S(1)} %get-tuple-element.58.num_in, ...), custom_call_target="tpu_custom_call", output_to_operand_aliasing={{0}: (2, {}), {1}: (3, {})} | custom-call | flops 4294967296 | bytes 4194304 | tf_op jit(solution)/shard_map/pallas_call | solution.py:303
  45.5 4.4 %collective-permute-done.10.refs_0_ = bf16[256,256]{1,0:T(8,128)(2,1)S(1)} collective-permute-done((bf16[256,256]{1,0:T(8,128)(2,1)S(1)}, bf16[256,256]{1,0:T(8,128)(2,1)S(1)}, u32[]{:S(2)}, u32[]{:S(2)}) %collective-permute-start.10) | collective-permute-done | bytes 131104 | tf_op jit(solution)/shard_map/ppermute | solution.py:337
  49.9 4.1 %shard_map.147 = (f32[512,1024]{1,0:T(8,128)S(1)}, f32[512,1024]{1,0:T(8,128)S(1)}, bf16[512,512]{1,0:T(8,128)(2,1)S(1)}) custom-call(s32[4]{0:T(128)S(1)} %pad_add_fusion.info, bf16[512,1024]{1,0:T(8,128)(2,1)S(1)} %get-tuple-element.50.q_ref, f32[512,1024]{1,0:T(8,128)S(1)} %get-tuple-element.62.num_in, ...), custom_call_target="tpu_custom_call", output_to_operand_aliasing={{0}: (2, {}), {1}: (3, {})} | custom-call | flops 5368709120 | bytes 4194304 | tf_op jit(solution)/shard_map/pallas_call | solution.py:303
  54.0 3.2 %collective-permute-start.18 = (bf16[512,512]{1,0:T(8,128)(2,1)S(1)}, bf16[512,512]{1,0:T(8,128)(2,1)S(1)}, u32[]{:S(2)}, u32[]{:S(2)}) collective-permute-start(bf16[512,512]{1,0:T(8,128)(2,1)S(1)} %get-tuple-element.67.ga), channel_id=1, source_target_pairs={{0,1},{1,0},{2,3},{3,2},{4,5},{5,4},{6,7},{7,6},{8,9},{9,8},{10,11... | collective-permute-start | bytes 1572872 | tf_op jit(solution)/shard_map/ppermute | solution.py:338
  57.2 2.2 %shard_map.148 = (f32[512,1024]{1,0:T(8,128)S(1)}, f32[512,1024]{1,0:T(8,128)S(1)}, bf16[512,512]{1,0:T(8,128)(2,1)S(1)}) custom-call(s32[4]{0:T(128)S(1)} %pad_add_fusion.info, bf16[512,1024]{1,0:T(8,128)(2,1)S(1)} %get-tuple-element.50.q_ref, f32[512,1024]{1,0:T(8,128)S(1)} %get-tuple-element.64.num_in, ...), custom_call_target="tpu_custom_call", output_to_operand_aliasing={{0}: (2, {}), {1}: (3, {})} | custom-call | flops 2147483648 | bytes 4194304 | tf_op jit(solution)/shard_map/pallas_call | solution.py:303
  59.5 4.0 %shard_map.149.mixed_ref = f32[512,2048]{1,0:T(8,128)S(1)} custom-call(s32[4]{0:T(128)S(1)} %pad_add_fusion.info, bf16[512,512]{1,0:T(8,128)(2,1)S(1)} %get-tuple-element.67.ga, bf16[512,512]{1,0:T(8,128)(2,1)S(1)} %get-tuple-element.66.gb, bf16[512,512]{1,0:T(8,128)(2,1)S(1)} %collective-permute-done.18.ha, bf16[1024,4096]{1,0:T(8,128)(2,1)S(1)} %bitcast.9, ...), custom_call_target="tpu_custom_call" | custom-call | flops 3221225472 | bytes 8388608 | tf_op jit(solution)/shard_map/pallas_call | solution.py:303
  63.5 2.6 %shard_map.150 = (bf16[256,2048]{1,0:T(8,128)(2,1)}, bf16[256,2048]{1,0:T(8,128)(2,1)}) custom-call(s32[4]{0:T(128)S(1)} %pad_add_fusion.info, s32[4]{0:T(128)S(1)} %bitcast.12, bf16[512,512]{1,0:T(8,128)(2,1)S(1)} %collective-permute-done.17.hb, f32[512,2048]{1,0:T(8,128)S(1)} %shard_map.149.mixed_ref, bf16[1024,2048]{1,0:T(8,128)(2,1)S(1)} %collective-permute-done.5.w_far), custom_call_target="tpu_custom_call" | custom-call | flops 1073741824 | bytes 4194304 | tf_op jit(solution)/shard_map/pallas_call | solution.py:303
  (39 shorter events, 5.6 us)
Async XLA Ops:
  2.2 3.7 %collective-permute-start.1 = (f32[1,256]{1,0:T(1,128)S(1)}, f32[1,256]{1,0:T(1,128)S(1)}, u32[]{:S(2)}, u32[]{:S(2)}) collective-permute-start(f32[1,256]{1,0:T(1,128)S(1)} %get-tuple-element.38.own_ref), channel_id=1, source_target_pairs={{0,16},{16,0},{1,17},{17,1},{2,18},{18,2},{3,19},{19,3},{4,20},{20... | collective-permute-start | bytes 3080 | tf_op jit(solution)/shard_map/ppermute | solution.py:337
  3.5 12.5 %collective-permute-start = (bf16[128,2048]{1,0:T(8,128)(2,1)S(1)}, bf16[128,2048]{1,0:T(8,128)(2,1)S(1)}, u32[]{:S(2)}, u32[]{:S(2)}) collective-permute-start(bf16[128,2048]{1,0:T(8,128)(2,1)S(1)} %get-tuple-element.36), channel_id=1, source_target_pairs={{0,16},{16,0},{1,17},{17,1},{2,18},{18,2},{3,19},{19,3},{4,20},{20... | collective-permute-start | bytes 1572872 | tf_op jit(solution)/shard_map/ppermute | solution.py:337
  5.9 13.5 %copy-start = (f32[128]{0:T(128)S(1)}, f32[128]{0:T(128)}, u32[]{:S(2)}) copy-start(f32[128]{0:T(128)} %param.22) | copy-start | bytes 1540
  16.0 3.4 %collective-permute-start.2 = (bf16[128,2048]{1,0:T(8,128)(2,1)S(1)}, bf16[128,2048]{1,0:T(8,128)(2,1)S(1)}, u32[]{:S(2)}, u32[]{:S(2)}) collective-permute-start(bf16[128,2048]{1,0:T(8,128)(2,1)S(1)} %collective-permute-done.near_ref), channel_id=1, source_target_pairs={{0,1},{1,0},{2,3},{3,2},{4,5},{5,4},{6,7},{7,6},{8,9},{9,8},{10,11... | collective-permute-start | bytes 1572872 | tf_op jit(solution)/shard_map/ppermute | solution.py:338
  19.4 6.7 %copy-start.2 = (f32[128]{0:T(128)S(1)}, f32[128]{0:T(128)}, u32[]{:S(2)}) copy-start(f32[128]{0:T(128)} %param.21) | copy-start | bytes 1540
  20.9 11.6 %collective-permute-start.5 = (bf16[1024,2048]{1,0:T(8,128)(2,1)S(1)}, bf16[1024,2048]{1,0:T(8,128)(2,1)S(1)}, u32[]{:S(2)}, u32[]{:S(2)}) collective-permute-start(bf16[1024,2048]{1,0:T(8,128)(2,1)S(1)} %get-tuple-element.56), channel_id=1, source_target_pairs={{0,1},{1,0},{2,3},{3,2},{4,5},{5,4},{6,7},{7,6},{8,9},{9,8},{10,11... | collective-permute-start | bytes 12582920 | tf_op jit(solution)/shard_map/ppermute | solution.py:338
  21.3 12.8 %collective-permute-start.9 = (bf16[256,256]{1,0:T(8,128)(2,1)S(1)}, bf16[256,256]{1,0:T(8,128)(2,1)S(1)}, u32[]{:S(2)}, u32[]{:S(2)}) collective-permute-start(bf16[256,256]{1,0:T(8,128)(2,1)S(1)} %get-tuple-element.54), channel_id=1, source_target_pairs={{0,12},{2,14},{4,8},{6,10},{8,4},{10,6},{12,0},{14,2},{1,13},{3,15... | collective-permute-start | bytes 393224 | tf_op jit(solution)/shard_map/ppermute | solution.py:379
  21.3 13.3 %collective-permute-start.8 = (bf16[256,256]{1,0:T(8,128)(2,1)S(1)}, bf16[256,256]{1,0:T(8,128)(2,1)S(1)}, u32[]{:S(2)}, u32[]{:S(2)}) collective-permute-start(bf16[256,256]{1,0:T(8,128)(2,1)S(1)} %get-tuple-element.54), channel_id=1, source_target_pairs={{0,8},{2,10},{4,12},{6,14},{8,0},{10,2},{12,4},{14,6},{1,9},{3,11}... | collective-permute-start | bytes 393224 | tf_op jit(solution)/shard_map/ppermute | solution.py:379
  22.6 9.9 %collective-permute-start.4 = (bf16[256,256]{1,0:T(8,128)(2,1)S(1)}, bf16[256,256]{1,0:T(8,128)(2,1)S(1)}, u32[]{:S(2)}, u32[]{:S(2)}) collective-permute-start(bf16[256,256]{1,0:T(8,128)(2,1)S(1)} %get-tuple-element.54), channel_id=1, source_target_pairs={{0,4},{2,6},{4,0},{6,2},{8,12},{10,14},{12,8},{14,10},{1,5},{3,7},... | collective-permute-start | bytes 393224 | tf_op jit(solution)/shard_map/ppermute | solution.py:379
  24.8 7.7 %collective-permute-start.3 = (bf16[256,512]{1,0:T(8,128)(2,1)S(1)}, bf16[256,512]{1,0:T(8,128)(2,1)S(1)}, u32[]{:S(2)}, u32[]{:S(2)}) collective-permute-start(bf16[256,512]{1,0:T(8,128)(2,1)S(1)} %get-tuple-element.46.kv_ref), channel_id=1, source_target_pairs={{0,2},{2,0},{4,6},{6,4},{8,10},{10,8},{12,14},{14,12},{1,3},{3,1},... | collective-permute-start | bytes 786440 | tf_op jit(solution)/shard_map/ppermute | solution.py:379
  34.6 3.8 %collective-permute-start.11 = (bf16[256,256]{1,0:T(8,128)(2,1)S(1)}, bf16[256,256]{1,0:T(8,128)(2,1)S(1)}, u32[]{:S(2)}, u32[]{:S(2)}) collective-permute-start(bf16[256,256]{1,0:T(8,128)(2,1)S(1)} %collective-permute-done.8.refs_2_), channel_id=1, source_target_pairs={{0,2},{2,0},{4,6},{6,4},{8,10},{10,8},{12,14},{14,12},{1,3},{3,1},... | collective-permute-start | bytes 393224 | tf_op jit(solution)/shard_map/ppermute | solution.py:379
  35.9 4.1 %collective-permute-start.14 = (bf16[256,256]{1,0:T(8,128)(2,1)S(1)}, bf16[256,256]{1,0:T(8,128)(2,1)S(1)}, u32[]{:S(2)}, u32[]{:S(2)}) collective-permute-start(bf16[256,256]{1,0:T(8,128)(2,1)S(1)} %collective-permute-done.9.refs_3_), channel_id=1, source_target_pairs={{0,16},{16,0},{1,17},{17,1},{2,18},{18,2},{3,19},{19,3},{4,20},{20... | collective-permute-start | bytes 393224 | tf_op jit(solution)/shard_map/ppermute | solution.py:337
  36.2 5.2 %collective-permute-start.7 = (bf16[256,256]{1,0:T(8,128)(2,1)S(1)}, bf16[256,256]{1,0:T(8,128)(2,1)S(1)}, u32[]{:S(2)}, u32[]{:S(2)}) collective-permute-start(bf16[256,256]{1,0:T(8,128)(2,1)S(1)} %collective-permute-done.4.refs_1_), channel_id=1, source_target_pairs={{0,2},{2,0},{4,6},{6,4},{8,10},{10,8},{12,14},{14,12},{1,3},{3,1},... | collective-permute-start | bytes 393224 | tf_op jit(solution)/shard_map/ppermute | solution.py:379
  36.3 5.5 %collective-permute-start.6 = (bf16[256,256]{1,0:T(8,128)(2,1)S(1)}, bf16[256,256]{1,0:T(8,128)(2,1)S(1)}, u32[]{:S(2)}, u32[]{:S(2)}) collective-permute-start(bf16[256,256]{1,0:T(8,128)(2,1)S(1)} %collective-permute-done.4.refs_1_), channel_id=1, source_target_pairs={{0,16},{16,0},{1,17},{17,1},{2,18},{18,2},{3,19},{19,3},{4,20},{20... | collective-permute-start | bytes 393224 | tf_op jit(solution)/shard_map/ppermute | solution.py:337
  37.5 8.0 %collective-permute-start.13 = (bf16[256,256]{1,0:T(8,128)(2,1)S(1)}, bf16[256,256]{1,0:T(8,128)(2,1)S(1)}, u32[]{:S(2)}, u32[]{:S(2)}) collective-permute-start(bf16[256,256]{1,0:T(8,128)(2,1)S(1)} %collective-permute-done.8.refs_2_), channel_id=1, source_target_pairs={{0,16},{16,0},{1,17},{17,1},{2,18},{18,2},{3,19},{19,3},{4,20},{20... | collective-permute-start | bytes 393224 | tf_op jit(solution)/shard_map/ppermute | solution.py:337
  38.4 7.2 %collective-permute-start.12 = (bf16[256,256]{1,0:T(8,128)(2,1)S(1)}, bf16[256,256]{1,0:T(8,128)(2,1)S(1)}, u32[]{:S(2)}, u32[]{:S(2)}) collective-permute-start(bf16[256,256]{1,0:T(8,128)(2,1)S(1)} %collective-permute-done.9.refs_3_), channel_id=1, source_target_pairs={{0,2},{2,0},{4,6},{6,4},{8,10},{10,8},{12,14},{14,12},{1,3},{3,1},... | collective-permute-start | bytes 393224 | tf_op jit(solution)/shard_map/ppermute | solution.py:379
  40.0 17.2 %collective-permute-start.15 = (bf16[256,256]{1,0:T(8,128)(2,1)S(1)}, bf16[256,256]{1,0:T(8,128)(2,1)S(1)}, u32[]{:S(2)}, u32[]{:S(2)}) collective-permute-start(bf16[256,256]{1,0:T(8,128)(2,1)S(1)} %collective-permute-done.11.refs_1_), channel_id=1, source_target_pairs={{0,16},{16,0},{1,17},{17,1},{2,18},{18,2},{3,19},{19,3},{4,20},{20... | collective-permute-start | bytes 393224 | tf_op jit(solution)/shard_map/ppermute | solution.py:337
  41.4 15.8 %collective-permute-start.16 = (bf16[256,256]{1,0:T(8,128)(2,1)S(1)}, bf16[256,256]{1,0:T(8,128)(2,1)S(1)}, u32[]{:S(2)}, u32[]{:S(2)}) collective-permute-start(bf16[256,256]{1,0:T(8,128)(2,1)S(1)} %collective-permute-done.14.refs_4_), channel_id=1, source_target_pairs={{0,2},{2,0},{4,6},{6,4},{8,10},{10,8},{12,14},{14,12},{1,3},{3,1},... | collective-permute-start | bytes 393224 | tf_op jit(solution)/shard_map/ppermute | solution.py:379
  41.8 8.1 %collective-permute-start.10 = (bf16[256,256]{1,0:T(8,128)(2,1)S(1)}, bf16[256,256]{1,0:T(8,128)(2,1)S(1)}, u32[]{:S(2)}, u32[]{:S(2)}) collective-permute-start(bf16[256,256]{1,0:T(8,128)(2,1)S(1)} %collective-permute-done.7.refs_1_), channel_id=1, source_target_pairs={{0,16},{16,0},{1,17},{17,1},{2,18},{18,2},{3,19},{19,3},{4,20},{20... | collective-permute-start | bytes 393224 | tf_op jit(solution)/shard_map/ppermute | solution.py:337
  42.3 17.2 %slice-start = ((s8[8388608]{0:T(1024)(128)(4,1)}), s8[4194304]{0:T(1024)(128)(4,1)S(1)}, s32[]{:S(2)}) async-start(s8[8388608]{0:T(1024)(128)(4,1)} %bitcast.8), calls=%async_computation | async-start | bytes 8388608
  49.9 9.6 %slice-start.1 = ((s8[8388608]{0:T(1024)(128)(4,1)}), s8[4194304]{0:T(1024)(128)(4,1)S(1)}, s32[]{:S(2)}) async-start(s8[8388608]{0:T(1024)(128)(4,1)} %bitcast.8), calls=%async_computation.1 | async-start | bytes 8388608
  54.0 5.5 %collective-permute-start.18 = (bf16[512,512]{1,0:T(8,128)(2,1)S(1)}, bf16[512,512]{1,0:T(8,128)(2,1)S(1)}, u32[]{:S(2)}, u32[]{:S(2)}) collective-permute-start(bf16[512,512]{1,0:T(8,128)(2,1)S(1)} %get-tuple-element.67.ga), channel_id=1, source_target_pairs={{0,1},{1,0},{2,3},{3,2},{4,5},{5,4},{6,7},{7,6},{8,9},{9,8},{10,11... | collective-permute-start | bytes 1572872 | tf_op jit(solution)/shard_map/ppermute | solution.py:338
  59.4 4.1 %copy-start.1 = (s32[1,4]{1,0:T(1,128)S(1)}, s32[1,4]{1,0:T(1,128)}, u32[]{:S(2)}) copy-start(s32[1,4]{1,0:T(1,128)} %param.24) | copy-start | bytes 52
  59.4 4.1 %collective-permute-start.17 = (bf16[512,512]{1,0:T(8,128)(2,1)S(1)}, bf16[512,512]{1,0:T(8,128)(2,1)S(1)}, u32[]{:S(2)}, u32[]{:S(2)}) collective-permute-start(bf16[512,512]{1,0:T(8,128)(2,1)S(1)} %get-tuple-element.66.gb), channel_id=1, source_target_pairs={{0,1},{1,0},{2,3},{3,2},{4,5},{5,4},{6,7},{7,6},{8,9},{9,8},{10,11... | collective-permute-start | bytes 1572872 | tf_op jit(solution)/shard_map/ppermute | solution.py:338

commit v8 on v7

--- a/solution.py
+++ b/solution.py
@@ -236,7 +236,7 @@
                 den_ref[rows:, cols] += den[number * rows : (number + 1) * rows]
 
 
-def attention_kernel(info, q_ref, num_in, den_in, *refs, pieces, ends):
+def attention_kernel(info, q_ref, num_in, den_in, *refs, pieces):
     count = len(pieces)
     num_ref, den_ref = refs[count : count + 2]
     width = q_ref.shape[1] // 2
@@ -255,34 +255,26 @@
                 cols = slice(2 * kv_head * HD, 2 * (kv_head + 1) * HD)
                 add_pieces(q_ref, num_ref, den_ref, kv_head * width, heads, [ref[:, cols] for ref in found])
 
-    for which, out_ref in zip(ends, refs[count + 2 :]):
-        base = head_base(info, which, width)
-        for head in range(heads):
-            cols = pl.ds(base + head * HD, HD)
+    for out_ref in refs[count + 2 :]:
+        for start in range(0, q_ref.shape[1], HD):
+            cols = slice(start, start + HD)
             total = jnp.sum(den_ref[:, cols], axis=1, keepdims=True)
-            out_ref[:, head * HD : (head + 1) * HD] = (num_ref[:, cols] / total).astype(BF16)
-
-
-def out_first_kernel(info, ga, gb, ha, w_out, w_far, mixed_ref, *, tile):
-    part = ga.shape[1]
+            out_ref[:, cols] = (num_ref[:, cols] / total).astype(BF16)
+
+
+def out_first_kernel(info, heads, w_out, mixed_ref, *, tile):
     total = mixed_ref.shape[1]
-    first = pl.ds(pl.multiple_of(info[0] * part, 128), part)
-    second = pl.ds(pl.multiple_of((1 - info[0]) * part, 128), part)
     for start in range(0, total, tile):
         mine = pl.ds(pl.multiple_of(info[1] * total + start, 128), tile)
-        cols = slice(start, start + tile)
-        mixed = dot(ga[...], w_out[first, mine]) + dot(gb[...], w_out[second, mine])
-        mixed_ref[:, cols] = mixed + dot(ha[...], w_far[first, cols])
-
-
-def out_last_kernel(info, live, hb, mixed_ref, w_far, clean_out, noisy_out, clean_ref, noisy_ref, sems, *, tile):
+        mixed_ref[:, start : start + tile] = dot(heads[...], w_out[:, mine])
+
+
+def out_last_kernel(info, live, heads, mixed_ref, w_far, clean_out, noisy_out, clean_ref, noisy_ref, sems, *, tile):
     rows, total = clean_ref.shape
-    part = hb.shape[1]
-    second = pl.ds(pl.multiple_of((1 - info[0]) * part, 128), part)
     moves = []
     for start in range(0, total, tile):
         cols = slice(start, start + tile)
-        mixed = mixed_ref[:, cols] + dot(hb[...], w_far[second, cols])
+        mixed = mixed_ref[:, cols] + dot(heads[...], w_far[:, cols])
         clean_ref[:, cols] = mixed[:rows].astype(BF16)
         for block in range(rows // BLK):
             part_rows = mixed[rows + block * BLK : rows + (block + 1) * BLK]
@@ -329,7 +321,6 @@
     rows, half = clean_tokens.shape
     heads_width = w_query.shape[1]
     kv_width = w_key.shape[1]
-    part = heads_width // 2
     ctx = mesh.shape["ctx"]
     c, p, t = lax.axis_index("copy"), lax.axis_index("ctx"), lax.axis_index("tp")
     info = jnp.stack([c, t, p, timesteps[0]]).astype(jnp.int32)
@@ -377,9 +368,10 @@
     )
 
     trade = lambda v, offset: lax.ppermute(v, "ctx", [(i, i ^ offset) for i in range(ctx)])
-    offsets = list(range(2, ctx, 2))
+    later = list(range(4, ctx, 2))
+    column = {offset: trade(kva, offset) for offset in later}
+    left = trade(kv, 2)
     beside = trade(kv, 1)
-    column = {offset: trade(kva, offset) for offset in offsets}
     w_far = cross_core(after(w_send, kv))
     near = after(near, kv)
     q, own = call(
@@ -394,47 +386,39 @@
     cost = lambda units: (16 * HD * unit * units, 8 * unit, (), unit * units)
     in_place = {2: 0, 3: 1}
     num, den = call(attention_own_kernel, [info], [WHOLE] * 3, acc, [q, kv, own], *cost(3))
-    first, later = offsets[0], offsets[1:]
-
-    def attend(num, den, pieces, ends=()):
+    def attend(num, den, pieces, outs=()):
         return call(
-            functools.partial(attention_kernel, pieces=tuple(key for key, _ in pieces), ends=ends), [info],
-            [WHOLE] * (3 + len(pieces)), acc + [vmem((2 * rows, part), BF16)] * len(ends),
+            functools.partial(attention_kernel, pieces=tuple(key for key, _ in pieces)), [info],
+            [WHOLE] * (3 + len(pieces)), acc + list(outs),
             [q, num, den] + [piece for _, piece in pieces], *cost(len(pieces)), aliases=in_place,
         )
 
-    column[first] = after(column[first], num, w_far)
-    over_x, over_y, corner = {}, {}, {}
-    over_x[first], over_y[first] = cross_x(column[first]), trade(column[first], 1)
-    num, den = attend(num, den, [((1, 2), beside), ((first, 0), column[first])])
-    corner[first] = cross_x(over_y[first])
+    num, den = attend(num, den, [((1, 2), beside)])
+    over_x, over_y = {}, {}
+    left = after(left, num, w_far)
     for offset in later:
         column[offset] = after(column[offset], num)
-        over_x[offset], over_y[offset] = cross_x(column[offset]), trade(column[offset], 1)
-    num, den = attend(
-        num, den,
-        [((first, 1), over_x[first]), ((first, 0), over_y[first])] + [((o, 0), column[o]) for o in later],
-    )
-    for number, offset in enumerate(later):
-        corner[offset] = trade(over_x[offset], 1) if number % 2 else cross_x(over_y[offset])
-    num, den, ga = attend(
-        num, den,
-        [((first, 1), corner[first])]
-        + [((o, 0), over_y[o]) for o in later] + [((o, 1), over_x[o]) for o in later], (0,),
-    )
-    ha = cross_core(ga)
-    num, den, gb = attend(num, den, [((o, 1), corner[o]) for o in later], (1,))
-    hb = cross_core(gb)
+        over_y[offset], over_x[offset] = trade(column[offset], 1), cross_x(column[offset])
+    num, den = attend(num, den, [((2, 2), left)] + [((o, 0), column[o]) for o in later])
+    right = trade(after(left, num), 1)
+    over_y = {offset: after(piece, num) for offset, piece in over_y.items()}
+    corner = {offset: cross_x(piece) for offset, piece in over_y.items()}
+    pieces = [((o, 0), over_y[o]) for o in later] + [((o, 1), over_x[o]) for o in later]
+    num, den = attend(num, den, pieces)
+    num, den = attend(num, den, [((o, 1), corner[o]) for o in later])
+    num, den, near_heads = attend(num, den, [((3, 2), right)], [vmem((2 * rows, heads_width), BF16)])
+    far_heads = cross_core(near_heads)
 
     tile = 512
+    half_cost = 4 * rows * heads_width * out_cols, heads_width * out_cols * 2
     mixed, = call(
-        functools.partial(out_first_kernel, tile=tile), [info], [WHOLE] * 5, [vmem((2 * rows, out_cols), F32)],
-        [ga, gb, ha, w_out, w_far], 6 * rows * heads_width * out_cols, 2 * heads_width * out_cols * 2,
+        functools.partial(out_first_kernel, tile=tile), [info], [WHOLE] * 2, [vmem((2 * rows, out_cols), F32)],
+        [near_heads, w_out], *half_cost,
     )
     out = shape((rows, out_cols), BF16)
     clean_out, noised_out = call(
         functools.partial(out_last_kernel, tile=tile), [info, block_live[0]], [WHOLE] * 3, [(HBM, out), (HBM, out)],
-        [hb, mixed, w_far], 2 * rows * heads_width * out_cols, heads_width * out_cols * 2,
+        [far_heads, mixed, w_far], *half_cost,
         [pltpu.VMEM((rows, out_cols), BF16)] * 2 + [pltpu.SemaphoreType.DMA((2 * (out_cols // tile),))],
     )
     return (clean_out, noised_out[None])

time: 66.5 us -> 62.9 us (0.946)
  waiting for transfers between devices: 11.6 us -> 6.79 us
    ppermute x7 -> x6, waiting for transfers between devices: 7.84 us -> 3.18 us  [on_device(): cross_x = lambda v: lax.ppermute(v, 'copy', pair)]
    ppermute x8 -> x7, starting transfers between devices: 7.96 us -> 8.66 us  [on_device(): lax.ppermute(v, 'ctx', [(i, i ^ offset) for i in range(ctx)])]
    ppermute x4 -> x3, starting transfers between devices: 5.56 us -> 4.99 us  [on_device(): cross_core = lambda v: lax.ppermute(v, 'tp', pair)]
    ppermute x7 -> x6, starting transfers between devices: 4.11 us -> 4.46 us  [on_device(): cross_x = lambda v: lax.ppermute(v, 'copy', pair)]
    pallas_call x11 -> x12, Pallas kernels: 33.9 us -> 34.1 us  [call(): pl.pallas_call(kernel, grid_spec=pltpu.PrefetchScalarGridSpec(num_scalar_...]
    ppermute x8 -> x7, waiting for transfers between devices: 2.18 us -> 2.07 us  [on_device(): lax.ppermute(v, 'ctx', [(i, i ^ offset) for i in range(ctx)])]
    ppermute x4 -> x3, waiting for transfers between devices: 1.54 us -> 1.54 us  [on_device(): cross_core = lambda v: lax.ppermute(v, 'tp', pair)]
  transfers between devices with their start and end apart: 19 -> 16, of which waited for: 7 -> 4; matrix products, arithmetic and copies ran while one was open for 2% -> 2% of each run, Pallas kernels for 43% -> 40%
where the time goes in v8:
time: 62.9 us; the launch traced here: 62.1 us
  Pallas kernels  34.1 us (54%)
  starting transfers between devices  18.1 us (29%)
  waiting for transfers between devices  6.79 us (11%)
  between operations  1.62 us (3%)
  local copies, waits for them, and re-layouts  1.44 us (2%)
    pallas_call x12, Pallas kernels, call(): pl.pallas_call(kernel, grid_spec=pltpu.PrefetchScalarGridSpec(num_scalar_...  34.1 us
    ppermute x7, starting transfers between devices, on_device(): lax.ppermute(v, 'ctx', [(i, i ^ offset) for i in range(ctx)])  8.66 us
    ppermute x3, starting transfers between devices, on_device(): cross_core = lambda v: lax.ppermute(v, 'tp', pair)  4.99 us
    ppermute x6, starting transfers between devices, on_device(): cross_x = lambda v: lax.ppermute(v, 'copy', pair)  4.46 us
    ppermute x6, waiting for transfers between devices, on_device(): cross_x = lambda v: lax.ppermute(v, 'copy', pair)  3.18 us
    ppermute x7, waiting for transfers between devices, on_device(): lax.ppermute(v, 'ctx', [(i, i ^ offset) for i in range(ctx)])  2.07 us
    ppermute x3, waiting for transfers between devices, on_device(): cross_core = lambda v: lax.ppermute(v, 'tp', pair)  1.54 us
    broadcast_in_dim x2, local copies, waits for them, and re-layouts, on_device(): vectors = [norm_gain[None], mask_embed[None], shift]  1.42 us
  transfers between devices with their start and end apart: 16, of which 4 were waited for; matrix products, arithmetic and copies ran while one was open for 2% of the time, Pallas kernels for 40%

profile of v8, /device:TPU:25, one launch (start us, length us, event | category | flops | bytes accessed | tf_op | source)
XLA Modules:
  0.0 62.1 jit_solution(15617918762544717400)
XLA Ops:
  0.6 1.6 %shard_map.140 = (bf16[256,2048]{1,0:T(8,128)(2,1)S(1)}, s32[1,256]{1,0:T(1,128)S(1)}, f32[1,4096]{1,0:T(1,128)S(1)}, f32[1,256]{1,0:T(1,128)S(1)}, bf16[128,2048]{1,0:T(8,128)(2,1)S(1)}) custom-call(bf16[256,2048]{1,0:T(8,128)(2,1)} %x_hbm.1, s32[1,256]{1,0:T(1,128)} %mask_hbm.1, f32[1,4096]{1,0:T(1,128)} %bitcast.14), custom_call_target="tpu_custom_call" | custom-call | flops 1048576 | bytes 1048576 | tf_op jit(solution)/shard_map/pallas_call | solution.py:295
  2.2 1.3 %collective-permute-start.1 = (f32[1,256]{1,0:T(1,128)S(1)}, f32[1,256]{1,0:T(1,128)S(1)}, u32[]{:S(2)}, u32[]{:S(2)}) collective-permute-start(f32[1,256]{1,0:T(1,128)S(1)} %get-tuple-element.42.own_ref), channel_id=1, source_target_pairs={{0,16},{16,0},{1,17},{17,1},{2,18},{18,2},{3,19},{19,3},{4,20},{20... | collective-permute-start | bytes 3080 | tf_op jit(solution)/shard_map/ppermute | solution.py:328
  5.9 6.9 %shard_map.141 = (f32[512,1024]{1,0:T(8,128)S(1)}, f32[512,256]{1,0:T(8,128)S(1)}, f32[512,256]{1,0:T(8,128)S(1)}, bf16[2048,1024]{1,0:T(8,128)(2,1)S(1)}, bf16[...) custom-call(s32[4]{0:T(128)S(1)} %pad_add_fusion.info, ...), custom_call_target="tpu_custom_call" | custom-call | flops 25769803776 | bytes 12582912 | tf_op jit(solution)/shard_map/pallas_call | solution.py:295
  12.8 3.2 %collective-permute-done.near_ref = bf16[128,2048]{1,0:T(8,128)(2,1)S(1)} collective-permute-done((bf16[128,2048]{1,0:T(8,128)(2,1)S(1)}, bf16[128,2048]{1,0:T(8,128)(2,1)S(1)}, u32[]{:S(2)}, u32[]{:S(2)}) %collective-permute-start) | collective-permute-done | bytes 524320 | tf_op jit(solution)/shard_map/ppermute | solution.py:328
  16.0 1.9 %collective-permute-start.2 = (bf16[128,2048]{1,0:T(8,128)(2,1)S(1)}, bf16[128,2048]{1,0:T(8,128)(2,1)S(1)}, u32[]{:S(2)}, u32[]{:S(2)}) collective-permute-start(bf16[128,2048]{1,0:T(8,128)(2,1)S(1)} %collective-permute-done.near_ref), channel_id=1, source_target_pairs={{0,1},{1,0},{2,3},{3,2},{4,5},{5,4},{6,7},{7,6},{8,9},{9,8},{10,11... | collective-permute-start | bytes 1572872 | tf_op jit(solution)/shard_map/ppermute | solution.py:329
  17.8 1.5 %collective-permute-done.2.far_ref = bf16[128,2048]{1,0:T(8,128)(2,1)S(1)} collective-permute-done((bf16[128,2048]{1,0:T(8,128)(2,1)S(1)}, bf16[128,2048]{1,0:T(8,128)(2,1)S(1)}, u32[]{:S(2)}, u32[]{:S(2)}) %collective-permute-start.2) | collective-permute-done | bytes 524320 | tf_op jit(solution)/shard_map/ppermute | solution.py:329
  19.4 1.5 %shard_map.142 = (bf16[256,512]{1,0:T(8,128)(2,1)S(1)}, bf16[256,256]{1,0:T(8,128)(2,1)S(1)}) custom-call(s32[4]{0:T(128)S(1)} %pad_add_fusion.info, bf16[128,2048]{1,0:T(8,128)(2,1)S(1)} %collective-permute-done.near_ref, bf16[128,2048]{1,0:T(8,128)(2,1)S(1)} %collective-permute-done.2.far_ref, f32[1,256]{1,0:T(1,128)S(1)} %get-tuple-element.42.own_ref, ...), custom_call_target="tpu_custom_call" | custom-call | flops 536870912 | bytes 2097152 | tf_op jit(solution)/shard_map/pallas_call | solution.py:295
  21.3 1.3 %collective-permute-start.6 = (bf16[256,256]{1,0:T(8,128)(2,1)S(1)}, bf16[256,256]{1,0:T(8,128)(2,1)S(1)}, u32[]{:S(2)}, u32[]{:S(2)}) collective-permute-start(bf16[256,256]{1,0:T(8,128)(2,1)S(1)} %get-tuple-element.63), channel_id=1, source_target_pairs={{0,8},{2,10},{4,12},{6,14},{8,0},{10,2},{12,4},{14,6},{1,9},{3,11}... | collective-permute-start | bytes 393224 | tf_op jit(solution)/shard_map/ppermute | solution.py:370
  22.6 2.2 %collective-permute-start.4 = (bf16[256,512]{1,0:T(8,128)(2,1)S(1)}, bf16[256,512]{1,0:T(8,128)(2,1)S(1)}, u32[]{:S(2)}, u32[]{:S(2)}) collective-permute-start(bf16[256,512]{1,0:T(8,128)(2,1)S(1)} %get-tuple-element.50.kv_ref), channel_id=1, source_target_pairs={{0,4},{2,6},{4,0},{6,2},{8,12},{10,14},{12,8},{14,10},{1,5},{3,7},... | collective-permute-start | bytes 786440 | tf_op jit(solution)/shard_map/ppermute | solution.py:370
  24.8 1.2 %collective-permute-start.3 = (bf16[256,512]{1,0:T(8,128)(2,1)S(1)}, bf16[256,512]{1,0:T(8,128)(2,1)S(1)}, u32[]{:S(2)}, u32[]{:S(2)}) collective-permute-start(bf16[256,512]{1,0:T(8,128)(2,1)S(1)} %get-tuple-element.50.kv_ref), channel_id=1, source_target_pairs={{0,2},{2,0},{4,6},{6,4},{8,10},{10,8},{12,14},{14,12},{1,3},{3,1},... | collective-permute-start | bytes 786440 | tf_op jit(solution)/shard_map/ppermute | solution.py:370
  26.1 3.8 %shard_map.143 = (bf16[512,1024]{1,0:T(8,128)(2,1)S(1)}, bf16[256,512]{1,0:T(8,128)(2,1)S(1)}) custom-call(s32[4]{0:T(128)S(1)} %pad_add_fusion.info, bf16[128,2048]{1,0:T(8,128)(2,1)S(1)} %collective-permute-done.near_ref, bf16[128,2048]{1,0:T(8,128)(2,1)S(1)} %collective-permute-done.2.far_ref, f32[1,256]{1,0:T(1,128)S(1)} %get-tuple-element.42.own_ref, ...), custom_call_target="tpu_custom_call" | custom-call | flops 3221225472 | bytes 6291456 | tf_op jit(solution)/shard_map/pallas_call | solution.py:295
  29.9 2.5 %shard_map.144 = (f32[512,1024]{1,0:T(8,128)S(1)}, f32[512,1024]{1,0:T(8,128)S(1)}) custom-call(s32[4]{0:T(128)S(1)} %pad_add_fusion.info, bf16[512,1024]{1,0:T(8,128)(2,1)S(1)} %get-tuple-element.54.q_ref, bf16[256,512]{1,0:T(8,128)(2,1)S(1)} %get-tuple-element.50.kv_ref, bf16[256,512]{1,0:T(8,128)(2,1)S(1)} %get-tuple-element.55.self_ref), custom_call_target="tpu_custom_call" | custom-call | flops 3221225472 | bytes 4194304 | tf_op jit(solution)/shard_map/pallas_call | solution.py:295
  33.2 1.4 %collective-permute-done.6.refs_1_ = bf16[256,256]{1,0:T(8,128)(2,1)S(1)} collective-permute-done((bf16[256,256]{1,0:T(8,128)(2,1)S(1)}, bf16[256,256]{1,0:T(8,128)(2,1)S(1)}, u32[]{:S(2)}, u32[]{:S(2)}) %collective-permute-start.6) | collective-permute-done | bytes 131104 | tf_op jit(solution)/shard_map/ppermute | solution.py:370
  34.9 1.2 %collective-permute-start.8 = (bf16[256,256]{1,0:T(8,128)(2,1)S(1)}, bf16[256,256]{1,0:T(8,128)(2,1)S(1)}, u32[]{:S(2)}, u32[]{:S(2)}) collective-permute-start(bf16[256,256]{1,0:T(8,128)(2,1)S(1)} %collective-permute-done.6.refs_1_), channel_id=1, source_target_pairs={{0,2},{2,0},{4,6},{6,4},{8,10},{10,8},{12,14},{14,12},{1,3},{3,1},... | collective-permute-start | bytes 393224 | tf_op jit(solution)/shard_map/ppermute | solution.py:370
  36.1 1.2 %collective-permute-start.11 = (bf16[256,256]{1,0:T(8,128)(2,1)S(1)}, bf16[256,256]{1,0:T(8,128)(2,1)S(1)}, u32[]{:S(2)}, u32[]{:S(2)}) collective-permute-start(bf16[256,256]{1,0:T(8,128)(2,1)S(1)} %collective-permute-done.7.refs_2_), channel_id=1, source_target_pairs={{0,16},{16,0},{1,17},{17,1},{2,18},{18,2},{3,19},{19,3},{4,20},{20... | collective-permute-start | bytes 393224 | tf_op jit(solution)/shard_map/ppermute | solution.py:328
  37.3 1.0 %collective-permute-start.9 = (bf16[256,256]{1,0:T(8,128)(2,1)S(1)}, bf16[256,256]{1,0:T(8,128)(2,1)S(1)}, u32[]{:S(2)}, u32[]{:S(2)}) collective-permute-start(bf16[256,256]{1,0:T(8,128)(2,1)S(1)} %collective-permute-done.7.refs_2_), channel_id=1, source_target_pairs={{0,2},{2,0},{4,6},{6,4},{8,10},{10,8},{12,14},{14,12},{1,3},{3,1},... | collective-permute-start | bytes 393224 | tf_op jit(solution)/shard_map/ppermute | solution.py:370
  38.3 3.2 %shard_map.146 = (f32[512,1024]{1,0:T(8,128)S(1)}, f32[512,1024]{1,0:T(8,128)S(1)}) custom-call(s32[4]{0:T(128)S(1)} %pad_add_fusion.info, bf16[512,1024]{1,0:T(8,128)(2,1)S(1)} %get-tuple-element.54.q_ref, f32[512,1024]{1,0:T(8,128)S(1)} %get-tuple-element.58.num_in, ...), custom_call_target="tpu_custom_call", output_to_operand_aliasing={{0}: (2, {}), {1}: (3, {})} | custom-call | flops 3221225472 | bytes 4194304 | tf_op jit(solution)/shard_map/pallas_call | solution.py:295
  43.6 1.7 %collective-permute-start.14 = (bf16[256,512]{1,0:T(8,128)(2,1)S(1)}, bf16[256,512]{1,0:T(8,128)(2,1)S(1)}, u32[]{:S(2)}, u32[]{:S(2)}) collective-permute-start(bf16[256,512]{1,0:T(8,128)(2,1)S(1)} %collective-permute-done.4.refs_0_), channel_id=1, source_target_pairs={{0,2},{2,0},{4,6},{6,4},{8,10},{10,8},{12,14},{14,12},{1,3},{3,1},... | collective-permute-start | bytes 786440 | tf_op jit(solution)/shard_map/ppermute | solution.py:370
  45.3 2.9 %shard_map.147 = (f32[512,1024]{1,0:T(8,128)S(1)}, f32[512,1024]{1,0:T(8,128)S(1)}) custom-call(s32[4]{0:T(128)S(1)} %pad_add_fusion.info, bf16[512,1024]{1,0:T(8,128)(2,1)S(1)} %get-tuple-element.54.q_ref, f32[512,1024]{1,0:T(8,128)S(1)} %get-tuple-element.66.num_in, ...), custom_call_target="tpu_custom_call", output_to_operand_aliasing={{0}: (2, {}), {1}: (3, {})} | custom-call | flops 4294967296 | bytes 4194304 | tf_op jit(solution)/shard_map/pallas_call | solution.py:295
  48.2 1.8 %shard_map.148 = (f32[512,1024]{1,0:T(8,128)S(1)}, f32[512,1024]{1,0:T(8,128)S(1)}) custom-call(s32[4]{0:T(128)S(1)} %pad_add_fusion.info, bf16[512,1024]{1,0:T(8,128)(2,1)S(1)} %get-tuple-element.54.q_ref, f32[512,1024]{1,0:T(8,128)S(1)} %get-tuple-element.70.num_in, ...), custom_call_target="tpu_custom_call", output_to_operand_aliasing={{0}: (2, {}), {1}: (3, {})} | custom-call | flops 2147483648 | bytes 4194304 | tf_op jit(solution)/shard_map/pallas_call | solution.py:295
  50.1 2.6 %shard_map.149 = (f32[512,1024]{1,0:T(8,128)S(1)}, f32[512,1024]{1,0:T(8,128)S(1)}, bf16[512,1024]{1,0:T(8,128)(2,1)S(1)}) custom-call(s32[4]{0:T(128)S(1)} %pad_add_fusion.info, bf16[512,1024]{1,0:T(8,128)(2,1)S(1)} %get-tuple-element.54.q_ref, f32[512,1024]{1,0:T(8,128)S(1)} %get-tuple-element.72.num_in, ...), custom_call_target="tpu_custom_call", output_to_operand_aliasing={{0}: (2, {}), {1}: (3, {})} | custom-call | flops 1073741824 | bytes 4194304 | tf_op jit(solution)/shard_map/pallas_call | solution.py:295
  52.6 2.7 %collective-permute-start.15 = (bf16[512,1024]{1,0:T(8,128)(2,1)S(1)}, bf16[512,1024]{1,0:T(8,128)(2,1)S(1)}, u32[]{:S(2)}, u32[]{:S(2)}) collective-permute-start(bf16[512,1024]{1,0:T(8,128)(2,1)S(1)} %get-tuple-element.75.heads), channel_id=1, source_target_pairs={{0,1},{1,0},{2,3},{3,2},{4,5},{5,4},{6,7},{7,6},{8,9},{9,8},{10,11... | collective-permute-start | bytes 3145736 | tf_op jit(solution)/shard_map/ppermute | solution.py:329
  55.4 2.9 %shard_map.150.mixed_ref = f32[512,2048]{1,0:T(8,128)S(1)} custom-call(s32[4]{0:T(128)S(1)} %pad_add_fusion.info, bf16[512,1024]{1,0:T(8,128)(2,1)S(1)} %get-tuple-element.75.heads, bf16[1024,4096]{1,0:T(8,128)(2,1)S(1)} %bitcast.9), custom_call_target="tpu_custom_call" | custom-call | flops 2147483648 | bytes 4194304 | tf_op jit(solution)/shard_map/pallas_call | solution.py:295
  58.3 3.7 %shard_map.151 = (bf16[256,2048]{1,0:T(8,128)(2,1)}, bf16[256,2048]{1,0:T(8,128)(2,1)}) custom-call(s32[4]{0:T(128)S(1)} %pad_add_fusion.info, s32[4]{0:T(128)S(1)} %bitcast.12, bf16[512,1024]{1,0:T(8,128)(2,1)S(1)} %collective-permute-done.15.heads, f32[512,2048]{1,0:T(8,128)S(1)} %shard_map.150.mixed_ref, bf16[1024,2048]{1,0:T(8,128)(2,1)S(1)} %collective-permute-done.5.w_far), custom_call_target="tpu_custom_call" | custom-call | flops 2147483648 | bytes 4194304 | tf_op jit(solution)/shard_map/pallas_call | solution.py:295
  (34 shorter events, 5.3 us)
Async XLA Ops:
  2.2 3.7 %collective-permute-start.1 = (f32[1,256]{1,0:T(1,128)S(1)}, f32[1,256]{1,0:T(1,128)S(1)}, u32[]{:S(2)}, u32[]{:S(2)}) collective-permute-start(f32[1,256]{1,0:T(1,128)S(1)} %get-tuple-element.42.own_ref), channel_id=1, source_target_pairs={{0,16},{16,0},{1,17},{17,1},{2,18},{18,2},{3,19},{19,3},{4,20},{20... | collective-permute-start | bytes 3080 | tf_op jit(solution)/shard_map/ppermute | solution.py:328
  3.5 12.5 %collective-permute-start = (bf16[128,2048]{1,0:T(8,128)(2,1)S(1)}, bf16[128,2048]{1,0:T(8,128)(2,1)S(1)}, u32[]{:S(2)}, u32[]{:S(2)}) collective-permute-start(bf16[128,2048]{1,0:T(8,128)(2,1)S(1)} %get-tuple-element.40), channel_id=1, source_target_pairs={{0,16},{16,0},{1,17},{17,1},{2,18},{18,2},{3,19},{19,3},{4,20},{20... | collective-permute-start | bytes 1572872 | tf_op jit(solution)/shard_map/ppermute | solution.py:328
  5.9 13.5 %copy-start = (f32[128]{0:T(128)S(1)}, f32[128]{0:T(128)}, u32[]{:S(2)}) copy-start(f32[128]{0:T(128)} %param.22) | copy-start | bytes 1540
  16.0 3.4 %collective-permute-start.2 = (bf16[128,2048]{1,0:T(8,128)(2,1)S(1)}, bf16[128,2048]{1,0:T(8,128)(2,1)S(1)}, u32[]{:S(2)}, u32[]{:S(2)}) collective-permute-start(bf16[128,2048]{1,0:T(8,128)(2,1)S(1)} %collective-permute-done.near_ref), channel_id=1, source_target_pairs={{0,1},{1,0},{2,3},{3,2},{4,5},{5,4},{6,7},{7,6},{8,9},{9,8},{10,11... | collective-permute-start | bytes 1572872 | tf_op jit(solution)/shard_map/ppermute | solution.py:329
  19.4 6.7 %copy-start.2 = (f32[128]{0:T(128)S(1)}, f32[128]{0:T(128)}, u32[]{:S(2)}) copy-start(f32[128]{0:T(128)} %param.21) | copy-start | bytes 1540
  20.9 17.4 %collective-permute-start.5 = (bf16[1024,2048]{1,0:T(8,128)(2,1)S(1)}, bf16[1024,2048]{1,0:T(8,128)(2,1)S(1)}, u32[]{:S(2)}, u32[]{:S(2)}) collective-permute-start(bf16[1024,2048]{1,0:T(8,128)(2,1)S(1)} %get-tuple-element.61), channel_id=1, source_target_pairs={{0,1},{1,0},{2,3},{3,2},{4,5},{5,4},{6,7},{7,6},{8,9},{9,8},{10,11... | collective-permute-start | bytes 12582920 | tf_op jit(solution)/shard_map/ppermute | solution.py:329
  21.3 14.8 %collective-permute-start.7 = (bf16[256,256]{1,0:T(8,128)(2,1)S(1)}, bf16[256,256]{1,0:T(8,128)(2,1)S(1)}, u32[]{:S(2)}, u32[]{:S(2)}) collective-permute-start(bf16[256,256]{1,0:T(8,128)(2,1)S(1)} %get-tuple-element.63), channel_id=1, source_target_pairs={{0,12},{2,14},{4,8},{6,10},{8,4},{10,6},{12,0},{14,2},{1,13},{3,15... | collective-permute-start | bytes 393224 | tf_op jit(solution)/shard_map/ppermute | solution.py:370
  21.3 13.3 %collective-permute-start.6 = (bf16[256,256]{1,0:T(8,128)(2,1)S(1)}, bf16[256,256]{1,0:T(8,128)(2,1)S(1)}, u32[]{:S(2)}, u32[]{:S(2)}) collective-permute-start(bf16[256,256]{1,0:T(8,128)(2,1)S(1)} %get-tuple-element.63), channel_id=1, source_target_pairs={{0,8},{2,10},{4,12},{6,14},{8,0},{10,2},{12,4},{14,6},{1,9},{3,11}... | collective-permute-start | bytes 393224 | tf_op jit(solution)/shard_map/ppermute | solution.py:370
  22.6 14.7 %collective-permute-start.4 = (bf16[256,512]{1,0:T(8,128)(2,1)S(1)}, bf16[256,512]{1,0:T(8,128)(2,1)S(1)}, u32[]{:S(2)}, u32[]{:S(2)}) collective-permute-start(bf16[256,512]{1,0:T(8,128)(2,1)S(1)} %get-tuple-element.50.kv_ref), channel_id=1, source_target_pairs={{0,4},{2,6},{4,0},{6,2},{8,12},{10,14},{12,8},{14,10},{1,5},{3,7},... | collective-permute-start | bytes 786440 | tf_op jit(solution)/shard_map/ppermute | solution.py:370
  24.8 7.6 %collective-permute-start.3 = (bf16[256,512]{1,0:T(8,128)(2,1)S(1)}, bf16[256,512]{1,0:T(8,128)(2,1)S(1)}, u32[]{:S(2)}, u32[]{:S(2)}) collective-permute-start(bf16[256,512]{1,0:T(8,128)(2,1)S(1)} %get-tuple-element.50.kv_ref), channel_id=1, source_target_pairs={{0,2},{2,0},{4,6},{6,4},{8,10},{10,8},{12,14},{14,12},{1,3},{3,1},... | collective-permute-start | bytes 786440 | tf_op jit(solution)/shard_map/ppermute | solution.py:370
  34.6 10.7 %collective-permute-start.10 = (bf16[256,256]{1,0:T(8,128)(2,1)S(1)}, bf16[256,256]{1,0:T(8,128)(2,1)S(1)}, u32[]{:S(2)}, u32[]{:S(2)}) collective-permute-start(bf16[256,256]{1,0:T(8,128)(2,1)S(1)} %collective-permute-done.6.refs_1_), channel_id=1, source_target_pairs={{0,16},{16,0},{1,17},{17,1},{2,18},{18,2},{3,19},{19,3},{4,20},{20... | collective-permute-start | bytes 393224 | tf_op jit(solution)/shard_map/ppermute | solution.py:328
  34.9 7.3 %collective-permute-start.8 = (bf16[256,256]{1,0:T(8,128)(2,1)S(1)}, bf16[256,256]{1,0:T(8,128)(2,1)S(1)}, u32[]{:S(2)}, u32[]{:S(2)}) collective-permute-start(bf16[256,256]{1,0:T(8,128)(2,1)S(1)} %collective-permute-done.6.refs_1_), channel_id=1, source_target_pairs={{0,2},{2,0},{4,6},{6,4},{8,10},{10,8},{12,14},{14,12},{1,3},{3,1},... | collective-permute-start | bytes 393224 | tf_op jit(solution)/shard_map/ppermute | solution.py:370
  36.1 9.2 %collective-permute-start.11 = (bf16[256,256]{1,0:T(8,128)(2,1)S(1)}, bf16[256,256]{1,0:T(8,128)(2,1)S(1)}, u32[]{:S(2)}, u32[]{:S(2)}) collective-permute-start(bf16[256,256]{1,0:T(8,128)(2,1)S(1)} %collective-permute-done.7.refs_2_), channel_id=1, source_target_pairs={{0,16},{16,0},{1,17},{17,1},{2,18},{18,2},{3,19},{19,3},{4,20},{20... | collective-permute-start | bytes 393224 | tf_op jit(solution)/shard_map/ppermute | solution.py:328
  37.3 4.8 %collective-permute-start.9 = (bf16[256,256]{1,0:T(8,128)(2,1)S(1)}, bf16[256,256]{1,0:T(8,128)(2,1)S(1)}, u32[]{:S(2)}, u32[]{:S(2)}) collective-permute-start(bf16[256,256]{1,0:T(8,128)(2,1)S(1)} %collective-permute-done.7.refs_2_), channel_id=1, source_target_pairs={{0,2},{2,0},{4,6},{6,4},{8,10},{10,8},{12,14},{14,12},{1,3},{3,1},... | collective-permute-start | bytes 393224 | tf_op jit(solution)/shard_map/ppermute | solution.py:370
  38.3 17.1 %slice-start = ((s8[8388608]{0:T(1024)(128)(4,1)}), s8[4194304]{0:T(1024)(128)(4,1)S(1)}, s32[]{:S(2)}) async-start(s8[8388608]{0:T(1024)(128)(4,1)} %bitcast.8), calls=%async_computation | async-start | bytes 8388608
  42.2 6.1 %collective-permute-start.12 = (bf16[256,256]{1,0:T(8,128)(2,1)S(1)}, bf16[256,256]{1,0:T(8,128)(2,1)S(1)}, u32[]{:S(2)}, u32[]{:S(2)}) collective-permute-start(bf16[256,256]{1,0:T(8,128)(2,1)S(1)} %collective-permute-done.8.refs_0_), channel_id=1, source_target_pairs={{0,16},{16,0},{1,17},{17,1},{2,18},{18,2},{3,19},{19,3},{4,20},{20... | collective-permute-start | bytes 393224 | tf_op jit(solution)/shard_map/ppermute | solution.py:328
  42.9 5.4 %collective-permute-start.13 = (bf16[256,256]{1,0:T(8,128)(2,1)S(1)}, bf16[256,256]{1,0:T(8,128)(2,1)S(1)}, u32[]{:S(2)}, u32[]{:S(2)}) collective-permute-start(bf16[256,256]{1,0:T(8,128)(2,1)S(1)} %collective-permute-done.9.refs_1_), channel_id=1, source_target_pairs={{0,16},{16,0},{1,17},{17,1},{2,18},{18,2},{3,19},{19,3},{4,20},{20... | collective-permute-start | bytes 393224 | tf_op jit(solution)/shard_map/ppermute | solution.py:328
  43.6 6.4 %collective-permute-start.14 = (bf16[256,512]{1,0:T(8,128)(2,1)S(1)}, bf16[256,512]{1,0:T(8,128)(2,1)S(1)}, u32[]{:S(2)}, u32[]{:S(2)}) collective-permute-start(bf16[256,512]{1,0:T(8,128)(2,1)S(1)} %collective-permute-done.4.refs_0_), channel_id=1, source_target_pairs={{0,2},{2,0},{4,6},{6,4},{8,10},{10,8},{12,14},{14,12},{1,3},{3,1},... | collective-permute-start | bytes 786440 | tf_op jit(solution)/shard_map/ppermute | solution.py:370
  45.3 10.1 %slice-start.1 = ((s8[8388608]{0:T(1024)(128)(4,1)}), s8[4194304]{0:T(1024)(128)(4,1)S(1)}, s32[]{:S(2)}) async-start(s8[8388608]{0:T(1024)(128)(4,1)} %bitcast.8), calls=%async_computation.1 | async-start | bytes 8388608
  52.6 5.7 %copy-start.1 = (s32[1,4]{1,0:T(1,128)S(1)}, s32[1,4]{1,0:T(1,128)}, u32[]{:S(2)}) copy-start(s32[1,4]{1,0:T(1,128)} %param.24) | copy-start | bytes 52
  52.6 5.6 %collective-permute-start.15 = (bf16[512,1024]{1,0:T(8,128)(2,1)S(1)}, bf16[512,1024]{1,0:T(8,128)(2,1)S(1)}, u32[]{:S(2)}, u32[]{:S(2)}) collective-permute-start(bf16[512,1024]{1,0:T(8,128)(2,1)S(1)} %get-tuple-element.75.heads), channel_id=1, source_target_pairs={{0,1},{1,0},{2,3},{3,2},{4,5},{5,4},{6,7},{7,6},{8,9},{9,8},{10,11... | collective-permute-start | bytes 3145736 | tf_op jit(solution)/shard_map/ppermute | solution.py:329

commit v9 on v8

--- a/solution.py
+++ b/solution.py
@@ -369,7 +369,8 @@
 
     trade = lambda v, offset: lax.ppermute(v, "ctx", [(i, i ^ offset) for i in range(ctx)])
     later = list(range(4, ctx, 2))
-    column = {offset: trade(kva, offset) for offset in later}
+    early, late = later[: len(later) // 2], later[len(later) // 2 :]
+    column = {offset: trade(kva, offset) for offset in early}
     left = trade(kv, 2)
     beside = trade(kv, 1)
     w_far = cross_core(after(w_send, kv))
@@ -381,6 +382,7 @@
         4 * rows * half * per_row, half * per_row * 2,
     )
 
+    column.update({offset: trade(after(kva, q), offset) for offset in late})
     acc = [vmem((2 * rows, heads_width), F32)] * 2
     unit = rows * rows * heads_width // HD
     cost = lambda units: (16 * HD * unit * units, 8 * unit, (), unit * units)
@@ -393,20 +395,32 @@
             [q, num, den] + [piece for _, piece in pieces], *cost(len(pieces)), aliases=in_place,
         )
 
-    num, den = attend(num, den, [((1, 2), beside)])
-    over_x, over_y = {}, {}
-    left = after(left, num, w_far)
-    for offset in later:
-        column[offset] = after(column[offset], num)
-        over_y[offset], over_x[offset] = trade(column[offset], 1), cross_x(column[offset])
-    num, den = attend(num, den, [((2, 2), left)] + [((o, 0), column[o]) for o in later])
+    over_x, over_y, corner = {}, {}, {}
+
+    def turn(offsets, done):
+        for offset in offsets:
+            column[offset] = after(column[offset], done)
+            over_y[offset], over_x[offset] = trade(column[offset], 1), cross_x(column[offset])
+
+    turn(early, num)
+    num, den = attend(num, den, [((1, 2), beside)] + [((o, 0), column[o]) for o in early])
     right = trade(after(left, num), 1)
-    over_y = {offset: after(piece, num) for offset, piece in over_y.items()}
-    corner = {offset: cross_x(piece) for offset, piece in over_y.items()}
-    pieces = [((o, 0), over_y[o]) for o in later] + [((o, 1), over_x[o]) for o in later]
-    num, den = attend(num, den, pieces)
-    num, den = attend(num, den, [((o, 1), corner[o]) for o in later])
-    num, den, near_heads = attend(num, den, [((3, 2), right)], [vmem((2 * rows, heads_width), BF16)])
+    corner.update({o: cross_x(after(over_y[o], num)) for o in early})
+    turn(late, num)
+    num, den = attend(
+        num, den,
+        [((2, 2), left)] + [((o, 0), column[o]) for o in late]
+        + [((o, 0), over_y[o]) for o in early] + [((o, 1), over_x[o]) for o in early],
+    )
+    corner.update({o: cross_x(after(over_y[o], num)) for o in late})
+    num, den = attend(
+        num, den,
+        [((3, 2), right)] + [((o, 0), over_y[o]) for o in late]
+        + [((o, 1), over_x[o]) for o in late] + [((o, 1), corner[o]) for o in early],
+    )
+    num, den, near_heads = attend(
+        num, den, [((o, 1), corner[o]) for o in late], [vmem((2 * rows, heads_width), BF16)]
+    )
     far_heads = cross_core(near_heads)
 
     tile = 512

time: 62.9 us -> 61.9 us (0.984)
  starting transfers between devices: 18.1 us -> 17.1 us
    ppermute x7, starting transfers between devices: 8.66 us -> 7.76 us  [on_device(): lax.ppermute(v, 'ctx', [(i, i ^ offset) for i in range(ctx)])]
    pallas_call x12 -> x11, Pallas kernels: 34.1 us -> 34.1 us  [call(): pl.pallas_call(kernel, grid_spec=pltpu.PrefetchScalarGridSpec(num_scalar_...]
  transfers between devices with their start and end apart: 16 -> 16, of which waited for: 4 -> 3; matrix products, arithmetic and copies ran while one was open for 2% -> 2% of each run, Pallas kernels for 40% -> 44%
where the time goes in v9:
time: 61.9 us; the launch traced here: 61.6 us
  Pallas kernels  34.1 us (55%)
  starting transfers between devices  17.1 us (28%)
  waiting for transfers between devices  7.33 us (12%)
  between operations  1.6 us (3%)
  local copies, waits for them, and re-layouts  1.44 us (2%)
    pallas_call x11, Pallas kernels, call(): pl.pallas_call(kernel, grid_spec=pltpu.PrefetchScalarGridSpec(num_scalar_...  34.1 us
    ppermute x7, starting transfers between devices, on_device(): lax.ppermute(v, 'ctx', [(i, i ^ offset) for i in range(ctx)])  7.76 us
    ppermute x6, starting transfers between devices, on_device(): cross_x = lambda v: lax.ppermute(v, 'copy', pair)  4.66 us
    ppermute x3, starting transfers between devices, on_device(): cross_core = lambda v: lax.ppermute(v, 'tp', pair)  4.64 us
    ppermute x6, waiting for transfers between devices, on_device(): cross_x = lambda v: lax.ppermute(v, 'copy', pair)  3.18 us
    ppermute x7, waiting for transfers between devices, on_device(): lax.ppermute(v, 'ctx', [(i, i ^ offset) for i in range(ctx)])  2.61 us
    ppermute x3, waiting for transfers between devices, on_device(): cross_core = lambda v: lax.ppermute(v, 'tp', pair)  1.54 us
    broadcast_in_dim x2, local copies, waits for them, and re-layouts, on_device(): vectors = [norm_gain[None], mask_embed[None], shift]  1.42 us
  transfers between devices with their start and end apart: 16, of which 3 were waited for; matrix products, arithmetic and copies ran while one was open for 2% of the time, Pallas kernels for 44%

profile of v9, /device:TPU:25, one launch (start us, length us, event | category | flops | bytes accessed | tf_op | source)
XLA Modules:
  0.0 61.6 jit_solution(5763857701399263209)
XLA Ops:
  0.6 1.6 %shard_map.140 = (bf16[256,2048]{1,0:T(8,128)(2,1)S(1)}, s32[1,256]{1,0:T(1,128)S(1)}, f32[1,4096]{1,0:T(1,128)S(1)}, f32[1,256]{1,0:T(1,128)S(1)}, bf16[128,2048]{1,0:T(8,128)(2,1)S(1)}) custom-call(bf16[256,2048]{1,0:T(8,128)(2,1)} %x_hbm.1, s32[1,256]{1,0:T(1,128)} %mask_hbm.1, f32[1,4096]{1,0:T(1,128)} %bitcast.14), custom_call_target="tpu_custom_call" | custom-call | flops 1048576 | bytes 1048576 | tf_op jit(solution)/shard_map/pallas_call | solution.py:295
  2.2 1.3 %collective-permute-start.1 = (f32[1,256]{1,0:T(1,128)S(1)}, f32[1,256]{1,0:T(1,128)S(1)}, u32[]{:S(2)}, u32[]{:S(2)}) collective-permute-start(f32[1,256]{1,0:T(1,128)S(1)} %get-tuple-element.40.own_ref), channel_id=1, source_target_pairs={{0,16},{16,0},{1,17},{17,1},{2,18},{18,2},{3,19},{19,3},{4,20},{20... | collective-permute-start | bytes 3080 | tf_op jit(solution)/shard_map/ppermute | solution.py:328
  4.5 0.7 %broadcast_in_dim.19.gain_ref = bf16[1,4096]{1,0:T(2,128)(2,1)S(1)} reshape(bf16[4096]{0:T(1024)(128)(2,1)} %param.14) | data formatting | bytes 16384 | tf_op jit(solution)/shard_map/broadcast_in_dim | solution.py:348
  5.2 0.7 %broadcast_in_dim.20.embed_ref = bf16[1,4096]{1,0:T(2,128)(2,1)S(1)} reshape(bf16[4096]{0:T(1024)(128)(2,1)} %param.15) | data formatting | bytes 16384 | tf_op jit(solution)/shard_map/broadcast_in_dim | solution.py:348
  5.9 6.9 %shard_map.141 = (f32[512,1024]{1,0:T(8,128)S(1)}, f32[512,256]{1,0:T(8,128)S(1)}, f32[512,256]{1,0:T(8,128)S(1)}, bf16[2048,1024]{1,0:T(8,128)(2,1)S(1)}, bf16[...) custom-call(s32[4]{0:T(128)S(1)} %pad_add_fusion.info, ...), custom_call_target="tpu_custom_call" | custom-call | flops 25769803776 | bytes 12582912 | tf_op jit(solution)/shard_map/pallas_call | solution.py:295
  12.8 3.2 %collective-permute-done.near_ref = bf16[128,2048]{1,0:T(8,128)(2,1)S(1)} collective-permute-done((bf16[128,2048]{1,0:T(8,128)(2,1)S(1)}, bf16[128,2048]{1,0:T(8,128)(2,1)S(1)}, u32[]{:S(2)}, u32[]{:S(2)}) %collective-permute-start) | collective-permute-done | bytes 524320 | tf_op jit(solution)/shard_map/ppermute | solution.py:328
  16.0 1.9 %collective-permute-start.2 = (bf16[128,2048]{1,0:T(8,128)(2,1)S(1)}, bf16[128,2048]{1,0:T(8,128)(2,1)S(1)}, u32[]{:S(2)}, u32[]{:S(2)}) collective-permute-start(bf16[128,2048]{1,0:T(8,128)(2,1)S(1)} %collective-permute-done.near_ref), channel_id=1, source_target_pairs={{0,1},{1,0},{2,3},{3,2},{4,5},{5,4},{6,7},{7,6},{8,9},{9,8},{10,11... | collective-permute-start | bytes 1572872 | tf_op jit(solution)/shard_map/ppermute | solution.py:329
  17.8 1.5 %collective-permute-done.2.far_ref = bf16[128,2048]{1,0:T(8,128)(2,1)S(1)} collective-permute-done((bf16[128,2048]{1,0:T(8,128)(2,1)S(1)}, bf16[128,2048]{1,0:T(8,128)(2,1)S(1)}, u32[]{:S(2)}, u32[]{:S(2)}) %collective-permute-start.2) | collective-permute-done | bytes 524320 | tf_op jit(solution)/shard_map/ppermute | solution.py:329
  19.4 1.5 %shard_map.142 = (bf16[256,512]{1,0:T(8,128)(2,1)S(1)}, bf16[256,256]{1,0:T(8,128)(2,1)S(1)}) custom-call(s32[4]{0:T(128)S(1)} %pad_add_fusion.info, bf16[128,2048]{1,0:T(8,128)(2,1)S(1)} %collective-permute-done.near_ref, bf16[128,2048]{1,0:T(8,128)(2,1)S(1)} %collective-permute-done.2.far_ref, f32[1,256]{1,0:T(1,128)S(1)} %get-tuple-element.40.own_ref, ...), custom_call_target="tpu_custom_call" | custom-call | flops 536870912 | bytes 2097152 | tf_op jit(solution)/shard_map/pallas_call | solution.py:295
  21.5 1.2 %collective-permute-start.3 = (bf16[256,512]{1,0:T(8,128)(2,1)S(1)}, bf16[256,512]{1,0:T(8,128)(2,1)S(1)}, u32[]{:S(2)}, u32[]{:S(2)}) collective-permute-start(bf16[256,512]{1,0:T(8,128)(2,1)S(1)} %get-tuple-element.48.kv_ref), channel_id=1, source_target_pairs={{0,2},{2,0},{4,6},{6,4},{8,10},{10,8},{12,14},{14,12},{1,3},{3,1},... | collective-permute-start | bytes 786440 | tf_op jit(solution)/shard_map/ppermute | solution.py:370
  22.8 3.8 %shard_map.143 = (bf16[512,1024]{1,0:T(8,128)(2,1)S(1)}, bf16[256,512]{1,0:T(8,128)(2,1)S(1)}) custom-call(s32[4]{0:T(128)S(1)} %pad_add_fusion.info, bf16[128,2048]{1,0:T(8,128)(2,1)S(1)} %collective-permute-done.near_ref, bf16[128,2048]{1,0:T(8,128)(2,1)S(1)} %collective-permute-done.2.far_ref, f32[1,256]{1,0:T(1,128)S(1)} %get-tuple-element.40.own_ref, ...), custom_call_target="tpu_custom_call" | custom-call | flops 3221225472 | bytes 6291456 | tf_op jit(solution)/shard_map/pallas_call | solution.py:295
  26.7 3.3 %collective-permute-start.6 = (bf16[256,256]{1,0:T(8,128)(2,1)S(1)}, bf16[256,256]{1,0:T(8,128)(2,1)S(1)}, u32[]{:S(2)}, u32[]{:S(2)}) collective-permute-start(bf16[256,256]{1,0:T(8,128)(2,1)S(1)} %get-tuple-element.60), channel_id=1, source_target_pairs={{0,12},{2,14},{4,8},{6,10},{8,4},{10,6},{12,0},{14,2},{1,13},{3,15... | collective-permute-start | bytes 393224 | tf_op jit(solution)/shard_map/ppermute | solution.py:370
  30.0 2.5 %shard_map.144 = (f32[512,1024]{1,0:T(8,128)S(1)}, f32[512,1024]{1,0:T(8,128)S(1)}) custom-call(s32[4]{0:T(128)S(1)} %pad_add_fusion.info, bf16[512,1024]{1,0:T(8,128)(2,1)S(1)} %get-tuple-element.52.q_ref, bf16[256,512]{1,0:T(8,128)(2,1)S(1)} %get-tuple-element.48.kv_ref, bf16[256,512]{1,0:T(8,128)(2,1)S(1)} %get-tuple-element.53.self_ref), custom_call_target="tpu_custom_call" | custom-call | flops 3221225472 | bytes 4194304 | tf_op jit(solution)/shard_map/pallas_call | solution.py:295
  33.1 1.5 %shard_map.145 = (f32[512,1024]{1,0:T(8,128)S(1)}, f32[512,1024]{1,0:T(8,128)S(1)}) custom-call(s32[4]{0:T(128)S(1)} %pad_add_fusion.info, bf16[512,1024]{1,0:T(8,128)(2,1)S(1)} %get-tuple-element.52.q_ref, f32[512,1024]{1,0:T(8,128)S(1)} %get-tuple-element.54.num_in, ...), custom_call_target="tpu_custom_call", output_to_operand_aliasing={{0}: (2, {}), {1}: (3, {})} | custom-call | flops 2147483648 | bytes 4194304 | tf_op jit(solution)/shard_map/pallas_call | solution.py:295
  34.6 1.3 %collective-permute-start.11 = (bf16[256,256]{1,0:T(8,128)(2,1)S(1)}, bf16[256,256]{1,0:T(8,128)(2,1)S(1)}, u32[]{:S(2)}, u32[]{:S(2)}) collective-permute-start(bf16[256,256]{1,0:T(8,128)(2,1)S(1)} %collective-permute-done.6.refs_1_), channel_id=1, source_target_pairs={{0,16},{16,0},{1,17},{17,1},{2,18},{18,2},{3,19},{19,3},{4,20},{20... | collective-permute-start | bytes 393224 | tf_op jit(solution)/shard_map/ppermute | solution.py:328
  35.9 2.6 %collective-permute-start.10 = (bf16[256,256]{1,0:T(8,128)(2,1)S(1)}, bf16[256,256]{1,0:T(8,128)(2,1)S(1)}, u32[]{:S(2)}, u32[]{:S(2)}) collective-permute-start(bf16[256,256]{1,0:T(8,128)(2,1)S(1)} %collective-permute-done.6.refs_1_), channel_id=1, source_target_pairs={{0,2},{2,0},{4,6},{6,4},{8,10},{10,8},{12,14},{14,12},{1,3},{3,1},... | collective-permute-start | bytes 393224 | tf_op jit(solution)/shard_map/ppermute | solution.py:370
  38.9 3.9 %shard_map.146 = (f32[512,1024]{1,0:T(8,128)S(1)}, f32[512,1024]{1,0:T(8,128)S(1)}) custom-call(s32[4]{0:T(128)S(1)} %pad_add_fusion.info, bf16[512,1024]{1,0:T(8,128)(2,1)S(1)} %get-tuple-element.52.q_ref, f32[512,1024]{1,0:T(8,128)S(1)} %get-tuple-element.58.num_in, ...), custom_call_target="tpu_custom_call", output_to_operand_aliasing={{0}: (2, {}), {1}: (3, {})} | custom-call | flops 4294967296 | bytes 4194304 | tf_op jit(solution)/shard_map/pallas_call | solution.py:295
  42.7 1.3 %collective-permute-start.13 = (bf16[256,256]{1,0:T(8,128)(2,1)S(1)}, bf16[256,256]{1,0:T(8,128)(2,1)S(1)}, u32[]{:S(2)}, u32[]{:S(2)}) collective-permute-start(bf16[256,256]{1,0:T(8,128)(2,1)S(1)} %collective-permute-done.10.refs_1_), channel_id=1, source_target_pairs={{0,16},{16,0},{1,17},{17,1},{2,18},{18,2},{3,19},{19,3},{4,20},{20... | collective-permute-start | bytes 393224 | tf_op jit(solution)/shard_map/ppermute | solution.py:328
  44.0 2.6 %collective-permute-done.9.refs_0_ = bf16[256,512]{1,0:T(8,128)(2,1)S(1)} collective-permute-done((bf16[256,512]{1,0:T(8,128)(2,1)S(1)}, bf16[256,512]{1,0:T(8,128)(2,1)S(1)}, u32[]{:S(2)}, u32[]{:S(2)}) %collective-permute-start.9) | collective-permute-done | bytes 262176 | tf_op jit(solution)/shard_map/ppermute | solution.py:370
  46.6 3.8 %shard_map.147 = (f32[512,1024]{1,0:T(8,128)S(1)}, f32[512,1024]{1,0:T(8,128)S(1)}) custom-call(s32[4]{0:T(128)S(1)} %pad_add_fusion.info, bf16[512,1024]{1,0:T(8,128)(2,1)S(1)} %get-tuple-element.52.q_ref, f32[512,1024]{1,0:T(8,128)S(1)} %get-tuple-element.62.num_in, ...), custom_call_target="tpu_custom_call", output_to_operand_aliasing={{0}: (2, {}), {1}: (3, {})} | custom-call | flops 4294967296 | bytes 4194304 | tf_op jit(solution)/shard_map/pallas_call | solution.py:295
  50.5 2.0 %shard_map.148 = (f32[512,1024]{1,0:T(8,128)S(1)}, f32[512,1024]{1,0:T(8,128)S(1)}, bf16[512,1024]{1,0:T(8,128)(2,1)S(1)}) custom-call(s32[4]{0:T(128)S(1)} %pad_add_fusion.info, bf16[512,1024]{1,0:T(8,128)(2,1)S(1)} %get-tuple-element.52.q_ref, f32[512,1024]{1,0:T(8,128)S(1)} %get-tuple-element.66.num_in, ...), custom_call_target="tpu_custom_call", output_to_operand_aliasing={{0}: (2, {}), {1}: (3, {})} | custom-call | flops 1073741824 | bytes 4194304 | tf_op jit(solution)/shard_map/pallas_call | solution.py:295
  52.5 2.4 %collective-permute-start.14 = (bf16[512,1024]{1,0:T(8,128)(2,1)S(1)}, bf16[512,1024]{1,0:T(8,128)(2,1)S(1)}, u32[]{:S(2)}, u32[]{:S(2)}) collective-permute-start(bf16[512,1024]{1,0:T(8,128)(2,1)S(1)} %get-tuple-element.69.heads), channel_id=1, source_target_pairs={{0,1},{1,0},{2,3},{3,2},{4,5},{5,4},{6,7},{7,6},{8,9},{9,8},{10,11... | collective-permute-start | bytes 3145736 | tf_op jit(solution)/shard_map/ppermute | solution.py:329
  54.9 2.9 %shard_map.149.mixed_ref = f32[512,2048]{1,0:T(8,128)S(1)} custom-call(s32[4]{0:T(128)S(1)} %pad_add_fusion.info, bf16[512,1024]{1,0:T(8,128)(2,1)S(1)} %get-tuple-element.69.heads, bf16[1024,4096]{1,0:T(8,128)(2,1)S(1)} %bitcast.9), custom_call_target="tpu_custom_call" | custom-call | flops 2147483648 | bytes 4194304 | tf_op jit(solution)/shard_map/pallas_call | solution.py:295
  57.8 3.7 %shard_map.150 = (bf16[256,2048]{1,0:T(8,128)(2,1)}, bf16[256,2048]{1,0:T(8,128)(2,1)}) custom-call(s32[4]{0:T(128)S(1)} %pad_add_fusion.info, s32[4]{0:T(128)S(1)} %bitcast.12, bf16[512,1024]{1,0:T(8,128)(2,1)S(1)} %collective-permute-done.14.heads, f32[512,2048]{1,0:T(8,128)S(1)} %shard_map.149.mixed_ref, bf16[1024,2048]{1,0:T(8,128)(2,1)S(1)} %collective-permute-done.15.w_far), custom_call_target="tpu_custom_call" | custom-call | flops 2147483648 | bytes 4194304 | tf_op jit(solution)/shard_map/pallas_call | solution.py:295
  (33 shorter events, 2.0 us)
Async XLA Ops:
  2.2 3.7 %collective-permute-start.1 = (f32[1,256]{1,0:T(1,128)S(1)}, f32[1,256]{1,0:T(1,128)S(1)}, u32[]{:S(2)}, u32[]{:S(2)}) collective-permute-start(f32[1,256]{1,0:T(1,128)S(1)} %get-tuple-element.40.own_ref), channel_id=1, source_target_pairs={{0,16},{16,0},{1,17},{17,1},{2,18},{18,2},{3,19},{19,3},{4,20},{20... | collective-permute-start | bytes 3080 | tf_op jit(solution)/shard_map/ppermute | solution.py:328
  3.5 12.5 %collective-permute-start = (bf16[128,2048]{1,0:T(8,128)(2,1)S(1)}, bf16[128,2048]{1,0:T(8,128)(2,1)S(1)}, u32[]{:S(2)}, u32[]{:S(2)}) collective-permute-start(bf16[128,2048]{1,0:T(8,128)(2,1)S(1)} %get-tuple-element.38), channel_id=1, source_target_pairs={{0,16},{16,0},{1,17},{17,1},{2,18},{18,2},{3,19},{19,3},{4,20},{20... | collective-permute-start | bytes 1572872 | tf_op jit(solution)/shard_map/ppermute | solution.py:328
  5.9 13.5 %copy-start = (f32[128]{0:T(128)S(1)}, f32[128]{0:T(128)}, u32[]{:S(2)}) copy-start(f32[128]{0:T(128)} %param.22) | copy-start | bytes 1540
  16.0 3.4 %collective-permute-start.2 = (bf16[128,2048]{1,0:T(8,128)(2,1)S(1)}, bf16[128,2048]{1,0:T(8,128)(2,1)S(1)}, u32[]{:S(2)}, u32[]{:S(2)}) collective-permute-start(bf16[128,2048]{1,0:T(8,128)(2,1)S(1)} %collective-permute-done.near_ref), channel_id=1, source_target_pairs={{0,1},{1,0},{2,3},{3,2},{4,5},{5,4},{6,7},{7,6},{8,9},{9,8},{10,11... | collective-permute-start | bytes 1572872 | tf_op jit(solution)/shard_map/ppermute | solution.py:329
  19.4 3.5 %copy-start.2 = (f32[128]{0:T(128)S(1)}, f32[128]{0:T(128)}, u32[]{:S(2)}) copy-start(f32[128]{0:T(128)} %param.21) | copy-start | bytes 1540
  20.9 36.9 %collective-permute-start.15 = (bf16[1024,2048]{1,0:T(8,128)(2,1)S(1)}, bf16[1024,2048]{1,0:T(8,128)(2,1)S(1)}, u32[]{:S(2)}, u32[]{:S(2)}) collective-permute-start(bf16[1024,2048]{1,0:T(8,128)(2,1)S(1)} %get-tuple-element.71), channel_id=1, source_target_pairs={{0,1},{1,0},{2,3},{3,2},{4,5},{5,4},{6,7},{7,6},{8,9},{9,8},{10,11... | collective-permute-start | bytes 12582920 | tf_op jit(solution)/shard_map/ppermute | solution.py:329
  21.3 14.6 %collective-permute-start.5 = (bf16[256,512]{1,0:T(8,128)(2,1)S(1)}, bf16[256,512]{1,0:T(8,128)(2,1)S(1)}, u32[]{:S(2)}, u32[]{:S(2)}) collective-permute-start(bf16[256,512]{1,0:T(8,128)(2,1)S(1)} %get-tuple-element.48.kv_ref), channel_id=1, source_target_pairs={{0,4},{2,6},{4,0},{6,2},{8,12},{10,14},{12,8},{14,10},{1,5},{3,7},... | collective-permute-start | bytes 786440 | tf_op jit(solution)/shard_map/ppermute | solution.py:370
  21.5 11.4 %collective-permute-start.3 = (bf16[256,512]{1,0:T(8,128)(2,1)S(1)}, bf16[256,512]{1,0:T(8,128)(2,1)S(1)}, u32[]{:S(2)}, u32[]{:S(2)}) collective-permute-start(bf16[256,512]{1,0:T(8,128)(2,1)S(1)} %get-tuple-element.48.kv_ref), channel_id=1, source_target_pairs={{0,2},{2,0},{4,6},{6,4},{8,10},{10,8},{12,14},{14,12},{1,3},{3,1},... | collective-permute-start | bytes 786440 | tf_op jit(solution)/shard_map/ppermute | solution.py:370
  22.7 9.8 %collective-permute-start.4 = (bf16[256,256]{1,0:T(8,128)(2,1)S(1)}, bf16[256,256]{1,0:T(8,128)(2,1)S(1)}, u32[]{:S(2)}, u32[]{:S(2)}) collective-permute-start(bf16[256,256]{1,0:T(8,128)(2,1)S(1)} %get-tuple-element.60), channel_id=1, source_target_pairs={{0,8},{2,10},{4,12},{6,14},{8,0},{10,2},{12,4},{14,6},{1,9},{3,11}... | collective-permute-start | bytes 393224 | tf_op jit(solution)/shard_map/ppermute | solution.py:370
  26.7 8.0 %collective-permute-start.6 = (bf16[256,256]{1,0:T(8,128)(2,1)S(1)}, bf16[256,256]{1,0:T(8,128)(2,1)S(1)}, u32[]{:S(2)}, u32[]{:S(2)}) collective-permute-start(bf16[256,256]{1,0:T(8,128)(2,1)S(1)} %get-tuple-element.60), channel_id=1, source_target_pairs={{0,12},{2,14},{4,8},{6,10},{8,4},{10,6},{12,0},{14,2},{1,13},{3,15... | collective-permute-start | bytes 393224 | tf_op jit(solution)/shard_map/ppermute | solution.py:370
  32.5 6.3 %collective-permute-start.8 = (bf16[256,256]{1,0:T(8,128)(2,1)S(1)}, bf16[256,256]{1,0:T(8,128)(2,1)S(1)}, u32[]{:S(2)}, u32[]{:S(2)}) collective-permute-start(bf16[256,256]{1,0:T(8,128)(2,1)S(1)} %collective-permute-done.4.refs_1_), channel_id=1, source_target_pairs={{0,16},{16,0},{1,17},{17,1},{2,18},{18,2},{3,19},{19,3},{4,20},{20... | collective-permute-start | bytes 393224 | tf_op jit(solution)/shard_map/ppermute | solution.py:328
  32.8 5.7 %collective-permute-start.7 = (bf16[256,256]{1,0:T(8,128)(2,1)S(1)}, bf16[256,256]{1,0:T(8,128)(2,1)S(1)}, u32[]{:S(2)}, u32[]{:S(2)}) collective-permute-start(bf16[256,256]{1,0:T(8,128)(2,1)S(1)} %collective-permute-done.4.refs_1_), channel_id=1, source_target_pairs={{0,2},{2,0},{4,6},{6,4},{8,10},{10,8},{12,14},{14,12},{1,3},{3,1},... | collective-permute-start | bytes 393224 | tf_op jit(solution)/shard_map/ppermute | solution.py:370
  34.6 9.4 %collective-permute-start.11 = (bf16[256,256]{1,0:T(8,128)(2,1)S(1)}, bf16[256,256]{1,0:T(8,128)(2,1)S(1)}, u32[]{:S(2)}, u32[]{:S(2)}) collective-permute-start(bf16[256,256]{1,0:T(8,128)(2,1)S(1)} %collective-permute-done.6.refs_1_), channel_id=1, source_target_pairs={{0,16},{16,0},{1,17},{17,1},{2,18},{18,2},{3,19},{19,3},{4,20},{20... | collective-permute-start | bytes 393224 | tf_op jit(solution)/shard_map/ppermute | solution.py:328
  35.9 6.8 %collective-permute-start.10 = (bf16[256,256]{1,0:T(8,128)(2,1)S(1)}, bf16[256,256]{1,0:T(8,128)(2,1)S(1)}, u32[]{:S(2)}, u32[]{:S(2)}) collective-permute-start(bf16[256,256]{1,0:T(8,128)(2,1)S(1)} %collective-permute-done.6.refs_1_), channel_id=1, source_target_pairs={{0,2},{2,0},{4,6},{6,4},{8,10},{10,8},{12,14},{14,12},{1,3},{3,1},... | collective-permute-start | bytes 393224 | tf_op jit(solution)/shard_map/ppermute | solution.py:370
  38.5 5.5 %collective-permute-start.12 = (bf16[256,256]{1,0:T(8,128)(2,1)S(1)}, bf16[256,256]{1,0:T(8,128)(2,1)S(1)}, u32[]{:S(2)}, u32[]{:S(2)}) collective-permute-start(bf16[256,256]{1,0:T(8,128)(2,1)S(1)} %collective-permute-done.7.refs_2_), channel_id=1, source_target_pairs={{0,16},{16,0},{1,17},{17,1},{2,18},{18,2},{3,19},{19,3},{4,20},{20... | collective-permute-start | bytes 393224 | tf_op jit(solution)/shard_map/ppermute | solution.py:328
  38.8 7.8 %collective-permute-start.9 = (bf16[256,512]{1,0:T(8,128)(2,1)S(1)}, bf16[256,512]{1,0:T(8,128)(2,1)S(1)}, u32[]{:S(2)}, u32[]{:S(2)}) collective-permute-start(bf16[256,512]{1,0:T(8,128)(2,1)S(1)} %collective-permute-done.5.refs_0_), channel_id=1, source_target_pairs={{0,2},{2,0},{4,6},{6,4},{8,10},{10,8},{12,14},{14,12},{1,3},{3,1},... | collective-permute-start | bytes 786440 | tf_op jit(solution)/shard_map/ppermute | solution.py:370
  38.9 16.0 %slice-start = ((s8[8388608]{0:T(1024)(128)(4,1)}), s8[4194304]{0:T(1024)(128)(4,1)S(1)}, s32[]{:S(2)}) async-start(s8[8388608]{0:T(1024)(128)(4,1)} %bitcast.8), calls=%async_computation | async-start | bytes 8388608
  42.7 7.7 %collective-permute-start.13 = (bf16[256,256]{1,0:T(8,128)(2,1)S(1)}, bf16[256,256]{1,0:T(8,128)(2,1)S(1)}, u32[]{:S(2)}, u32[]{:S(2)}) collective-permute-start(bf16[256,256]{1,0:T(8,128)(2,1)S(1)} %collective-permute-done.10.refs_1_), channel_id=1, source_target_pairs={{0,16},{16,0},{1,17},{17,1},{2,18},{18,2},{3,19},{19,3},{4,20},{20... | collective-permute-start | bytes 393224 | tf_op jit(solution)/shard_map/ppermute | solution.py:328
  46.6 8.2 %slice-start.1 = ((s8[8388608]{0:T(1024)(128)(4,1)}), s8[4194304]{0:T(1024)(128)(4,1)S(1)}, s32[]{:S(2)}) async-start(s8[8388608]{0:T(1024)(128)(4,1)} %bitcast.8), calls=%async_computation.1 | async-start | bytes 8388608
  52.5 5.3 %copy-start.1 = (s32[1,4]{1,0:T(1,128)S(1)}, s32[1,4]{1,0:T(1,128)}, u32[]{:S(2)}) copy-start(s32[1,4]{1,0:T(1,128)} %param.24) | copy-start | bytes 52
  52.5 5.3 %collective-permute-start.14 = (bf16[512,1024]{1,0:T(8,128)(2,1)S(1)}, bf16[512,1024]{1,0:T(8,128)(2,1)S(1)}, u32[]{:S(2)}, u32[]{:S(2)}) collective-permute-start(bf16[512,1024]{1,0:T(8,128)(2,1)S(1)} %get-tuple-element.69.heads), channel_id=1, source_target_pairs={{0,1},{1,0},{2,3},{3,2},{4,5},{5,4},{6,7},{7,6},{8,9},{9,8},{10,11... | collective-permute-start | bytes 3145736 | tf_op jit(solution)/shard_map/ppermute | solution.py:329

commit v10 on v9

--- a/solution.py
+++ b/solution.py
@@ -403,13 +403,13 @@
             over_y[offset], over_x[offset] = trade(column[offset], 1), cross_x(column[offset])
 
     turn(early, num)
-    num, den = attend(num, den, [((1, 2), beside)] + [((o, 0), column[o]) for o in early])
+    num, den = attend(num, den, [((1, 2), beside)])
     right = trade(after(left, num), 1)
     corner.update({o: cross_x(after(over_y[o], num)) for o in early})
     turn(late, num)
     num, den = attend(
         num, den,
-        [((2, 2), left)] + [((o, 0), column[o]) for o in late]
+        [((2, 2), left)] + [((o, 0), column[o]) for o in later]
         + [((o, 0), over_y[o]) for o in early] + [((o, 1), over_x[o]) for o in early],
     )
     corner.update({o: cross_x(after(over_y[o], num)) for o in late})

time: 61.9 us -> 61.3 us (level)
  starting transfers between devices: 17.1 us -> 16 us
    ppermute x7, starting transfers between devices: 7.76 us -> 6.63 us  [on_device(): lax.ppermute(v, 'ctx', [(i, i ^ offset) for i in range(ctx)])]
    ppermute x3, starting transfers between devices: 4.64 us -> 5.49 us  [on_device(): cross_core = lambda v: lax.ppermute(v, 'tp', pair)]
    ppermute x6, starting transfers between devices: 4.66 us -> 3.9 us  [on_device(): cross_x = lambda v: lax.ppermute(v, 'copy', pair)]
  transfers between devices with their start and end apart: 16 -> 16, of which waited for: 3 -> 5; matrix products, arithmetic and copies ran while one was open for 2% -> 2% of each run, Pallas kernels for 44% -> 45%
where the time goes in v10:
time: 61.3 us; the launch traced here: 60.8 us
  Pallas kernels  33.9 us (55%)
  starting transfers between devices  16 us (26%)
  waiting for transfers between devices  7.8 us (13%)
  between operations  1.6 us (3%)
  local copies, waits for them, and re-layouts  1.44 us (2%)
    pallas_call x11, Pallas kernels, call(): pl.pallas_call(kernel, grid_spec=pltpu.PrefetchScalarGridSpec(num_scalar_...  33.9 us
    ppermute x7, starting transfers between devices, on_device(): lax.ppermute(v, 'ctx', [(i, i ^ offset) for i in range(ctx)])  6.63 us
    ppermute x3, starting transfers between devices, on_device(): cross_core = lambda v: lax.ppermute(v, 'tp', pair)  5.49 us
    ppermute x6, starting transfers between devices, on_device(): cross_x = lambda v: lax.ppermute(v, 'copy', pair)  3.9 us
    ppermute x6, waiting for transfers between devices, on_device(): cross_x = lambda v: lax.ppermute(v, 'copy', pair)  3.18 us
    ppermute x7, waiting for transfers between devices, on_device(): lax.ppermute(v, 'ctx', [(i, i ^ offset) for i in range(ctx)])  3.08 us
    ppermute x3, waiting for transfers between devices, on_device(): cross_core = lambda v: lax.ppermute(v, 'tp', pair)  1.54 us
    broadcast_in_dim x2, local copies, waits for them, and re-layouts, on_device(): vectors = [norm_gain[None], mask_embed[None], shift]  1.42 us
  transfers between devices with their start and end apart: 16, of which 5 were waited for; matrix products, arithmetic and copies ran while one was open for 2% of the time, Pallas kernels for 45%

profile of v10, /device:TPU:25, one launch (start us, length us, event | category | flops | bytes accessed | tf_op | source)
XLA Modules:
  0.0 60.8 jit_solution(6902791380147343554)
XLA Ops:
  0.6 1.6 %shard_map.140 = (bf16[256,2048]{1,0:T(8,128)(2,1)S(1)}, s32[1,256]{1,0:T(1,128)S(1)}, f32[1,4096]{1,0:T(1,128)S(1)}, f32[1,256]{1,0:T(1,128)S(1)}, bf16[128,2048]{1,0:T(8,128)(2,1)S(1)}) custom-call(bf16[256,2048]{1,0:T(8,128)(2,1)} %x_hbm.1, s32[1,256]{1,0:T(1,128)} %mask_hbm.1, f32[1,4096]{1,0:T(1,128)} %bitcast.14), custom_call_target="tpu_custom_call" | custom-call | flops 1048576 | bytes 1048576 | tf_op jit(solution)/shard_map/pallas_call | solution.py:295
  2.2 1.3 %collective-permute-start.1 = (f32[1,256]{1,0:T(1,128)S(1)}, f32[1,256]{1,0:T(1,128)S(1)}, u32[]{:S(2)}, u32[]{:S(2)}) collective-permute-start(f32[1,256]{1,0:T(1,128)S(1)} %get-tuple-element.40.own_ref), channel_id=1, source_target_pairs={{0,16},{16,0},{1,17},{17,1},{2,18},{18,2},{3,19},{19,3},{4,20},{20... | collective-permute-start | bytes 3080 | tf_op jit(solution)/shard_map/ppermute | solution.py:328
  4.5 0.7 %broadcast_in_dim.19.gain_ref = bf16[1,4096]{1,0:T(2,128)(2,1)S(1)} reshape(bf16[4096]{0:T(1024)(128)(2,1)} %param.14) | data formatting | bytes 16384 | tf_op jit(solution)/shard_map/broadcast_in_dim | solution.py:348
  5.2 0.7 %broadcast_in_dim.20.embed_ref = bf16[1,4096]{1,0:T(2,128)(2,1)S(1)} reshape(bf16[4096]{0:T(1024)(128)(2,1)} %param.15) | data formatting | bytes 16384 | tf_op jit(solution)/shard_map/broadcast_in_dim | solution.py:348
  5.9 6.9 %shard_map.141 = (f32[512,1024]{1,0:T(8,128)S(1)}, f32[512,256]{1,0:T(8,128)S(1)}, f32[512,256]{1,0:T(8,128)S(1)}, bf16[2048,1024]{1,0:T(8,128)(2,1)S(1)}, bf16[...) custom-call(s32[4]{0:T(128)S(1)} %pad_add_fusion.info, ...), custom_call_target="tpu_custom_call" | custom-call | flops 25769803776 | bytes 12582912 | tf_op jit(solution)/shard_map/pallas_call | solution.py:295
  12.8 3.2 %collective-permute-done.near_ref = bf16[128,2048]{1,0:T(8,128)(2,1)S(1)} collective-permute-done((bf16[128,2048]{1,0:T(8,128)(2,1)S(1)}, bf16[128,2048]{1,0:T(8,128)(2,1)S(1)}, u32[]{:S(2)}, u32[]{:S(2)}) %collective-permute-start) | collective-permute-done | bytes 524320 | tf_op jit(solution)/shard_map/ppermute | solution.py:328
  16.0 1.9 %collective-permute-start.2 = (bf16[128,2048]{1,0:T(8,128)(2,1)S(1)}, bf16[128,2048]{1,0:T(8,128)(2,1)S(1)}, u32[]{:S(2)}, u32[]{:S(2)}) collective-permute-start(bf16[128,2048]{1,0:T(8,128)(2,1)S(1)} %collective-permute-done.near_ref), channel_id=1, source_target_pairs={{0,1},{1,0},{2,3},{3,2},{4,5},{5,4},{6,7},{7,6},{8,9},{9,8},{10,11... | collective-permute-start | bytes 1572872 | tf_op jit(solution)/shard_map/ppermute | solution.py:329
  17.8 1.5 %collective-permute-done.2.far_ref = bf16[128,2048]{1,0:T(8,128)(2,1)S(1)} collective-permute-done((bf16[128,2048]{1,0:T(8,128)(2,1)S(1)}, bf16[128,2048]{1,0:T(8,128)(2,1)S(1)}, u32[]{:S(2)}, u32[]{:S(2)}) %collective-permute-start.2) | collective-permute-done | bytes 524320 | tf_op jit(solution)/shard_map/ppermute | solution.py:329
  19.4 1.5 %shard_map.142 = (bf16[256,512]{1,0:T(8,128)(2,1)S(1)}, bf16[256,256]{1,0:T(8,128)(2,1)S(1)}) custom-call(s32[4]{0:T(128)S(1)} %pad_add_fusion.info, bf16[128,2048]{1,0:T(8,128)(2,1)S(1)} %collective-permute-done.near_ref, bf16[128,2048]{1,0:T(8,128)(2,1)S(1)} %collective-permute-done.2.far_ref, f32[1,256]{1,0:T(1,128)S(1)} %get-tuple-element.40.own_ref, ...), custom_call_target="tpu_custom_call" | custom-call | flops 536870912 | bytes 2097152 | tf_op jit(solution)/shard_map/pallas_call | solution.py:295
  21.5 1.2 %collective-permute-start.3 = (bf16[256,512]{1,0:T(8,128)(2,1)S(1)}, bf16[256,512]{1,0:T(8,128)(2,1)S(1)}, u32[]{:S(2)}, u32[]{:S(2)}) collective-permute-start(bf16[256,512]{1,0:T(8,128)(2,1)S(1)} %get-tuple-element.48.kv_ref), channel_id=1, source_target_pairs={{0,2},{2,0},{4,6},{6,4},{8,10},{10,8},{12,14},{14,12},{1,3},{3,1},... | collective-permute-start | bytes 786440 | tf_op jit(solution)/shard_map/ppermute | solution.py:370
  22.8 3.8 %shard_map.143 = (bf16[512,1024]{1,0:T(8,128)(2,1)S(1)}, bf16[256,512]{1,0:T(8,128)(2,1)S(1)}) custom-call(s32[4]{0:T(128)S(1)} %pad_add_fusion.info, bf16[128,2048]{1,0:T(8,128)(2,1)S(1)} %collective-permute-done.near_ref, bf16[128,2048]{1,0:T(8,128)(2,1)S(1)} %collective-permute-done.2.far_ref, f32[1,256]{1,0:T(1,128)S(1)} %get-tuple-element.40.own_ref, ...), custom_call_target="tpu_custom_call" | custom-call | flops 3221225472 | bytes 6291456 | tf_op jit(solution)/shard_map/pallas_call | solution.py:295
  26.7 3.3 %collective-permute-start.6 = (bf16[256,256]{1,0:T(8,128)(2,1)S(1)}, bf16[256,256]{1,0:T(8,128)(2,1)S(1)}, u32[]{:S(2)}, u32[]{:S(2)}) collective-permute-start(bf16[256,256]{1,0:T(8,128)(2,1)S(1)} %get-tuple-element.60), channel_id=1, source_target_pairs={{0,12},{2,14},{4,8},{6,10},{8,4},{10,6},{12,0},{14,2},{1,13},{3,15... | collective-permute-start | bytes 393224 | tf_op jit(solution)/shard_map/ppermute | solution.py:370
  30.0 2.5 %shard_map.144 = (f32[512,1024]{1,0:T(8,128)S(1)}, f32[512,1024]{1,0:T(8,128)S(1)}) custom-call(s32[4]{0:T(128)S(1)} %pad_add_fusion.info, bf16[512,1024]{1,0:T(8,128)(2,1)S(1)} %get-tuple-element.52.q_ref, bf16[256,512]{1,0:T(8,128)(2,1)S(1)} %get-tuple-element.48.kv_ref, bf16[256,512]{1,0:T(8,128)(2,1)S(1)} %get-tuple-element.53.self_ref), custom_call_target="tpu_custom_call" | custom-call | flops 3221225472 | bytes 4194304 | tf_op jit(solution)/shard_map/pallas_call | solution.py:295
  33.1 0.7 %shard_map.145 = (f32[512,1024]{1,0:T(8,128)S(1)}, f32[512,1024]{1,0:T(8,128)S(1)}) custom-call(s32[4]{0:T(128)S(1)} %pad_add_fusion.info, bf16[512,1024]{1,0:T(8,128)(2,1)S(1)} %get-tuple-element.52.q_ref, f32[512,1024]{1,0:T(8,128)S(1)} %get-tuple-element.54.num_in, ...), custom_call_target="tpu_custom_call", output_to_operand_aliasing={{0}: (2, {}), {1}: (3, {})} | custom-call | flops 1073741824 | bytes 4194304 | tf_op jit(solution)/shard_map/pallas_call | solution.py:295
  35.1 1.3 %collective-permute-done.7.refs_3_ = bf16[256,256]{1,0:T(8,128)(2,1)S(1)} collective-permute-done((bf16[256,256]{1,0:T(8,128)(2,1)S(1)}, bf16[256,256]{1,0:T(8,128)(2,1)S(1)}, u32[]{:S(2)}, u32[]{:S(2)}) %collective-permute-start.7) | collective-permute-done | bytes 131104 | tf_op jit(solution)/shard_map/ppermute | solution.py:370
  36.4 1.3 %collective-permute-start.10 = (bf16[256,256]{1,0:T(8,128)(2,1)S(1)}, bf16[256,256]{1,0:T(8,128)(2,1)S(1)}, u32[]{:S(2)}, u32[]{:S(2)}) collective-permute-start(bf16[256,256]{1,0:T(8,128)(2,1)S(1)} %collective-permute-done.6.refs_2_), channel_id=1, source_target_pairs={{0,2},{2,0},{4,6},{6,4},{8,10},{10,8},{12,14},{14,12},{1,3},{3,1},... | collective-permute-start | bytes 393224 | tf_op jit(solution)/shard_map/ppermute | solution.py:370
  38.2 4.5 %shard_map.146 = (f32[512,1024]{1,0:T(8,128)S(1)}, f32[512,1024]{1,0:T(8,128)S(1)}) custom-call(s32[4]{0:T(128)S(1)} %pad_add_fusion.info, bf16[512,1024]{1,0:T(8,128)(2,1)S(1)} %get-tuple-element.52.q_ref, f32[512,1024]{1,0:T(8,128)S(1)} %get-tuple-element.56.num_in, ...), custom_call_target="tpu_custom_call", output_to_operand_aliasing={{0}: (2, {}), {1}: (3, {})} | custom-call | flops 5368709120 | bytes 4194304 | tf_op jit(solution)/shard_map/pallas_call | solution.py:295
  42.6 1.2 %collective-permute-start.13 = (bf16[256,256]{1,0:T(8,128)(2,1)S(1)}, bf16[256,256]{1,0:T(8,128)(2,1)S(1)}, u32[]{:S(2)}, u32[]{:S(2)}) collective-permute-start(bf16[256,256]{1,0:T(8,128)(2,1)S(1)} %collective-permute-done.10.refs_1_), channel_id=1, source_target_pairs={{0,16},{16,0},{1,17},{17,1},{2,18},{18,2},{3,19},{19,3},{4,20},{20... | collective-permute-start | bytes 393224 | tf_op jit(solution)/shard_map/ppermute | solution.py:328
  43.9 1.1 %collective-permute-done.9.refs_0_ = bf16[256,512]{1,0:T(8,128)(2,1)S(1)} collective-permute-done((bf16[256,512]{1,0:T(8,128)(2,1)S(1)}, bf16[256,512]{1,0:T(8,128)(2,1)S(1)}, u32[]{:S(2)}, u32[]{:S(2)}) %collective-permute-start.9) | collective-permute-done | bytes 262176 | tf_op jit(solution)/shard_map/ppermute | solution.py:370
  45.0 3.9 %shard_map.147 = (f32[512,1024]{1,0:T(8,128)S(1)}, f32[512,1024]{1,0:T(8,128)S(1)}) custom-call(s32[4]{0:T(128)S(1)} %pad_add_fusion.info, bf16[512,1024]{1,0:T(8,128)(2,1)S(1)} %get-tuple-element.52.q_ref, f32[512,1024]{1,0:T(8,128)S(1)} %get-tuple-element.62.num_in, ...), custom_call_target="tpu_custom_call", output_to_operand_aliasing={{0}: (2, {}), {1}: (3, {})} | custom-call | flops 4294967296 | bytes 4194304 | tf_op jit(solution)/shard_map/pallas_call | solution.py:295
  48.8 2.0 %shard_map.148 = (f32[512,1024]{1,0:T(8,128)S(1)}, f32[512,1024]{1,0:T(8,128)S(1)}, bf16[512,1024]{1,0:T(8,128)(2,1)S(1)}) custom-call(s32[4]{0:T(128)S(1)} %pad_add_fusion.info, bf16[512,1024]{1,0:T(8,128)(2,1)S(1)} %get-tuple-element.52.q_ref, f32[512,1024]{1,0:T(8,128)S(1)} %get-tuple-element.66.num_in, ...), custom_call_target="tpu_custom_call", output_to_operand_aliasing={{0}: (2, {}), {1}: (3, {})} | custom-call | flops 1073741824 | bytes 4194304 | tf_op jit(solution)/shard_map/pallas_call | solution.py:295
  50.8 3.2 %collective-permute-start.14 = (bf16[512,1024]{1,0:T(8,128)(2,1)S(1)}, bf16[512,1024]{1,0:T(8,128)(2,1)S(1)}, u32[]{:S(2)}, u32[]{:S(2)}) collective-permute-start(bf16[512,1024]{1,0:T(8,128)(2,1)S(1)} %get-tuple-element.69.heads), channel_id=1, source_target_pairs={{0,1},{1,0},{2,3},{3,2},{4,5},{5,4},{6,7},{7,6},{8,9},{9,8},{10,11... | collective-permute-start | bytes 3145736 | tf_op jit(solution)/shard_map/ppermute | solution.py:329
  54.1 2.9 %shard_map.149.mixed_ref = f32[512,2048]{1,0:T(8,128)S(1)} custom-call(s32[4]{0:T(128)S(1)} %pad_add_fusion.info, bf16[512,1024]{1,0:T(8,128)(2,1)S(1)} %get-tuple-element.69.heads, bf16[1024,4096]{1,0:T(8,128)(2,1)S(1)} %bitcast.9), custom_call_target="tpu_custom_call" | custom-call | flops 2147483648 | bytes 4194304 | tf_op jit(solution)/shard_map/pallas_call | solution.py:295
  57.0 3.7 %shard_map.150 = (bf16[256,2048]{1,0:T(8,128)(2,1)}, bf16[256,2048]{1,0:T(8,128)(2,1)}) custom-call(s32[4]{0:T(128)S(1)} %pad_add_fusion.info, s32[4]{0:T(128)S(1)} %bitcast.12, bf16[512,1024]{1,0:T(8,128)(2,1)S(1)} %collective-permute-done.14.heads, f32[512,2048]{1,0:T(8,128)S(1)} %shard_map.149.mixed_ref, bf16[1024,2048]{1,0:T(8,128)(2,1)S(1)} %collective-permute-done.15.w_far), custom_call_target="tpu_custom_call" | custom-call | flops 2147483648 | bytes 4194304 | tf_op jit(solution)/shard_map/pallas_call | solution.py:295
  (33 shorter events, 3.4 us)
Async XLA Ops:
  2.2 3.7 %collective-permute-start.1 = (f32[1,256]{1,0:T(1,128)S(1)}, f32[1,256]{1,0:T(1,128)S(1)}, u32[]{:S(2)}, u32[]{:S(2)}) collective-permute-start(f32[1,256]{1,0:T(1,128)S(1)} %get-tuple-element.40.own_ref), channel_id=1, source_target_pairs={{0,16},{16,0},{1,17},{17,1},{2,18},{18,2},{3,19},{19,3},{4,20},{20... | collective-permute-start | bytes 3080 | tf_op jit(solution)/shard_map/ppermute | solution.py:328
  3.5 12.5 %collective-permute-start = (bf16[128,2048]{1,0:T(8,128)(2,1)S(1)}, bf16[128,2048]{1,0:T(8,128)(2,1)S(1)}, u32[]{:S(2)}, u32[]{:S(2)}) collective-permute-start(bf16[128,2048]{1,0:T(8,128)(2,1)S(1)} %get-tuple-element.38), channel_id=1, source_target_pairs={{0,16},{16,0},{1,17},{17,1},{2,18},{18,2},{3,19},{19,3},{4,20},{20... | collective-permute-start | bytes 1572872 | tf_op jit(solution)/shard_map/ppermute | solution.py:328
  5.9 13.5 %copy-start = (f32[128]{0:T(128)S(1)}, f32[128]{0:T(128)}, u32[]{:S(2)}) copy-start(f32[128]{0:T(128)} %param.22) | copy-start | bytes 1540
  16.0 3.4 %collective-permute-start.2 = (bf16[128,2048]{1,0:T(8,128)(2,1)S(1)}, bf16[128,2048]{1,0:T(8,128)(2,1)S(1)}, u32[]{:S(2)}, u32[]{:S(2)}) collective-permute-start(bf16[128,2048]{1,0:T(8,128)(2,1)S(1)} %collective-permute-done.near_ref), channel_id=1, source_target_pairs={{0,1},{1,0},{2,3},{3,2},{4,5},{5,4},{6,7},{7,6},{8,9},{9,8},{10,11... | collective-permute-start | bytes 1572872 | tf_op jit(solution)/shard_map/ppermute | solution.py:329
  19.4 3.5 %copy-start.2 = (f32[128]{0:T(128)S(1)}, f32[128]{0:T(128)}, u32[]{:S(2)}) copy-start(f32[128]{0:T(128)} %param.21) | copy-start | bytes 1540
  20.9 36.1 %collective-permute-start.15 = (bf16[1024,2048]{1,0:T(8,128)(2,1)S(1)}, bf16[1024,2048]{1,0:T(8,128)(2,1)S(1)}, u32[]{:S(2)}, u32[]{:S(2)}) collective-permute-start(bf16[1024,2048]{1,0:T(8,128)(2,1)S(1)} %get-tuple-element.71), channel_id=1, source_target_pairs={{0,1},{1,0},{2,3},{3,2},{4,5},{5,4},{6,7},{7,6},{8,9},{9,8},{10,11... | collective-permute-start | bytes 12582920 | tf_op jit(solution)/shard_map/ppermute | solution.py:329
  21.3 16.4 %collective-permute-start.4 = (bf16[256,512]{1,0:T(8,128)(2,1)S(1)}, bf16[256,512]{1,0:T(8,128)(2,1)S(1)}, u32[]{:S(2)}, u32[]{:S(2)}) collective-permute-start(bf16[256,512]{1,0:T(8,128)(2,1)S(1)} %get-tuple-element.48.kv_ref), channel_id=1, source_target_pairs={{0,4},{2,6},{4,0},{6,2},{8,12},{10,14},{12,8},{14,10},{1,5},{3,7},... | collective-permute-start | bytes 786440 | tf_op jit(solution)/shard_map/ppermute | solution.py:370
  21.5 11.3 %collective-permute-start.3 = (bf16[256,512]{1,0:T(8,128)(2,1)S(1)}, bf16[256,512]{1,0:T(8,128)(2,1)S(1)}, u32[]{:S(2)}, u32[]{:S(2)}) collective-permute-start(bf16[256,512]{1,0:T(8,128)(2,1)S(1)} %get-tuple-element.48.kv_ref), channel_id=1, source_target_pairs={{0,2},{2,0},{4,6},{6,4},{8,10},{10,8},{12,14},{14,12},{1,3},{3,1},... | collective-permute-start | bytes 786440 | tf_op jit(solution)/shard_map/ppermute | solution.py:370
  22.7 9.8 %collective-permute-start.5 = (bf16[256,256]{1,0:T(8,128)(2,1)S(1)}, bf16[256,256]{1,0:T(8,128)(2,1)S(1)}, u32[]{:S(2)}, u32[]{:S(2)}) collective-permute-start(bf16[256,256]{1,0:T(8,128)(2,1)S(1)} %get-tuple-element.60), channel_id=1, source_target_pairs={{0,8},{2,10},{4,12},{6,14},{8,0},{10,2},{12,4},{14,6},{1,9},{3,11}... | collective-permute-start | bytes 393224 | tf_op jit(solution)/shard_map/ppermute | solution.py:370
  26.7 7.8 %collective-permute-start.6 = (bf16[256,256]{1,0:T(8,128)(2,1)S(1)}, bf16[256,256]{1,0:T(8,128)(2,1)S(1)}, u32[]{:S(2)}, u32[]{:S(2)}) collective-permute-start(bf16[256,256]{1,0:T(8,128)(2,1)S(1)} %get-tuple-element.60), channel_id=1, source_target_pairs={{0,12},{2,14},{4,8},{6,10},{8,4},{10,6},{12,0},{14,2},{1,13},{3,15... | collective-permute-start | bytes 393224 | tf_op jit(solution)/shard_map/ppermute | solution.py:370
  32.5 3.9 %collective-permute-start.7 = (bf16[256,256]{1,0:T(8,128)(2,1)S(1)}, bf16[256,256]{1,0:T(8,128)(2,1)S(1)}, u32[]{:S(2)}, u32[]{:S(2)}) collective-permute-start(bf16[256,256]{1,0:T(8,128)(2,1)S(1)} %collective-permute-done.5.refs_1_), channel_id=1, source_target_pairs={{0,2},{2,0},{4,6},{6,4},{8,10},{10,8},{12,14},{14,12},{1,3},{3,1},... | collective-permute-start | bytes 393224 | tf_op jit(solution)/shard_map/ppermute | solution.py:370
  32.8 5.2 %collective-permute-start.8 = (bf16[256,256]{1,0:T(8,128)(2,1)S(1)}, bf16[256,256]{1,0:T(8,128)(2,1)S(1)}, u32[]{:S(2)}, u32[]{:S(2)}) collective-permute-start(bf16[256,256]{1,0:T(8,128)(2,1)S(1)} %collective-permute-done.5.refs_1_), channel_id=1, source_target_pairs={{0,16},{16,0},{1,17},{17,1},{2,18},{18,2},{3,19},{19,3},{4,20},{20... | collective-permute-start | bytes 393224 | tf_op jit(solution)/shard_map/ppermute | solution.py:328
  34.5 9.4 %collective-permute-start.11 = (bf16[256,256]{1,0:T(8,128)(2,1)S(1)}, bf16[256,256]{1,0:T(8,128)(2,1)S(1)}, u32[]{:S(2)}, u32[]{:S(2)}) collective-permute-start(bf16[256,256]{1,0:T(8,128)(2,1)S(1)} %collective-permute-done.6.refs_2_), channel_id=1, source_target_pairs={{0,16},{16,0},{1,17},{17,1},{2,18},{18,2},{3,19},{19,3},{4,20},{20... | collective-permute-start | bytes 393224 | tf_op jit(solution)/shard_map/ppermute | solution.py:328
  36.4 6.2 %collective-permute-start.10 = (bf16[256,256]{1,0:T(8,128)(2,1)S(1)}, bf16[256,256]{1,0:T(8,128)(2,1)S(1)}, u32[]{:S(2)}, u32[]{:S(2)}) collective-permute-start(bf16[256,256]{1,0:T(8,128)(2,1)S(1)} %collective-permute-done.6.refs_2_), channel_id=1, source_target_pairs={{0,2},{2,0},{4,6},{6,4},{8,10},{10,8},{12,14},{14,12},{1,3},{3,1},... | collective-permute-start | bytes 393224 | tf_op jit(solution)/shard_map/ppermute | solution.py:370
  37.7 6.2 %collective-permute-start.12 = (bf16[256,256]{1,0:T(8,128)(2,1)S(1)}, bf16[256,256]{1,0:T(8,128)(2,1)S(1)}, u32[]{:S(2)}, u32[]{:S(2)}) collective-permute-start(bf16[256,256]{1,0:T(8,128)(2,1)S(1)} %collective-permute-done.7.refs_3_), channel_id=1, source_target_pairs={{0,16},{16,0},{1,17},{17,1},{2,18},{18,2},{3,19},{19,3},{4,20},{20... | collective-permute-start | bytes 393224 | tf_op jit(solution)/shard_map/ppermute | solution.py:328
  38.0 7.0 %collective-permute-start.9 = (bf16[256,512]{1,0:T(8,128)(2,1)S(1)}, bf16[256,512]{1,0:T(8,128)(2,1)S(1)}, u32[]{:S(2)}, u32[]{:S(2)}) collective-permute-start(bf16[256,512]{1,0:T(8,128)(2,1)S(1)} %collective-permute-done.4.refs_0_), channel_id=1, source_target_pairs={{0,2},{2,0},{4,6},{6,4},{8,10},{10,8},{12,14},{14,12},{1,3},{3,1},... | collective-permute-start | bytes 786440 | tf_op jit(solution)/shard_map/ppermute | solution.py:370
  38.2 15.9 %slice-start = ((s8[8388608]{0:T(1024)(128)(4,1)}), s8[4194304]{0:T(1024)(128)(4,1)S(1)}, s32[]{:S(2)}) async-start(s8[8388608]{0:T(1024)(128)(4,1)} %bitcast.8), calls=%async_computation | async-start | bytes 8388608
  42.6 6.2 %collective-permute-start.13 = (bf16[256,256]{1,0:T(8,128)(2,1)S(1)}, bf16[256,256]{1,0:T(8,128)(2,1)S(1)}, u32[]{:S(2)}, u32[]{:S(2)}) collective-permute-start(bf16[256,256]{1,0:T(8,128)(2,1)S(1)} %collective-permute-done.10.refs_1_), channel_id=1, source_target_pairs={{0,16},{16,0},{1,17},{17,1},{2,18},{18,2},{3,19},{19,3},{4,20},{20... | collective-permute-start | bytes 393224 | tf_op jit(solution)/shard_map/ppermute | solution.py:328
  45.0 9.1 %slice-start.1 = ((s8[8388608]{0:T(1024)(128)(4,1)}), s8[4194304]{0:T(1024)(128)(4,1)S(1)}, s32[]{:S(2)}) async-start(s8[8388608]{0:T(1024)(128)(4,1)} %bitcast.8), calls=%async_computation.1 | async-start | bytes 8388608
  50.8 6.2 %copy-start.1 = (s32[1,4]{1,0:T(1,128)S(1)}, s32[1,4]{1,0:T(1,128)}, u32[]{:S(2)}) copy-start(s32[1,4]{1,0:T(1,128)} %param.24) | copy-start | bytes 52
  50.8 6.1 %collective-permute-start.14 = (bf16[512,1024]{1,0:T(8,128)(2,1)S(1)}, bf16[512,1024]{1,0:T(8,128)(2,1)S(1)}, u32[]{:S(2)}, u32[]{:S(2)}) collective-permute-start(bf16[512,1024]{1,0:T(8,128)(2,1)S(1)} %get-tuple-element.69.heads), channel_id=1, source_target_pairs={{0,1},{1,0},{2,3},{3,2},{4,5},{5,4},{6,7},{7,6},{8,9},{9,8},{10,11... | collective-permute-start | bytes 3145736 | tf_op jit(solution)/shard_map/ppermute | solution.py:329

commit v11 on v10

--- a/solution.py
+++ b/solution.py
@@ -236,9 +236,9 @@
                 den_ref[rows:, cols] += den[number * rows : (number + 1) * rows]
 
 
-def attention_kernel(info, q_ref, num_in, den_in, *refs, pieces):
+def attention_kernel(info, q_ref, num_in, den_in, *refs, pieces, end):
     count = len(pieces)
-    num_ref, den_ref = refs[count : count + 2]
+    num_ref, den_ref, out_ref = (*refs[-3:],) if end is not None else (*refs[-2:], None)
     width = q_ref.shape[1] // 2
     heads = width // HD
     for bit in sorted({offset.bit_length() for offset, _ in pieces}):
@@ -255,11 +255,10 @@
                 cols = slice(2 * kv_head * HD, 2 * (kv_head + 1) * HD)
                 add_pieces(q_ref, num_ref, den_ref, kv_head * width, heads, [ref[:, cols] for ref in found])
 
-    for out_ref in refs[count + 2 :]:
-        for start in range(0, q_ref.shape[1], HD):
-            cols = slice(start, start + HD)
-            total = jnp.sum(den_ref[:, cols], axis=1, keepdims=True)
-            out_ref[:, cols] = (num_ref[:, cols] / total).astype(BF16)
+    for head in range(heads if end is not None else 0):
+        cols = pl.ds(head_base(info, end, width) + head * HD, HD)
+        total = jnp.sum(den_ref[:, cols], axis=1, keepdims=True)
+        out_ref[:, cols] = (num_ref[:, cols] / total).astype(BF16)
 
 
 def out_first_kernel(info, heads, w_out, mixed_ref, *, tile):
@@ -388,11 +387,13 @@
     cost = lambda units: (16 * HD * unit * units, 8 * unit, (), unit * units)
     in_place = {2: 0, 3: 1}
     num, den = call(attention_own_kernel, [info], [WHOLE] * 3, acc, [q, kv, own], *cost(3))
-    def attend(num, den, pieces, outs=()):
+    def attend(num, den, pieces, end=None, before=()):
+        outs = [] if end is None else [vmem((2 * rows, heads_width), BF16)]
+        aliases = {**in_place, 4 + len(pieces): 2} if before else in_place
         return call(
-            functools.partial(attention_kernel, pieces=tuple(key for key, _ in pieces)), [info],
-            [WHOLE] * (3 + len(pieces)), acc + list(outs),
-            [q, num, den] + [piece for _, piece in pieces], *cost(len(pieces)), aliases=in_place,
+            functools.partial(attention_kernel, pieces=tuple(key for key, _ in pieces), end=end), [info],
+            [WHOLE] * (3 + len(pieces) + len(before)), acc + outs,
+            [q, num, den] + [piece for _, piece in pieces] + list(before), *cost(len(pieces)), aliases=aliases,
         )
 
     over_x, over_y, corner = {}, {}, {}
@@ -413,13 +414,13 @@
         + [((o, 0), over_y[o]) for o in early] + [((o, 1), over_x[o]) for o in early],
     )
     corner.update({o: cross_x(after(over_y[o], num)) for o in late})
-    num, den = attend(
+    num, den, near_heads = attend(
         num, den,
         [((3, 2), right)] + [((o, 0), over_y[o]) for o in late]
-        + [((o, 1), over_x[o]) for o in late] + [((o, 1), corner[o]) for o in early],
+        + [((o, 1), over_x[o]) for o in late] + [((o, 1), corner[o]) for o in early], 0,
     )
     num, den, near_heads = attend(
-        num, den, [((o, 1), corner[o]) for o in late], [vmem((2 * rows, heads_width), BF16)]
+        num, den, [((o, 1), corner[o]) for o in late], 1, [near_heads]
     )
     far_heads = cross_core(near_heads)
 

time: 61.3 us -> 61.4 us (level)
  no operation moved by 1% of the time
where the time goes in v11:
time: 61.4 us; the launch traced here: 61 us
  Pallas kernels  34 us (55%)
  starting transfers between devices  16 us (26%)
  waiting for transfers between devices  7.77 us (13%)
  between operations  1.61 us (3%)
  local copies, waits for them, and re-layouts  1.44 us (2%)
    pallas_call x11, Pallas kernels, call(): pl.pallas_call(kernel, grid_spec=pltpu.PrefetchScalarGridSpec(num_scalar_...  34 us
    ppermute x7, starting transfers between devices, on_device(): lax.ppermute(v, 'ctx', [(i, i ^ offset) for i in range(ctx)])  6.63 us
    ppermute x3, starting transfers between devices, on_device(): cross_core = lambda v: lax.ppermute(v, 'tp', pair)  5.5 us
    ppermute x6, starting transfers between devices, on_device(): cross_x = lambda v: lax.ppermute(v, 'copy', pair)  3.91 us
    ppermute x6, waiting for transfers between devices, on_device(): cross_x = lambda v: lax.ppermute(v, 'copy', pair)  3.18 us
    ppermute x7, waiting for transfers between devices, on_device(): lax.ppermute(v, 'ctx', [(i, i ^ offset) for i in range(ctx)])  3.05 us
    ppermute x3, waiting for transfers between devices, on_device(): cross_core = lambda v: lax.ppermute(v, 'tp', pair)  1.54 us
    broadcast_in_dim x2, local copies, waits for them, and re-layouts, on_device(): vectors = [norm_gain[None], mask_embed[None], shift]  1.42 us
  transfers between devices with their start and end apart: 16, of which 5 were waited for; matrix products, arithmetic and copies ran while one was open for 2% of the time, Pallas kernels for 45%

profile of v11, /device:TPU:25, one launch (start us, length us, event | category | flops | bytes accessed | tf_op | source)
XLA Modules:
  0.0 61.0 jit_solution(17614978849815794859)
XLA Ops:
  0.6 1.6 %shard_map.140 = (bf16[256,2048]{1,0:T(8,128)(2,1)S(1)}, s32[1,256]{1,0:T(1,128)S(1)}, f32[1,4096]{1,0:T(1,128)S(1)}, f32[1,256]{1,0:T(1,128)S(1)}, bf16[128,2048]{1,0:T(8,128)(2,1)S(1)}) custom-call(bf16[256,2048]{1,0:T(8,128)(2,1)} %x_hbm.1, s32[1,256]{1,0:T(1,128)} %mask_hbm.1, f32[1,4096]{1,0:T(1,128)} %bitcast.14), custom_call_target="tpu_custom_call" | custom-call | flops 1048576 | bytes 1048576 | tf_op jit(solution)/shard_map/pallas_call | solution.py:294
  2.2 1.3 %collective-permute-start.1 = (f32[1,256]{1,0:T(1,128)S(1)}, f32[1,256]{1,0:T(1,128)S(1)}, u32[]{:S(2)}, u32[]{:S(2)}) collective-permute-start(f32[1,256]{1,0:T(1,128)S(1)} %get-tuple-element.41.own_ref), channel_id=1, source_target_pairs={{0,16},{16,0},{1,17},{17,1},{2,18},{18,2},{3,19},{19,3},{4,20},{20... | collective-permute-start | bytes 3080 | tf_op jit(solution)/shard_map/ppermute | solution.py:327
  4.5 0.7 %broadcast_in_dim.19.gain_ref = bf16[1,4096]{1,0:T(2,128)(2,1)S(1)} reshape(bf16[4096]{0:T(1024)(128)(2,1)} %param.14) | data formatting | bytes 16384 | tf_op jit(solution)/shard_map/broadcast_in_dim | solution.py:347
  5.2 0.7 %broadcast_in_dim.20.embed_ref = bf16[1,4096]{1,0:T(2,128)(2,1)S(1)} reshape(bf16[4096]{0:T(1024)(128)(2,1)} %param.15) | data formatting | bytes 16384 | tf_op jit(solution)/shard_map/broadcast_in_dim | solution.py:347
  5.9 6.9 %shard_map.141 = (f32[512,1024]{1,0:T(8,128)S(1)}, f32[512,256]{1,0:T(8,128)S(1)}, f32[512,256]{1,0:T(8,128)S(1)}, bf16[2048,1024]{1,0:T(8,128)(2,1)S(1)}, bf16[...) custom-call(s32[4]{0:T(128)S(1)} %pad_add_fusion.info, ...), custom_call_target="tpu_custom_call" | custom-call | flops 25769803776 | bytes 12582912 | tf_op jit(solution)/shard_map/pallas_call | solution.py:294
  12.8 3.2 %collective-permute-done.near_ref = bf16[128,2048]{1,0:T(8,128)(2,1)S(1)} collective-permute-done((bf16[128,2048]{1,0:T(8,128)(2,1)S(1)}, bf16[128,2048]{1,0:T(8,128)(2,1)S(1)}, u32[]{:S(2)}, u32[]{:S(2)}) %collective-permute-start) | collective-permute-done | bytes 524320 | tf_op jit(solution)/shard_map/ppermute | solution.py:327
  16.0 1.9 %collective-permute-start.2 = (bf16[128,2048]{1,0:T(8,128)(2,1)S(1)}, bf16[128,2048]{1,0:T(8,128)(2,1)S(1)}, u32[]{:S(2)}, u32[]{:S(2)}) collective-permute-start(bf16[128,2048]{1,0:T(8,128)(2,1)S(1)} %collective-permute-done.near_ref), channel_id=1, source_target_pairs={{0,1},{1,0},{2,3},{3,2},{4,5},{5,4},{6,7},{7,6},{8,9},{9,8},{10,11... | collective-permute-start | bytes 1572872 | tf_op jit(solution)/shard_map/ppermute | solution.py:328
  17.8 1.5 %collective-permute-done.2.far_ref = bf16[128,2048]{1,0:T(8,128)(2,1)S(1)} collective-permute-done((bf16[128,2048]{1,0:T(8,128)(2,1)S(1)}, bf16[128,2048]{1,0:T(8,128)(2,1)S(1)}, u32[]{:S(2)}, u32[]{:S(2)}) %collective-permute-start.2) | collective-permute-done | bytes 524320 | tf_op jit(solution)/shard_map/ppermute | solution.py:328
  19.4 1.5 %shard_map.142 = (bf16[256,512]{1,0:T(8,128)(2,1)S(1)}, bf16[256,256]{1,0:T(8,128)(2,1)S(1)}) custom-call(s32[4]{0:T(128)S(1)} %pad_add_fusion.info, bf16[128,2048]{1,0:T(8,128)(2,1)S(1)} %collective-permute-done.near_ref, bf16[128,2048]{1,0:T(8,128)(2,1)S(1)} %collective-permute-done.2.far_ref, f32[1,256]{1,0:T(1,128)S(1)} %get-tuple-element.41.own_ref, ...), custom_call_target="tpu_custom_call" | custom-call | flops 536870912 | bytes 2097152 | tf_op jit(solution)/shard_map/pallas_call | solution.py:294
  21.5 1.2 %collective-permute-start.3 = (bf16[256,512]{1,0:T(8,128)(2,1)S(1)}, bf16[256,512]{1,0:T(8,128)(2,1)S(1)}, u32[]{:S(2)}, u32[]{:S(2)}) collective-permute-start(bf16[256,512]{1,0:T(8,128)(2,1)S(1)} %get-tuple-element.49.kv_ref), channel_id=1, source_target_pairs={{0,2},{2,0},{4,6},{6,4},{8,10},{10,8},{12,14},{14,12},{1,3},{3,1},... | collective-permute-start | bytes 786440 | tf_op jit(solution)/shard_map/ppermute | solution.py:369
  22.8 3.8 %shard_map.143 = (bf16[512,1024]{1,0:T(8,128)(2,1)S(1)}, bf16[256,512]{1,0:T(8,128)(2,1)S(1)}) custom-call(s32[4]{0:T(128)S(1)} %pad_add_fusion.info, bf16[128,2048]{1,0:T(8,128)(2,1)S(1)} %collective-permute-done.near_ref, bf16[128,2048]{1,0:T(8,128)(2,1)S(1)} %collective-permute-done.2.far_ref, f32[1,256]{1,0:T(1,128)S(1)} %get-tuple-element.41.own_ref, ...), custom_call_target="tpu_custom_call" | custom-call | flops 3221225472 | bytes 6291456 | tf_op jit(solution)/shard_map/pallas_call | solution.py:294
  26.7 3.3 %collective-permute-start.6 = (bf16[256,256]{1,0:T(8,128)(2,1)S(1)}, bf16[256,256]{1,0:T(8,128)(2,1)S(1)}, u32[]{:S(2)}, u32[]{:S(2)}) collective-permute-start(bf16[256,256]{1,0:T(8,128)(2,1)S(1)} %get-tuple-element.61), channel_id=1, source_target_pairs={{0,12},{2,14},{4,8},{6,10},{8,4},{10,6},{12,0},{14,2},{1,13},{3,15... | collective-permute-start | bytes 393224 | tf_op jit(solution)/shard_map/ppermute | solution.py:369
  30.0 2.5 %shard_map.144 = (f32[512,1024]{1,0:T(8,128)S(1)}, f32[512,1024]{1,0:T(8,128)S(1)}) custom-call(s32[4]{0:T(128)S(1)} %pad_add_fusion.info, bf16[512,1024]{1,0:T(8,128)(2,1)S(1)} %get-tuple-element.53.q_ref, bf16[256,512]{1,0:T(8,128)(2,1)S(1)} %get-tuple-element.49.kv_ref, bf16[256,512]{1,0:T(8,128)(2,1)S(1)} %get-tuple-element.54.self_ref), custom_call_target="tpu_custom_call" | custom-call | flops 3221225472 | bytes 4194304 | tf_op jit(solution)/shard_map/pallas_call | solution.py:294
  33.1 0.7 %shard_map.145 = (f32[512,1024]{1,0:T(8,128)S(1)}, f32[512,1024]{1,0:T(8,128)S(1)}) custom-call(s32[4]{0:T(128)S(1)} %pad_add_fusion.info, bf16[512,1024]{1,0:T(8,128)(2,1)S(1)} %get-tuple-element.53.q_ref, f32[512,1024]{1,0:T(8,128)S(1)} %get-tuple-element.55.num_in, ...), custom_call_target="tpu_custom_call", output_to_operand_aliasing={{0}: (2, {}), {1}: (3, {})} | custom-call | flops 1073741824 | bytes 4194304 | tf_op jit(solution)/shard_map/pallas_call | solution.py:294
  35.1 1.3 %collective-permute-done.7.refs_3_ = bf16[256,256]{1,0:T(8,128)(2,1)S(1)} collective-permute-done((bf16[256,256]{1,0:T(8,128)(2,1)S(1)}, bf16[256,256]{1,0:T(8,128)(2,1)S(1)}, u32[]{:S(2)}, u32[]{:S(2)}) %collective-permute-start.7) | collective-permute-done | bytes 131104 | tf_op jit(solution)/shard_map/ppermute | solution.py:369
  36.4 1.3 %collective-permute-start.10 = (bf16[256,256]{1,0:T(8,128)(2,1)S(1)}, bf16[256,256]{1,0:T(8,128)(2,1)S(1)}, u32[]{:S(2)}, u32[]{:S(2)}) collective-permute-start(bf16[256,256]{1,0:T(8,128)(2,1)S(1)} %collective-permute-done.6.refs_2_), channel_id=1, source_target_pairs={{0,2},{2,0},{4,6},{6,4},{8,10},{10,8},{12,14},{14,12},{1,3},{3,1},... | collective-permute-start | bytes 393224 | tf_op jit(solution)/shard_map/ppermute | solution.py:369
  38.2 4.4 %shard_map.146 = (f32[512,1024]{1,0:T(8,128)S(1)}, f32[512,1024]{1,0:T(8,128)S(1)}) custom-call(s32[4]{0:T(128)S(1)} %pad_add_fusion.info, bf16[512,1024]{1,0:T(8,128)(2,1)S(1)} %get-tuple-element.53.q_ref, f32[512,1024]{1,0:T(8,128)S(1)} %get-tuple-element.57.num_in, ...), custom_call_target="tpu_custom_call", output_to_operand_aliasing={{0}: (2, {}), {1}: (3, {})} | custom-call | flops 5368709120 | bytes 4194304 | tf_op jit(solution)/shard_map/pallas_call | solution.py:294
  42.6 1.2 %collective-permute-start.13 = (bf16[256,256]{1,0:T(8,128)(2,1)S(1)}, bf16[256,256]{1,0:T(8,128)(2,1)S(1)}, u32[]{:S(2)}, u32[]{:S(2)}) collective-permute-start(bf16[256,256]{1,0:T(8,128)(2,1)S(1)} %collective-permute-done.10.refs_1_), channel_id=1, source_target_pairs={{0,16},{16,0},{1,17},{17,1},{2,18},{18,2},{3,19},{19,3},{4,20},{20... | collective-permute-start | bytes 393224 | tf_op jit(solution)/shard_map/ppermute | solution.py:327
  43.9 1.0 %collective-permute-done.9.refs_0_ = bf16[256,512]{1,0:T(8,128)(2,1)S(1)} collective-permute-done((bf16[256,512]{1,0:T(8,128)(2,1)S(1)}, bf16[256,512]{1,0:T(8,128)(2,1)S(1)}, u32[]{:S(2)}, u32[]{:S(2)}) %collective-permute-start.9) | collective-permute-done | bytes 262176 | tf_op jit(solution)/shard_map/ppermute | solution.py:369
  44.9 4.2 %shard_map.147 = (f32[512,1024]{1,0:T(8,128)S(1)}, f32[512,1024]{1,0:T(8,128)S(1)}, bf16[512,1024]{1,0:T(8,128)(2,1)S(1)}) custom-call(s32[4]{0:T(128)S(1)} %pad_add_fusion.info, bf16[512,1024]{1,0:T(8,128)(2,1)S(1)} %get-tuple-element.53.q_ref, f32[512,1024]{1,0:T(8,128)S(1)} %get-tuple-element.63.num_in, ...), custom_call_target="tpu_custom_call", output_to_operand_aliasing={{0}: (2, {}), {1}: (3, {})} | custom-call | flops 4294967296 | bytes 4194304 | tf_op jit(solution)/shard_map/pallas_call | solution.py:294
  49.2 1.7 %shard_map.148 = (f32[512,1024]{1,0:T(8,128)S(1)}, f32[512,1024]{1,0:T(8,128)S(1)}, bf16[512,1024]{1,0:T(8,128)(2,1)S(1)}) custom-call(s32[4]{0:T(128)S(1)} %pad_add_fusion.info, bf16[512,1024]{1,0:T(8,128)(2,1)S(1)} %get-tuple-element.53.q_ref, ...), custom_call_target="tpu_custom_call", output_to_operand_aliasing={{0}: (2, {}), {1}: (3, {}), {2}: (5, {})} | custom-call | flops 1073741824 | bytes 4194304 | tf_op jit(solution)/shard_map/pallas_call | solution.py:294
  50.9 3.2 %collective-permute-start.14 = (bf16[512,1024]{1,0:T(8,128)(2,1)S(1)}, bf16[512,1024]{1,0:T(8,128)(2,1)S(1)}, u32[]{:S(2)}, u32[]{:S(2)}) collective-permute-start(bf16[512,1024]{1,0:T(8,128)(2,1)S(1)} %get-tuple-element.71.heads), channel_id=1, source_target_pairs={{0,1},{1,0},{2,3},{3,2},{4,5},{5,4},{6,7},{7,6},{8,9},{9,8},{10,11... | collective-permute-start | bytes 3145736 | tf_op jit(solution)/shard_map/ppermute | solution.py:328
  54.1 2.9 %shard_map.149.mixed_ref = f32[512,2048]{1,0:T(8,128)S(1)} custom-call(s32[4]{0:T(128)S(1)} %pad_add_fusion.info, bf16[512,1024]{1,0:T(8,128)(2,1)S(1)} %get-tuple-element.71.heads, bf16[1024,4096]{1,0:T(8,128)(2,1)S(1)} %bitcast.9), custom_call_target="tpu_custom_call" | custom-call | flops 2147483648 | bytes 4194304 | tf_op jit(solution)/shard_map/pallas_call | solution.py:294
  57.1 3.7 %shard_map.150 = (bf16[256,2048]{1,0:T(8,128)(2,1)}, bf16[256,2048]{1,0:T(8,128)(2,1)}) custom-call(s32[4]{0:T(128)S(1)} %pad_add_fusion.info, s32[4]{0:T(128)S(1)} %bitcast.12, bf16[512,1024]{1,0:T(8,128)(2,1)S(1)} %collective-permute-done.14.heads, f32[512,2048]{1,0:T(8,128)S(1)} %shard_map.149.mixed_ref, bf16[1024,2048]{1,0:T(8,128)(2,1)S(1)} %collective-permute-done.15.w_far), custom_call_target="tpu_custom_call" | custom-call | flops 2147483648 | bytes 4194304 | tf_op jit(solution)/shard_map/pallas_call | solution.py:294
  (33 shorter events, 3.4 us)
Async XLA Ops:
  2.2 3.7 %collective-permute-start.1 = (f32[1,256]{1,0:T(1,128)S(1)}, f32[1,256]{1,0:T(1,128)S(1)}, u32[]{:S(2)}, u32[]{:S(2)}) collective-permute-start(f32[1,256]{1,0:T(1,128)S(1)} %get-tuple-element.41.own_ref), channel_id=1, source_target_pairs={{0,16},{16,0},{1,17},{17,1},{2,18},{18,2},{3,19},{19,3},{4,20},{20... | collective-permute-start | bytes 3080 | tf_op jit(solution)/shard_map/ppermute | solution.py:327
  3.5 12.5 %collective-permute-start = (bf16[128,2048]{1,0:T(8,128)(2,1)S(1)}, bf16[128,2048]{1,0:T(8,128)(2,1)S(1)}, u32[]{:S(2)}, u32[]{:S(2)}) collective-permute-start(bf16[128,2048]{1,0:T(8,128)(2,1)S(1)} %get-tuple-element.39), channel_id=1, source_target_pairs={{0,16},{16,0},{1,17},{17,1},{2,18},{18,2},{3,19},{19,3},{4,20},{20... | collective-permute-start | bytes 1572872 | tf_op jit(solution)/shard_map/ppermute | solution.py:327
  5.9 13.5 %copy-start = (f32[128]{0:T(128)S(1)}, f32[128]{0:T(128)}, u32[]{:S(2)}) copy-start(f32[128]{0:T(128)} %param.22) | copy-start | bytes 1540
  16.0 3.4 %collective-permute-start.2 = (bf16[128,2048]{1,0:T(8,128)(2,1)S(1)}, bf16[128,2048]{1,0:T(8,128)(2,1)S(1)}, u32[]{:S(2)}, u32[]{:S(2)}) collective-permute-start(bf16[128,2048]{1,0:T(8,128)(2,1)S(1)} %collective-permute-done.near_ref), channel_id=1, source_target_pairs={{0,1},{1,0},{2,3},{3,2},{4,5},{5,4},{6,7},{7,6},{8,9},{9,8},{10,11... | collective-permute-start | bytes 1572872 | tf_op jit(solution)/shard_map/ppermute | solution.py:328
  19.4 3.5 %copy-start.2 = (f32[128]{0:T(128)S(1)}, f32[128]{0:T(128)}, u32[]{:S(2)}) copy-start(f32[128]{0:T(128)} %param.21) | copy-start | bytes 1540
  20.9 36.2 %collective-permute-start.15 = (bf16[1024,2048]{1,0:T(8,128)(2,1)S(1)}, bf16[1024,2048]{1,0:T(8,128)(2,1)S(1)}, u32[]{:S(2)}, u32[]{:S(2)}) collective-permute-start(bf16[1024,2048]{1,0:T(8,128)(2,1)S(1)} %get-tuple-element.73), channel_id=1, source_target_pairs={{0,1},{1,0},{2,3},{3,2},{4,5},{5,4},{6,7},{7,6},{8,9},{9,8},{10,11... | collective-permute-start | bytes 12582920 | tf_op jit(solution)/shard_map/ppermute | solution.py:328
  21.3 16.4 %collective-permute-start.4 = (bf16[256,512]{1,0:T(8,128)(2,1)S(1)}, bf16[256,512]{1,0:T(8,128)(2,1)S(1)}, u32[]{:S(2)}, u32[]{:S(2)}) collective-permute-start(bf16[256,512]{1,0:T(8,128)(2,1)S(1)} %get-tuple-element.49.kv_ref), channel_id=1, source_target_pairs={{0,4},{2,6},{4,0},{6,2},{8,12},{10,14},{12,8},{14,10},{1,5},{3,7},... | collective-permute-start | bytes 786440 | tf_op jit(solution)/shard_map/ppermute | solution.py:369
  21.5 11.3 %collective-permute-start.3 = (bf16[256,512]{1,0:T(8,128)(2,1)S(1)}, bf16[256,512]{1,0:T(8,128)(2,1)S(1)}, u32[]{:S(2)}, u32[]{:S(2)}) collective-permute-start(bf16[256,512]{1,0:T(8,128)(2,1)S(1)} %get-tuple-element.49.kv_ref), channel_id=1, source_target_pairs={{0,2},{2,0},{4,6},{6,4},{8,10},{10,8},{12,14},{14,12},{1,3},{3,1},... | collective-permute-start | bytes 786440 | tf_op jit(solution)/shard_map/ppermute | solution.py:369
  22.7 9.8 %collective-permute-start.5 = (bf16[256,256]{1,0:T(8,128)(2,1)S(1)}, bf16[256,256]{1,0:T(8,128)(2,1)S(1)}, u32[]{:S(2)}, u32[]{:S(2)}) collective-permute-start(bf16[256,256]{1,0:T(8,128)(2,1)S(1)} %get-tuple-element.61), channel_id=1, source_target_pairs={{0,8},{2,10},{4,12},{6,14},{8,0},{10,2},{12,4},{14,6},{1,9},{3,11}... | collective-permute-start | bytes 393224 | tf_op jit(solution)/shard_map/ppermute | solution.py:369
  26.7 7.8 %collective-permute-start.6 = (bf16[256,256]{1,0:T(8,128)(2,1)S(1)}, bf16[256,256]{1,0:T(8,128)(2,1)S(1)}, u32[]{:S(2)}, u32[]{:S(2)}) collective-permute-start(bf16[256,256]{1,0:T(8,128)(2,1)S(1)} %get-tuple-element.61), channel_id=1, source_target_pairs={{0,12},{2,14},{4,8},{6,10},{8,4},{10,6},{12,0},{14,2},{1,13},{3,15... | collective-permute-start | bytes 393224 | tf_op jit(solution)/shard_map/ppermute | solution.py:369
  32.5 3.9 %collective-permute-start.7 = (bf16[256,256]{1,0:T(8,128)(2,1)S(1)}, bf16[256,256]{1,0:T(8,128)(2,1)S(1)}, u32[]{:S(2)}, u32[]{:S(2)}) collective-permute-start(bf16[256,256]{1,0:T(8,128)(2,1)S(1)} %collective-permute-done.5.refs_1_), channel_id=1, source_target_pairs={{0,2},{2,0},{4,6},{6,4},{8,10},{10,8},{12,14},{14,12},{1,3},{3,1},... | collective-permute-start | bytes 393224 | tf_op jit(solution)/shard_map/ppermute | solution.py:369
  32.8 5.2 %collective-permute-start.8 = (bf16[256,256]{1,0:T(8,128)(2,1)S(1)}, bf16[256,256]{1,0:T(8,128)(2,1)S(1)}, u32[]{:S(2)}, u32[]{:S(2)}) collective-permute-start(bf16[256,256]{1,0:T(8,128)(2,1)S(1)} %collective-permute-done.5.refs_1_), channel_id=1, source_target_pairs={{0,16},{16,0},{1,17},{17,1},{2,18},{18,2},{3,19},{19,3},{4,20},{20... | collective-permute-start | bytes 393224 | tf_op jit(solution)/shard_map/ppermute | solution.py:327
  34.5 9.4 %collective-permute-start.11 = (bf16[256,256]{1,0:T(8,128)(2,1)S(1)}, bf16[256,256]{1,0:T(8,128)(2,1)S(1)}, u32[]{:S(2)}, u32[]{:S(2)}) collective-permute-start(bf16[256,256]{1,0:T(8,128)(2,1)S(1)} %collective-permute-done.6.refs_2_), channel_id=1, source_target_pairs={{0,16},{16,0},{1,17},{17,1},{2,18},{18,2},{3,19},{19,3},{4,20},{20... | collective-permute-start | bytes 393224 | tf_op jit(solution)/shard_map/ppermute | solution.py:327
  36.4 6.2 %collective-permute-start.10 = (bf16[256,256]{1,0:T(8,128)(2,1)S(1)}, bf16[256,256]{1,0:T(8,128)(2,1)S(1)}, u32[]{:S(2)}, u32[]{:S(2)}) collective-permute-start(bf16[256,256]{1,0:T(8,128)(2,1)S(1)} %collective-permute-done.6.refs_2_), channel_id=1, source_target_pairs={{0,2},{2,0},{4,6},{6,4},{8,10},{10,8},{12,14},{14,12},{1,3},{3,1},... | collective-permute-start | bytes 393224 | tf_op jit(solution)/shard_map/ppermute | solution.py:369
  37.7 6.2 %collective-permute-start.12 = (bf16[256,256]{1,0:T(8,128)(2,1)S(1)}, bf16[256,256]{1,0:T(8,128)(2,1)S(1)}, u32[]{:S(2)}, u32[]{:S(2)}) collective-permute-start(bf16[256,256]{1,0:T(8,128)(2,1)S(1)} %collective-permute-done.7.refs_3_), channel_id=1, source_target_pairs={{0,16},{16,0},{1,17},{17,1},{2,18},{18,2},{3,19},{19,3},{4,20},{20... | collective-permute-start | bytes 393224 | tf_op jit(solution)/shard_map/ppermute | solution.py:327
  38.0 7.0 %collective-permute-start.9 = (bf16[256,512]{1,0:T(8,128)(2,1)S(1)}, bf16[256,512]{1,0:T(8,128)(2,1)S(1)}, u32[]{:S(2)}, u32[]{:S(2)}) collective-permute-start(bf16[256,512]{1,0:T(8,128)(2,1)S(1)} %collective-permute-done.4.refs_0_), channel_id=1, source_target_pairs={{0,2},{2,0},{4,6},{6,4},{8,10},{10,8},{12,14},{14,12},{1,3},{3,1},... | collective-permute-start | bytes 786440 | tf_op jit(solution)/shard_map/ppermute | solution.py:369
  38.2 16.0 %slice-start = ((s8[8388608]{0:T(1024)(128)(4,1)}), s8[4194304]{0:T(1024)(128)(4,1)S(1)}, s32[]{:S(2)}) async-start(s8[8388608]{0:T(1024)(128)(4,1)} %bitcast.8), calls=%async_computation | async-start | bytes 8388608
  42.6 6.5 %collective-permute-start.13 = (bf16[256,256]{1,0:T(8,128)(2,1)S(1)}, bf16[256,256]{1,0:T(8,128)(2,1)S(1)}, u32[]{:S(2)}, u32[]{:S(2)}) collective-permute-start(bf16[256,256]{1,0:T(8,128)(2,1)S(1)} %collective-permute-done.10.refs_1_), channel_id=1, source_target_pairs={{0,16},{16,0},{1,17},{17,1},{2,18},{18,2},{3,19},{19,3},{4,20},{20... | collective-permute-start | bytes 393224 | tf_op jit(solution)/shard_map/ppermute | solution.py:327
  44.9 9.2 %slice-start.1 = ((s8[8388608]{0:T(1024)(128)(4,1)}), s8[4194304]{0:T(1024)(128)(4,1)S(1)}, s32[]{:S(2)}) async-start(s8[8388608]{0:T(1024)(128)(4,1)} %bitcast.8), calls=%async_computation.1 | async-start | bytes 8388608
  50.9 6.2 %copy-start.1 = (s32[1,4]{1,0:T(1,128)S(1)}, s32[1,4]{1,0:T(1,128)}, u32[]{:S(2)}) copy-start(s32[1,4]{1,0:T(1,128)} %param.24) | copy-start | bytes 52
  50.9 6.2 %collective-permute-start.14 = (bf16[512,1024]{1,0:T(8,128)(2,1)S(1)}, bf16[512,1024]{1,0:T(8,128)(2,1)S(1)}, u32[]{:S(2)}, u32[]{:S(2)}) collective-permute-start(bf16[512,1024]{1,0:T(8,128)(2,1)S(1)} %get-tuple-element.71.heads), channel_id=1, source_target_pairs={{0,1},{1,0},{2,3},{3,2},{4,5},{5,4},{6,7},{7,6},{8,9},{9,8},{10,11... | collective-permute-start | bytes 3145736 | tf_op jit(solution)/shard_map/ppermute | solution.py:328
